TPU v7x, 32 devices: a whole 2x2x4 slice. The times are simulated.
32 devices in a mesh: opair: 8 (over z, core), vpair: 4 (over y, x).
Axes of the slice: x: 2, y: 2, z: 4, core: 2. Of those that a mesh axis runs over, the one named last changes fastest.
Arguments:
- amplitudes: bfloat16 [2048, 4096], P('opair', 'vpair'), may hold values from -6 to 6
- tile_live: int32 [16, 32], P('opair', 'vpair'), may hold values 0 or 1
- integrals: bfloat16 [32, 24, 128, 128], P('vpair', 'opair'), may hold values from -0.109375 to 0.109375
- integral_columns: int32 [32, 24], P('vpair', 'opair'), may hold values from 0 to 31, as said below
- driver_terms: bfloat16 [2048, 4096], P('opair', 'vpair'), may hold values from -6 to 6
- occupied_energy: float32 [2048], P('opair'), may hold values from -3 to -0.8
- virtual_energy: float32 [4096], P('vpair'), may hold values from 0.4 to 4
Outputs:
- new_amplitudes: bfloat16 [2048, 4096], P('opair', 'vpair')
- residual: float32 [2048, 4096], P('opair', 'vpair')
Inputs may be any that keep to these rules, and one draw needn't show every extreme that they name: `integral_columns`: the 24 entries of one row are distinct. Of the 24 entries that one device holds, at most 6 name column tiles of one index d of vpair (tiles d * 8 to d * 8 + 7), and on every device some index of vpair is named exactly 6 times.
All inputs are finite; a program needn't handle non-finite values. No bound on the sum of `tile_live` on one device may be relied on, other than what follows from the above.
Results may differ from a plain program's by a relative error of at most 0.015.
Values may be sent and summed in bfloat16 or wider, within the bound.
No kernel may reach another device: no remote copies, remote signals or barrier semaphores. Data moves between devices by JAX's collectives and lax.ppermute only.
A program may use at most 128 MiB of HBM per device.

v0:
```python
import jax
import jax.numpy as jnp
from jax import lax
from jax.sharding import PartitionSpec as P


def on_device(
    amplitudes,
    tile_live,
    integrals,
    integral_columns,
    driver_terms,
    occupied_energy,
    virtual_energy,
):
    row_count, total_width = amplitudes.shape
    tile_size = integrals.shape[-1]
    local_rows, local_cols = tile_live.shape
    live_mask = jnp.broadcast_to(
        tile_live[:, None, :, None].astype(jnp.float32),
        (local_rows, tile_size, local_cols, tile_size),
    ).reshape(row_count, total_width)
    masked = (amplitudes.astype(jnp.float32) * live_mask).astype(jnp.bfloat16)
    masked_tiles = masked.reshape(row_count, local_cols, tile_size)
    gathered, tile_columns = (
        lax.all_gather(integrals, "opair", axis=1, tiled=True),
        lax.all_gather(integral_columns, "opair", axis=1, tiled=True),
    )
    first_tile = jnp.int32(0)
    tile_span = lax.axis_size("vpair") * local_cols
    term = jnp.zeros((tile_span, row_count, tile_size), jnp.float32)
    for source in range(local_cols):
        products = jnp.einsum(
            "rx,kxy->kry",
            masked_tiles[:, source, :],
            gathered[source],
            preferred_element_type=jnp.float32,
        )
        offsets = tile_columns[source] - first_tile
        inside = (offsets >= 0) & (offsets < tile_span)
        landing = jnp.where(inside, offsets, tile_span).astype(jnp.int32)
        term = term.at[landing].add(products, mode="drop")
    ladder_tiles = lax.psum_scatter(
        term.astype(jnp.bfloat16), "vpair", scatter_dimension=0, tiled=True
    ).astype(jnp.float32)
    ladder = ladder_tiles.transpose(1, 0, 2).reshape(row_count, total_width)
    denominator = occupied_energy[:, None] - virtual_energy[None, :]
    residual = (
        driver_terms.astype(jnp.float32) + ladder + denominator * amplitudes.astype(jnp.float32)
    ) * live_mask
    new_amplitudes = (masked.astype(jnp.float32) - residual / denominator).astype(jnp.bfloat16)
    return (new_amplitudes, residual)


def solution(mesh):
    in_specs = (
        P("opair", "vpair"),
        P("opair", "vpair"),
        P("vpair", "opair", None, None),
        P("vpair", "opair"),
        P("opair", "vpair"),
        P("opair"),
        P("vpair"),
    )
    out_specs = (P("opair", "vpair"), P("opair", "vpair"))
    return jax.shard_map(
        on_device, mesh=mesh, in_specs=in_specs, out_specs=out_specs, check_vma=False
    )
```

profile of v0, /device:TPU:0, one launch (start us, length us, event | category | flops | bytes accessed | tf_op | source)
XLA Modules:
  0.0 217.8 jit_solution(14649667180381538154)
XLA Ops:
  10.0 14.5 %all-gather = s32[8,3,8]{2,1,0:T(4,128)S(1)} all-gather(s32[1,3,8]{2,1,0:T(4,128)} %bitcast.143), channel_id=1, replica_groups=mesh['opair'=8,'vpair'=4] {'opair'}, dimensions={0}, use_global_device_ids=true | all-gather | bytes 864 | tf_op jit(solution)/shard_map/all_gather | solution.py:27
  27.1 50.0 %all-gather.3.cloned.1.call-done = bf16[8,24,128,128]{3,2,1,0:T(8,128)(2,1)} async-done(((bf16[8,3,128,128]{3,2,1,0:T(8,128)(2,1)}), bf16[8,24,128,128]{3,2,1,0:T(8,128)(2,1)}) %all-gather.3.cloned.1.call-update) | async-done | bytes 6291472 | tf_op jit(solution)/shard_map/all_gather | solution.py:26
  77.1 1.8 convolution_bitcast_fusion.7
  78.8 2.5 %broadcast_in_dim.14 = f32[32,256,128]{2,1,0:T(8,128)} broadcast(f32[]{:T(128)} %constant.3.clone.1), dimensions={} | broadcast | bytes 4194308 | tf_op jit(solution)/shard_map/broadcast_in_dim | solution.py:31
  81.3 8.5 %scatter_fusion = f32[32,256,128]{2,1,0:T(8,128)} fusion(f32[32,256,128]{2,1,0:T(8,128)} %broadcast_in_dim.14, s32[24]{0:T(128)S(1)} %get-tuple-element.18, f32[24,256,128]{2,1,0:T(8,128)S(1)} %convolution_bitcast_fusion.7), kind=kCustom, calls=%fused_computation | custom fusion | flops 786432 | bytes 9437280 | tf_op jit(solution)/shard_map/scatter-add | solution.py:42
  89.9 1.8 convolution_bitcast_fusion.6
  91.7 8.5 %scatter_fusion.1 = f32[32,256,128]{2,1,0:T(8,128)} fusion(f32[32,256,128]{2,1,0:T(8,128)} %scatter_fusion, s32[24]{0:T(128)S(1)} %get-tuple-element.19, f32[24,256,128]{2,1,0:T(8,128)S(1)} %convolution_bitcast_fusion.6), kind=kCustom, calls=%fused_computation.1 | custom fusion | flops 786432 | bytes 9437280 | tf_op jit(solution)/shard_map/scatter-add | solution.py:42
  100.2 1.8 convolution_bitcast_fusion.5
  102.0 8.5 %scatter_fusion.2 = f32[32,256,128]{2,1,0:T(8,128)} fusion(f32[32,256,128]{2,1,0:T(8,128)} %scatter_fusion.1, s32[24]{0:T(128)S(1)} %get-tuple-element.20, f32[24,256,128]{2,1,0:T(8,128)S(1)} %convolution_bitcast_fusion.5), kind=kCustom, calls=%fused_computation.2 | custom fusion | flops 786432 | bytes 9437280 | tf_op jit(solution)/shard_map/scatter-add | solution.py:42
  110.5 1.8 convolution_bitcast_fusion.4
  112.3 8.5 %scatter_fusion.3 = f32[32,256,128]{2,1,0:T(8,128)} fusion(f32[32,256,128]{2,1,0:T(8,128)} %scatter_fusion.2, s32[24]{0:T(128)S(1)} %get-tuple-element.21, f32[24,256,128]{2,1,0:T(8,128)S(1)} %convolution_bitcast_fusion.4), kind=kCustom, calls=%fused_computation.3 | custom fusion | flops 786432 | bytes 9437280 | tf_op jit(solution)/shard_map/scatter-add | solution.py:42
  120.7 1.8 convolution_bitcast_fusion.3
  122.5 8.6 %scatter_fusion.4 = f32[32,256,128]{2,1,0:T(8,128)} fusion(f32[32,256,128]{2,1,0:T(8,128)} %scatter_fusion.3, s32[24]{0:T(128)S(1)} %get-tuple-element.22, f32[24,256,128]{2,1,0:T(8,128)S(1)} %convolution_bitcast_fusion.3), kind=kCustom, calls=%fused_computation.4 | custom fusion | flops 786432 | bytes 9437280 | tf_op jit(solution)/shard_map/scatter-add | solution.py:42
  131.1 1.8 convolution_bitcast_fusion.2
  132.8 8.4 %scatter_fusion.5 = f32[32,256,128]{2,1,0:T(8,128)} fusion(f32[32,256,128]{2,1,0:T(8,128)} %scatter_fusion.4, s32[24]{0:T(128)S(1)} %get-tuple-element.23, f32[24,256,128]{2,1,0:T(8,128)S(1)} %convolution_bitcast_fusion.2), kind=kCustom, calls=%fused_computation.5 | custom fusion | flops 786432 | bytes 9437280 | tf_op jit(solution)/shard_map/scatter-add | solution.py:42
  141.2 1.8 convolution_bitcast_fusion.1
  142.9 8.6 %scatter_fusion.6 = f32[32,256,128]{2,1,0:T(8,128)} fusion(f32[32,256,128]{2,1,0:T(8,128)} %scatter_fusion.5, s32[24]{0:T(128)S(1)} %get-tuple-element.24, f32[24,256,128]{2,1,0:T(8,128)S(1)} %convolution_bitcast_fusion.1), kind=kCustom, calls=%fused_computation.6 | custom fusion | flops 786432 | bytes 9437280 | tf_op jit(solution)/shard_map/scatter-add | solution.py:42
  153.4 8.7 %scatter_fusion.7 = f32[32,256,128]{2,1,0:T(8,128)} fusion(f32[32,256,128]{2,1,0:T(8,128)} %scatter_fusion.6, s32[24]{0:T(128)S(1)} %get-tuple-element.25, f32[24,256,128]{2,1,0:T(8,128)S(1)} %convolution_bitcast_fusion), kind=kCustom, calls=%fused_computation.7 | custom fusion | flops 786432 | bytes 9437280 | tf_op jit(solution)/shard_map/scatter-add | solution.py:42
  162.0 3.9 %convert_element_type.29 = bf16[32,256,128]{2,1,0:T(8,128)(2,1)} convert(f32[32,256,128]{2,1,0:T(8,128)} %scatter_fusion.7) | non-fusion elementwise | flops 1048576 | bytes 6291456 | tf_op jit(solution)/shard_map/convert_element_type | solution.py:44
  167.0 33.0 %reduce-scatter.2.cloned.1.call-done = bf16[8,256,128]{2,1,0:T(8,128)(2,1)} async-done(((bf16[32,256,128]{2,1,0:T(8,128)(2,1)}), bf16[8,256,128]{2,1,0:T(8,128)(2,1)}) %reduce-scatter.2.cloned.1.call-update) | async-done | bytes 524304 | tf_op jit(solution)/shard_map/reduce_scatter | solution.py:43
  200.0 2.1 convert_bitcast_fusion
  203.7 2.8 %fusion.4 = (bf16[256,1024]{0,1:T(8,128)(2,1)}, f32[256,1024]{0,1:T(8,128)}) fusion(bf16[256,1024]{0,1:T(8,128)(2,1)S(1)} %copy-done.2, f32[1024]{0:T(1024)S(1)} %copy-done.6, f32[256]{0:T(256)S(1)} %copy-done.7, f32[128,8,2,128]{3,2,1,0:T(2,128)S(1)} %bitcast.133, bf16[256,1024]{0,1:T(8,128)(2,1)S(1)} %copy-done.4, f32[256,8,128]{0,2,1:T(8,128)S(1)} %copy.49, ...), kind=kLoop, calls=%fused_computation.23 | loop fusion | flops 2883584 | bytes 5248000 | tf_op jit(solution)/shard_map/convert_element_type | solution.py:51
  206.4 2.5 %copy.51 = f32[256,1024]{1,0:T(8,128)} copy(f32[256,1024]{0,1:T(8,128)} %get-tuple-element.17) | data formatting | bytes 2097152
  209.0 2.0 copy.50
  (34 shorter events, 9.7 us)
Async XLA Ops:
  7.2 69.9 %all-gather.3.cloned.1.call-start = ((), (), s32[]{:S(2)}) async-start(), calls=%async_computation.1 | async-start | bytes 7077888 | tf_op jit(solution)/shard_map/all_gather | solution.py:26
  7.9 192.1 %reduce-scatter.2.cloned.1.call-start = ((), (), s32[]{:S(2)}) async-start(), calls=%async_computation.2 | async-start | bytes 2621440 | tf_op jit(solution)/shard_map/reduce_scatter | solution.py:43
  10.0 67.1 %copy-start.3 = (bf16[256,1024]{0,1:T(8,128)(2,1)}, bf16[256,1024]{0,1:T(8,128)(2,1)S(1)}, u32[]{:S(2)}) copy-start(bf16[256,1024]{0,1:T(8,128)(2,1)S(1)} %copy.38) | copy-start | bytes 1572868
  25.2 1.0 copy-start
  162.0 4.0 %copy-start.5 = (bf16[256,1024]{1,0:T(8,128)(2,1)S(1)}, bf16[256,1024]{1,0:T(8,128)(2,1)}, u32[]{:S(2)}) copy-start(bf16[256,1024]{1,0:T(8,128)(2,1)} %param.11) | copy-start | bytes 1572868
  165.9 37.7 %copy-start.1 = (f32[2,128,8,128]{1,0,3,2:T(2,128)S(1)}, f32[2,128,8,128]{1,0,3,2:T(2,128)}, u32[]{:S(2)}) copy-start(f32[2,128,8,128]{1,0,3,2:T(2,128)} %copy-done) | copy-start | bytes 3145732
  165.9 37.7 %copy-start.2 = (bf16[256,1024]{0,1:T(8,128)(2,1)S(1)}, bf16[256,1024]{0,1:T(8,128)(2,1)}, u32[]{:S(2)}) copy-start(bf16[256,1024]{0,1:T(8,128)(2,1)} %fusion) | copy-start | bytes 1572868
  165.9 37.7 %copy-start.4 = (bf16[256,1024]{0,1:T(8,128)(2,1)S(1)}, bf16[256,1024]{0,1:T(8,128)(2,1)}, u32[]{:S(2)}) copy-start(bf16[256,1024]{0,1:T(8,128)(2,1)} %copy-done.3) | copy-start | bytes 1572868
  165.9 37.7 %copy-start.6 = (f32[1024]{0:T(1024)S(1)}, f32[1024]{0:T(1024)}, u32[]{:S(2)}) copy-start(f32[1024]{0:T(1024)} %param.13) | copy-start | bytes 12292
  165.9 37.7 %copy-start.7 = (f32[256]{0:T(256)S(1)}, f32[256]{0:T(256)}, u32[]{:S(2)}) copy-start(f32[256]{0:T(256)} %param.12) | copy-start | bytes 3076
Sparse Core Ops, SparseCore 0:
  9.6 67.4 all-gather.2
  166.1 33.8 reduce-scatter.1
where the time goes:
time: 219 us; the launch traced here: 218 us
  waiting for transfers between devices  83.6 us (38%)
  other arithmetic  78.7 us (36%)
  blocking collectives  14.5 us (7%)
  between operations  14.2 us (6%)
  matrix products  14.1 us (6%)
  local copies, waits for them, and re-layouts  12.6 us (6%)
    scatter-add x8, other arithmetic, on_device(): term = term.at[landing].add(products, mode='drop')  68.3 us
    all_gather x1, waiting for transfers between devices, on_device(): lax.all_gather(integrals, 'opair', axis=1, tiled=True)  50 us
    reduce_scatter x1, waiting for transfers between devices, on_device(): lax.psum_scatter(term.astype(jnp.bfloat16), 'vpair', scatter_dimension=0,...  33 us
    all_gather x1, blocking collectives, on_device(): lax.all_gather(integral_columns, 'opair', axis=1, tiled=True)  14.5 us
    dot_general x8, matrix products, on_device(): jnp.einsum('rx,kxy->kry', masked_tiles[:, source, :], gathered[source], p...  14.1 us
    unnamed x21, local copies, waits for them, and re-layouts  7.82 us
  transfers between devices with their start and end apart: 2, of which 2 were waited for; matrix products, arithmetic and copies ran while one was open for 2% of the time, Pallas kernels for 0%

commit v1 on v0

v1 whole, which is shorter than its diff:
```python
import functools

import jax
import jax.numpy as jnp
from jax import lax
from jax.experimental import pallas as pl
from jax.experimental.pallas import tpu as pltpu
from jax.sharding import PartitionSpec as P

VMEM_BYTES = 56 * 1024 * 1024
CORES = 2


def pack_kernel(n_v, columns, live, integrals, amplitudes, *refs):
    packed, masked, counts, sems = refs[:n_v], refs[n_v], refs[n_v + 1], refs[n_v + 2]
    rows, slots, tile, _ = integrals.shape
    me = lax.axis_index("vpair")
    for j in range(n_v):
        counts[j] = 0

    def send(entry, carry):
        row, slot = lax.div(entry, slots), lax.rem(entry, slots)
        partner = lax.div(columns[entry], rows) ^ me
        place = counts[partner]
        counts[partner] = place + 1
        for j in range(n_v):

            @pl.when(partner == j)
            def _():
                pltpu.make_async_copy(
                    integrals.at[row, slot], packed[j].at[place], sems.at[entry]
                ).start()

        return carry

    lax.fori_loop(0, rows * slots, send, 0)
    for o in range(live.shape[0]):
        for c in range(live.shape[1]):
            at = (pl.ds(o * tile, tile), pl.ds(c * tile, tile))
            kept = live[o, c].astype(jnp.float32)
            masked[at] = (amplitudes[at].astype(jnp.float32) * kept).astype(masked.dtype)

    def finish(entry, carry):
        pltpu.make_async_copy(integrals.at[0, 0], packed[0].at[0], sems.at[entry]).wait()
        return carry

    lax.fori_loop(0, rows * slots, finish, 0)


def ladder_kernel(n_v, n_z, n_groups, cap, table, *refs):
    n_steps = 2 * n_z - 1
    n_shards = n_groups * n_steps
    group = n_v // n_groups
    own_a, refs = refs[:n_v], refs[n_v:]
    twin_a, refs = refs[:n_v], refs[n_v:]
    shards, refs = refs[:n_shards], refs[n_shards:]
    own_out, twin_out, a_buf, tile_buf, total, a_sems, tile_sems = refs
    n_rows, _ = own_a[0].shape
    tile = tile_buf.shape[-1]
    col_tiles = own_out.shape[0]
    v = lax.axis_index("vpair")
    o = lax.axis_index("opair")
    z, core = lax.div(o, CORES), lax.rem(o, CORES)

    def source_z(step):
        return jnp.where(step < n_z, z - step, z + step - n_z + 1)

    def valid(step):
        return (source_z(step) >= 0) & (source_z(step) < n_z)

    a_copies = []
    for j in range(n_v):
        for half, ref in ((0, own_a[j]), (1, twin_a[j])):
            copy = pltpu.make_async_copy(
                ref, a_buf.at[j, pl.ds(half * n_rows, n_rows)], a_sems.at[2 * j + half]
            )
            copy.start()
            a_copies.append(copy)
    for i in range(n_shards):

        @pl.when(valid(i % n_steps))
        def _(i=i):
            pltpu.make_async_copy(shards[i], tile_buf.at[i], tile_sems.at[i]).start()

    total[...] = jnp.zeros_like(total)
    for copy in a_copies:
        copy.wait()

    def one_shard(i, carry):
        step = lax.rem(i, n_steps)

        @pl.when(valid(step))
        def _():
            pltpu.make_async_copy(shards[0], tile_buf.at[i], tile_sems.at[i]).wait()
            for member in range(group):
                j = lax.div(i, n_steps) * group + member
                device = (source_z(step) * CORES + core) * n_v + (v ^ j)

                def one_entry(entry, place):
                    column = table[device, entry]
                    hit = lax.div(column, col_tiles) == v

                    @pl.when(hit)
                    def _():
                        row = lax.div(entry, table.shape[1] // col_tiles)
                        left = a_buf[j, :, pl.ds(pl.multiple_of(row * tile, tile), tile)]
                        total[lax.rem(column, col_tiles)] += jnp.dot(
                            left,
                            tile_buf[i, member * cap + place],
                            preferred_element_type=jnp.float32,
                        )

                    return place + hit.astype(jnp.int32)

                lax.fori_loop(0, table.shape[1], one_entry, 0)

        return carry

    lax.fori_loop(0, n_shards, one_shard, 0)
    own_out[...] = total[:, :n_rows]
    twin_out[...] = total[:, n_rows:].astype(twin_out.dtype)


def update_kernel(live, amplitudes, driver, own, twin, occupied, virtual, new, residual):
    tile = own.shape[-1]
    for o in range(live.shape[0]):
        for c in range(live.shape[1]):
            rows = pl.ds(o * tile, tile)
            at = (rows, pl.ds(c * tile, tile))
            kept = live[o, c].astype(jnp.float32)
            amps = amplitudes[at].astype(jnp.float32)
            masked = (amps * kept).astype(jnp.bfloat16).astype(jnp.float32)
            ladder = own[c, rows] + twin[c, rows].astype(jnp.float32)
            denominator = occupied[rows, :] - virtual[:, pl.ds(c * tile, tile)]
            rest = (driver[at].astype(jnp.float32) + ladder + denominator * amps) * kept
            residual[at] = rest
            new[at] = (masked - rest / denominator).astype(new.dtype)


def on_device(
    amplitudes,
    tile_live,
    integrals,
    integral_columns,
    driver_terms,
    occupied_energy,
    virtual_energy,
):
    n_rows, width = amplitudes.shape
    row_tiles, slots, tile, _ = integrals.shape
    n_v, n_o = lax.axis_size("vpair"), lax.axis_size("opair")
    n_z = n_o // CORES
    entries = row_tiles * slots
    cap = -(-entries // n_v)
    n_groups = min(n_v, 4)
    group = n_v // n_groups
    in_smem = pl.BlockSpec(memory_space=pltpu.SMEM)
    in_vmem = pl.BlockSpec(memory_space=pltpu.VMEM)
    anywhere = pl.BlockSpec(memory_space=pl.ANY)
    flat_columns = integral_columns.reshape(entries)

    *packed, masked = pl.pallas_call(
        functools.partial(pack_kernel, n_v),
        out_shape=[jax.ShapeDtypeStruct((cap, tile, tile), integrals.dtype)] * n_v
        + [jax.ShapeDtypeStruct(amplitudes.shape, amplitudes.dtype)],
        in_specs=[in_smem, in_smem, anywhere, in_vmem],
        out_specs=[anywhere] * n_v + [in_vmem],
        scratch_shapes=[pltpu.SMEM((n_v,), jnp.int32), pltpu.SemaphoreType.DMA((entries,))],
        compiler_params=pltpu.CompilerParams(vmem_limit_bytes=VMEM_BYTES),
        name="pack",
    )(flat_columns, tile_live, integrals, amplitudes)

    table = lax.all_gather(flat_columns, ("opair", "vpair"))

    def across_v(value, j):
        return lax.ppermute(value, "vpair", [(i, i ^ j) for i in range(n_v)]) if j else value

    def across_core(value):
        return lax.ppermute(value, "opair", [(i, i ^ 1) for i in range(n_o)])

    def along_z(value, hop):
        pairs = [(i, i + hop * CORES) for i in range(n_o) if 0 <= i + hop * CORES < n_o]
        return lax.ppermute(value, "opair", pairs)

    chunks = [across_v(packed[j], j) for j in range(n_v)]
    shards = []
    for g in range(n_groups):
        members = chunks[g * group : (g + 1) * group]
        start = members[0] if group == 1 else jnp.concatenate(members)
        shards.append(start)
        for hop in (1, -1):
            moving = start
            for _ in range(n_z - 1):
                moving = along_z(moving, hop)
                shards.append(moving)
    own_a = [across_v(masked, j) for j in range(n_v)]
    twin_a = [across_core(value) for value in own_a]

    own, twin = pl.pallas_call(
        functools.partial(ladder_kernel, n_v, n_z, n_groups, cap),
        out_shape=[
            jax.ShapeDtypeStruct((row_tiles, n_rows, tile), jnp.float32),
            jax.ShapeDtypeStruct((row_tiles, n_rows, tile), jnp.bfloat16),
        ],
        in_specs=[in_smem] + [anywhere] * (2 * n_v + len(shards)),
        out_specs=[in_vmem, in_vmem],
        scratch_shapes=[
            pltpu.VMEM((n_v, CORES * n_rows, width), amplitudes.dtype),
            pltpu.VMEM((len(shards), group * cap, tile, tile), integrals.dtype),
            pltpu.VMEM((row_tiles, CORES * n_rows, tile), jnp.float32),
            pltpu.SemaphoreType.DMA((2 * n_v,)),
            pltpu.SemaphoreType.DMA((len(shards),)),
        ],
        compiler_params=pltpu.CompilerParams(vmem_limit_bytes=VMEM_BYTES),
        name="ladder",
    )(table, *own_a, *twin_a, *shards)
    twin = across_core(twin)

    return pl.pallas_call(
        update_kernel,
        out_shape=[
            jax.ShapeDtypeStruct((n_rows, width), jnp.bfloat16),
            jax.ShapeDtypeStruct((n_rows, width), jnp.float32),
        ],
        in_specs=[in_smem] + [in_vmem] * 6,
        out_specs=[in_vmem, in_vmem],
        compiler_params=pltpu.CompilerParams(vmem_limit_bytes=VMEM_BYTES),
        name="update",
    )(
        tile_live,
        amplitudes,
        driver_terms,
        own,
        twin,
        jnp.broadcast_to(occupied_energy[:, None], (n_rows, tile)),
        virtual_energy.reshape(1, width),
    )


def solution(mesh):
    in_specs = (
        P("opair", "vpair"),
        P("opair", "vpair"),
        P("vpair", "opair", None, None),
        P("vpair", "opair"),
        P("opair", "vpair"),
        P("opair"),
        P("vpair"),
    )
    out_specs = (P("opair", "vpair"), P("opair", "vpair"))
    return jax.shard_map(
        on_device, mesh=mesh, in_specs=in_specs, out_specs=out_specs, check_vma=False
    )
```

time: 219 us -> 230 us (1.050)
  starting transfers between devices: 0.08 us -> 78.8 us
  other arithmetic: 78.7 us -> 0 us
  waiting for transfers between devices: 83.6 us -> 15.8 us
  Pallas kernels: 0 us -> 60.1 us
  blocking collectives: 14.5 us -> 68.7 us
  matrix products: 14.1 us -> 0 us
  between operations: 14.2 us -> 1.33 us
  local copies, waits for them, and re-layouts: 12.6 us -> 4 us
    ppermute x0 -> x35, starting transfers between devices: none -> 78.8 us  [the longest x24 69.9 us: along_z(): return lax.ppermute(value, 'opair', pairs)]
    scatter-add x8 -> x0, other arithmetic: 68.3 us -> none  [on_device(): term = term.at[landing].add(products, mode='drop')]
    pallas_call x0 -> x3, Pallas kernels: none -> 60.1 us  [the longest x1 29.7 us: on_device(): pl.pallas_call(functools.partial(ladder_kernel, n_v, n_z, n_groups, cap),...]
    all_gather x1, blocking collectives: 14.5 us -> 68.7 us  [on_device(): table = lax.all_gather(flat_columns, ('opair', 'vpair'))]
    all_gather x1 -> x0, waiting for transfers between devices: 50 us -> none  [on_device(): lax.all_gather(integrals, 'opair', axis=1, tiled=True)]
    reduce_scatter x1 -> x0, waiting for transfers between devices: 33 us -> none  [on_device(): lax.psum_scatter(term.astype(jnp.bfloat16), 'vpair', scatter_dimension=0,...]
    ppermute x0 -> x35, waiting for transfers between devices: none -> 15.8 us  [the longest x24 13.7 us: along_z(): return lax.ppermute(value, 'opair', pairs)]
    dot_general x8 -> x0, matrix products: 14.1 us -> none  [on_device(): jnp.einsum('rx,kxy->kry', masked_tiles[:, source, :], gathered[source], p...]
  transfers between devices with their start and end apart: 2 -> 35, of which waited for: 2 -> 6; matrix products, arithmetic and copies ran while one was open for 2% -> 0% of each run, Pallas kernels for 0% -> 0%
where the time goes in v1:
time: 230 us; the launch traced here: 229 us
  starting transfers between devices  78.8 us (34%)
  blocking collectives  68.7 us (30%)
  Pallas kernels  60.1 us (26%)
  waiting for transfers between devices  15.8 us (7%)
  local copies, waits for them, and re-layouts  4 us (2%)
    ppermute x24, starting transfers between devices, along_z(): return lax.ppermute(value, 'opair', pairs)  69.9 us
    all_gather x1, blocking collectives, on_device(): table = lax.all_gather(flat_columns, ('opair', 'vpair'))  68.7 us
    pallas_call x1, Pallas kernels, on_device(): pl.pallas_call(functools.partial(ladder_kernel, n_v, n_z, n_groups, cap),...  29.7 us
    pallas_call x1, Pallas kernels, on_device(): pl.pallas_call(functools.partial(pack_kernel, n_v), out_shape=[jax.ShapeD...  27 us
    ppermute x24, waiting for transfers between devices, along_z(): return lax.ppermute(value, 'opair', pairs)  13.7 us
    ppermute x6, starting transfers between devices, across_v(): lax.ppermute(value, 'vpair', [(i, i ^ j) for i in range(n_v)])  8.1 us
  transfers between devices with their start and end apart: 35, of which 6 were waited for; matrix products, arithmetic and copies ran while one was open for 0% of the time, Pallas kernels for 0%

profile of v1, /device:TPU:0, one launch (start us, length us, event | category | flops | bytes accessed | tf_op | source)
XLA Modules:
  0.0 228.8 jit_solution(7588957276191242964)
XLA Ops:
  2.0 27.0 %pack.1 = (bf16[6,128,128]{2,1,0:T(8,128)(2,1)}, bf16[6,128,128]{2,1,0:T(8,128)(2,1)}, bf16[6,128,128]{2,1,0:T(8,128)(2,1)}, bf16[6,128,128]{2,1,0:T(8,128)(2,1)}, bf16[256,1024]{1,0:T(8,128)(2,1)}) custom-call(s32[24]{0:T(128)} %reshape.11.columns, s32[2,8]{1,0:T(2,128)} %live.3, bf16[8,3,128,128]{3,2,1,0:T(8,128)(2,1)} %integrals.1, ...), custom_call_target="tpu_custom_call" | custom-call | tf_op jit(solution)/shard_map/pack/pallas_call | solution.py:162
  29.0 3.0 %collective-permute-start.13 = (bf16[6,128,128]{2,1,0:T(8,128)(2,1)}, bf16[6,128,128]{2,1,0:T(8,128)(2,1)S(1)}, u32[]{:S(2)}, u32[]{:S(2)}) collective-permute-start(bf16[6,128,128]{2,1,0:T(8,128)(2,1)} %get-tuple-element.11), channel_id=1, source_target_pairs={{0,1},{1,0},{2,3},{3,2},{4,5},{5,4},{6,7},{7,6},{8,9},{9,8},{10,11... | collective-permute-start | bytes 589832 | tf_op jit(solution)/shard_map/ppermute | solution.py:176
  32.1 1.5 collective-permute-start.20
  34.9 4.6 %collective-permute-start.7 = (bf16[6,128,128]{2,1,0:T(8,128)(2,1)}, bf16[6,128,128]{2,1,0:T(8,128)(2,1)S(1)}, u32[]{:S(2)}, u32[]{:S(2)}) collective-permute-start(bf16[6,128,128]{2,1,0:T(8,128)(2,1)} %get-tuple-element.10.refs_8_), channel_id=1, source_target_pairs={{0,8},{4,12},{8,16},{12,20},{16,24},{20,28},{1,9},{5,13},{9,17},{1... | collective-permute-start | bytes 589832 | tf_op jit(solution)/shard_map/ppermute | solution.py:183
  39.5 3.9 %collective-permute-start.14 = (bf16[6,128,128]{2,1,0:T(8,128)(2,1)S(1)}, bf16[6,128,128]{2,1,0:T(8,128)(2,1)S(1)}, u32[]{:S(2)}, u32[]{:S(2)}) collective-permute-start(bf16[6,128,128]{2,1,0:T(8,128)(2,1)S(1)} %collective-permute-done.13.refs_15_), channel_id=1, source_target_pairs={{0,8},{4,12},{8,16},{12,20},{16,24},{20,28},{1,9},{5,13},{9,17},{1... | collective-permute-start | bytes 589832 | tf_op jit(solution)/shard_map/ppermute | solution.py:183
  44.8 4.6 %collective-permute-start.21 = (bf16[6,128,128]{2,1,0:T(8,128)(2,1)S(1)}, bf16[6,128,128]{2,1,0:T(8,128)(2,1)S(1)}, u32[]{:S(2)}, u32[]{:S(2)}) collective-permute-start(bf16[6,128,128]{2,1,0:T(8,128)(2,1)S(1)} %collective-permute-done.20.refs_22_), channel_id=1, source_target_pairs={{0,8},{4,12},{8,16},{12,20},{16,24},{20,28},{1,9},{5,13},{9,17},{1... | collective-permute-start | bytes 589832 | tf_op jit(solution)/shard_map/ppermute | solution.py:183
  50.7 4.6 %collective-permute-start.28 = (bf16[6,128,128]{2,1,0:T(8,128)(2,1)S(1)}, bf16[6,128,128]{2,1,0:T(8,128)(2,1)S(1)}, u32[]{:S(2)}, u32[]{:S(2)}) collective-permute-start(bf16[6,128,128]{2,1,0:T(8,128)(2,1)S(1)} %collective-permute-done.27.refs_29_), channel_id=1, source_target_pairs={{0,8},{4,12},{8,16},{12,20},{16,24},{20,28},{1,9},{5,13},{9,17},{1... | collective-permute-start | bytes 589832 | tf_op jit(solution)/shard_map/ppermute | solution.py:183
  56.6 1.6 collective-permute-start
  61.4 2.8 %collective-permute-done.31.refs_33_ = bf16[6,128,128]{2,1,0:T(8,128)(2,1)S(1)} collective-permute-done((bf16[6,128,128]{2,1,0:T(8,128)(2,1)S(1)}, bf16[6,128,128]{2,1,0:T(8,128)(2,1)S(1)}, u32[]{:S(2)}, u32[]{:S(2)}) %collective-permute-start.31) | collective-permute-done | bytes 196640 | tf_op jit(solution)/shard_map/ppermute | solution.py:183
  64.2 4.1 %collective-permute-done.11.refs_13_ = bf16[6,128,128]{2,1,0:T(8,128)(2,1)S(1)} collective-permute-done((bf16[6,128,128]{2,1,0:T(8,128)(2,1)S(1)}, bf16[6,128,128]{2,1,0:T(8,128)(2,1)S(1)}, u32[]{:S(2)}, u32[]{:S(2)}) %collective-permute-start.11) | collective-permute-done | bytes 196640 | tf_op jit(solution)/shard_map/ppermute | solution.py:183
  68.3 3.9 %collective-permute-start.8 = (bf16[6,128,128]{2,1,0:T(8,128)(2,1)S(1)}, bf16[6,128,128]{2,1,0:T(8,128)(2,1)S(1)}, u32[]{:S(2)}, u32[]{:S(2)}) collective-permute-start(bf16[6,128,128]{2,1,0:T(8,128)(2,1)S(1)} %collective-permute-done.7.refs_9_), channel_id=1, source_target_pairs={{0,8},{4,12},{8,16},{12,20},{16,24},{20,28},{1,9},{5,13},{9,17},{1... | collective-permute-start | bytes 589832 | tf_op jit(solution)/shard_map/ppermute | solution.py:183
  72.3 3.2 %collective-permute-done.8.refs_10_ = bf16[6,128,128]{2,1,0:T(8,128)(2,1)S(1)} collective-permute-done((bf16[6,128,128]{2,1,0:T(8,128)(2,1)S(1)}, bf16[6,128,128]{2,1,0:T(8,128)(2,1)S(1)}, u32[]{:S(2)}, u32[]{:S(2)}) %collective-permute-start.8) | collective-permute-done | bytes 196640 | tf_op jit(solution)/shard_map/ppermute | solution.py:183
  75.4 4.4 %collective-permute-start.15 = (bf16[6,128,128]{2,1,0:T(8,128)(2,1)S(1)}, bf16[6,128,128]{2,1,0:T(8,128)(2,1)S(1)}, u32[]{:S(2)}, u32[]{:S(2)}) collective-permute-start(bf16[6,128,128]{2,1,0:T(8,128)(2,1)S(1)} %collective-permute-done.14.refs_16_), channel_id=1, source_target_pairs={{0,8},{4,12},{8,16},{12,20},{16,24},{20,28},{1,9},{5,13},{9,17},{1... | collective-permute-start | bytes 589832 | tf_op jit(solution)/shard_map/ppermute | solution.py:183
  81.2 4.7 %collective-permute-start.22 = (bf16[6,128,128]{2,1,0:T(8,128)(2,1)S(1)}, bf16[6,128,128]{2,1,0:T(8,128)(2,1)S(1)}, u32[]{:S(2)}, u32[]{:S(2)}) collective-permute-start(bf16[6,128,128]{2,1,0:T(8,128)(2,1)S(1)} %collective-permute-done.21.refs_23_), channel_id=1, source_target_pairs={{0,8},{4,12},{8,16},{12,20},{16,24},{20,28},{1,9},{5,13},{9,17},{1... | collective-permute-start | bytes 589832 | tf_op jit(solution)/shard_map/ppermute | solution.py:183
  87.2 5.2 %collective-permute-start.29 = (bf16[6,128,128]{2,1,0:T(8,128)(2,1)S(1)}, bf16[6,128,128]{2,1,0:T(8,128)(2,1)}, u32[]{:S(2)}, u32[]{:S(2)}) collective-permute-start(bf16[6,128,128]{2,1,0:T(8,128)(2,1)S(1)} %collective-permute-done.28.refs_30_), channel_id=1, source_target_pairs={{0,8},{4,12},{8,16},{12,20},{16,24},{20,28},{1,9},{5,13},{9,17},{1... | collective-permute-start | bytes 589832 | tf_op jit(solution)/shard_map/ppermute | solution.py:183
  95.1 5.2 %collective-permute-start.9 = (bf16[6,128,128]{2,1,0:T(8,128)(2,1)S(1)}, bf16[6,128,128]{2,1,0:T(8,128)(2,1)S(1)}, u32[]{:S(2)}, u32[]{:S(2)}) collective-permute-start(bf16[6,128,128]{2,1,0:T(8,128)(2,1)S(1)} %collective-permute-done.8.refs_10_), channel_id=1, source_target_pairs={{0,8},{4,12},{8,16},{12,20},{16,24},{20,28},{1,9},{5,13},{9,17},{1... | collective-permute-start | bytes 589832 | tf_op jit(solution)/shard_map/ppermute | solution.py:183
  100.3 3.9 %collective-permute-start.16 = (bf16[6,128,128]{2,1,0:T(8,128)(2,1)S(1)}, bf16[6,128,128]{2,1,0:T(8,128)(2,1)S(1)}, u32[]{:S(2)}, u32[]{:S(2)}) collective-permute-start(bf16[6,128,128]{2,1,0:T(8,128)(2,1)S(1)} %collective-permute-done.15.refs_17_), channel_id=1, source_target_pairs={{0,8},{4,12},{8,16},{12,20},{16,24},{20,28},{1,9},{5,13},{9,17},{1... | collective-permute-start | bytes 589832 | tf_op jit(solution)/shard_map/ppermute | solution.py:183
  107.4 4.4 %collective-permute-start.23 = (bf16[6,128,128]{2,1,0:T(8,128)(2,1)S(1)}, bf16[6,128,128]{2,1,0:T(8,128)(2,1)S(1)}, u32[]{:S(2)}, u32[]{:S(2)}) collective-permute-start(bf16[6,128,128]{2,1,0:T(8,128)(2,1)S(1)} %collective-permute-done.22.refs_24_), channel_id=1, source_target_pairs={{0,8},{4,12},{8,16},{12,20},{16,24},{20,28},{1,9},{5,13},{9,17},{1... | collective-permute-start | bytes 589832 | tf_op jit(solution)/shard_map/ppermute | solution.py:183
  113.2 2.6 %collective-permute-done.23.refs_25_ = bf16[6,128,128]{2,1,0:T(8,128)(2,1)S(1)} collective-permute-done((bf16[6,128,128]{2,1,0:T(8,128)(2,1)S(1)}, bf16[6,128,128]{2,1,0:T(8,128)(2,1)S(1)}, u32[]{:S(2)}, u32[]{:S(2)}) %collective-permute-start.23) | collective-permute-done | bytes 196640 | tf_op jit(solution)/shard_map/ppermute | solution.py:183
  115.8 5.1 %collective-permute-start.30 = (bf16[6,128,128]{2,1,0:T(8,128)(2,1)}, bf16[6,128,128]{2,1,0:T(8,128)(2,1)}, u32[]{:S(2)}, u32[]{:S(2)}) collective-permute-start(bf16[6,128,128]{2,1,0:T(8,128)(2,1)} %collective-permute-done.29.refs_31_), channel_id=1, source_target_pairs={{0,8},{4,12},{8,16},{12,20},{16,24},{20,28},{1,9},{5,13},{9,17},{1... | collective-permute-start | bytes 589832 | tf_op jit(solution)/shard_map/ppermute | solution.py:183
  122.9 68.7 %all-gather = s32[32,1,24]{2,1,0:T(1,128)} all-gather(s32[1,1,24]{2,1,0:T(1,128)S(1)} %reshape.13), channel_id=1, replica_groups=mesh['opair'=8,'vpair'=4] {'opair','vpair'}, dimensions={0}, use_global_device_ids=true | all-gather | bytes 3168 | tf_op jit(solution)/shard_map/all_gather | solution.py:173
  192.6 29.7 %ladder.1 = (f32[8,256,128]{2,1,0:T(8,128)}, bf16[8,256,128]{2,1,0:T(8,128)(2,1)}) custom-call(s32[32,24]{1,0:T(8,128)} %bitcast.2, bf16[256,1024]{1,0:T(8,128)(2,1)} %get-tuple-element.9.refs_0_, bf16[256,1024]{1,0:T(8,128)(2,1)} %copy-done, bf16[256,1024]{1,0:T(8,128)(2,1)} %copy-done.1, bf16[256,1024]{1,0:T(8,128)(2,1)} %copy-done.2, ...), custom_call_target="tpu_custom_call" | custom-call | tf_op jit(solution)/shard_map/ladder/pallas_call | solution.py:199
  222.5 2.1 collective-permute-done.34.twin
  225.4 3.4 %update.1 = (bf16[256,1024]{1,0:T(8,128)(2,1)}, f32[256,1024]{1,0:T(8,128)}) custom-call(s32[2,8]{1,0:T(2,128)} %live.3, bf16[256,1024]{1,0:T(8,128)(2,1)} %amplitudes.3, bf16[256,1024]{1,0:T(8,128)(2,1)} %driver.1, f32[8,256,128]{2,1,0:T(8,128)} %get-tuple-element.14.own, bf16[8,256,128]{2,1,0:T(8,128)(2,1)} %copy-done.6, ...), custom_call_target="tpu_custom_call" | custom-call | tf_op jit(solution)/shard_map/update/pallas_call | solution.py:219
  (116 shorter events, 23.4 us)
Async XLA Ops:
  32.1 11.4 %collective-permute-start.20 = (bf16[6,128,128]{2,1,0:T(8,128)(2,1)}, bf16[6,128,128]{2,1,0:T(8,128)(2,1)S(1)}, u32[]{:S(2)}, u32[]{:S(2)}) collective-permute-start(bf16[6,128,128]{2,1,0:T(8,128)(2,1)} %get-tuple-element.12), channel_id=1, source_target_pairs={{0,2},{1,3},{2,0},{3,1},{4,6},{5,7},{6,4},{7,5},{8,10},{9,11},{10,... | collective-permute-start | bytes 589832 | tf_op jit(solution)/shard_map/ppermute | solution.py:176
  33.6 11.2 %collective-permute-start.27 = (bf16[6,128,128]{2,1,0:T(8,128)(2,1)}, bf16[6,128,128]{2,1,0:T(8,128)(2,1)S(1)}, u32[]{:S(2)}, u32[]{:S(2)}) collective-permute-start(bf16[6,128,128]{2,1,0:T(8,128)(2,1)} %get-tuple-element.13), channel_id=1, source_target_pairs={{0,3},{1,2},{2,1},{3,0},{4,7},{5,6},{6,5},{7,4},{8,11},{9,10},{10,... | collective-permute-start | bytes 589832 | tf_op jit(solution)/shard_map/ppermute | solution.py:176
  33.6 15.7 %collective-permute-start.10 = (bf16[6,128,128]{2,1,0:T(8,128)(2,1)}, bf16[6,128,128]{2,1,0:T(8,128)(2,1)S(1)}, u32[]{:S(2)}, u32[]{:S(2)}) collective-permute-start(bf16[6,128,128]{2,1,0:T(8,128)(2,1)} %get-tuple-element.10.refs_8_), channel_id=1, source_target_pairs={{8,0},{12,4},{16,8},{20,12},{24,16},{28,20},{9,1},{13,5},{17,9},{2... | collective-permute-start | bytes 589832 | tf_op jit(solution)/shard_map/ppermute | solution.py:183
  34.9 15.8 %collective-permute-start.7 = (bf16[6,128,128]{2,1,0:T(8,128)(2,1)}, bf16[6,128,128]{2,1,0:T(8,128)(2,1)S(1)}, u32[]{:S(2)}, u32[]{:S(2)}) collective-permute-start(bf16[6,128,128]{2,1,0:T(8,128)(2,1)} %get-tuple-element.10.refs_8_), channel_id=1, source_target_pairs={{0,8},{4,12},{8,16},{12,20},{16,24},{20,28},{1,9},{5,13},{9,17},{1... | collective-permute-start | bytes 589832 | tf_op jit(solution)/shard_map/ppermute | solution.py:183
  39.5 15.7 %collective-permute-start.14 = (bf16[6,128,128]{2,1,0:T(8,128)(2,1)S(1)}, bf16[6,128,128]{2,1,0:T(8,128)(2,1)S(1)}, u32[]{:S(2)}, u32[]{:S(2)}) collective-permute-start(bf16[6,128,128]{2,1,0:T(8,128)(2,1)S(1)} %collective-permute-done.13.refs_15_), channel_id=1, source_target_pairs={{0,8},{4,12},{8,16},{12,20},{16,24},{20,28},{1,9},{5,13},{9,17},{1... | collective-permute-start | bytes 589832 | tf_op jit(solution)/shard_map/ppermute | solution.py:183
  43.4 13.1 %collective-permute-start.17 = (bf16[6,128,128]{2,1,0:T(8,128)(2,1)S(1)}, bf16[6,128,128]{2,1,0:T(8,128)(2,1)S(1)}, u32[]{:S(2)}, u32[]{:S(2)}) collective-permute-start(bf16[6,128,128]{2,1,0:T(8,128)(2,1)S(1)} %collective-permute-done.13.refs_15_), channel_id=1, source_target_pairs={{8,0},{12,4},{16,8},{20,12},{24,16},{28,20},{9,1},{13,5},{17,9},{2... | collective-permute-start | bytes 589832 | tf_op jit(solution)/shard_map/ppermute | solution.py:183
  44.8 13.4 %collective-permute-start.21 = (bf16[6,128,128]{2,1,0:T(8,128)(2,1)S(1)}, bf16[6,128,128]{2,1,0:T(8,128)(2,1)S(1)}, u32[]{:S(2)}, u32[]{:S(2)}) collective-permute-start(bf16[6,128,128]{2,1,0:T(8,128)(2,1)S(1)} %collective-permute-done.20.refs_22_), channel_id=1, source_target_pairs={{0,8},{4,12},{8,16},{12,20},{16,24},{20,28},{1,9},{5,13},{9,17},{1... | collective-permute-start | bytes 589832 | tf_op jit(solution)/shard_map/ppermute | solution.py:183
  56.6 23.3 %collective-permute-start = (bf16[256,1024]{1,0:T(8,128)(2,1)}, bf16[256,1024]{1,0:T(8,128)(2,1)S(1)}, u32[]{:S(2)}, u32[]{:S(2)}) collective-permute-start(bf16[256,1024]{1,0:T(8,128)(2,1)} %get-tuple-element.9.refs_0_), channel_id=1, source_target_pairs={{0,1},{1,0},{2,3},{3,2},{4,5},{5,4},{6,7},{7,6},{8,9},{9,8},{10,11... | collective-permute-start | bytes 1572872 | tf_op jit(solution)/shard_map/ppermute | solution.py:176
  58.1 23.0 %collective-permute-start.1 = (bf16[256,1024]{1,0:T(8,128)(2,1)}, bf16[256,1024]{1,0:T(8,128)(2,1)S(1)}, u32[]{:S(2)}, u32[]{:S(2)}) collective-permute-start(bf16[256,1024]{1,0:T(8,128)(2,1)} %get-tuple-element.9.refs_0_), channel_id=1, source_target_pairs={{0,2},{1,3},{2,0},{3,1},{4,6},{5,7},{6,4},{7,5},{8,10},{9,11},{10,... | collective-permute-start | bytes 1572872 | tf_op jit(solution)/shard_map/ppermute | solution.py:176
  59.7 26.2 %collective-permute-start.2 = (bf16[256,1024]{1,0:T(8,128)(2,1)}, bf16[256,1024]{1,0:T(8,128)(2,1)S(1)}, u32[]{:S(2)}, u32[]{:S(2)}) collective-permute-start(bf16[256,1024]{1,0:T(8,128)(2,1)} %get-tuple-element.9.refs_0_), channel_id=1, source_target_pairs={{0,3},{1,2},{2,1},{3,0},{4,7},{5,6},{6,5},{7,4},{8,11},{9,10},{10,... | collective-permute-start | bytes 1572872 | tf_op jit(solution)/shard_map/ppermute | solution.py:176
  64.2 23.0 %collective-permute-start.3 = (bf16[256,1024]{1,0:T(8,128)(2,1)}, bf16[256,1024]{1,0:T(8,128)(2,1)S(1)}, u32[]{:S(2)}, u32[]{:S(2)}) collective-permute-start(bf16[256,1024]{1,0:T(8,128)(2,1)} %get-tuple-element.9.refs_0_), channel_id=1, source_target_pairs={{0,4},{4,0},{8,12},{12,8},{16,20},{20,16},{24,28},{28,24},{1,5},{5... | collective-permute-start | bytes 1572872 | tf_op jit(solution)/shard_map/ppermute | solution.py:179
  75.4 17.1 %collective-permute-start.15 = (bf16[6,128,128]{2,1,0:T(8,128)(2,1)S(1)}, bf16[6,128,128]{2,1,0:T(8,128)(2,1)S(1)}, u32[]{:S(2)}, u32[]{:S(2)}) collective-permute-start(bf16[6,128,128]{2,1,0:T(8,128)(2,1)S(1)} %collective-permute-done.14.refs_16_), channel_id=1, source_target_pairs={{0,8},{4,12},{8,16},{12,20},{16,24},{20,28},{1,9},{5,13},{9,17},{1... | collective-permute-start | bytes 589832 | tf_op jit(solution)/shard_map/ppermute | solution.py:183
  79.9 13.9 %collective-permute-start.18 = (bf16[6,128,128]{2,1,0:T(8,128)(2,1)S(1)}, bf16[6,128,128]{2,1,0:T(8,128)(2,1)S(1)}, u32[]{:S(2)}, u32[]{:S(2)}) collective-permute-start(bf16[6,128,128]{2,1,0:T(8,128)(2,1)S(1)} %collective-permute-done.17.refs_19_), channel_id=1, source_target_pairs={{8,0},{12,4},{16,8},{20,12},{24,16},{28,20},{9,1},{13,5},{17,9},{2... | collective-permute-start | bytes 589832 | tf_op jit(solution)/shard_map/ppermute | solution.py:183
  81.2 13.9 %collective-permute-start.22 = (bf16[6,128,128]{2,1,0:T(8,128)(2,1)S(1)}, bf16[6,128,128]{2,1,0:T(8,128)(2,1)S(1)}, u32[]{:S(2)}, u32[]{:S(2)}) collective-permute-start(bf16[6,128,128]{2,1,0:T(8,128)(2,1)S(1)} %collective-permute-done.21.refs_23_), channel_id=1, source_target_pairs={{0,8},{4,12},{8,16},{12,20},{16,24},{20,28},{1,9},{5,13},{9,17},{1... | collective-permute-start | bytes 589832 | tf_op jit(solution)/shard_map/ppermute | solution.py:183
  85.9 14.4 %collective-permute-start.25 = (bf16[6,128,128]{2,1,0:T(8,128)(2,1)S(1)}, bf16[6,128,128]{2,1,0:T(8,128)(2,1)S(1)}, u32[]{:S(2)}, u32[]{:S(2)}) collective-permute-start(bf16[6,128,128]{2,1,0:T(8,128)(2,1)S(1)} %collective-permute-done.24.refs_26_), channel_id=1, source_target_pairs={{8,0},{12,4},{16,8},{20,12},{24,16},{28,20},{9,1},{13,5},{17,9},{2... | collective-permute-start | bytes 589832 | tf_op jit(solution)/shard_map/ppermute | solution.py:183
  87.2 17.0 %collective-permute-start.29 = (bf16[6,128,128]{2,1,0:T(8,128)(2,1)S(1)}, bf16[6,128,128]{2,1,0:T(8,128)(2,1)}, u32[]{:S(2)}, u32[]{:S(2)}) collective-permute-start(bf16[6,128,128]{2,1,0:T(8,128)(2,1)S(1)} %collective-permute-done.28.refs_30_), channel_id=1, source_target_pairs={{0,8},{4,12},{8,16},{12,20},{16,24},{20,28},{1,9},{5,13},{9,17},{1... | collective-permute-start | bytes 589832 | tf_op jit(solution)/shard_map/ppermute | solution.py:183
  92.5 13.1 %collective-permute-start.32 = (bf16[6,128,128]{2,1,0:T(8,128)(2,1)S(1)}, bf16[6,128,128]{2,1,0:T(8,128)(2,1)}, u32[]{:S(2)}, u32[]{:S(2)}) collective-permute-start(bf16[6,128,128]{2,1,0:T(8,128)(2,1)S(1)} %collective-permute-done.31.refs_33_), channel_id=1, source_target_pairs={{8,0},{12,4},{16,8},{20,12},{24,16},{28,20},{9,1},{13,5},{17,9},{2... | collective-permute-start | bytes 589832 | tf_op jit(solution)/shard_map/ppermute | solution.py:183
  93.8 11.9 %collective-permute-start.12 = (bf16[6,128,128]{2,1,0:T(8,128)(2,1)S(1)}, bf16[6,128,128]{2,1,0:T(8,128)(2,1)S(1)}, u32[]{:S(2)}, u32[]{:S(2)}) collective-permute-start(bf16[6,128,128]{2,1,0:T(8,128)(2,1)S(1)} %collective-permute-done.11.refs_13_), channel_id=1, source_target_pairs={{8,0},{12,4},{16,8},{20,12},{24,16},{28,20},{9,1},{13,5},{17,9},{2... | collective-permute-start | bytes 589832 | tf_op jit(solution)/shard_map/ppermute | solution.py:183
  95.1 11.2 %collective-permute-start.9 = (bf16[6,128,128]{2,1,0:T(8,128)(2,1)S(1)}, bf16[6,128,128]{2,1,0:T(8,128)(2,1)S(1)}, u32[]{:S(2)}, u32[]{:S(2)}) collective-permute-start(bf16[6,128,128]{2,1,0:T(8,128)(2,1)S(1)} %collective-permute-done.8.refs_10_), channel_id=1, source_target_pairs={{0,8},{4,12},{8,16},{12,20},{16,24},{20,28},{1,9},{5,13},{9,17},{1... | collective-permute-start | bytes 589832 | tf_op jit(solution)/shard_map/ppermute | solution.py:183
  105.6 86.0 %collective-permute-start.4 = (bf16[256,1024]{1,0:T(8,128)(2,1)S(1)}, bf16[256,1024]{1,0:T(8,128)(2,1)S(1)}, u32[]{:S(2)}, u32[]{:S(2)}) collective-permute-start(bf16[256,1024]{1,0:T(8,128)(2,1)S(1)} %collective-permute-done.refs_1_), channel_id=1, source_target_pairs={{0,4},{4,0},{8,12},{12,8},{16,20},{20,16},{24,28},{28,24},{1,5},{5... | collective-permute-start | bytes 1572872 | tf_op jit(solution)/shard_map/ppermute | solution.py:179
  105.7 85.9 %collective-permute-start.5 = (bf16[256,1024]{1,0:T(8,128)(2,1)S(1)}, bf16[256,1024]{1,0:T(8,128)(2,1)S(1)}, u32[]{:S(2)}, u32[]{:S(2)}) collective-permute-start(bf16[256,1024]{1,0:T(8,128)(2,1)S(1)} %collective-permute-done.1.refs_2_), channel_id=1, source_target_pairs={{0,4},{4,0},{8,12},{12,8},{16,20},{20,16},{24,28},{28,24},{1,5},{5... | collective-permute-start | bytes 1572872 | tf_op jit(solution)/shard_map/ppermute | solution.py:179
  106.3 85.4 %collective-permute-start.6 = (bf16[256,1024]{1,0:T(8,128)(2,1)S(1)}, bf16[256,1024]{1,0:T(8,128)(2,1)}, u32[]{:S(2)}, u32[]{:S(2)}) collective-permute-start(bf16[256,1024]{1,0:T(8,128)(2,1)S(1)} %collective-permute-done.2.refs_3_), channel_id=1, source_target_pairs={{0,4},{4,0},{8,12},{12,8},{16,20},{20,16},{24,28},{28,24},{1,5},{5... | collective-permute-start | bytes 1572872 | tf_op jit(solution)/shard_map/ppermute | solution.py:179
  115.8 75.9 %collective-permute-start.30 = (bf16[6,128,128]{2,1,0:T(8,128)(2,1)}, bf16[6,128,128]{2,1,0:T(8,128)(2,1)}, u32[]{:S(2)}, u32[]{:S(2)}) collective-permute-start(bf16[6,128,128]{2,1,0:T(8,128)(2,1)} %collective-permute-done.29.refs_31_), channel_id=1, source_target_pairs={{0,8},{4,12},{8,16},{12,20},{16,24},{20,28},{1,9},{5,13},{9,17},{1... | collective-permute-start | bytes 589832 | tf_op jit(solution)/shard_map/ppermute | solution.py:183
  121.6 70.1 %collective-permute-start.33 = (bf16[6,128,128]{2,1,0:T(8,128)(2,1)}, bf16[6,128,128]{2,1,0:T(8,128)(2,1)}, u32[]{:S(2)}, u32[]{:S(2)}) collective-permute-start(bf16[6,128,128]{2,1,0:T(8,128)(2,1)} %collective-permute-done.32.refs_34_), channel_id=1, source_target_pairs={{8,0},{12,4},{16,8},{20,12},{24,16},{28,20},{9,1},{13,5},{17,9},{2... | collective-permute-start | bytes 589832 | tf_op jit(solution)/shard_map/ppermute | solution.py:183
  (42 other events, 1449.7 us)

commit v2 on v0

v2 whole, which is shorter than its diff:
```python
import functools

import jax
import jax.numpy as jnp
from jax import lax
from jax.experimental import pallas as pl
from jax.experimental.pallas import tpu as pltpu
from jax.sharding import PartitionSpec as P

VMEM_BYTES = 56 * 1024 * 1024
CORES = 2
NOTE_ROWS = 16


def pack_kernel(n_v, cap, columns, live, integrals, amplitudes, *refs):
    parcels, masked, origin, codes = refs[:n_v], refs[n_v], refs[n_v + 1], refs[n_v + 2]
    rows, slots, tile, _ = integrals.shape
    me = lax.axis_index("vpair")
    counts = [jnp.int32(0)] * n_v
    for i in range(n_v * cap):
        origin[i] = 0
        codes[i] = -1
    for row in range(rows):
        for slot in range(slots):
            column = columns[slot, row]
            partner = lax.div(column, rows) ^ me
            place = counts[0]
            for j in range(1, n_v):
                place = jnp.where(partner == j, counts[j], place)
            counts = [counts[j] + (partner == j).astype(jnp.int32) for j in range(n_v)]
            at = partner * cap + place
            origin[at] = row * slots + slot
            codes[at] = row * rows + lax.rem(column, rows)
    lane = lax.broadcasted_iota(jnp.int32, (NOTE_ROWS, tile), 1)
    for j in range(n_v):
        note = jnp.full((NOTE_ROWS, tile), -1, jnp.int32)
        for k in range(cap):
            entry = origin[j * cap + k]
            parcels[j][0, pl.ds(k * tile, tile)] = integrals[
                lax.div(entry, slots), lax.rem(entry, slots)
            ]
            note = jnp.where(lane == k, codes[j * cap + k], note)
        parcels[j][0, pl.ds(cap * tile, NOTE_ROWS)] = note.astype(jnp.float32).astype(
            integrals.dtype
        )
    for o in range(live.shape[0]):
        for c in range(live.shape[1]):
            at = (pl.ds(o * tile, tile), pl.ds(c * tile, tile))
            kept = live[o, c].astype(jnp.float32)
            masked[at] = (amplitudes[at].astype(jnp.float32) * kept).astype(masked.dtype)


def read_notes(units, n_units, cap, rows, notes_wide, notes, sem):
    tile = units.shape[-1]
    for u in range(n_units):
        note = units[u, pl.ds(cap * tile, NOTE_ROWS)].astype(jnp.float32).astype(jnp.int32)
        notes_wide[pl.ds(u, 1)] = note[:1]
    copy = pltpu.make_async_copy(notes_wide, notes, sem)
    copy.start()
    copy.wait()


def add_unit(unit, j, cap, rows, amps, units, notes, total):
    tile = units.shape[-1]
    for k in range(cap):
        code = notes[unit, k]
        used = code >= 0
        row = jnp.where(used, lax.div(code, rows), 0)
        column = jnp.where(used, lax.rem(code, rows), rows)
        total[column] += jnp.dot(
            amps[j, :, pl.ds(pl.multiple_of(row * tile, tile), tile)],
            units[unit, pl.ds(k * tile, tile)],
            preferred_element_type=jnp.float32,
        )


def ladder_kernel(n_v, n_z, cap, rows, layout, occupied, *refs):
    own_a, refs = refs[:n_v], refs[n_v:]
    twin_a, refs = refs[:n_v], refs[n_v:]
    arrays, refs = refs[: len(layout)], refs[len(layout) :]
    own_out, twin_out, occupied_out = refs[:3]
    a_buf, units, notes_wide, notes, queue, total, a_sems, sems, note_sem = refs[3:]
    n_rows, _ = own_a[0].shape
    tile = units.shape[-1]
    z = lax.div(lax.axis_index("opair"), CORES)
    even = lax.rem(z, 2) == 0

    def valid(kind, hop):
        if kind == "own":
            return z >= 0
        upward = ~even if kind == "even" else even
        source = jnp.where(upward, z - 1 - hop, z + 1 + hop)
        return (source >= 0) & (source < n_z)

    a_copies = []
    for j in range(n_v):
        for half, ref in ((0, own_a[j]), (1, twin_a[j])):
            copy = pltpu.make_async_copy(
                ref, a_buf.at[j, pl.ds(half * n_rows, n_rows)], a_sems.at[2 * j + half]
            )
            copy.start()
            a_copies.append(copy)
    copies, first = [], 0
    for i, (kind, hop, partners) in enumerate(layout):
        copy = pltpu.make_async_copy(
            arrays[i], units.at[pl.ds(first, len(partners))], sems.at[i]
        )
        copy.start()
        copies.append(copy)
        first += len(partners)

    count, unit = jnp.int32(0), 0
    for kind, hop, partners in layout:
        use = valid(kind, hop).astype(jnp.int32)
        for j in partners:
            queue[0, count] = unit
            queue[1, count] = j
            count += use
            unit += 1
    total[...] = jnp.zeros_like(total)
    for o in range(n_rows // tile):
        wide = jnp.broadcast_to(occupied[pl.ds(o, 1)], (tile, tile))
        occupied_out[pl.ds(o * tile, tile)] = wide.T
    for copy in copies:
        copy.wait()
    read_notes(units, first, cap, rows, notes_wide, notes, note_sem)
    for copy in a_copies:
        copy.wait()

    def one(i, carry):
        add_unit(queue[0, i], queue[1, i], cap, rows, a_buf, units, notes, total)
        return carry

    lax.fori_loop(0, count, one, 0)
    own_out[...] = total[:rows, :n_rows]
    twin_out[...] = total[:rows, n_rows:].astype(twin_out.dtype)


def update_kernel(
    n_v, n_z, cap, partners, live, amplitudes, driver, own, twin, occupied, virtual, *refs
):
    a_own, refs = refs[:n_v], refs[n_v:]
    arrays, (new, residual, a_buf, units, notes_wide, notes, total, a_sems, sems, note_sem) = (
        refs[:CORES],
        refs[CORES:],
    )
    rows, _, tile = own.shape
    z = lax.div(lax.axis_index("opair"), CORES)
    total[pl.ds(0, rows)] = own[...] + twin[...].astype(jnp.float32)

    @pl.when((z == 0) | (z == n_z - 1))
    def _():
        a_copies = [
            pltpu.make_async_copy(a_own[j], a_buf.at[j], a_sems.at[j]) for j in range(n_v)
        ]
        copies = [
            pltpu.make_async_copy(
                arrays[i], units.at[pl.ds(i * len(partners), len(partners))], sems.at[i]
            )
            for i in range(CORES)
        ]
        for copy in copies + a_copies:
            copy.start()
        total[rows] = jnp.zeros_like(total[rows])
        for copy in copies:
            copy.wait()
        n_units = CORES * len(partners)
        read_notes(units, n_units, cap, rows, notes_wide, notes, note_sem)
        for copy in a_copies:
            copy.wait()

        def one(i, carry):
            j = lax.rem(i, len(partners)) + partners[0]
            add_unit(i, j, cap, rows, a_buf, units, notes, total)
            return carry

        lax.fori_loop(0, n_units, one, 0)

    for o in range(live.shape[0]):
        for c in range(live.shape[1]):
            here = pl.ds(o * tile, tile)
            at = (here, pl.ds(c * tile, tile))
            kept = live[o, c].astype(jnp.float32)
            amps = amplitudes[at].astype(jnp.float32)
            masked = (amps * kept).astype(jnp.bfloat16).astype(jnp.float32)
            denominator = occupied[here, :] - virtual[:, pl.ds(c * tile, tile)]
            rest = (
                driver[at].astype(jnp.float32) + total[c, here] + denominator * amps
            ) * kept
            residual[at] = rest
            new[at] = (masked - rest / denominator).astype(new.dtype)


def on_device(
    amplitudes,
    tile_live,
    integrals,
    integral_columns,
    driver_terms,
    occupied_energy,
    virtual_energy,
):
    n_rows, width = amplitudes.shape
    rows, slots, tile, _ = integrals.shape
    n_v, n_o = lax.axis_size("vpair"), lax.axis_size("opair")
    n_z = n_o // CORES
    cap = -(-(rows * slots) // n_v)
    height = cap * tile + NOTE_ROWS
    dtype = integrals.dtype
    in_smem = pl.BlockSpec(memory_space=pltpu.SMEM)
    in_vmem = pl.BlockSpec(memory_space=pltpu.VMEM)
    anywhere = pl.BlockSpec(memory_space=pl.ANY)
    params = pltpu.CompilerParams(vmem_limit_bytes=VMEM_BYTES)

    *parcels, masked = pl.pallas_call(
        functools.partial(pack_kernel, n_v, cap),
        out_shape=[jax.ShapeDtypeStruct((1, height, tile), dtype)] * n_v
        + [jax.ShapeDtypeStruct(amplitudes.shape, amplitudes.dtype)],
        in_specs=[in_smem, in_smem, in_vmem, in_vmem],
        out_specs=[in_vmem] * (n_v + 1),
        scratch_shapes=[pltpu.SMEM((n_v * cap,), jnp.int32)] * 2,
        compiler_params=params,
        name="pack",
    )(integral_columns.T, tile_live, integrals, amplitudes)

    def across_v(value, j):
        return lax.ppermute(value, "vpair", [(i, i ^ j) for i in range(n_v)]) if j else value

    def across_core(value):
        return lax.ppermute(value, "opair", [(i, i ^ 1) for i in range(n_o)])

    def swap_z(value, odd):
        pairs = []
        for z in range(n_z):
            partner = ((z + odd) ^ 1) - odd
            for core in range(CORES):
                target = (partner, core) if 0 <= partner < n_z else (z, core ^ 1)
                pairs.append((z * CORES + core, target[0] * CORES + target[1]))
        return lax.ppermute(value, "opair", pairs)

    def along_z(start):
        even, odd = [swap_z(start, 0)], [swap_z(start, 1)]
        for hop in range(1, n_z - 1):
            even.append(swap_z(odd[hop - 1], 0))
            if hop < n_z - 2:
                odd.append(swap_z(even[hop - 1], 1))
        return even, odd

    others = list(range(1, n_v))
    near = parcels[0]
    far = jnp.concatenate([across_v(parcels[j], j) for j in others])
    arrays, layout = [], []
    last = None
    for start, partners in ((near, [0]), (far, others)):
        even, odd = along_z(start)
        if start is far:
            last = even.pop()
        arrays += [start, *even, *odd]
        layout += [("own", 0, partners)]
        layout += [("even", hop, partners) for hop in range(len(even))]
        layout += [("odd", hop, partners) for hop in range(len(odd))]
    own_a = [across_v(masked, j) for j in range(n_v)]
    twin_a = [across_core(value) for value in own_a]
    n_units = sum(len(partners) for _, _, partners in layout)

    own, twin, occupied = pl.pallas_call(
        functools.partial(ladder_kernel, n_v, n_z, cap, rows, layout),
        out_shape=[
            jax.ShapeDtypeStruct((rows, n_rows, tile), jnp.float32),
            jax.ShapeDtypeStruct((rows, n_rows, tile), jnp.bfloat16),
            jax.ShapeDtypeStruct((n_rows, tile), jnp.float32),
        ],
        in_specs=[in_vmem] + [anywhere] * (2 * n_v + len(arrays)),
        out_specs=[in_vmem] * 3,
        scratch_shapes=[
            pltpu.VMEM((n_v, CORES * n_rows, width), amplitudes.dtype),
            pltpu.VMEM((n_units, height, tile), dtype),
            pltpu.VMEM((n_units, tile), jnp.int32),
            pltpu.SMEM((n_units, tile), jnp.int32),
            pltpu.SMEM((2, n_units + 1), jnp.int32),
            pltpu.VMEM((rows + 1, CORES * n_rows, tile), jnp.float32),
            pltpu.SemaphoreType.DMA((2 * n_v,)),
            pltpu.SemaphoreType.DMA((len(arrays),)),
            pltpu.SemaphoreType.DMA,
        ],
        compiler_params=params,
        cost_estimate=pl.CostEstimate(
            flops=8 * n_units * cap * n_rows * tile * tile * CORES,
            bytes_accessed=16 * 1024 * 1024,
            transcendentals=0,
        ),
        name="ladder",
    )(occupied_energy.reshape(-1, tile), *own_a, *twin_a, *arrays)
    twin = across_core(twin)
    n_last = CORES * len(others)

    return pl.pallas_call(
        functools.partial(update_kernel, n_v, n_z, cap, others),
        out_shape=[
            jax.ShapeDtypeStruct((n_rows, width), jnp.bfloat16),
            jax.ShapeDtypeStruct((n_rows, width), jnp.float32),
        ],
        in_specs=[in_smem] + [in_vmem] * 6 + [anywhere] * (n_v + CORES),
        out_specs=[in_vmem] * 2,
        scratch_shapes=[
            pltpu.VMEM((n_v, n_rows, width), amplitudes.dtype),
            pltpu.VMEM((n_last, height, tile), dtype),
            pltpu.VMEM((n_last, tile), jnp.int32),
            pltpu.SMEM((n_last, tile), jnp.int32),
            pltpu.VMEM((rows + 1, n_rows, tile), jnp.float32),
            pltpu.SemaphoreType.DMA((n_v,)),
            pltpu.SemaphoreType.DMA((CORES,)),
            pltpu.SemaphoreType.DMA,
        ],
        compiler_params=params,
        name="update",
    )(
        tile_live,
        amplitudes,
        driver_terms,
        own,
        twin,
        occupied,
        virtual_energy.reshape(1, width),
        *own_a,
        last,
        across_core(last),
    )


def solution(mesh):
    in_specs = (
        P("opair", "vpair"),
        P("opair", "vpair"),
        P("vpair", "opair", None, None),
        P("vpair", "opair"),
        P("opair", "vpair"),
        P("opair"),
        P("vpair"),
    )
    out_specs = (P("opair", "vpair"), P("opair", "vpair"))
    return jax.shard_map(
        on_device, mesh=mesh, in_specs=in_specs, out_specs=out_specs, check_vma=False
    )
```

time: 219 us -> 109 us (0.50)
  other arithmetic: 78.7 us -> 0 us
  starting transfers between devices: 0.08 us -> 31.8 us
  waiting for transfers between devices: 83.6 us -> 52.6 us
  Pallas kernels: 0 us -> 22.1 us
  blocking collectives: 14.5 us -> 0 us
  matrix products: 14.1 us -> 0 us
  between operations: 14.2 us -> 0.88 us
  local copies, waits for them, and re-layouts: 12.6 us -> 1.85 us
    scatter-add x8 -> x0, other arithmetic: 68.3 us -> none  [on_device(): term = term.at[landing].add(products, mode='drop')]
    ppermute x0 -> x22, waiting for transfers between devices: none -> 52.6 us  [the longest x10 29.7 us: swap_z(): return lax.ppermute(value, 'opair', pairs)]
    all_gather x1 -> x0, waiting for transfers between devices: 50 us -> none  [on_device(): lax.all_gather(integrals, 'opair', axis=1, tiled=True)]
    reduce_scatter x1 -> x0, waiting for transfers between devices: 33 us -> none  [on_device(): lax.psum_scatter(term.astype(jnp.bfloat16), 'vpair', scatter_dimension=0,...]
    ppermute x0 -> x22, starting transfers between devices: none -> 31.8 us  [the longest x10 22.7 us: swap_z(): return lax.ppermute(value, 'opair', pairs)]
    pallas_call x0 -> x3, Pallas kernels: none -> 22.1 us  [the longest x1 11.9 us: on_device(): pl.pallas_call(functools.partial(ladder_kernel, n_v, n_z, cap, rows, layo...]
    all_gather x1 -> x0, blocking collectives: 14.5 us -> none  [on_device(): lax.all_gather(integral_columns, 'opair', axis=1, tiled=True)]
    dot_general x8 -> x0, matrix products: 14.1 us -> none  [on_device(): jnp.einsum('rx,kxy->kry', masked_tiles[:, source, :], gathered[source], p...]
  transfers between devices with their start and end apart: 2 -> 22, of which waited for: 2 -> 8; matrix products, arithmetic and copies ran while one was open for 2% -> 0% of each run, Pallas kernels for 0% -> 11%
where the time goes in v2:
time: 109 us
  waiting for transfers between devices  52.6 us (48%)
  starting transfers between devices  31.8 us (29%)
  Pallas kernels  22.1 us (20%)
  local copies, waits for them, and re-layouts  1.85 us (2%)
    ppermute x10, waiting for transfers between devices, swap_z(): return lax.ppermute(value, 'opair', pairs)  29.7 us
    ppermute x10, starting transfers between devices, swap_z(): return lax.ppermute(value, 'opair', pairs)  22.7 us
    ppermute x6, waiting for transfers between devices, across_v(): lax.ppermute(value, 'vpair', [(i, i ^ j) for i in range(n_v)])  20.7 us
    pallas_call x1, Pallas kernels, on_device(): pl.pallas_call(functools.partial(ladder_kernel, n_v, n_z, cap, rows, layo...  11.9 us
    ppermute x6, starting transfers between devices, across_v(): lax.ppermute(value, 'vpair', [(i, i ^ j) for i in range(n_v)])  7.96 us
    pallas_call x1, Pallas kernels, on_device(): pl.pallas_call(functools.partial(update_kernel, n_v, n_z, cap, others), o...  7.36 us
    pallas_call x1, Pallas kernels, on_device(): pl.pallas_call(functools.partial(pack_kernel, n_v, cap), out_shape=[jax.S...  2.8 us
  transfers between devices with their start and end apart: 22, of which 8 were waited for; matrix products, arithmetic and copies ran while one was open for 0% of the time, Pallas kernels for 11%

profile of v2, /device:TPU:0, one launch (start us, length us, event | category | flops | bytes accessed | tf_op | source)
XLA Modules:
  0.0 109.2 jit_solution(4362022652774697418)
XLA Ops:
  0.6 2.8 %pack.1 = (bf16[1,784,128]{2,1,0:T(8,128)(2,1)}, bf16[1,784,128]{2,1,0:T(8,128)(2,1)}, bf16[1,784,128]{2,1,0:T(8,128)(2,1)}, bf16[1,784,128]{2,1,0:T(8,128)(2,1)}, bf16[256,1024]{1,0:T(8,128)(2,1)}) custom-call(s32[3,8]{1,0:T(4,128)} %bitcast.4, s32[2,8]{1,0:T(2,128)} %live.3, bf16[8,3,128,128]{3,2,1,0:T(8,128)(2,1)} %integrals.1, bf16[256,1024]{1,0:T(8,128)(2,1)} %amplitudes.3), custom_call_target="tpu_custom_call" | custom-call | tf_op jit(solution)/shard_map/pack/pallas_call | solution.py:215
  3.4 2.9 %collective-permute-start.12 = (bf16[1,784,128]{2,1,0:T(8,128)(2,1)}, bf16[1,784,128]{2,1,0:T(8,128)(2,1)S(1)}, u32[]{:S(2)}, u32[]{:S(2)}) collective-permute-start(bf16[1,784,128]{2,1,0:T(8,128)(2,1)} %get-tuple-element.12), channel_id=1, source_target_pairs={{0,1},{1,0},{2,3},{3,2},{4,5},{5,4},{6,7},{7,6},{8,9},{9,8},{10,11... | collective-permute-start | bytes 602120 | tf_op jit(solution)/shard_map/ppermute | solution.py:227
  6.4 1.5 %collective-permute-start.13 = (bf16[1,784,128]{2,1,0:T(8,128)(2,1)}, bf16[1,784,128]{2,1,0:T(8,128)(2,1)S(1)}, u32[]{:S(2)}, u32[]{:S(2)}) collective-permute-start(bf16[1,784,128]{2,1,0:T(8,128)(2,1)} %get-tuple-element.13), channel_id=1, source_target_pairs={{0,2},{1,3},{2,0},{3,1},{4,6},{5,7},{6,4},{7,5},{8,10},{9,11},{10,... | collective-permute-start | bytes 602120 | tf_op jit(solution)/shard_map/ppermute | solution.py:227
  7.9 4.5 %collective-permute-done.12 = bf16[1,784,128]{2,1,0:T(8,128)(2,1)S(1)} collective-permute-done((bf16[1,784,128]{2,1,0:T(8,128)(2,1)}, bf16[1,784,128]{2,1,0:T(8,128)(2,1)S(1)}, u32[]{:S(2)}, u32[]{:S(2)}) %collective-permute-start.12) | collective-permute-done | bytes 200736 | tf_op jit(solution)/shard_map/ppermute | solution.py:227
  12.4 4.9 %collective-permute-done.13 = bf16[1,784,128]{2,1,0:T(8,128)(2,1)S(1)} collective-permute-done((bf16[1,784,128]{2,1,0:T(8,128)(2,1)}, bf16[1,784,128]{2,1,0:T(8,128)(2,1)S(1)}, u32[]{:S(2)}, u32[]{:S(2)}) %collective-permute-start.13) | collective-permute-done | bytes 200736 | tf_op jit(solution)/shard_map/ppermute | solution.py:227
  17.4 1.6 %collective-permute-start.15 = (bf16[3,784,128]{2,1,0:T(8,128)(2,1)S(1)}, bf16[3,784,128]{2,1,0:T(8,128)(2,1)S(1)}, u32[]{:S(2)}, u32[]{:S(2)}) collective-permute-start(bf16[3,784,128]{2,1,0:T(8,128)(2,1)S(1)} %constant_dynamic-update-slice_fusion.refs_14_), channel_id=1, source_target_pairs={{0,8},{4,12},{8,0},{12,4},{16,24},{20,28},{24,16},{28,20},{1,9},{5... | collective-permute-start | bytes 1806344 | tf_op jit(solution)/shard_map/ppermute | solution.py:239
  19.6 2.6 %collective-permute-start.7 = (bf16[1,784,128]{2,1,0:T(8,128)(2,1)S(1)}, bf16[1,784,128]{2,1,0:T(8,128)(2,1)S(1)}, u32[]{:S(2)}, u32[]{:S(2)}) collective-permute-start(bf16[1,784,128]{2,1,0:T(8,128)(2,1)S(1)} %copy-done.16), channel_id=1, source_target_pairs={{0,8},{4,12},{8,0},{12,4},{16,24},{20,28},{24,16},{28,20},{1,9},{5... | collective-permute-start | bytes 602120 | tf_op jit(solution)/shard_map/ppermute | solution.py:239
  22.2 3.7 %collective-permute-start.9 = (bf16[1,784,128]{2,1,0:T(8,128)(2,1)S(1)}, bf16[1,784,128]{2,1,0:T(8,128)(2,1)}, u32[]{:S(2)}, u32[]{:S(2)}) collective-permute-start(bf16[1,784,128]{2,1,0:T(8,128)(2,1)S(1)} %collective-permute-done.8.refs_12_), channel_id=1, source_target_pairs={{0,8},{4,12},{8,0},{12,4},{16,24},{20,28},{24,16},{28,20},{1,9},{5... | collective-permute-start | bytes 602120 | tf_op jit(solution)/shard_map/ppermute | solution.py:239
  25.9 12.2 %collective-permute-done.7.refs_9_ = bf16[1,784,128]{2,1,0:T(8,128)(2,1)S(1)} collective-permute-done((bf16[1,784,128]{2,1,0:T(8,128)(2,1)S(1)}, bf16[1,784,128]{2,1,0:T(8,128)(2,1)S(1)}, u32[]{:S(2)}, u32[]{:S(2)}) %collective-permute-start.7) | collective-permute-done | bytes 200736 | tf_op jit(solution)/shard_map/ppermute | solution.py:239
  38.1 1.4 %collective-permute-start.2 = (bf16[256,1024]{1,0:T(8,128)(2,1)S(1)}, bf16[256,1024]{1,0:T(8,128)(2,1)S(1)}, u32[]{:S(2)}, u32[]{:S(2)}) collective-permute-start(bf16[256,1024]{1,0:T(8,128)(2,1)S(1)} %copy-done.2), channel_id=1, source_target_pairs={{0,3},{1,2},{2,1},{3,0},{4,7},{5,6},{6,5},{7,4},{8,11},{9,10},{10,... | collective-permute-start | bytes 1572872 | tf_op jit(solution)/shard_map/ppermute | solution.py:227
  39.8 0.6 collective-permute-done.9.refs_10_
  40.4 1.1 %collective-permute-start.1 = (bf16[256,1024]{1,0:T(8,128)(2,1)S(1)}, bf16[256,1024]{1,0:T(8,128)(2,1)S(1)}, u32[]{:S(2)}, u32[]{:S(2)}) collective-permute-start(bf16[256,1024]{1,0:T(8,128)(2,1)S(1)} %copy-done.2), channel_id=1, source_target_pairs={{0,2},{1,3},{2,0},{3,1},{4,6},{5,7},{6,4},{7,5},{8,10},{9,11},{10,... | collective-permute-start | bytes 1572872 | tf_op jit(solution)/shard_map/ppermute | solution.py:227
  41.6 0.9 collective-permute-start
  42.5 11.3 %collective-permute-done.2.refs_3_ = bf16[256,1024]{1,0:T(8,128)(2,1)S(1)} collective-permute-done((bf16[256,1024]{1,0:T(8,128)(2,1)S(1)}, bf16[256,1024]{1,0:T(8,128)(2,1)S(1)}, u32[]{:S(2)}, u32[]{:S(2)}) %collective-permute-start.2) | collective-permute-done | bytes 524320 | tf_op jit(solution)/shard_map/ppermute | solution.py:227
  53.8 3.2 %collective-permute-start.11 = (bf16[1,784,128]{2,1,0:T(8,128)(2,1)S(1)}, bf16[1,784,128]{2,1,0:T(8,128)(2,1)}, u32[]{:S(2)}, u32[]{:S(2)}) collective-permute-start(bf16[1,784,128]{2,1,0:T(8,128)(2,1)S(1)} %collective-permute-done.10.refs_13_), channel_id=1, source_target_pairs={{0,8},{4,12},{8,0},{12,4},{16,24},{20,28},{24,16},{28,20},{1,9},{5... | collective-permute-start | bytes 602120 | tf_op jit(solution)/shard_map/ppermute | solution.py:239
  57.0 3.5 %collective-permute-start.20 = (bf16[3,784,128]{2,1,0:T(8,128)(2,1)S(1)}, bf16[3,784,128]{2,1,0:T(8,128)(2,1)S(1)}, u32[]{:S(2)}, u32[]{:S(2)}) collective-permute-start(bf16[3,784,128]{2,1,0:T(8,128)(2,1)S(1)} %collective-permute-done.18.refs_18_), channel_id=1, source_target_pairs={{0,8},{4,12},{8,0},{12,4},{16,24},{20,28},{24,16},{28,20},{1,9},{5... | collective-permute-start | bytes 1806344 | tf_op jit(solution)/shard_map/ppermute | solution.py:239
  60.6 7.7 %collective-permute-start.17 = (bf16[3,784,128]{2,1,0:T(8,128)(2,1)S(1)}, bf16[3,784,128]{2,1,0:T(8,128)(2,1)S(1)}, u32[]{:S(2)}, u32[]{:S(2)}) collective-permute-start(bf16[3,784,128]{2,1,0:T(8,128)(2,1)S(1)} %collective-permute-done.16.refs_17_), channel_id=1, source_target_pairs={{0,8},{4,12},{8,0},{12,4},{16,24},{20,28},{24,16},{28,20},{1,9},{5... | collective-permute-start | bytes 1806344 | tf_op jit(solution)/shard_map/ppermute | solution.py:239
  68.9 6.9 %collective-permute-done.20.refs_4_ = bf16[3,784,128]{2,1,0:T(8,128)(2,1)S(1)} collective-permute-done((bf16[3,784,128]{2,1,0:T(8,128)(2,1)S(1)}, bf16[3,784,128]{2,1,0:T(8,128)(2,1)S(1)}, u32[]{:S(2)}, u32[]{:S(2)}) %collective-permute-start.20) | collective-permute-done | bytes 602144 | tf_op jit(solution)/shard_map/ppermute | solution.py:239
  75.9 10.0 %collective-permute-done.17.refs_16_ = bf16[3,784,128]{2,1,0:T(8,128)(2,1)S(1)} collective-permute-done((bf16[3,784,128]{2,1,0:T(8,128)(2,1)S(1)}, bf16[3,784,128]{2,1,0:T(8,128)(2,1)S(1)}, u32[]{:S(2)}, u32[]{:S(2)}) %collective-permute-start.17) | collective-permute-done | bytes 602144 | tf_op jit(solution)/shard_map/ppermute | solution.py:239
  86.0 0.7 copy-done.11
  86.7 11.9 %ladder.1 = (f32[8,256,128]{2,1,0:T(8,128)}, bf16[8,256,128]{2,1,0:T(8,128)(2,1)}, f32[256,128]{1,0:T(8,128)}) custom-call(f32[2,128]{1,0:T(2,128)} %bitcast.5, bf16[256,1024]{1,0:T(8,128)(2,1)} %get-tuple-element.10.refs_0_, bf16[256,1024]{1,0:T(8,128)(2,1)} %copy-done.5, bf16[256,1024]{1,0:T(8,128)(2,1)} %copy-done.4, bf16[256,1024]{1,0:T(8,128)(2,1)} %copy-done.3, ...), custom_call_target="tpu_custom_call" | custom-call | flops 8455716864 | bytes 16777216 | tf_op jit(solution)/shard_map/ladder/pallas_call | solution.py:266
  98.7 2.1 %collective-permute-done.19.twin = bf16[8,256,128]{2,1,0:T(8,128)(2,1)S(1)} collective-permute-done((bf16[8,256,128]{2,1,0:T(8,128)(2,1)}, bf16[8,256,128]{2,1,0:T(8,128)(2,1)S(1)}, u32[]{:S(2)}, u32[]{:S(2)}) %collective-permute-start.19) | collective-permute-done | bytes 524320 | tf_op jit(solution)/shard_map/ppermute | solution.py:230
  100.8 0.8 copy-done.6
  101.8 7.4 %update.1 = (bf16[256,1024]{1,0:T(8,128)(2,1)}, f32[256,1024]{1,0:T(8,128)}) custom-call(s32[2,8]{1,0:T(2,128)} %live.3, bf16[256,1024]{1,0:T(8,128)(2,1)} %amplitudes.3, bf16[256,1024]{1,0:T(8,128)(2,1)} %driver.1, f32[8,256,128]{2,1,0:T(8,128)} %get-tuple-element.15.own, bf16[8,256,128]{2,1,0:T(8,128)(2,1)} %copy-done.6, ...), custom_call_target="tpu_custom_call" | custom-call | tf_op jit(solution)/shard_map/update/pallas_call | solution.py:297
  (66 shorter events, 1.8 us)
Async XLA Ops:
  3.4 9.0 %collective-permute-start.12 = (bf16[1,784,128]{2,1,0:T(8,128)(2,1)}, bf16[1,784,128]{2,1,0:T(8,128)(2,1)S(1)}, u32[]{:S(2)}, u32[]{:S(2)}) collective-permute-start(bf16[1,784,128]{2,1,0:T(8,128)(2,1)} %get-tuple-element.12), channel_id=1, source_target_pairs={{0,1},{1,0},{2,3},{3,2},{4,5},{5,4},{6,7},{7,6},{8,9},{9,8},{10,11... | collective-permute-start | bytes 602120 | tf_op jit(solution)/shard_map/ppermute | solution.py:227
  6.4 11.0 %collective-permute-start.13 = (bf16[1,784,128]{2,1,0:T(8,128)(2,1)}, bf16[1,784,128]{2,1,0:T(8,128)(2,1)S(1)}, u32[]{:S(2)}, u32[]{:S(2)}) collective-permute-start(bf16[1,784,128]{2,1,0:T(8,128)(2,1)} %get-tuple-element.13), channel_id=1, source_target_pairs={{0,2},{1,3},{2,0},{3,1},{4,6},{5,7},{6,4},{7,5},{8,10},{9,11},{10,... | collective-permute-start | bytes 602120 | tf_op jit(solution)/shard_map/ppermute | solution.py:227
  7.9 9.5 %collective-permute-start.14 = (bf16[1,784,128]{2,1,0:T(8,128)(2,1)}, bf16[1,784,128]{2,1,0:T(8,128)(2,1)S(1)}, u32[]{:S(2)}, u32[]{:S(2)}) collective-permute-start(bf16[1,784,128]{2,1,0:T(8,128)(2,1)} %get-tuple-element.14), channel_id=1, source_target_pairs={{0,3},{1,2},{2,1},{3,0},{4,7},{5,6},{6,5},{7,4},{8,11},{9,10},{10,... | collective-permute-start | bytes 602120 | tf_op jit(solution)/shard_map/ppermute | solution.py:227
  17.4 68.4 %copy-start.7 = (bf16[3,784,128]{2,1,0:T(8,128)(2,1)}, bf16[3,784,128]{2,1,0:T(8,128)(2,1)S(1)}, u32[]{:S(2)}) copy-start(bf16[3,784,128]{2,1,0:T(8,128)(2,1)S(1)} %constant_dynamic-update-slice_fusion.refs_14_) | copy-start | bytes 1806340
  17.4 22.2 %collective-permute-start.15 = (bf16[3,784,128]{2,1,0:T(8,128)(2,1)S(1)}, bf16[3,784,128]{2,1,0:T(8,128)(2,1)S(1)}, u32[]{:S(2)}, u32[]{:S(2)}) collective-permute-start(bf16[3,784,128]{2,1,0:T(8,128)(2,1)S(1)} %constant_dynamic-update-slice_fusion.refs_14_), channel_id=1, source_target_pairs={{0,8},{4,12},{8,0},{12,4},{16,24},{20,28},{24,16},{28,20},{1,9},{5... | collective-permute-start | bytes 1806344 | tf_op jit(solution)/shard_map/ppermute | solution.py:239
  19.1 3.2 %collective-permute-start.8 = (bf16[1,784,128]{2,1,0:T(8,128)(2,1)S(1)}, bf16[1,784,128]{2,1,0:T(8,128)(2,1)S(1)}, u32[]{:S(2)}, u32[]{:S(2)}) collective-permute-start(bf16[1,784,128]{2,1,0:T(8,128)(2,1)S(1)} %copy-done.16), channel_id=1, source_target_pairs={{0,4},{4,0},{8,16},{12,20},{16,8},{20,12},{24,28},{28,24},{1,5},{5... | collective-permute-start | bytes 602120 | tf_op jit(solution)/shard_map/ppermute | solution.py:239
  19.1 22.5 %collective-permute-start.3 = (bf16[256,1024]{1,0:T(8,128)(2,1)S(1)}, bf16[256,1024]{1,0:T(8,128)(2,1)S(1)}, u32[]{:S(2)}, u32[]{:S(2)}) collective-permute-start(bf16[256,1024]{1,0:T(8,128)(2,1)S(1)} %copy-done.2), channel_id=1, source_target_pairs={{0,4},{4,0},{8,12},{12,8},{16,20},{20,16},{24,28},{28,24},{1,5},{5... | collective-permute-start | bytes 1572872 | tf_op jit(solution)/shard_map/ppermute | solution.py:230
  19.6 18.6 %collective-permute-start.7 = (bf16[1,784,128]{2,1,0:T(8,128)(2,1)S(1)}, bf16[1,784,128]{2,1,0:T(8,128)(2,1)S(1)}, u32[]{:S(2)}, u32[]{:S(2)}) collective-permute-start(bf16[1,784,128]{2,1,0:T(8,128)(2,1)S(1)} %copy-done.16), channel_id=1, source_target_pairs={{0,8},{4,12},{8,0},{12,4},{16,24},{20,28},{24,16},{28,20},{1,9},{5... | collective-permute-start | bytes 602120 | tf_op jit(solution)/shard_map/ppermute | solution.py:239
  22.2 63.6 %copy-start.17 = (bf16[1,784,128]{2,1,0:T(8,128)(2,1)}, bf16[1,784,128]{2,1,0:T(8,128)(2,1)S(1)}, u32[]{:S(2)}) copy-start(bf16[1,784,128]{2,1,0:T(8,128)(2,1)S(1)} %collective-permute-done.8.refs_12_) | copy-start | bytes 602116
  22.2 18.2 %collective-permute-start.9 = (bf16[1,784,128]{2,1,0:T(8,128)(2,1)S(1)}, bf16[1,784,128]{2,1,0:T(8,128)(2,1)}, u32[]{:S(2)}, u32[]{:S(2)}) collective-permute-start(bf16[1,784,128]{2,1,0:T(8,128)(2,1)S(1)} %collective-permute-done.8.refs_12_), channel_id=1, source_target_pairs={{0,8},{4,12},{8,0},{12,4},{16,24},{20,28},{24,16},{28,20},{1,9},{5... | collective-permute-start | bytes 602120 | tf_op jit(solution)/shard_map/ppermute | solution.py:239
  38.1 2.3 %collective-permute-start.10 = (bf16[1,784,128]{2,1,0:T(8,128)(2,1)S(1)}, bf16[1,784,128]{2,1,0:T(8,128)(2,1)S(1)}, u32[]{:S(2)}, u32[]{:S(2)}) collective-permute-start(bf16[1,784,128]{2,1,0:T(8,128)(2,1)S(1)} %collective-permute-done.7.refs_9_), channel_id=1, source_target_pairs={{0,4},{4,0},{8,16},{12,20},{16,8},{20,12},{24,28},{28,24},{1,5},{5... | collective-permute-start | bytes 602120 | tf_op jit(solution)/shard_map/ppermute | solution.py:239
  38.1 15.7 %collective-permute-start.2 = (bf16[256,1024]{1,0:T(8,128)(2,1)S(1)}, bf16[256,1024]{1,0:T(8,128)(2,1)S(1)}, u32[]{:S(2)}, u32[]{:S(2)}) collective-permute-start(bf16[256,1024]{1,0:T(8,128)(2,1)S(1)} %copy-done.2), channel_id=1, source_target_pairs={{0,3},{1,2},{2,1},{3,0},{4,7},{5,6},{6,5},{7,4},{8,11},{9,10},{10,... | collective-permute-start | bytes 1572872 | tf_op jit(solution)/shard_map/ppermute | solution.py:227
  39.6 17.4 %collective-permute-start.18 = (bf16[3,784,128]{2,1,0:T(8,128)(2,1)S(1)}, bf16[3,784,128]{2,1,0:T(8,128)(2,1)S(1)}, u32[]{:S(2)}, u32[]{:S(2)}) collective-permute-start(bf16[3,784,128]{2,1,0:T(8,128)(2,1)S(1)} %collective-permute-done.15.refs_15_), channel_id=1, source_target_pairs={{0,4},{4,0},{8,16},{12,20},{16,8},{20,12},{24,28},{28,24},{1,5},{5... | collective-permute-start | bytes 1806344 | tf_op jit(solution)/shard_map/ppermute | solution.py:239
  40.4 20.2 %collective-permute-start.16 = (bf16[3,784,128]{2,1,0:T(8,128)(2,1)S(1)}, bf16[3,784,128]{2,1,0:T(8,128)(2,1)S(1)}, u32[]{:S(2)}, u32[]{:S(2)}) collective-permute-start(bf16[3,784,128]{2,1,0:T(8,128)(2,1)S(1)} %constant_dynamic-update-slice_fusion.refs_14_), channel_id=1, source_target_pairs={{0,4},{4,0},{8,16},{12,20},{16,8},{20,12},{24,28},{28,24},{1,5},{5... | collective-permute-start | bytes 1806344 | tf_op jit(solution)/shard_map/ppermute | solution.py:239
  40.4 27.9 %collective-permute-start.1 = (bf16[256,1024]{1,0:T(8,128)(2,1)S(1)}, bf16[256,1024]{1,0:T(8,128)(2,1)S(1)}, u32[]{:S(2)}, u32[]{:S(2)}) collective-permute-start(bf16[256,1024]{1,0:T(8,128)(2,1)S(1)} %copy-done.2), channel_id=1, source_target_pairs={{0,2},{1,3},{2,0},{3,1},{4,6},{5,7},{6,4},{7,5},{8,10},{9,11},{10,... | collective-permute-start | bytes 1572872 | tf_op jit(solution)/shard_map/ppermute | solution.py:227
  41.6 26.7 %collective-permute-start = (bf16[256,1024]{1,0:T(8,128)(2,1)S(1)}, bf16[256,1024]{1,0:T(8,128)(2,1)S(1)}, u32[]{:S(2)}, u32[]{:S(2)}) collective-permute-start(bf16[256,1024]{1,0:T(8,128)(2,1)S(1)} %copy-done.2), channel_id=1, source_target_pairs={{0,1},{1,0},{2,3},{3,2},{4,5},{5,4},{6,7},{7,6},{8,9},{9,8},{10,11... | collective-permute-start | bytes 1572872 | tf_op jit(solution)/shard_map/ppermute | solution.py:227
  53.8 15.0 %collective-permute-start.11 = (bf16[1,784,128]{2,1,0:T(8,128)(2,1)S(1)}, bf16[1,784,128]{2,1,0:T(8,128)(2,1)}, u32[]{:S(2)}, u32[]{:S(2)}) collective-permute-start(bf16[1,784,128]{2,1,0:T(8,128)(2,1)S(1)} %collective-permute-done.10.refs_13_), channel_id=1, source_target_pairs={{0,8},{4,12},{8,0},{12,4},{16,24},{20,28},{24,16},{28,20},{1,9},{5... | collective-permute-start | bytes 602120 | tf_op jit(solution)/shard_map/ppermute | solution.py:239
  57.0 18.8 %collective-permute-start.20 = (bf16[3,784,128]{2,1,0:T(8,128)(2,1)S(1)}, bf16[3,784,128]{2,1,0:T(8,128)(2,1)S(1)}, u32[]{:S(2)}, u32[]{:S(2)}) collective-permute-start(bf16[3,784,128]{2,1,0:T(8,128)(2,1)S(1)} %collective-permute-done.18.refs_18_), channel_id=1, source_target_pairs={{0,8},{4,12},{8,0},{12,4},{16,24},{20,28},{24,16},{28,20},{1,9},{5... | collective-permute-start | bytes 1806344 | tf_op jit(solution)/shard_map/ppermute | solution.py:239
  60.6 25.3 %collective-permute-start.17 = (bf16[3,784,128]{2,1,0:T(8,128)(2,1)S(1)}, bf16[3,784,128]{2,1,0:T(8,128)(2,1)S(1)}, u32[]{:S(2)}, u32[]{:S(2)}) collective-permute-start(bf16[3,784,128]{2,1,0:T(8,128)(2,1)S(1)} %collective-permute-done.16.refs_17_), channel_id=1, source_target_pairs={{0,8},{4,12},{8,0},{12,4},{16,24},{20,28},{24,16},{28,20},{1,9},{5... | collective-permute-start | bytes 1806344 | tf_op jit(solution)/shard_map/ppermute | solution.py:239
  68.3 7.5 %collective-permute-start.6 = (bf16[256,1024]{1,0:T(8,128)(2,1)S(1)}, bf16[256,1024]{1,0:T(8,128)(2,1)S(1)}, u32[]{:S(2)}, u32[]{:S(2)}) collective-permute-start(bf16[256,1024]{1,0:T(8,128)(2,1)S(1)} %collective-permute-done.2.refs_3_), channel_id=1, source_target_pairs={{0,4},{4,0},{8,12},{12,8},{16,20},{20,16},{24,28},{28,24},{1,5},{5... | collective-permute-start | bytes 1572872 | tf_op jit(solution)/shard_map/ppermute | solution.py:230
  68.3 7.5 %collective-permute-start.5 = (bf16[256,1024]{1,0:T(8,128)(2,1)S(1)}, bf16[256,1024]{1,0:T(8,128)(2,1)S(1)}, u32[]{:S(2)}, u32[]{:S(2)}) collective-permute-start(bf16[256,1024]{1,0:T(8,128)(2,1)S(1)} %collective-permute-done.1.refs_2_), channel_id=1, source_target_pairs={{0,4},{4,0},{8,12},{12,8},{16,20},{20,16},{24,28},{28,24},{1,5},{5... | collective-permute-start | bytes 1572872 | tf_op jit(solution)/shard_map/ppermute | solution.py:230
  68.8 7.1 %collective-permute-start.4 = (bf16[256,1024]{1,0:T(8,128)(2,1)S(1)}, bf16[256,1024]{1,0:T(8,128)(2,1)S(1)}, u32[]{:S(2)}, u32[]{:S(2)}) collective-permute-start(bf16[256,1024]{1,0:T(8,128)(2,1)S(1)} %collective-permute-done.refs_1_), channel_id=1, source_target_pairs={{0,4},{4,0},{8,12},{12,8},{16,20},{20,16},{24,28},{28,24},{1,5},{5... | collective-permute-start | bytes 1572872 | tf_op jit(solution)/shard_map/ppermute | solution.py:230
  75.8 25.0 %collective-permute-start.21 = (bf16[3,784,128]{2,1,0:T(8,128)(2,1)S(1)}, bf16[3,784,128]{2,1,0:T(8,128)(2,1)S(1)}, u32[]{:S(2)}, u32[]{:S(2)}) collective-permute-start(bf16[3,784,128]{2,1,0:T(8,128)(2,1)S(1)} %collective-permute-done.20.refs_4_), channel_id=1, source_target_pairs={{0,4},{4,0},{8,12},{12,8},{16,20},{20,16},{24,28},{28,24},{1,5},{5... | collective-permute-start | bytes 1806344 | tf_op jit(solution)/shard_map/ppermute | solution.py:230
  98.6 2.2 %collective-permute-start.19 = (bf16[8,256,128]{2,1,0:T(8,128)(2,1)}, bf16[8,256,128]{2,1,0:T(8,128)(2,1)S(1)}, u32[]{:S(2)}, u32[]{:S(2)}) collective-permute-start(bf16[8,256,128]{2,1,0:T(8,128)(2,1)} %get-tuple-element.16), channel_id=1, source_target_pairs={{0,4},{4,0},{8,12},{12,8},{16,20},{20,16},{24,28},{28,24},{1,5},{5... | collective-permute-start | bytes 1572872 | tf_op jit(solution)/shard_map/ppermute | solution.py:230
  (18 other events, 328.4 us)

commit v3 on v0

v3 whole, which is shorter than its diff:
```python
import functools
import math

import jax
import jax.numpy as jnp
from jax import lax
from jax.experimental import pallas as pl
from jax.experimental.pallas import tpu as pltpu
from jax.sharding import PartitionSpec as P

SPARE_VMEM = 4 * 1024 * 1024
CORES = 2
NOTE_ROWS = 16
FIRST_FLOPS = 10**8
SECOND_FLOPS = 10**9


def pack_kernel(n_v, cap, columns, live, integrals, amplitudes, *refs):
    parcels, (masked, origin, codes, tiles, amps, sems) = refs[:n_v], refs[n_v:]
    rows, slots, tile, _ = integrals.shape
    me = lax.axis_index("vpair")
    copies = [
        pltpu.make_async_copy(integrals, tiles, sems.at[0]),
        pltpu.make_async_copy(amplitudes, amps, sems.at[1]),
    ]
    for copy in copies:
        copy.start()
    counts = [jnp.int32(0)] * n_v
    for i in range(n_v * cap):
        origin[i] = 0
        codes[i] = -1
    for row in range(rows):
        for slot in range(slots):
            column = columns[slot, row]
            partner = lax.div(column, rows) ^ me
            place = counts[0]
            for j in range(1, n_v):
                place = jnp.where(partner == j, counts[j], place)
            counts = [counts[j] + (partner == j).astype(jnp.int32) for j in range(n_v)]
            at = partner * cap + place
            origin[at] = row * slots + slot
            codes[at] = row * rows + lax.rem(column, rows)
    copies[0].wait()
    lane = lax.broadcasted_iota(jnp.int32, (NOTE_ROWS, tile), 1)
    for j in range(n_v):
        note = jnp.full((NOTE_ROWS, tile), -1, jnp.int32)
        for k in range(cap):
            entry = origin[j * cap + k]
            parcels[j][0, pl.ds(k * tile, tile)] = tiles[
                lax.div(entry, slots), lax.rem(entry, slots)
            ]
            note = jnp.where(lane == k, codes[j * cap + k], note)
        parcels[j][0, pl.ds(cap * tile, NOTE_ROWS)] = note.astype(jnp.float32).astype(
            integrals.dtype
        )
    copies[1].wait()
    for o in range(live.shape[0]):
        for c in range(live.shape[1]):
            at = (pl.ds(o * tile, tile), pl.ds(c * tile, tile))
            kept = live[o, c].astype(jnp.float32)
            masked[at] = (amps[at].astype(jnp.float32) * kept).astype(masked.dtype)


def fetch(arrays, units, note_buf, unit_sems, note_sems):
    tile = units.shape[-1]
    bounds, first = [], 0
    for array in arrays:
        bounds.append(pl.ds(first, array.shape[0]))
        first += array.shape[0]
    note_rows = pl.ds(units.shape[1] - NOTE_ROWS, NOTE_ROWS)
    note_copies = [
        pltpu.make_async_copy(array.at[:, note_rows], note_buf.at[part], note_sems.at[i])
        for i, (array, part) in enumerate(zip(arrays, bounds))
    ]
    unit_copies = [
        pltpu.make_async_copy(array, units.at[part], unit_sems.at[i])
        for i, (array, part) in enumerate(zip(arrays, bounds))
    ]
    for copy in note_copies + unit_copies:
        copy.start()
    return note_copies, unit_copies


def read_notes(note_copies, note_buf, notes_wide, notes, sem):
    for copy in note_copies:
        copy.wait()
    for u in range(note_buf.shape[0]):
        notes_wide[pl.ds(u, 1)] = note_buf[u].astype(jnp.float32).astype(jnp.int32)[:1]
    copy = pltpu.make_async_copy(notes_wide, notes, sem)
    copy.start()
    copy.wait()


def clear_pairs(pairs):
    pairs[...] = jnp.zeros_like(pairs)


def add_unit(unit, j, cap, rows, amps, units, notes, pairs, total):
    tile = units.shape[-1]

    def place(k):
        code = notes[unit, k]
        used = code >= 0
        row = jnp.where(used, lax.div(code, rows), 0)
        column = jnp.where(used, lax.rem(code, rows), rows)
        return amps[j, :, pl.ds(pl.multiple_of(row * tile, tile), tile)], column

    for k in range(0, cap - 1, 2):
        pair = pairs.at[k // 2]
        pair[pl.ds(0, tile), pl.ds(0, tile)] = units[unit, pl.ds(k * tile, tile)]
        pair[pl.ds(tile, tile), pl.ds(tile, tile)] = units[unit, pl.ds((k + 1) * tile, tile)]
        (left, first), (right, second) = place(k), place(k + 1)
        both = jnp.dot(
            jnp.concatenate([left, right], axis=1),
            pair[...],
            preferred_element_type=jnp.float32,
        )
        total[first] += both[:, :tile]
        total[second] += both[:, tile:]
    if cap % 2:
        left, column = place(cap - 1)
        total[column] += jnp.dot(
            left,
            units[unit, pl.ds((cap - 1) * tile, tile)],
            preferred_element_type=jnp.float32,
        )


def ladder_kernel(cap, layout, amps, *refs):
    arrays, (total, units, note_buf, notes_wide, notes, pairs, *sems) = (
        refs[: len(layout)],
        refs[len(layout) :],
    )
    rows = total.shape[0] - 1
    note_copies, unit_copies = fetch(arrays, units, note_buf, sems[0], sems[1])
    clear_pairs(pairs)
    total[...] = jnp.zeros_like(total)
    read_notes(note_copies, note_buf, notes_wide, notes, sems[2])
    first = 0
    for copy, partners in zip(unit_copies, layout):
        copy.wait()

        def one(i, carry, first=first, partners=partners):
            add_unit(first + i, partners[0] + i, cap, rows, amps, units, notes, pairs, total)
            return carry

        lax.fori_loop(0, len(partners), one, 0)
        first += len(partners)


def first_ladder_kernel(cap, layout, occupied, *refs):
    n_in = 1 + len(layout)
    occupied_out = refs[n_in + 1]
    tile = occupied_out.shape[-1]
    for o in range(occupied.shape[0]):
        wide = jnp.broadcast_to(occupied[pl.ds(o, 1)], (tile, tile))
        occupied_out[pl.ds(o * tile, tile)] = wide.T
    ladder_kernel(cap, layout, *refs[: n_in + 1], *refs[n_in + 2 :])


def second_ladder_kernel(cap, layout, before, *refs):
    n_in = 1 + len(layout)
    own, twin, total = refs[n_in : n_in + 3]
    ladder_kernel(cap, layout, *refs[:n_in], total, *refs[n_in + 3 :])
    rows, n_rows, _ = own.shape
    own[...] = before[:rows, :n_rows] + total[:rows, :n_rows]
    twin[...] = (before[:rows, n_rows:] + total[:rows, n_rows:]).astype(twin.dtype)


def update_kernel(
    cap, live, amplitudes, driver, own, twin, occupied, virtual, *refs
):
    amps_all, *arrays = refs[: 1 + CORES]
    new, residual, a_buf, units, note_buf, notes_wide, notes, pairs, total = refs[1 + CORES : -4]
    a_sem, *sems = refs[-4:]
    group, n_rows, tile = own.shape
    rows = live.shape[1]
    step = pl.program_id(0)
    n_a = a_buf.shape[0]

    @pl.when(step == 0)
    def _():
        total[...] = jnp.zeros_like(total)
        note_copies, unit_copies = fetch(arrays, units, note_buf, sems[0], sems[1])
        a_copy = pltpu.make_async_copy(
            amps_all.at[pl.ds(amps_all.shape[0] - n_a, n_a), pl.ds(0, n_rows)], a_buf, a_sem
        )
        a_copy.start()
        clear_pairs(pairs)
        read_notes(note_copies, note_buf, notes_wide, notes, sems[2])
        a_copy.wait()
        for copy in unit_copies:
            copy.wait()

        def one(i, carry):
            add_unit(i, lax.rem(i, n_a), cap, rows, a_buf, units, notes, pairs, total)
            return carry

        lax.fori_loop(0, CORES * n_a, one, 0)

    for o in range(live.shape[0]):
        for c in range(group):
            here = pl.ds(o * tile, tile)
            at = (here, pl.ds(c * tile, tile))
            kept = live[o, step * group + c].astype(jnp.float32)
            amps = amplitudes[at].astype(jnp.float32)
            masked = (amps * kept).astype(jnp.bfloat16).astype(jnp.float32)
            denominator = occupied[here, :] - virtual[:, pl.ds(c * tile, tile)]
            ladder = (
                own[c, here] + twin[c, here].astype(jnp.float32) + total[step * group + c, here]
            )
            rest = (driver[at].astype(jnp.float32) + ladder + denominator * amps) * kept
            residual[at] = rest
            new[at] = (masked - rest / denominator).astype(new.dtype)


def on_device(
    amplitudes,
    tile_live,
    integrals,
    integral_columns,
    driver_terms,
    occupied_energy,
    virtual_energy,
):
    n_rows, width = amplitudes.shape
    rows, slots, tile, _ = integrals.shape
    n_v, n_o = lax.axis_size("vpair"), lax.axis_size("opair")
    n_z = n_o // CORES
    cap = -(-(rows * slots) // n_v)
    height = cap * tile + NOTE_ROWS
    dtype = integrals.dtype
    in_smem = pl.BlockSpec(memory_space=pltpu.SMEM)
    in_vmem = pl.BlockSpec(memory_space=pltpu.VMEM)
    anywhere = pl.BlockSpec(memory_space=pl.ANY)
    in_hbm = pl.BlockSpec(memory_space=pltpu.HBM)

    def params(*buffers):
        size = sum(math.prod(shape) * jnp.dtype(kind).itemsize for shape, kind in buffers)
        return pltpu.CompilerParams(vmem_limit_bytes=size + SPARE_VMEM)

    parcel = (1, height, tile)
    *parcels, masked = pl.pallas_call(
        functools.partial(pack_kernel, n_v, cap),
        out_shape=[jax.ShapeDtypeStruct(parcel, dtype)] * n_v
        + [jax.ShapeDtypeStruct(amplitudes.shape, amplitudes.dtype)],
        in_specs=[in_smem, in_smem, in_hbm, in_hbm],
        out_specs=[in_vmem] * (n_v + 1),
        scratch_shapes=[pltpu.SMEM((n_v * cap,), jnp.int32)] * 2
        + [
            pltpu.VMEM(integrals.shape, dtype),
            pltpu.VMEM(amplitudes.shape, dtype),
            pltpu.SemaphoreType.DMA((2,)),
        ],
        compiler_params=params(
            (integrals.shape, dtype), ((n_v, *parcel), dtype), ((2, n_rows, width), dtype)
        ),
        name="pack",
    )(integral_columns.T, tile_live, integrals, amplitudes)

    def across_v(value, j):
        name = "amplitudes" if value.ndim == 2 else "parcels"
        with jax.named_scope(f"{name}_from_partner_{j}"):
            return lax.ppermute(value, "vpair", [(i, i ^ j) for i in range(n_v)])

    def across_core(value):
        return lax.ppermute(value, "opair", [(i, i ^ 1) for i in range(n_o)])

    def next_on_ring(value, name):
        ring = [*range(0, n_z, 2), *range(n_z - 1 - n_z % 2, 0, -2)]
        pairs = [
            (source * CORES + core, target * CORES + core)
            for source, target in zip(ring, ring[1:] + ring[:1])
            for core in range(CORES)
        ]
        with jax.named_scope(name):
            return lax.ppermute(value, "opair", pairs)

    def join(values):
        return jnp.concatenate(values) if len(values) > 1 else values[0]

    def after(values, others):
        return lax.optimization_barrier((values, others))[0]

    others = list(range(1, n_v))
    groups = {"near": [0], "early": others[: n_v // 2 - 1], "late": others[n_v // 2 - 1 :]}
    arrived = {0: parcels[0]} | {j: across_v(parcels[j], j) for j in others}
    hops = {name: [join([arrived[j] for j in groups[name]])] for name in groups}
    for hop in range(1, n_z):
        for name in groups:
            hops[name].append(next_on_ring(hops[name][-1], f"{name}_hop_{hop}"))

    a_parts = {0: masked}
    ready = after(masked, hops["late"][0])
    for j in others:
        a_parts[j] = across_v(ready, j)
    with jax.named_scope("twin_amplitudes"):
        a_twins = {j: across_core(a_parts[j]) for j in range(n_v)}
    amps = jnp.stack([jnp.concatenate([a_parts[j], a_twins[j]]) for j in range(n_v)])

    sums = (rows + 1, CORES * n_rows, tile)
    pairs = (max(cap // 2, 1), 2 * tile, 2 * tile)

    def ladder_call(kernel, found, before, out_shape, extra_scratch, flops, name):
        arrays, layout = [hops[name][hop] for name, hop in found], [groups[name] for name, _ in found]
        n_units = sum(len(partners) for partners in layout)
        units = (n_units, height, tile)
        return pl.pallas_call(
            functools.partial(kernel, cap, layout),
            out_shape=out_shape,
            in_specs=[in_vmem, in_vmem] + [anywhere] * len(arrays),
            out_specs=[in_vmem] * len(out_shape),
            scratch_shapes=extra_scratch
            + [
                pltpu.VMEM(units, dtype),
                pltpu.VMEM((n_units, NOTE_ROWS, tile), dtype),
                pltpu.VMEM((n_units, tile), jnp.int32),
                pltpu.SMEM((n_units, tile), jnp.int32),
                pltpu.VMEM(pairs, dtype),
                pltpu.SemaphoreType.DMA((len(arrays),)),
                pltpu.SemaphoreType.DMA((len(arrays),)),
                pltpu.SemaphoreType.DMA,
            ],
            compiler_params=params(
                (units, dtype), (sums, jnp.float32), (sums, jnp.float32), (amps.shape, dtype)
            ),
            cost_estimate=pl.CostEstimate(
                flops=flops,
                bytes_accessed=1024 * 1024,
                transcendentals=0,
            ),
            name=name,
        )(before, amps, *arrays)

    tail = [("late", n_z - 2), ("near", n_z - 1), ("early", n_z - 1)]
    head = [(name, hop) for hop in range(n_z - 1) for name in groups if (name, hop) not in tail]
    total, occupied = ladder_call(
        first_ladder_kernel,
        head,
        occupied_energy.reshape(-1, tile),
        [
            jax.ShapeDtypeStruct(sums, jnp.float32),
            jax.ShapeDtypeStruct((n_rows, tile), jnp.float32),
        ],
        [],
        FIRST_FLOPS,
        "ladder_first",
    )
    own, twin = ladder_call(
        second_ladder_kernel,
        tail,
        total,
        [
            jax.ShapeDtypeStruct((rows, n_rows, tile), jnp.float32),
            jax.ShapeDtypeStruct((rows, n_rows, tile), jnp.bfloat16),
        ],
        [pltpu.VMEM(sums, jnp.float32)],
        SECOND_FLOPS,
        "ladder_second",
    )
    last, behind = after(hops["late"][-1], twin), groups["late"]
    twin = across_core(twin)

    group = 2 if rows % 2 == 0 else 1
    a_buf = (len(behind), n_rows, width)
    units = (CORES * len(behind), height, tile)
    sums = (rows + 1, n_rows, tile)
    block = pl.BlockSpec((n_rows, group * tile), lambda c: (0, c))
    tiles = pl.BlockSpec((group, n_rows, tile), lambda c: (c, 0, 0))
    return pl.pallas_call(
        functools.partial(update_kernel, cap),
        grid=(rows // group,),
        out_shape=[
            jax.ShapeDtypeStruct((n_rows, width), jnp.bfloat16),
            jax.ShapeDtypeStruct((n_rows, width), jnp.float32),
        ],
        in_specs=[
            in_smem,
            block,
            block,
            tiles,
            tiles,
            pl.BlockSpec((n_rows, tile), lambda c: (0, 0)),
            pl.BlockSpec((1, group * tile), lambda c: (0, c)),
        ]
        + [anywhere] * (1 + CORES),
        out_specs=[block, block],
        scratch_shapes=[
            pltpu.VMEM(a_buf, amplitudes.dtype),
            pltpu.VMEM(units, dtype),
            pltpu.VMEM((units[0], NOTE_ROWS, tile), dtype),
            pltpu.VMEM((units[0], tile), jnp.int32),
            pltpu.SMEM((units[0], tile), jnp.int32),
            pltpu.VMEM(pairs, dtype),
            pltpu.VMEM(sums, jnp.float32),
            pltpu.SemaphoreType.DMA,
            pltpu.SemaphoreType.DMA((CORES,)),
            pltpu.SemaphoreType.DMA((CORES,)),
            pltpu.SemaphoreType.DMA,
        ],
        compiler_params=params(
            (a_buf, dtype), (units, dtype), (sums, jnp.float32), (sums, jnp.float32)
        ),
        name="update",
    )(
        tile_live,
        amplitudes,
        driver_terms,
        own,
        twin,
        occupied,
        virtual_energy.reshape(1, width),
        amps,
        last,
        across_core(last),
    )


def solution(mesh):
    in_specs = (
        P("opair", "vpair"),
        P("opair", "vpair"),
        P("vpair", "opair", None, None),
        P("vpair", "opair"),
        P("opair", "vpair"),
        P("opair"),
        P("vpair"),
    )
    out_specs = (P("opair", "vpair"), P("opair", "vpair"))
    return jax.shard_map(
        on_device, mesh=mesh, in_specs=in_specs, out_specs=out_specs, check_vma=False
    )
```

time: 219 us -> 80.5 us (0.37)
  other arithmetic: 78.7 us -> 0.85 us
  waiting for transfers between devices: 83.6 us -> 30.6 us
  starting transfers between devices: 0.08 us -> 26 us
  Pallas kernels: 0 us -> 18.3 us
  blocking collectives: 14.5 us -> 0 us
  matrix products: 14.1 us -> 0 us
  between operations: 14.2 us -> 0.83 us
  local copies, waits for them, and re-layouts: 12.6 us -> 3.69 us
    scatter-add x8 -> x0, other arithmetic: 68.3 us -> none  [on_device(): term = term.at[landing].add(products, mode='drop')]
    all_gather x1 -> x0, waiting for transfers between devices: 50 us -> none  [on_device(): lax.all_gather(integrals, 'opair', axis=1, tiled=True)]
    reduce_scatter x1 -> x0, waiting for transfers between devices: 33 us -> none  [on_device(): lax.psum_scatter(term.astype(jnp.bfloat16), 'vpair', scatter_dimension=0,...]
    ppermute x0 -> x21, waiting for transfers between devices: none -> 30.6 us  [the longest x9 17.8 us: next_on_ring(): return lax.ppermute(value, 'opair', pairs)]
    ppermute x0 -> x21, starting transfers between devices: none -> 26 us  [the longest x9 15.4 us: next_on_ring(): return lax.ppermute(value, 'opair', pairs)]
    pallas_call x0 -> x4, Pallas kernels: none -> 18.3 us  [the longest x2 11.8 us: ladder_call(): pl.pallas_call(functools.partial(kernel, cap, layout), out_shape=out_shap...]
    all_gather x1 -> x0, blocking collectives: 14.5 us -> none  [on_device(): lax.all_gather(integral_columns, 'opair', axis=1, tiled=True)]
    dot_general x8 -> x0, matrix products: 14.1 us -> none  [on_device(): jnp.einsum('rx,kxy->kry', masked_tiles[:, source, :], gathered[source], p...]
  transfers between devices with their start and end apart: 2 -> 21, of which waited for: 2 -> 9; matrix products, arithmetic and copies ran while one was open for 2% -> 1% of each run, Pallas kernels for 0% -> 15%
where the time goes in v3:
time: 80.5 us; the launch traced here: 80.3 us
  waiting for transfers between devices  30.6 us (38%)
  starting transfers between devices  26 us (32%)
  Pallas kernels  18.3 us (23%)
  local copies, waits for them, and re-layouts  3.69 us (5%)
  other arithmetic  0.85 us (1%)
  between operations  0.83 us (1%)
    ppermute x9, waiting for transfers between devices, next_on_ring(): return lax.ppermute(value, 'opair', pairs)  17.8 us
    ppermute x9, starting transfers between devices, next_on_ring(): return lax.ppermute(value, 'opair', pairs)  15.4 us
    pallas_call x2, Pallas kernels, ladder_call(): pl.pallas_call(functools.partial(kernel, cap, layout), out_shape=out_shap...  11.8 us
    ppermute x6, waiting for transfers between devices, across_v(): return lax.ppermute(value, 'vpair', [(i, i ^ j) for i in range(n_v)])  11.1 us
    ppermute x6, starting transfers between devices, across_v(): return lax.ppermute(value, 'vpair', [(i, i ^ j) for i in range(n_v)])  9.92 us
    pallas_call x1, Pallas kernels, on_device(): pl.pallas_call(functools.partial(update_kernel, cap), grid=(rows // group...  5.32 us
    unnamed x19, local copies, waits for them, and re-layouts  3.66 us
    ppermute x6, waiting for transfers between devices, across_core(): return lax.ppermute(value, 'opair', [(i, i ^ 1) for i in range(n_o)])  1.74 us
  transfers between devices with their start and end apart: 21, of which 9 were waited for; matrix products, arithmetic and copies ran while one was open for 1% of the time, Pallas kernels for 15%

profile of v3, /device:TPU:0, one launch (start us, length us, event | category | flops | bytes accessed | tf_op | source)
XLA Modules:
  0.0 80.3 jit_solution(5963251011249579129)
XLA Ops:
  1.7 1.1 %copy-done.2 = bf16[8,3,128,128]{3,2,1,0:T(8,128)(2,1)S(1)} copy-done((bf16[8,3,128,128]{3,2,1,0:T(8,128)(2,1)S(1)}, bf16[8,3,128,128]{3,2,1,0:T(8,128)(2,1)}, u32[]{:S(2)}) %copy-start.2) | copy-done | bytes 786456
  4.2 1.2 %pack.1 = (bf16[1,784,128]{2,1,0:T(8,128)(2,1)S(1)}, bf16[1,784,128]{2,1,0:T(8,128)(2,1)S(1)}, bf16[1,784,128]{2,1,0:T(8,128)(2,1)S(1)}, bf16[1,784,128]{2,1,0:T(8,128)(2,1)S(1)}, bf16[256,1024]{1,0:T(8,128)(2,1)S(1)}) custom-call(s32[3,8]{1,0:T(4,128)S(1)} %bitcast.12, s32[2,8]{1,0:T(2,128)S(1)} %copy-done.5, bf16[8,3,128,128]{3,2,1,0:T(8,128)(2,1)S(1)} %copy-done.2, ...), custom_call_target="tpu_custom_call" | custom-call | tf_op jit(solution)/shard_map/pack/pallas_call | solution.py:243
  5.4 3.0 %collective-permute-start.1 = (bf16[1,784,128]{2,1,0:T(8,128)(2,1)S(1)}, bf16[1,784,128]{2,1,0:T(8,128)(2,1)S(1)}, u32[]{:S(2)}, u32[]{:S(2)}) collective-permute-start(bf16[1,784,128]{2,1,0:T(8,128)(2,1)S(1)} %get-tuple-element.14), channel_id=1, source_target_pairs={{0,2},{1,3},{2,0},{3,1},{4,6},{5,7},{6,4},{7,5},{8,10},{9,11},{10,... | collective-permute-start | bytes 602120 | tf_op jit(solution)/shard_map/parcels_from_partner_2/ppermute | solution.py:264
  8.4 1.4 %collective-permute-start.2 = (bf16[1,784,128]{2,1,0:T(8,128)(2,1)S(1)}, bf16[1,784,128]{2,1,0:T(8,128)(2,1)S(1)}, u32[]{:S(2)}, u32[]{:S(2)}) collective-permute-start(bf16[1,784,128]{2,1,0:T(8,128)(2,1)S(1)} %get-tuple-element.15), channel_id=1, source_target_pairs={{0,3},{1,2},{2,1},{3,0},{4,7},{5,6},{6,5},{7,4},{8,11},{9,10},{10,... | collective-permute-start | bytes 602120 | tf_op jit(solution)/shard_map/parcels_from_partner_3/ppermute | solution.py:264
  10.0 3.0 %collective-permute-start.10 = (bf16[1,784,128]{2,1,0:T(8,128)(2,1)S(1)}, bf16[1,784,128]{2,1,0:T(8,128)(2,1)S(1)}, u32[]{:S(2)}, u32[]{:S(2)}) collective-permute-start(bf16[1,784,128]{2,1,0:T(8,128)(2,1)S(1)} %get-tuple-element.17.refs_1_), channel_id=1, source_target_pairs={{0,16},{4,20},{16,24},{20,28},{24,8},{28,12},{8,0},{12,4},{1,17},{... | collective-permute-start | bytes 602120 | tf_op jit(solution)/shard_map/near_hop_1/ppermute | solution.py:277
  13.0 4.7 %collective-permute-done.1 = bf16[1,784,128]{2,1,0:T(8,128)(2,1)S(1)} collective-permute-done((bf16[1,784,128]{2,1,0:T(8,128)(2,1)S(1)}, bf16[1,784,128]{2,1,0:T(8,128)(2,1)S(1)}, u32[]{:S(2)}, u32[]{:S(2)}) %collective-permute-start.1) | collective-permute-done | bytes 200736 | tf_op jit(solution)/shard_map/parcels_from_partner_2/ppermute | solution.py:264
  17.8 1.8 %collective-permute-start.3 = (bf16[256,1024]{1,0:T(8,128)(2,1)S(1)}, bf16[256,1024]{1,0:T(8,128)(2,1)S(1)}, u32[]{:S(2)}, u32[]{:S(2)}) collective-permute-start(bf16[256,1024]{1,0:T(8,128)(2,1)S(1)} %get-tuple-element.16), channel_id=1, source_target_pairs={{0,1},{1,0},{2,3},{3,2},{4,5},{5,4},{6,7},{7,6},{8,9},{9,8},{10,11... | collective-permute-start | bytes 1572872 | tf_op jit(solution)/shard_map/amplitudes_from_partner_1/ppermute | solution.py:264
  19.6 2.6 %collective-permute-start.11 = (bf16[1,784,128]{2,1,0:T(8,128)(2,1)S(1)}, bf16[1,784,128]{2,1,0:T(8,128)(2,1)S(1)}, u32[]{:S(2)}, u32[]{:S(2)}) collective-permute-start(bf16[1,784,128]{2,1,0:T(8,128)(2,1)S(1)} %collective-permute-done.9.refs_2_), channel_id=1, source_target_pairs={{0,16},{4,20},{16,24},{20,28},{24,8},{28,12},{8,0},{12,4},{1,17},{... | collective-permute-start | bytes 602120 | tf_op jit(solution)/shard_map/early_hop_1/ppermute | solution.py:277
  22.2 1.6 %collective-permute-start.13 = (bf16[1,784,128]{2,1,0:T(8,128)(2,1)S(1)}, bf16[1,784,128]{2,1,0:T(8,128)(2,1)S(1)}, u32[]{:S(2)}, u32[]{:S(2)}) collective-permute-start(bf16[1,784,128]{2,1,0:T(8,128)(2,1)S(1)} %collective-permute-done.10.refs_4_), channel_id=1, source_target_pairs={{0,16},{4,20},{16,24},{20,28},{24,8},{28,12},{8,0},{12,4},{1,17},{... | collective-permute-start | bytes 602120 | tf_op jit(solution)/shard_map/near_hop_2/ppermute | solution.py:277
  23.7 1.5 %collective-permute-start.5 = (bf16[256,1024]{1,0:T(8,128)(2,1)S(1)}, bf16[256,1024]{1,0:T(8,128)(2,1)S(1)}, u32[]{:S(2)}, u32[]{:S(2)}) collective-permute-start(bf16[256,1024]{1,0:T(8,128)(2,1)S(1)} %get-tuple-element.16), channel_id=1, source_target_pairs={{0,2},{1,3},{2,0},{3,1},{4,6},{5,7},{6,4},{7,5},{8,10},{9,11},{10,... | collective-permute-start | bytes 1572872 | tf_op jit(solution)/shard_map/amplitudes_from_partner_2/ppermute | solution.py:264
  25.6 2.0 %collective-permute-done.11.refs_5_ = bf16[1,784,128]{2,1,0:T(8,128)(2,1)S(1)} collective-permute-done((bf16[1,784,128]{2,1,0:T(8,128)(2,1)S(1)}, bf16[1,784,128]{2,1,0:T(8,128)(2,1)S(1)}, u32[]{:S(2)}, u32[]{:S(2)}) %collective-permute-start.11) | collective-permute-done | bytes 200736 | tf_op jit(solution)/shard_map/early_hop_1/ppermute | solution.py:277
  27.6 2.0 %collective-permute-start.7 = (bf16[256,1024]{1,0:T(8,128)(2,1)S(1)}, bf16[256,1024]{1,0:T(8,128)(2,1)S(1)}, u32[]{:S(2)}, u32[]{:S(2)}) collective-permute-start(bf16[256,1024]{1,0:T(8,128)(2,1)S(1)} %get-tuple-element.16), channel_id=1, source_target_pairs={{0,3},{1,2},{2,1},{3,0},{4,7},{5,6},{6,5},{7,4},{8,11},{9,10},{10,... | collective-permute-start | bytes 1572872 | tf_op jit(solution)/shard_map/amplitudes_from_partner_3/ppermute | solution.py:264
  29.7 2.3 %collective-permute-done.13.refs_7_ = bf16[1,784,128]{2,1,0:T(8,128)(2,1)S(1)} collective-permute-done((bf16[1,784,128]{2,1,0:T(8,128)(2,1)S(1)}, bf16[1,784,128]{2,1,0:T(8,128)(2,1)S(1)}, u32[]{:S(2)}, u32[]{:S(2)}) %collective-permute-start.13) | collective-permute-done | bytes 200736 | tf_op jit(solution)/shard_map/near_hop_2/ppermute | solution.py:277
  32.7 5.1 %collective-permute-done.12.refs_6_ = bf16[2,784,128]{2,1,0:T(8,128)(2,1)S(1)} collective-permute-done((bf16[2,784,128]{2,1,0:T(8,128)(2,1)S(1)}, bf16[2,784,128]{2,1,0:T(8,128)(2,1)S(1)}, u32[]{:S(2)}, u32[]{:S(2)}) %collective-permute-start.12) | collective-permute-done | bytes 401440 | tf_op jit(solution)/shard_map/late_hop_1/ppermute | solution.py:277
  37.8 3.3 %collective-permute-start.15 = (bf16[2,784,128]{2,1,0:T(8,128)(2,1)S(1)}, bf16[2,784,128]{2,1,0:T(8,128)(2,1)S(1)}, u32[]{:S(2)}, u32[]{:S(2)}) collective-permute-start(bf16[2,784,128]{2,1,0:T(8,128)(2,1)S(1)} %collective-permute-done.12.refs_6_), channel_id=1, source_target_pairs={{0,16},{4,20},{16,24},{20,28},{24,8},{28,12},{8,0},{12,4},{1,17},{... | collective-permute-start | bytes 1204232 | tf_op jit(solution)/shard_map/late_hop_2/ppermute | solution.py:277
  41.2 5.6 %collective-permute-done.5 = bf16[256,1024]{1,0:T(8,128)(2,1)S(1)} collective-permute-done((bf16[256,1024]{1,0:T(8,128)(2,1)S(1)}, bf16[256,1024]{1,0:T(8,128)(2,1)S(1)}, u32[]{:S(2)}, u32[]{:S(2)}) %collective-permute-start.5) | collective-permute-done | bytes 524320 | tf_op jit(solution)/shard_map/amplitudes_from_partner_2/ppermute | solution.py:264
  47.6 6.5 %collective-permute-done.14.refs_8_ = bf16[1,784,128]{2,1,0:T(8,128)(2,1)S(1)} collective-permute-done((bf16[1,784,128]{2,1,0:T(8,128)(2,1)S(1)}, bf16[1,784,128]{2,1,0:T(8,128)(2,1)S(1)}, u32[]{:S(2)}, u32[]{:S(2)}) %collective-permute-start.14) | collective-permute-done | bytes 200736 | tf_op jit(solution)/shard_map/early_hop_2/ppermute | solution.py:277
  54.2 1.2 %collective-permute-start.16 = (bf16[1,784,128]{2,1,0:T(8,128)(2,1)S(1)}, bf16[1,784,128]{2,1,0:T(8,128)(2,1)S(1)}, u32[]{:S(2)}, u32[]{:S(2)}) collective-permute-start(bf16[1,784,128]{2,1,0:T(8,128)(2,1)S(1)} %collective-permute-done.13.refs_7_), channel_id=1, source_target_pairs={{0,16},{4,20},{16,24},{20,28},{24,8},{28,12},{8,0},{12,4},{1,17},{... | collective-permute-start | bytes 602120 | tf_op jit(solution)/shard_map/near_hop_3/ppermute | solution.py:277
  55.5 3.0 %collective-permute-start.19 = (bf16[2,784,128]{2,1,0:T(8,128)(2,1)S(1)}, bf16[2,784,128]{2,1,0:T(8,128)(2,1)S(1)}, u32[]{:S(2)}, u32[]{:S(2)}) collective-permute-start(bf16[2,784,128]{2,1,0:T(8,128)(2,1)S(1)} %collective-permute-done.15.refs_1_), channel_id=1, source_target_pairs={{0,16},{4,20},{16,24},{20,28},{24,8},{28,12},{8,0},{12,4},{1,17},{... | collective-permute-start | bytes 1204232 | tf_op jit(solution)/shard_map/late_hop_3/ppermute | solution.py:277
  59.4 8.0 %ladder_first.1 = (f32[9,512,128]{2,1,0:T(8,128)S(1)}, f32[256,128]{1,0:T(8,128)S(1)}) custom-call(f32[2,128]{1,0:T(2,128)S(1)} %bitcast.13, bf16[4,512,1024]{2,1,0:T(8,128)(2,1)S(1)} %pad_maximum_fusion.refs_0_, bf16[1,784,128]{2,1,0:T(8,128)(2,1)S(1)} %get-tuple-element.17.refs_1_, bf16[1,784,128]{2,1,0:T(8,128)(2,1)S(1)} %collective-permute-done.9.refs_2_, ...), custom_call_target="tpu_custom_call" | custom-call | flops 100000000 | bytes 1048576 | tf_op jit(solution)/shard_map/ladder_first/pallas_call | solution.py:308
  67.4 3.8 %ladder_second.1 = (f32[8,256,128]{2,1,0:T(8,128)S(1)}, bf16[8,256,128]{2,1,0:T(8,128)(2,1)S(1)}) custom-call(f32[9,512,128]{2,1,0:T(8,128)S(1)} %get-tuple-element.19.before, bf16[4,512,1024]{2,1,0:T(8,128)(2,1)S(1)} %pad_maximum_fusion.refs_0_, bf16[2,784,128]{2,1,0:T(8,128)(2,1)S(1)} %collective-permute-done.15.refs_1_, ...), custom_call_target="tpu_custom_call" | custom-call | flops 1000000000 | bytes 1048576 | tf_op jit(solution)/shard_map/ladder_second/pallas_call | solution.py:308
  71.3 1.9 %collective-permute-done.19.refs_1_ = bf16[2,784,128]{2,1,0:T(8,128)(2,1)S(1)} collective-permute-done((bf16[2,784,128]{2,1,0:T(8,128)(2,1)S(1)}, bf16[2,784,128]{2,1,0:T(8,128)(2,1)S(1)}, u32[]{:S(2)}, u32[]{:S(2)}) %collective-permute-start.19) | collective-permute-done | bytes 401440 | tf_op jit(solution)/shard_map/late_hop_3/ppermute | solution.py:277
  73.2 1.7 %collective-permute-done.20.refs_2_ = bf16[2,784,128]{2,1,0:T(8,128)(2,1)S(1)} collective-permute-done((bf16[2,784,128]{2,1,0:T(8,128)(2,1)S(1)}, bf16[2,784,128]{2,1,0:T(8,128)(2,1)S(1)}, u32[]{:S(2)}, u32[]{:S(2)}) %collective-permute-start.20) | collective-permute-done | bytes 401440 | tf_op jit(solution)/shard_map/ppermute | solution.py:267
  74.9 5.3 %update.1 = (bf16[256,1024]{1,0:T(8,128)(2,1)}, f32[256,1024]{1,0:T(8,128)}) custom-call(s32[2,8]{1,0:T(2,128)S(1)} %copy-done.6, bf16[256,1024]{1,0:T(8,128)(2,1)S(1)} %copy-done.1, bf16[256,1024]{1,0:T(8,128)(2,1)S(1)} %copy-done.3, f32[8,256,128]{2,1,0:T(8,128)S(1)} %get-tuple-element.20.own, bf16[8,256,128]{2,1,0:T(8,128)(2,1)S(1)} %collective-permute-done.18.twin, ...), custom_call_target="tpu_custom_call" | custom-call | tf_op jit(solution)/shard_map/update/pallas_call | solution.py:370
  (47 shorter events, 5.7 us)
Async XLA Ops:
  5.4 12.3 %collective-permute-start.1 = (bf16[1,784,128]{2,1,0:T(8,128)(2,1)S(1)}, bf16[1,784,128]{2,1,0:T(8,128)(2,1)S(1)}, u32[]{:S(2)}, u32[]{:S(2)}) collective-permute-start(bf16[1,784,128]{2,1,0:T(8,128)(2,1)S(1)} %get-tuple-element.14), channel_id=1, source_target_pairs={{0,2},{1,3},{2,0},{3,1},{4,6},{5,7},{6,4},{7,5},{8,10},{9,11},{10,... | collective-permute-start | bytes 602120 | tf_op jit(solution)/shard_map/parcels_from_partner_2/ppermute | solution.py:264
  8.4 9.3 %collective-permute-start.2 = (bf16[1,784,128]{2,1,0:T(8,128)(2,1)S(1)}, bf16[1,784,128]{2,1,0:T(8,128)(2,1)S(1)}, u32[]{:S(2)}, u32[]{:S(2)}) collective-permute-start(bf16[1,784,128]{2,1,0:T(8,128)(2,1)S(1)} %get-tuple-element.15), channel_id=1, source_target_pairs={{0,3},{1,2},{2,1},{3,0},{4,7},{5,6},{6,5},{7,4},{8,11},{9,10},{10,... | collective-permute-start | bytes 602120 | tf_op jit(solution)/shard_map/parcels_from_partner_3/ppermute | solution.py:264
  9.9 9.7 %collective-permute-start.9 = (bf16[1,784,128]{2,1,0:T(8,128)(2,1)S(1)}, bf16[1,784,128]{2,1,0:T(8,128)(2,1)S(1)}, u32[]{:S(2)}, u32[]{:S(2)}) collective-permute-start(bf16[1,784,128]{2,1,0:T(8,128)(2,1)S(1)} %get-tuple-element.18), channel_id=1, source_target_pairs={{0,1},{1,0},{2,3},{3,2},{4,5},{5,4},{6,7},{7,6},{8,9},{9,8},{10,11... | collective-permute-start | bytes 602120 | tf_op jit(solution)/shard_map/parcels_from_partner_1/ppermute | solution.py:264
  10.0 12.2 %collective-permute-start.10 = (bf16[1,784,128]{2,1,0:T(8,128)(2,1)S(1)}, bf16[1,784,128]{2,1,0:T(8,128)(2,1)S(1)}, u32[]{:S(2)}, u32[]{:S(2)}) collective-permute-start(bf16[1,784,128]{2,1,0:T(8,128)(2,1)S(1)} %get-tuple-element.17.refs_1_), channel_id=1, source_target_pairs={{0,16},{4,20},{16,24},{20,28},{24,8},{28,12},{8,0},{12,4},{1,17},{... | collective-permute-start | bytes 602120 | tf_op jit(solution)/shard_map/near_hop_1/ppermute | solution.py:277
  17.8 14.9 %collective-permute-start.3 = (bf16[256,1024]{1,0:T(8,128)(2,1)S(1)}, bf16[256,1024]{1,0:T(8,128)(2,1)S(1)}, u32[]{:S(2)}, u32[]{:S(2)}) collective-permute-start(bf16[256,1024]{1,0:T(8,128)(2,1)S(1)} %get-tuple-element.16), channel_id=1, source_target_pairs={{0,1},{1,0},{2,3},{3,2},{4,5},{5,4},{6,7},{7,6},{8,9},{9,8},{10,11... | collective-permute-start | bytes 1572872 | tf_op jit(solution)/shard_map/amplitudes_from_partner_1/ppermute | solution.py:264
  19.6 8.0 %collective-permute-start.11 = (bf16[1,784,128]{2,1,0:T(8,128)(2,1)S(1)}, bf16[1,784,128]{2,1,0:T(8,128)(2,1)S(1)}, u32[]{:S(2)}, u32[]{:S(2)}) collective-permute-start(bf16[1,784,128]{2,1,0:T(8,128)(2,1)S(1)} %collective-permute-done.9.refs_2_), channel_id=1, source_target_pairs={{0,16},{4,20},{16,24},{20,28},{24,8},{28,12},{8,0},{12,4},{1,17},{... | collective-permute-start | bytes 602120 | tf_op jit(solution)/shard_map/early_hop_1/ppermute | solution.py:277
  22.2 9.7 %collective-permute-start.13 = (bf16[1,784,128]{2,1,0:T(8,128)(2,1)S(1)}, bf16[1,784,128]{2,1,0:T(8,128)(2,1)S(1)}, u32[]{:S(2)}, u32[]{:S(2)}) collective-permute-start(bf16[1,784,128]{2,1,0:T(8,128)(2,1)S(1)} %collective-permute-done.10.refs_4_), channel_id=1, source_target_pairs={{0,16},{4,20},{16,24},{20,28},{24,8},{28,12},{8,0},{12,4},{1,17},{... | collective-permute-start | bytes 602120 | tf_op jit(solution)/shard_map/near_hop_2/ppermute | solution.py:277
  23.7 23.0 %collective-permute-start.5 = (bf16[256,1024]{1,0:T(8,128)(2,1)S(1)}, bf16[256,1024]{1,0:T(8,128)(2,1)S(1)}, u32[]{:S(2)}, u32[]{:S(2)}) collective-permute-start(bf16[256,1024]{1,0:T(8,128)(2,1)S(1)} %get-tuple-element.16), channel_id=1, source_target_pairs={{0,2},{1,3},{2,0},{3,1},{4,6},{5,7},{6,4},{7,5},{8,10},{9,11},{10,... | collective-permute-start | bytes 1572872 | tf_op jit(solution)/shard_map/amplitudes_from_partner_2/ppermute | solution.py:264
  25.3 12.6 %collective-permute-start.12 = (bf16[2,784,128]{2,1,0:T(8,128)(2,1)S(1)}, bf16[2,784,128]{2,1,0:T(8,128)(2,1)S(1)}, u32[]{:S(2)}, u32[]{:S(2)}) collective-permute-start(bf16[2,784,128]{2,1,0:T(8,128)(2,1)S(1)} %constant_dynamic-update-slice_fusion.refs_3_), channel_id=1, source_target_pairs={{0,16},{4,20},{16,24},{20,28},{24,8},{28,12},{8,0},{12,4},{1,17},{... | collective-permute-start | bytes 1204232 | tf_op jit(solution)/shard_map/late_hop_1/ppermute | solution.py:277
  27.6 19.1 %collective-permute-start.7 = (bf16[256,1024]{1,0:T(8,128)(2,1)S(1)}, bf16[256,1024]{1,0:T(8,128)(2,1)S(1)}, u32[]{:S(2)}, u32[]{:S(2)}) collective-permute-start(bf16[256,1024]{1,0:T(8,128)(2,1)S(1)} %get-tuple-element.16), channel_id=1, source_target_pairs={{0,3},{1,2},{2,1},{3,0},{4,7},{5,6},{6,5},{7,4},{8,11},{9,10},{10,... | collective-permute-start | bytes 1572872 | tf_op jit(solution)/shard_map/amplitudes_from_partner_3/ppermute | solution.py:264
  31.9 15.3 %collective-permute-start = (bf16[256,1024]{1,0:T(8,128)(2,1)S(1)}, bf16[256,1024]{1,0:T(8,128)(2,1)S(1)}, u32[]{:S(2)}, u32[]{:S(2)}) collective-permute-start(bf16[256,1024]{1,0:T(8,128)(2,1)S(1)} %get-tuple-element.16), channel_id=1, source_target_pairs={{0,4},{4,0},{8,12},{12,8},{16,20},{20,16},{24,28},{28,24},{1,5},{5... | collective-permute-start | bytes 1572872 | tf_op jit(solution)/shard_map/twin_amplitudes/ppermute | solution.py:267
  32.7 22.7 %collective-permute-start.4 = (bf16[256,1024]{1,0:T(8,128)(2,1)S(1)}, bf16[256,1024]{1,0:T(8,128)(2,1)S(1)}, u32[]{:S(2)}, u32[]{:S(2)}) collective-permute-start(bf16[256,1024]{1,0:T(8,128)(2,1)S(1)} %collective-permute-done.3), channel_id=1, source_target_pairs={{0,4},{4,0},{8,12},{12,8},{16,20},{20,16},{24,28},{28,24},{1,5},{5... | collective-permute-start | bytes 1572872 | tf_op jit(solution)/shard_map/twin_amplitudes/ppermute | solution.py:267
  37.8 17.6 %collective-permute-start.15 = (bf16[2,784,128]{2,1,0:T(8,128)(2,1)S(1)}, bf16[2,784,128]{2,1,0:T(8,128)(2,1)S(1)}, u32[]{:S(2)}, u32[]{:S(2)}) collective-permute-start(bf16[2,784,128]{2,1,0:T(8,128)(2,1)S(1)} %collective-permute-done.12.refs_6_), channel_id=1, source_target_pairs={{0,16},{4,20},{16,24},{20,28},{24,8},{28,12},{8,0},{12,4},{1,17},{... | collective-permute-start | bytes 1204232 | tf_op jit(solution)/shard_map/late_hop_2/ppermute | solution.py:277
  46.7 11.8 %collective-permute-start.6 = (bf16[256,1024]{1,0:T(8,128)(2,1)S(1)}, bf16[256,1024]{1,0:T(8,128)(2,1)S(1)}, u32[]{:S(2)}, u32[]{:S(2)}) collective-permute-start(bf16[256,1024]{1,0:T(8,128)(2,1)S(1)} %collective-permute-done.5), channel_id=1, source_target_pairs={{0,4},{4,0},{8,12},{12,8},{16,20},{20,16},{24,28},{28,24},{1,5},{5... | collective-permute-start | bytes 1572872 | tf_op jit(solution)/shard_map/twin_amplitudes/ppermute | solution.py:267
  46.7 11.9 %collective-permute-start.8 = (bf16[256,1024]{1,0:T(8,128)(2,1)S(1)}, bf16[256,1024]{1,0:T(8,128)(2,1)S(1)}, u32[]{:S(2)}, u32[]{:S(2)}) collective-permute-start(bf16[256,1024]{1,0:T(8,128)(2,1)S(1)} %collective-permute-done.7), channel_id=1, source_target_pairs={{0,4},{4,0},{8,12},{12,8},{16,20},{20,16},{24,28},{28,24},{1,5},{5... | collective-permute-start | bytes 1572872 | tf_op jit(solution)/shard_map/twin_amplitudes/ppermute | solution.py:267
  47.2 7.0 %collective-permute-start.14 = (bf16[1,784,128]{2,1,0:T(8,128)(2,1)S(1)}, bf16[1,784,128]{2,1,0:T(8,128)(2,1)S(1)}, u32[]{:S(2)}, u32[]{:S(2)}) collective-permute-start(bf16[1,784,128]{2,1,0:T(8,128)(2,1)S(1)} %collective-permute-done.11.refs_5_), channel_id=1, source_target_pairs={{0,16},{4,20},{16,24},{20,28},{24,8},{28,12},{8,0},{12,4},{1,17},{... | collective-permute-start | bytes 602120 | tf_op jit(solution)/shard_map/early_hop_2/ppermute | solution.py:277
  54.2 13.2 %collective-permute-start.16 = (bf16[1,784,128]{2,1,0:T(8,128)(2,1)S(1)}, bf16[1,784,128]{2,1,0:T(8,128)(2,1)S(1)}, u32[]{:S(2)}, u32[]{:S(2)}) collective-permute-start(bf16[1,784,128]{2,1,0:T(8,128)(2,1)S(1)} %collective-permute-done.13.refs_7_), channel_id=1, source_target_pairs={{0,16},{4,20},{16,24},{20,28},{24,8},{28,12},{8,0},{12,4},{1,17},{... | collective-permute-start | bytes 602120 | tf_op jit(solution)/shard_map/near_hop_3/ppermute | solution.py:277
  55.4 12.0 %collective-permute-start.17 = (bf16[1,784,128]{2,1,0:T(8,128)(2,1)S(1)}, bf16[1,784,128]{2,1,0:T(8,128)(2,1)S(1)}, u32[]{:S(2)}, u32[]{:S(2)}) collective-permute-start(bf16[1,784,128]{2,1,0:T(8,128)(2,1)S(1)} %collective-permute-done.14.refs_8_), channel_id=1, source_target_pairs={{0,16},{4,20},{16,24},{20,28},{24,8},{28,12},{8,0},{12,4},{1,17},{... | collective-permute-start | bytes 602120 | tf_op jit(solution)/shard_map/early_hop_3/ppermute | solution.py:277
  55.5 17.7 %collective-permute-start.19 = (bf16[2,784,128]{2,1,0:T(8,128)(2,1)S(1)}, bf16[2,784,128]{2,1,0:T(8,128)(2,1)S(1)}, u32[]{:S(2)}, u32[]{:S(2)}) collective-permute-start(bf16[2,784,128]{2,1,0:T(8,128)(2,1)S(1)} %collective-permute-done.15.refs_1_), channel_id=1, source_target_pairs={{0,16},{4,20},{16,24},{20,28},{24,8},{28,12},{8,0},{12,4},{1,17},{... | collective-permute-start | bytes 1204232 | tf_op jit(solution)/shard_map/late_hop_3/ppermute | solution.py:277
  67.4 7.5 %copy-start.1 = (bf16[256,1024]{1,0:T(8,128)(2,1)S(1)}, bf16[256,1024]{1,0:T(8,128)(2,1)}, u32[]{:S(2)}) copy-start(bf16[256,1024]{1,0:T(8,128)(2,1)} %amplitudes.3) | copy-start | bytes 1572868
  67.4 7.5 %copy-start.3 = (bf16[256,1024]{1,0:T(8,128)(2,1)S(1)}, bf16[256,1024]{1,0:T(8,128)(2,1)}, u32[]{:S(2)}) copy-start(bf16[256,1024]{1,0:T(8,128)(2,1)} %driver.1) | copy-start | bytes 1572868
  67.4 7.5 %copy-start.4 = (f32[1024]{0:T(1024)S(1)}, f32[1024]{0:T(1024)}, u32[]{:S(2)}) copy-start(f32[1024]{0:T(1024)} %param.13) | copy-start | bytes 12292
  71.2 2.0 %collective-permute-start.18 = (bf16[8,256,128]{2,1,0:T(8,128)(2,1)S(1)}, bf16[8,256,128]{2,1,0:T(8,128)(2,1)S(1)}, u32[]{:S(2)}, u32[]{:S(2)}) collective-permute-start(bf16[8,256,128]{2,1,0:T(8,128)(2,1)S(1)} %get-tuple-element.21), channel_id=1, source_target_pairs={{0,4},{4,0},{8,12},{12,8},{16,20},{20,16},{24,28},{28,24},{1,5},{5... | collective-permute-start | bytes 1572872 | tf_op jit(solution)/shard_map/ppermute | solution.py:267
  73.2 1.7 %collective-permute-start.20 = (bf16[2,784,128]{2,1,0:T(8,128)(2,1)S(1)}, bf16[2,784,128]{2,1,0:T(8,128)(2,1)S(1)}, u32[]{:S(2)}, u32[]{:S(2)}) collective-permute-start(bf16[2,784,128]{2,1,0:T(8,128)(2,1)S(1)} %collective-permute-done.19.refs_1_), channel_id=1, source_target_pairs={{0,4},{4,0},{8,12},{12,8},{16,20},{20,16},{24,28},{28,24},{1,5},{5... | collective-permute-start | bytes 1204232 | tf_op jit(solution)/shard_map/ppermute | solution.py:267
  (6 other events, 11.7 us)

commit v4 on v3

v4 whole, which is shorter than its diff:
```python
import functools
import math

import jax
import jax.numpy as jnp
from jax import lax
from jax.experimental import pallas as pl
from jax.experimental.pallas import tpu as pltpu
from jax.sharding import PartitionSpec as P

SPARE_VMEM = 4 * 1024 * 1024
ALL_VMEM = 60 * 1024 * 1024
CORES = 2
NOTE_ROWS = 16
FIRST_FLOPS = 10**8
SECOND_FLOPS = 10**9


def pack_kernel(n_v, cap, columns, integrals, *refs):
    parcels, (origin, codes, tiles, sem) = refs[:n_v], refs[n_v:]
    rows, slots, tile, _ = integrals.shape
    me = lax.axis_index("vpair")
    copy = pltpu.make_async_copy(integrals, tiles, sem)
    copy.start()
    counts = [jnp.int32(0)] * n_v
    for i in range(n_v * cap):
        origin[i] = 0
        codes[i] = -1
    for row in range(rows):
        for slot in range(slots):
            column = columns[slot, row]
            partner = lax.div(column, rows) ^ me
            place = counts[0]
            for j in range(1, n_v):
                place = jnp.where(partner == j, counts[j], place)
            counts = [counts[j] + (partner == j).astype(jnp.int32) for j in range(n_v)]
            at = partner * cap + place
            origin[at] = row * slots + slot
            codes[at] = row * rows + lax.rem(column, rows)
    copy.wait()
    lane = lax.broadcasted_iota(jnp.int32, (NOTE_ROWS, tile), 1)
    for j in range(n_v):
        note = jnp.full((NOTE_ROWS, tile), -1, jnp.int32)
        for k in range(cap):
            entry = origin[j * cap + k]
            parcels[j][0, pl.ds(k * tile, tile)] = tiles[
                lax.div(entry, slots), lax.rem(entry, slots)
            ]
            note = jnp.where(lane == k, codes[j * cap + k], note)
        parcels[j][0, pl.ds(cap * tile, NOTE_ROWS)] = note.astype(jnp.float32).astype(
            integrals.dtype
        )


def mask_kernel(live, amplitudes, masked):
    tile = amplitudes.shape[1] // live.shape[1]
    for o in range(live.shape[0]):
        for c in range(live.shape[1]):
            at = (pl.ds(o * tile, tile), pl.ds(c * tile, tile))
            kept = live[o, c].astype(jnp.float32)
            masked[at] = (amplitudes[at].astype(jnp.float32) * kept).astype(masked.dtype)


def read_notes(arrays, notes_wide, notes, sem):
    unit = 0
    for array in arrays:
        _, height, _ = array.shape
        for member in range(array.shape[0]):
            note = array[member, pl.ds(height - NOTE_ROWS, NOTE_ROWS)]
            notes_wide[pl.ds(unit, 1)] = note.astype(jnp.float32).astype(jnp.int32)[:1]
            unit += 1
    copy = pltpu.make_async_copy(notes_wide, notes, sem)
    copy.start()
    return copy


def clear_pairs(pairs):
    pairs[...] = jnp.zeros_like(pairs)


def add_unit(array, member, unit, j, n_rows, cap, rows, amps, notes, pairs, total):
    tile = array.shape[-1]

    def place(k):
        code = notes[unit, k]
        used = code >= 0
        row = jnp.where(used, lax.div(code, rows), 0)
        column = jnp.where(used, lax.rem(code, rows), rows)
        lanes = pl.ds(pl.multiple_of(row * tile, tile), tile)
        return amps[j, pl.ds(0, n_rows), lanes], column

    for k in range(0, cap - 1, 2):
        pair = pairs.at[k // 2]
        pair[pl.ds(0, tile), pl.ds(0, tile)] = array[member, pl.ds(k * tile, tile)]
        pair[pl.ds(tile, tile), pl.ds(tile, tile)] = array[member, pl.ds((k + 1) * tile, tile)]
        (left, first), (right, second) = place(k), place(k + 1)
        both = jnp.dot(
            jnp.concatenate([left, right], axis=1),
            pair[...],
            preferred_element_type=jnp.float32,
        )
        total[first] += both[:, :tile]
        total[second] += both[:, tile:]
    if cap % 2:
        left, column = place(cap - 1)
        total[column] += jnp.dot(
            left,
            array[member, pl.ds((cap - 1) * tile, tile)],
            preferred_element_type=jnp.float32,
        )


def add_arrays(arrays, layout, cap, rows, amps, notes_wide, notes, pairs, total, sem):
    copy = read_notes(arrays, notes_wide, notes, sem)
    pairs[...] = jnp.zeros_like(pairs)
    total[...] = jnp.zeros_like(total)
    copy.wait()
    unit = 0
    for array, partners in zip(arrays, layout):

        def one(i, carry, unit=unit, array=array, partners=partners):
            add_unit(
                array, i, unit + i, partners[0] + i, total.shape[1], cap, rows, amps, notes, pairs, total
            )
            return carry

        lax.fori_loop(0, len(partners), one, 0)
        unit += len(partners)


def first_ladder_kernel(cap, layout, occupied, amps, *refs):
    arrays, (total, occupied_out, notes_wide, notes, pairs, sem) = (
        refs[: len(layout)],
        refs[len(layout) :],
    )
    rows = total.shape[0] - 1
    add_arrays(arrays, layout, cap, rows, amps, notes_wide, notes, pairs, total, sem)
    tile = occupied_out.shape[-1]
    for o in range(occupied.shape[0]):
        wide = jnp.broadcast_to(occupied[pl.ds(o, 1)], (tile, tile))
        occupied_out[pl.ds(o * tile, tile)] = wide.T


def second_ladder_kernel(cap, layout, before, amps, *refs):
    arrays, (own, twin, total, notes_wide, notes, pairs, sem) = (
        refs[: len(layout)],
        refs[len(layout) :],
    )
    rows, n_rows, _ = own.shape
    add_arrays(arrays, layout, cap, rows, amps, notes_wide, notes, pairs, total, sem)
    own[...] = before[:rows, :n_rows] + total[:rows, :n_rows]
    twin[...] = (before[:rows, n_rows:] + total[:rows, n_rows:]).astype(twin.dtype)


def update_kernel(cap, partners, live, amplitudes, driver, own, twin, occupied, virtual, *refs):
    amps, *arrays = refs[: 1 + CORES]
    new, residual, new_buf, residual_buf, notes_wide, notes, pairs, total, sem, sems = refs[
        1 + CORES :
    ]
    rows, _, tile = own.shape
    layout = [partners] * CORES
    add_arrays(arrays, layout, cap, rows, amps, notes_wide, notes, pairs, total, sem)
    copies = []
    for c in range(rows):
        lanes = pl.ds(c * tile, tile)
        for o in range(live.shape[0]):
            here = pl.ds(o * tile, tile)
            at = (here, lanes)
            kept = live[o, c].astype(jnp.float32)
            plain = amplitudes[at].astype(jnp.float32)
            masked = (plain * kept).astype(jnp.bfloat16).astype(jnp.float32)
            denominator = occupied[here, :] - virtual[:, lanes]
            ladder = own[c, here] + twin[c, here].astype(jnp.float32) + total[c, here]
            rest = (driver[at].astype(jnp.float32) + ladder + denominator * plain) * kept
            residual_buf[at] = rest
            new_buf[at] = (masked - rest / denominator).astype(new.dtype)
        for i, (source, target) in enumerate(((new_buf, new), (residual_buf, residual))):
            copies.append(
                pltpu.make_async_copy(source.at[:, lanes], target.at[:, lanes], sems.at[i, c])
            )
            copies[-1].start()
    for copy in copies:
        copy.wait()


def on_device(
    amplitudes,
    tile_live,
    integrals,
    integral_columns,
    driver_terms,
    occupied_energy,
    virtual_energy,
):
    n_rows, width = amplitudes.shape
    rows, slots, tile, _ = integrals.shape
    n_v, n_o = lax.axis_size("vpair"), lax.axis_size("opair")
    n_z = n_o // CORES
    cap = -(-(rows * slots) // n_v)
    height = cap * tile + NOTE_ROWS
    dtype = integrals.dtype
    in_smem = pl.BlockSpec(memory_space=pltpu.SMEM)
    in_vmem = pl.BlockSpec(memory_space=pltpu.VMEM)
    anywhere = pl.BlockSpec(memory_space=pl.ANY)
    in_hbm = pl.BlockSpec(memory_space=pltpu.HBM)

    def params(*buffers):
        size = sum(math.prod(shape) * jnp.dtype(kind).itemsize for shape, kind in buffers)
        return pltpu.CompilerParams(vmem_limit_bytes=size + SPARE_VMEM)

    parcel = (1, height, tile)
    parcels = pl.pallas_call(
        functools.partial(pack_kernel, n_v, cap),
        out_shape=[jax.ShapeDtypeStruct(parcel, dtype)] * n_v,
        in_specs=[in_smem, in_hbm],
        out_specs=[in_vmem] * n_v,
        scratch_shapes=[pltpu.SMEM((n_v * cap,), jnp.int32)] * 2
        + [pltpu.VMEM(integrals.shape, dtype), pltpu.SemaphoreType.DMA],
        compiler_params=pltpu.CompilerParams(vmem_limit_bytes=ALL_VMEM),
        name="pack",
    )(integral_columns.T, integrals)
    masked = pl.pallas_call(
        mask_kernel,
        out_shape=jax.ShapeDtypeStruct(amplitudes.shape, amplitudes.dtype),
        in_specs=[in_smem, in_vmem],
        out_specs=in_vmem,
        compiler_params=params(((4, n_rows, width), dtype)),
        name="mask",
    )(tile_live, amplitudes)

    def across_v(value, j):
        name = "amplitudes" if value.ndim == 2 else "parcels"
        with jax.named_scope(f"{name}_from_partner_{j}"):
            return lax.ppermute(value, "vpair", [(i, i ^ j) for i in range(n_v)])

    def across_core(value):
        return lax.ppermute(value, "opair", [(i, i ^ 1) for i in range(n_o)])

    def next_on_ring(value, name):
        ring = [*range(0, n_z, 2), *range(n_z - 1 - n_z % 2, 0, -2)]
        pairs = [
            (source * CORES + core, target * CORES + core)
            for source, target in zip(ring, ring[1:] + ring[:1])
            for core in range(CORES)
        ]
        with jax.named_scope(name):
            return lax.ppermute(value, "opair", pairs)

    def join(values):
        return jnp.concatenate(values) if len(values) > 1 else values[0]

    def after(values, others):
        return lax.optimization_barrier((values, others))[0]

    others = list(range(1, n_v))
    groups = {"near": [0], "early": others[: n_v // 2 - 1], "late": others[n_v // 2 - 1 :]}
    arrived = {0: parcels[0]} | {j: across_v(parcels[j], j) for j in others}
    hops = {name: [join([arrived[j] for j in groups[name]])] for name in groups}
    groups["first"] = groups["near"] + groups["early"]
    for name in ("near", "early", "late"):
        hops[name].append(next_on_ring(hops[name][0], f"{name}_hop_1"))
    hops["first"] = [None, join([hops["near"][1], hops["early"][1]])]
    for hop in range(2, n_z):
        for name in ("first", "late"):
            hops[name].append(next_on_ring(hops[name][-1], f"{name}_hop_{hop}"))

    a_parts = {0: masked}
    ready = after(masked, hops["late"][0])
    for j in others:
        a_parts[j] = across_v(ready, j)
    a_parts = after(a_parts, (hops["first"][2], hops["late"][2]))
    own_a = jnp.stack([a_parts[j] for j in range(n_v)])
    with jax.named_scope("twin_amplitudes"):
        amps = jnp.concatenate([own_a, across_core(own_a)], axis=1)

    sums = (rows + 1, CORES * n_rows, tile)
    pairs = (max(cap // 2, 1), 2 * tile, 2 * tile)

    def ladder_call(kernel, found, before, out_shape, extra_scratch, flops, name):
        arrays, layout = [hops[name][hop] for name, hop in found], [groups[name] for name, _ in found]
        n_units = sum(len(partners) for partners in layout)
        return pl.pallas_call(
            functools.partial(kernel, cap, layout),
            out_shape=out_shape,
            in_specs=[in_vmem] * (2 + len(arrays)),
            out_specs=[in_vmem] * len(out_shape),
            scratch_shapes=extra_scratch
            + [
                pltpu.VMEM((n_units, tile), jnp.int32),
                pltpu.SMEM((n_units, tile), jnp.int32),
                pltpu.VMEM(pairs, dtype),
                pltpu.SemaphoreType.DMA,
            ],
            compiler_params=params(
                ((n_units, height, tile), dtype),
                (sums, jnp.float32),
                (sums, jnp.float32),
                (sums, jnp.float32),
                (amps.shape, dtype),
            ),
            cost_estimate=pl.CostEstimate(
                flops=flops,
                bytes_accessed=1024 * 1024,
                transcendentals=0,
            ),
            name=name,
        )(before, amps, *arrays)

    tail = [("late", n_z - 2), ("first", n_z - 1)]
    head = [("near", 0), ("early", 0), ("late", 0)]
    head += [("first", hop) for hop in range(1, n_z - 1)]
    head += [("late", hop) for hop in range(1, n_z - 2)]
    total, occupied = ladder_call(
        first_ladder_kernel,
        head,
        occupied_energy.reshape(-1, tile),
        [
            jax.ShapeDtypeStruct(sums, jnp.float32),
            jax.ShapeDtypeStruct((n_rows, tile), jnp.float32),
        ],
        [],
        FIRST_FLOPS,
        "ladder_first",
    )
    own, twin = ladder_call(
        second_ladder_kernel,
        tail,
        total,
        [
            jax.ShapeDtypeStruct((rows, n_rows, tile), jnp.float32),
            jax.ShapeDtypeStruct((rows, n_rows, tile), jnp.bfloat16),
        ],
        [pltpu.VMEM(sums, jnp.float32)],
        SECOND_FLOPS,
        "ladder_second",
    )
    last, behind = after(hops["late"][-1], twin), groups["late"]
    twin = across_core(twin)

    n_last = CORES * len(behind)
    sums = (rows + 1, n_rows, tile)
    return pl.pallas_call(
        functools.partial(update_kernel, cap, behind),
        out_shape=[
            jax.ShapeDtypeStruct((n_rows, width), jnp.bfloat16),
            jax.ShapeDtypeStruct((n_rows, width), jnp.float32),
        ],
        in_specs=[in_smem] + [in_vmem] * (7 + CORES),
        out_specs=[in_hbm] * 2,
        scratch_shapes=[
            pltpu.VMEM((n_rows, width), jnp.bfloat16),
            pltpu.VMEM((n_rows, width), jnp.float32),
            pltpu.VMEM((n_last, tile), jnp.int32),
            pltpu.SMEM((n_last, tile), jnp.int32),
            pltpu.VMEM(pairs, dtype),
            pltpu.VMEM(sums, jnp.float32),
            pltpu.SemaphoreType.DMA,
            pltpu.SemaphoreType.DMA((2, rows)),
        ],
        compiler_params=params(
            (amps.shape, dtype), ((n_last, height, tile), dtype), *[(sums, jnp.float32)] * 5
        ),
        name="update",
    )(
        tile_live,
        amplitudes,
        driver_terms,
        own,
        twin,
        occupied,
        virtual_energy.reshape(1, width),
        amps,
        last,
        across_core(last),
    )


def solution(mesh):
    in_specs = (
        P("opair", "vpair"),
        P("opair", "vpair"),
        P("vpair", "opair", None, None),
        P("vpair", "opair"),
        P("opair", "vpair"),
        P("opair"),
        P("vpair"),
    )
    out_specs = (P("opair", "vpair"), P("opair", "vpair"))
    return jax.shard_map(
        on_device, mesh=mesh, in_specs=in_specs, out_specs=out_specs, check_vma=False
    )
```

time: 80.5 us -> 76.9 us (0.955)
  starting transfers between devices: 26 us -> 22.6 us
  waiting for transfers between devices: 30.6 us -> 33.7 us
  Pallas kernels: 18.3 us -> 16.4 us
  local copies, waits for them, and re-layouts: 3.69 us -> 1.84 us
    ppermute x6, waiting for transfers between devices: 11.1 us -> 17.8 us  [across_v(): return lax.ppermute(value, 'vpair', [(i, i ^ j) for i in range(n_v)])]
    ppermute x9 -> x7, waiting for transfers between devices: 17.8 us -> 13.2 us  [next_on_ring(): return lax.ppermute(value, 'opair', pairs)]
    pallas_call x2, Pallas kernels: 11.8 us -> 8.89 us  [ladder_call(): pl.pallas_call(functools.partial(kernel, cap, layout), out_shape=out_shap...]
    unnamed x19 -> x18, local copies, waits for them, and re-layouts: 3.66 us -> 1.79 us
    pallas_call x1, Pallas kernels: 1.22 us -> 2.82 us  [on_device(): pl.pallas_call(functools.partial(pack_kernel, n_v, cap), out_shape=[jax.S...]
    ppermute x9 -> x7, starting transfers between devices: 15.4 us -> 13.9 us  [next_on_ring(): return lax.ppermute(value, 'opair', pairs)]
    ppermute x6, starting transfers between devices: 9.92 us -> 8.55 us  [across_v(): return lax.ppermute(value, 'vpair', [(i, i ^ j) for i in range(n_v)])]
    ppermute x6 -> x3, waiting for transfers between devices: 1.74 us -> 2.69 us  [across_core(): return lax.ppermute(value, 'opair', [(i, i ^ 1) for i in range(n_o)])]
  transfers between devices with their start and end apart: 21 -> 16, of which waited for: 9 -> 10; matrix products, arithmetic and copies ran while one was open for 1% -> 1% of each run, Pallas kernels for 15% -> 13%
where the time goes in v4:
time: 76.9 us; the launch traced here: 76.1 us
  waiting for transfers between devices  33.7 us (44%)
  starting transfers between devices  22.6 us (29%)
  Pallas kernels  16.4 us (21%)
  local copies, waits for them, and re-layouts  1.84 us (2%)
  other arithmetic  0.83 us (1%)
  between operations  0.82 us (1%)
    ppermute x6, waiting for transfers between devices, across_v(): return lax.ppermute(value, 'vpair', [(i, i ^ j) for i in range(n_v)])  17.8 us
    ppermute x7, starting transfers between devices, next_on_ring(): return lax.ppermute(value, 'opair', pairs)  13.9 us
    ppermute x7, waiting for transfers between devices, next_on_ring(): return lax.ppermute(value, 'opair', pairs)  13.2 us
    pallas_call x2, Pallas kernels, ladder_call(): pl.pallas_call(functools.partial(kernel, cap, layout), out_shape=out_shap...  8.89 us
    ppermute x6, starting transfers between devices, across_v(): return lax.ppermute(value, 'vpair', [(i, i ^ j) for i in range(n_v)])  8.55 us
    pallas_call x1, Pallas kernels, on_device(): pl.pallas_call(functools.partial(update_kernel, cap, behind), out_shape=[...  3.97 us
    pallas_call x1, Pallas kernels, on_device(): pl.pallas_call(functools.partial(pack_kernel, n_v, cap), out_shape=[jax.S...  2.82 us
    ppermute x3, waiting for transfers between devices, across_core(): return lax.ppermute(value, 'opair', [(i, i ^ 1) for i in range(n_o)])  2.69 us
  transfers between devices with their start and end apart: 16, of which 10 were waited for; matrix products, arithmetic and copies ran while one was open for 1% of the time, Pallas kernels for 13%

profile of v4, /device:TPU:0, one launch (start us, length us, event | category | flops | bytes accessed | tf_op | source)
XLA Modules:
  0.0 76.1 jit_solution(18149087354849785483)
XLA Ops:
  0.6 2.8 %pack.1 = (bf16[1,784,128]{2,1,0:T(8,128)(2,1)}, bf16[1,784,128]{2,1,0:T(8,128)(2,1)}, bf16[1,784,128]{2,1,0:T(8,128)(2,1)}, bf16[1,784,128]{2,1,0:T(8,128)(2,1)}) custom-call(s32[3,8]{1,0:T(4,128)} %bitcast.17, bf16[8,3,128,128]{3,2,1,0:T(8,128)(2,1)} %integrals.1), custom_call_target="tpu_custom_call" | custom-call | tf_op jit(solution)/shard_map/pack/pallas_call | solution.py:212
  3.5 3.0 %collective-permute-start = (bf16[1,784,128]{2,1,0:T(8,128)(2,1)}, bf16[1,784,128]{2,1,0:T(8,128)(2,1)S(1)}, u32[]{:S(2)}, u32[]{:S(2)}) collective-permute-start(bf16[1,784,128]{2,1,0:T(8,128)(2,1)} %get-tuple-element.16), channel_id=1, source_target_pairs={{0,2},{1,3},{2,0},{3,1},{4,6},{5,7},{6,4},{7,5},{8,10},{9,11},{10,... | collective-permute-start | bytes 602120 | tf_op jit(solution)/shard_map/parcels_from_partner_2/ppermute | solution.py:234
  6.5 1.4 %collective-permute-start.1 = (bf16[1,784,128]{2,1,0:T(8,128)(2,1)}, bf16[1,784,128]{2,1,0:T(8,128)(2,1)S(1)}, u32[]{:S(2)}, u32[]{:S(2)}) collective-permute-start(bf16[1,784,128]{2,1,0:T(8,128)(2,1)} %get-tuple-element.17), channel_id=1, source_target_pairs={{0,3},{1,2},{2,1},{3,0},{4,7},{5,6},{6,5},{7,4},{8,11},{9,10},{10,... | collective-permute-start | bytes 602120 | tf_op jit(solution)/shard_map/parcels_from_partner_3/ppermute | solution.py:234
  7.9 2.6 %collective-permute-start.5 = (bf16[1,784,128]{2,1,0:T(8,128)(2,1)}, bf16[1,784,128]{2,1,0:T(8,128)(2,1)S(1)}, u32[]{:S(2)}, u32[]{:S(2)}) collective-permute-start(bf16[1,784,128]{2,1,0:T(8,128)(2,1)} %get-tuple-element.19.refs_0_), channel_id=1, source_target_pairs={{0,16},{4,20},{16,24},{20,28},{24,8},{28,12},{8,0},{12,4},{1,17},{... | collective-permute-start | bytes 602120 | tf_op jit(solution)/shard_map/near_hop_1/ppermute | solution.py:247
  11.0 4.9 %collective-permute-done = bf16[1,784,128]{2,1,0:T(8,128)(2,1)S(1)} collective-permute-done((bf16[1,784,128]{2,1,0:T(8,128)(2,1)}, bf16[1,784,128]{2,1,0:T(8,128)(2,1)S(1)}, u32[]{:S(2)}, u32[]{:S(2)}) %collective-permute-start) | collective-permute-done | bytes 200736 | tf_op jit(solution)/shard_map/parcels_from_partner_2/ppermute | solution.py:234
  16.1 2.9 %collective-permute-start.9 = (bf16[2,784,128]{2,1,0:T(8,128)(2,1)S(1)}, bf16[2,784,128]{2,1,0:T(8,128)(2,1)S(1)}, u32[]{:S(2)}, u32[]{:S(2)}) collective-permute-start(bf16[2,784,128]{2,1,0:T(8,128)(2,1)S(1)} %constant_dynamic-update-slice_fusion.refs_2_), channel_id=1, source_target_pairs={{0,16},{4,20},{16,24},{20,28},{24,8},{28,12},{8,0},{12,4},{1,17},{... | collective-permute-start | bytes 1204232 | tf_op jit(solution)/shard_map/late_hop_1/ppermute | solution.py:247
  18.9 1.6 %collective-permute-start.7 = (bf16[1,784,128]{2,1,0:T(8,128)(2,1)S(1)}, bf16[1,784,128]{2,1,0:T(8,128)(2,1)S(1)}, u32[]{:S(2)}, u32[]{:S(2)}) collective-permute-start(bf16[1,784,128]{2,1,0:T(8,128)(2,1)S(1)} %collective-permute-done.6.refs_1_), channel_id=1, source_target_pairs={{0,16},{4,20},{16,24},{20,28},{24,8},{28,12},{8,0},{12,4},{1,17},{... | collective-permute-start | bytes 602120 | tf_op jit(solution)/shard_map/early_hop_1/ppermute | solution.py:247
  20.5 1.0 %copy-done = bf16[256,1024]{1,0:T(8,128)(2,1)S(1)} copy-done((bf16[256,1024]{1,0:T(8,128)(2,1)S(1)}, bf16[256,1024]{1,0:T(8,128)(2,1)}, u32[]{:S(2)}) %copy-start) | copy-done | bytes 524312
  22.9 1.6 %collective-permute-start.2 = (bf16[256,1024]{1,0:T(8,128)(2,1)S(1)}, bf16[256,1024]{1,0:T(8,128)(2,1)S(1)}, u32[]{:S(2)}, u32[]{:S(2)}) collective-permute-start(bf16[256,1024]{1,0:T(8,128)(2,1)S(1)} %mask.1), channel_id=1, source_target_pairs={{0,1},{1,0},{2,3},{3,2},{4,5},{5,4},{6,7},{7,6},{8,9},{9,8},{10,11... | collective-permute-start | bytes 1572872 | tf_op jit(solution)/shard_map/amplitudes_from_partner_1/ppermute | solution.py:234
  24.5 1.5 %collective-permute-start.3 = (bf16[256,1024]{1,0:T(8,128)(2,1)S(1)}, bf16[256,1024]{1,0:T(8,128)(2,1)S(1)}, u32[]{:S(2)}, u32[]{:S(2)}) collective-permute-start(bf16[256,1024]{1,0:T(8,128)(2,1)S(1)} %mask.1), channel_id=1, source_target_pairs={{0,2},{1,3},{2,0},{3,1},{4,6},{5,7},{6,4},{7,5},{8,10},{9,11},{10,... | collective-permute-start | bytes 1572872 | tf_op jit(solution)/shard_map/amplitudes_from_partner_2/ppermute | solution.py:234
  26.5 4.4 %collective-permute-done.7 = bf16[1,784,128]{2,1,0:T(8,128)(2,1)S(1)} collective-permute-done((bf16[1,784,128]{2,1,0:T(8,128)(2,1)S(1)}, bf16[1,784,128]{2,1,0:T(8,128)(2,1)S(1)}, u32[]{:S(2)}, u32[]{:S(2)}) %collective-permute-start.7) | collective-permute-done | bytes 200736 | tf_op jit(solution)/shard_map/early_hop_1/ppermute | solution.py:247
  30.9 3.0 %collective-permute-start.8 = (bf16[2,784,128]{2,1,0:T(8,128)(2,1)S(1)}, bf16[2,784,128]{2,1,0:T(8,128)(2,1)S(1)}, u32[]{:S(2)}, u32[]{:S(2)}) collective-permute-start(bf16[2,784,128]{2,1,0:T(8,128)(2,1)S(1)} %constant_dynamic-update-slice_fusion.2.refs_3_), channel_id=1, source_target_pairs={{0,16},{4,20},{16,24},{20,28},{24,8},{28,12},{8,0},{12,4},{1,17},{... | collective-permute-start | bytes 1204232 | tf_op jit(solution)/shard_map/first_hop_2/ppermute | solution.py:247
  34.6 3.3 %collective-permute-done.2 = bf16[256,1024]{1,0:T(8,128)(2,1)S(1)} collective-permute-done((bf16[256,1024]{1,0:T(8,128)(2,1)S(1)}, bf16[256,1024]{1,0:T(8,128)(2,1)S(1)}, u32[]{:S(2)}, u32[]{:S(2)}) %collective-permute-start.2) | collective-permute-done | bytes 524320 | tf_op jit(solution)/shard_map/amplitudes_from_partner_1/ppermute | solution.py:234
  37.8 8.9 %collective-permute-done.3 = bf16[256,1024]{1,0:T(8,128)(2,1)S(1)} collective-permute-done((bf16[256,1024]{1,0:T(8,128)(2,1)S(1)}, bf16[256,1024]{1,0:T(8,128)(2,1)S(1)}, u32[]{:S(2)}, u32[]{:S(2)}) %collective-permute-start.3) | collective-permute-done | bytes 524320 | tf_op jit(solution)/shard_map/amplitudes_from_partner_2/ppermute | solution.py:234
  46.7 0.7 collective-permute-done.4
  47.4 1.7 %collective-permute-done.10.refs_0_ = bf16[2,784,128]{2,1,0:T(8,128)(2,1)S(1)} collective-permute-done((bf16[2,784,128]{2,1,0:T(8,128)(2,1)S(1)}, bf16[2,784,128]{2,1,0:T(8,128)(2,1)S(1)}, u32[]{:S(2)}, u32[]{:S(2)}) %collective-permute-start.10) | collective-permute-done | bytes 401440 | tf_op jit(solution)/shard_map/late_hop_2/ppermute | solution.py:247
  49.5 3.1 %collective-permute-start.12 = (bf16[2,784,128]{2,1,0:T(8,128)(2,1)S(1)}, bf16[2,784,128]{2,1,0:T(8,128)(2,1)S(1)}, u32[]{:S(2)}, u32[]{:S(2)}) collective-permute-start(bf16[2,784,128]{2,1,0:T(8,128)(2,1)S(1)} %collective-permute-done.8.refs_4_), channel_id=1, source_target_pairs={{0,16},{4,20},{16,24},{20,28},{24,8},{28,12},{8,0},{12,4},{1,17},{... | collective-permute-start | bytes 1204232 | tf_op jit(solution)/shard_map/first_hop_3/ppermute | solution.py:247
  52.7 1.0 %collective-permute-done.11 = bf16[4,256,1024]{2,1,0:T(8,128)(2,1)S(1)} collective-permute-done((bf16[4,256,1024]{2,1,0:T(8,128)(2,1)S(1)}, bf16[4,256,1024]{2,1,0:T(8,128)(2,1)S(1)}, u32[]{:S(2)}, u32[]{:S(2)}) %collective-permute-start.11) | collective-permute-done | bytes 2097184 | tf_op jit(solution)/shard_map/twin_amplitudes/ppermute | solution.py:237
  54.2 5.9 %ladder_first.1 = (f32[9,512,128]{2,1,0:T(8,128)S(1)}, f32[256,128]{1,0:T(8,128)S(1)}) custom-call(f32[2,128]{1,0:T(2,128)S(1)} %bitcast.10, bf16[4,512,1024]{2,1,0:T(8,128)(2,1)S(1)} %pad_maximum_fusion.amps.refs_0_, bf16[1,784,128]{2,1,0:T(8,128)(2,1)S(1)} %copy-done.3, bf16[1,784,128]{2,1,0:T(8,128)(2,1)S(1)} %collective-permute-done.6.refs_1_, ...), custom_call_target="tpu_custom_call" | custom-call | flops 100000000 | bytes 1048576 | tf_op jit(solution)/shard_map/ladder_first/pallas_call | solution.py:282
  60.1 2.0 %collective-permute-done.12.refs_1_ = bf16[2,784,128]{2,1,0:T(8,128)(2,1)S(1)} collective-permute-done((bf16[2,784,128]{2,1,0:T(8,128)(2,1)S(1)}, bf16[2,784,128]{2,1,0:T(8,128)(2,1)S(1)}, u32[]{:S(2)}, u32[]{:S(2)}) %collective-permute-start.12) | collective-permute-done | bytes 401440 | tf_op jit(solution)/shard_map/first_hop_3/ppermute | solution.py:247
  62.2 3.0 %ladder_second.1 = (f32[8,256,128]{2,1,0:T(8,128)S(1)}, bf16[8,256,128]{2,1,0:T(8,128)(2,1)S(1)}) custom-call(f32[9,512,128]{2,1,0:T(8,128)S(1)} %get-tuple-element.25.before, bf16[4,512,1024]{2,1,0:T(8,128)(2,1)S(1)} %pad_maximum_fusion.amps.refs_0_, bf16[2,784,128]{2,1,0:T(8,128)(2,1)S(1)} %collective-permute-done.10.refs_0_, ...), custom_call_target="tpu_custom_call" | custom-call | flops 1000000000 | bytes 1048576 | tf_op jit(solution)/shard_map/ladder_second/pallas_call | solution.py:282
  65.3 5.0 %collective-permute-done.14.refs_1_ = bf16[2,784,128]{2,1,0:T(8,128)(2,1)S(1)} collective-permute-done((bf16[2,784,128]{2,1,0:T(8,128)(2,1)S(1)}, bf16[2,784,128]{2,1,0:T(8,128)(2,1)S(1)}, u32[]{:S(2)}, u32[]{:S(2)}) %collective-permute-start.14) | collective-permute-done | bytes 401440 | tf_op jit(solution)/shard_map/late_hop_3/ppermute | solution.py:247
  70.4 1.7 %collective-permute-done.15.refs_2_ = bf16[2,784,128]{2,1,0:T(8,128)(2,1)S(1)} collective-permute-done((bf16[2,784,128]{2,1,0:T(8,128)(2,1)S(1)}, bf16[2,784,128]{2,1,0:T(8,128)(2,1)S(1)}, u32[]{:S(2)}, u32[]{:S(2)}) %collective-permute-start.15) | collective-permute-done | bytes 401440 | tf_op jit(solution)/shard_map/ppermute | solution.py:237
  72.1 4.0 %update.1 = (bf16[256,1024]{1,0:T(8,128)(2,1)}, f32[256,1024]{1,0:T(8,128)}) custom-call(s32[2,8]{1,0:T(2,128)S(1)} %copy-done.6, bf16[256,1024]{1,0:T(8,128)(2,1)S(1)} %copy-done.1, bf16[256,1024]{1,0:T(8,128)(2,1)S(1)} %copy-done.2, f32[8,256,128]{2,1,0:T(8,128)S(1)} %get-tuple-element.26.own, bf16[8,256,128]{2,1,0:T(8,128)(2,1)S(1)} %collective-permute-done.13.twin, ...), custom_call_target="tpu_custom_call" | custom-call | tf_op jit(solution)/shard_map/update/pallas_call | solution.py:342
  (35 shorter events, 4.3 us)
Async XLA Ops:
  3.5 12.5 %collective-permute-start = (bf16[1,784,128]{2,1,0:T(8,128)(2,1)}, bf16[1,784,128]{2,1,0:T(8,128)(2,1)S(1)}, u32[]{:S(2)}, u32[]{:S(2)}) collective-permute-start(bf16[1,784,128]{2,1,0:T(8,128)(2,1)} %get-tuple-element.16), channel_id=1, source_target_pairs={{0,2},{1,3},{2,0},{3,1},{4,6},{5,7},{6,4},{7,5},{8,10},{9,11},{10,... | collective-permute-start | bytes 602120 | tf_op jit(solution)/shard_map/parcels_from_partner_2/ppermute | solution.py:234
  6.5 9.5 %collective-permute-start.1 = (bf16[1,784,128]{2,1,0:T(8,128)(2,1)}, bf16[1,784,128]{2,1,0:T(8,128)(2,1)S(1)}, u32[]{:S(2)}, u32[]{:S(2)}) collective-permute-start(bf16[1,784,128]{2,1,0:T(8,128)(2,1)} %get-tuple-element.17), channel_id=1, source_target_pairs={{0,3},{1,2},{2,1},{3,0},{4,7},{5,6},{6,5},{7,4},{8,11},{9,10},{10,... | collective-permute-start | bytes 602120 | tf_op jit(solution)/shard_map/parcels_from_partner_3/ppermute | solution.py:234
  7.9 18.1 %collective-permute-start.5 = (bf16[1,784,128]{2,1,0:T(8,128)(2,1)}, bf16[1,784,128]{2,1,0:T(8,128)(2,1)S(1)}, u32[]{:S(2)}, u32[]{:S(2)}) collective-permute-start(bf16[1,784,128]{2,1,0:T(8,128)(2,1)} %get-tuple-element.19.refs_0_), channel_id=1, source_target_pairs={{0,16},{4,20},{16,24},{20,28},{24,8},{28,12},{8,0},{12,4},{1,17},{... | collective-permute-start | bytes 602120 | tf_op jit(solution)/shard_map/near_hop_1/ppermute | solution.py:247
  10.5 8.4 %collective-permute-start.6 = (bf16[1,784,128]{2,1,0:T(8,128)(2,1)}, bf16[1,784,128]{2,1,0:T(8,128)(2,1)S(1)}, u32[]{:S(2)}, u32[]{:S(2)}) collective-permute-start(bf16[1,784,128]{2,1,0:T(8,128)(2,1)} %get-tuple-element.20), channel_id=1, source_target_pairs={{0,1},{1,0},{2,3},{3,2},{4,5},{5,4},{6,7},{7,6},{8,9},{9,8},{10,11... | collective-permute-start | bytes 602120 | tf_op jit(solution)/shard_map/parcels_from_partner_1/ppermute | solution.py:234
  16.1 17.8 %collective-permute-start.9 = (bf16[2,784,128]{2,1,0:T(8,128)(2,1)S(1)}, bf16[2,784,128]{2,1,0:T(8,128)(2,1)S(1)}, u32[]{:S(2)}, u32[]{:S(2)}) collective-permute-start(bf16[2,784,128]{2,1,0:T(8,128)(2,1)S(1)} %constant_dynamic-update-slice_fusion.refs_2_), channel_id=1, source_target_pairs={{0,16},{4,20},{16,24},{20,28},{24,8},{28,12},{8,0},{12,4},{1,17},{... | collective-permute-start | bytes 1204232 | tf_op jit(solution)/shard_map/late_hop_1/ppermute | solution.py:247
  18.9 12.0 %collective-permute-start.7 = (bf16[1,784,128]{2,1,0:T(8,128)(2,1)S(1)}, bf16[1,784,128]{2,1,0:T(8,128)(2,1)S(1)}, u32[]{:S(2)}, u32[]{:S(2)}) collective-permute-start(bf16[1,784,128]{2,1,0:T(8,128)(2,1)S(1)} %collective-permute-done.6.refs_1_), channel_id=1, source_target_pairs={{0,16},{4,20},{16,24},{20,28},{24,8},{28,12},{8,0},{12,4},{1,17},{... | collective-permute-start | bytes 602120 | tf_op jit(solution)/shard_map/early_hop_1/ppermute | solution.py:247
  20.5 1.0 %copy-start = (bf16[256,1024]{1,0:T(8,128)(2,1)S(1)}, bf16[256,1024]{1,0:T(8,128)(2,1)}, u32[]{:S(2)}) copy-start(bf16[256,1024]{1,0:T(8,128)(2,1)} %amplitudes.3) | copy-start | bytes 1572868
  21.5 0.7 copy-start.5
  22.9 14.9 %collective-permute-start.2 = (bf16[256,1024]{1,0:T(8,128)(2,1)S(1)}, bf16[256,1024]{1,0:T(8,128)(2,1)S(1)}, u32[]{:S(2)}, u32[]{:S(2)}) collective-permute-start(bf16[256,1024]{1,0:T(8,128)(2,1)S(1)} %mask.1), channel_id=1, source_target_pairs={{0,1},{1,0},{2,3},{3,2},{4,5},{5,4},{6,7},{7,6},{8,9},{9,8},{10,11... | collective-permute-start | bytes 1572872 | tf_op jit(solution)/shard_map/amplitudes_from_partner_1/ppermute | solution.py:234
  24.5 22.2 %collective-permute-start.3 = (bf16[256,1024]{1,0:T(8,128)(2,1)S(1)}, bf16[256,1024]{1,0:T(8,128)(2,1)S(1)}, u32[]{:S(2)}, u32[]{:S(2)}) collective-permute-start(bf16[256,1024]{1,0:T(8,128)(2,1)S(1)} %mask.1), channel_id=1, source_target_pairs={{0,2},{1,3},{2,0},{3,1},{4,6},{5,7},{6,4},{7,5},{8,10},{9,11},{10,... | collective-permute-start | bytes 1572872 | tf_op jit(solution)/shard_map/amplitudes_from_partner_2/ppermute | solution.py:234
  26.0 21.4 %collective-permute-start.4 = (bf16[256,1024]{1,0:T(8,128)(2,1)S(1)}, bf16[256,1024]{1,0:T(8,128)(2,1)S(1)}, u32[]{:S(2)}, u32[]{:S(2)}) collective-permute-start(bf16[256,1024]{1,0:T(8,128)(2,1)S(1)} %mask.1), channel_id=1, source_target_pairs={{0,3},{1,2},{2,1},{3,0},{4,7},{5,6},{6,5},{7,4},{8,11},{9,10},{10,... | collective-permute-start | bytes 1572872 | tf_op jit(solution)/shard_map/amplitudes_from_partner_3/ppermute | solution.py:234
  30.9 16.5 %collective-permute-start.8 = (bf16[2,784,128]{2,1,0:T(8,128)(2,1)S(1)}, bf16[2,784,128]{2,1,0:T(8,128)(2,1)S(1)}, u32[]{:S(2)}, u32[]{:S(2)}) collective-permute-start(bf16[2,784,128]{2,1,0:T(8,128)(2,1)S(1)} %constant_dynamic-update-slice_fusion.2.refs_3_), channel_id=1, source_target_pairs={{0,16},{4,20},{16,24},{20,28},{24,8},{28,12},{8,0},{12,4},{1,17},{... | collective-permute-start | bytes 1204232 | tf_op jit(solution)/shard_map/first_hop_2/ppermute | solution.py:247
  33.9 15.2 %collective-permute-start.10 = (bf16[2,784,128]{2,1,0:T(8,128)(2,1)S(1)}, bf16[2,784,128]{2,1,0:T(8,128)(2,1)S(1)}, u32[]{:S(2)}, u32[]{:S(2)}) collective-permute-start(bf16[2,784,128]{2,1,0:T(8,128)(2,1)S(1)} %collective-permute-done.9.refs_5_), channel_id=1, source_target_pairs={{0,16},{4,20},{16,24},{20,28},{24,8},{28,12},{8,0},{12,4},{1,17},{... | collective-permute-start | bytes 1204232 | tf_op jit(solution)/shard_map/late_hop_2/ppermute | solution.py:247
  49.4 4.8 %copy-start.3 = (bf16[1,784,128]{2,1,0:T(8,128)(2,1)S(1)}, bf16[1,784,128]{2,1,0:T(8,128)(2,1)}, u32[]{:S(2)}) copy-start(bf16[1,784,128]{2,1,0:T(8,128)(2,1)} %get-tuple-element.19.refs_0_) | copy-start | bytes 602116
  49.4 4.8 %copy-start.7 = (f32[256]{0:T(256)S(1)}, f32[256]{0:T(256)}, u32[]{:S(2)}) copy-start(f32[256]{0:T(256)} %param.12) | copy-start | bytes 3076
  49.4 4.2 %collective-permute-start.11 = (bf16[4,256,1024]{2,1,0:T(8,128)(2,1)S(1)}, bf16[4,256,1024]{2,1,0:T(8,128)(2,1)S(1)}, u32[]{:S(2)}, u32[]{:S(2)}) collective-permute-start(bf16[4,256,1024]{2,1,0:T(8,128)(2,1)S(1)} %pad_maximum_fusion.1), channel_id=1, source_target_pairs={{0,4},{4,0},{8,12},{12,8},{16,20},{20,16},{24,28},{28,24},{1,5},{5... | collective-permute-start | bytes 6291464 | tf_op jit(solution)/shard_map/twin_amplitudes/ppermute | solution.py:237
  49.5 12.7 %collective-permute-start.12 = (bf16[2,784,128]{2,1,0:T(8,128)(2,1)S(1)}, bf16[2,784,128]{2,1,0:T(8,128)(2,1)S(1)}, u32[]{:S(2)}, u32[]{:S(2)}) collective-permute-start(bf16[2,784,128]{2,1,0:T(8,128)(2,1)S(1)} %collective-permute-done.8.refs_4_), channel_id=1, source_target_pairs={{0,16},{4,20},{16,24},{20,28},{24,8},{28,12},{8,0},{12,4},{1,17},{... | collective-permute-start | bytes 1204232 | tf_op jit(solution)/shard_map/first_hop_3/ppermute | solution.py:247
  52.6 17.8 %collective-permute-start.14 = (bf16[2,784,128]{2,1,0:T(8,128)(2,1)S(1)}, bf16[2,784,128]{2,1,0:T(8,128)(2,1)S(1)}, u32[]{:S(2)}, u32[]{:S(2)}) collective-permute-start(bf16[2,784,128]{2,1,0:T(8,128)(2,1)S(1)} %collective-permute-done.10.refs_0_), channel_id=1, source_target_pairs={{0,16},{4,20},{16,24},{20,28},{24,8},{28,12},{8,0},{12,4},{1,17},{... | collective-permute-start | bytes 1204232 | tf_op jit(solution)/shard_map/late_hop_3/ppermute | solution.py:247
  60.1 12.0 %copy-start.1 = (bf16[256,1024]{1,0:T(8,128)(2,1)S(1)}, bf16[256,1024]{1,0:T(8,128)(2,1)}, u32[]{:S(2)}) copy-start(bf16[256,1024]{1,0:T(8,128)(2,1)} %amplitudes.3) | copy-start | bytes 1572868
  60.1 12.0 %copy-start.2 = (bf16[256,1024]{1,0:T(8,128)(2,1)S(1)}, bf16[256,1024]{1,0:T(8,128)(2,1)}, u32[]{:S(2)}) copy-start(bf16[256,1024]{1,0:T(8,128)(2,1)} %driver.1) | copy-start | bytes 1572868
  60.1 12.0 %copy-start.4 = (f32[1024]{0:T(1024)S(1)}, f32[1024]{0:T(1024)}, u32[]{:S(2)}) copy-start(f32[1024]{0:T(1024)} %param.13) | copy-start | bytes 12292
  60.1 12.0 %copy-start.6 = (s32[2,8]{1,0:T(2,128)S(1)}, s32[2,8]{1,0:T(2,128)}, u32[]{:S(2)}) copy-start(s32[2,8]{1,0:T(2,128)} %live.3) | copy-start | bytes 196
  65.2 6.9 %collective-permute-start.13 = (bf16[8,256,128]{2,1,0:T(8,128)(2,1)S(1)}, bf16[8,256,128]{2,1,0:T(8,128)(2,1)S(1)}, u32[]{:S(2)}, u32[]{:S(2)}) collective-permute-start(bf16[8,256,128]{2,1,0:T(8,128)(2,1)S(1)} %get-tuple-element.27), channel_id=1, source_target_pairs={{0,4},{4,0},{8,12},{12,8},{16,20},{20,16},{24,28},{28,24},{1,5},{5... | collective-permute-start | bytes 1572872 | tf_op jit(solution)/shard_map/ppermute | solution.py:237
  70.3 1.7 %collective-permute-start.15 = (bf16[2,784,128]{2,1,0:T(8,128)(2,1)S(1)}, bf16[2,784,128]{2,1,0:T(8,128)(2,1)S(1)}, u32[]{:S(2)}, u32[]{:S(2)}) collective-permute-start(bf16[2,784,128]{2,1,0:T(8,128)(2,1)S(1)} %collective-permute-done.14.refs_1_), channel_id=1, source_target_pairs={{0,4},{4,0},{8,12},{12,8},{16,20},{20,16},{24,28},{28,24},{1,5},{5... | collective-permute-start | bytes 1204232 | tf_op jit(solution)/shard_map/ppermute | solution.py:237

commit v5 on v4

--- a/solution.py
+++ b/solution.py
@@ -16,12 +16,10 @@
 SECOND_FLOPS = 10**9
 
 
-def pack_kernel(n_v, cap, columns, integrals, *refs):
-    parcels, (origin, codes, tiles, sem) = refs[:n_v], refs[n_v:]
+def pack_kernel(n_v, cap, columns, live, integrals, amplitudes, *refs):
+    parcels, (masked, origin, codes) = refs[:n_v], refs[n_v:]
     rows, slots, tile, _ = integrals.shape
     me = lax.axis_index("vpair")
-    copy = pltpu.make_async_copy(integrals, tiles, sem)
-    copy.start()
     counts = [jnp.int32(0)] * n_v
     for i in range(n_v * cap):
         origin[i] = 0
@@ -37,23 +35,18 @@
             at = partner * cap + place
             origin[at] = row * slots + slot
             codes[at] = row * rows + lax.rem(column, rows)
-    copy.wait()
     lane = lax.broadcasted_iota(jnp.int32, (NOTE_ROWS, tile), 1)
     for j in range(n_v):
         note = jnp.full((NOTE_ROWS, tile), -1, jnp.int32)
         for k in range(cap):
             entry = origin[j * cap + k]
-            parcels[j][0, pl.ds(k * tile, tile)] = tiles[
+            parcels[j][0, pl.ds(k * tile, tile)] = integrals[
                 lax.div(entry, slots), lax.rem(entry, slots)
             ]
             note = jnp.where(lane == k, codes[j * cap + k], note)
         parcels[j][0, pl.ds(cap * tile, NOTE_ROWS)] = note.astype(jnp.float32).astype(
             integrals.dtype
         )
-
-
-def mask_kernel(live, amplitudes, masked):
-    tile = amplitudes.shape[1] // live.shape[1]
     for o in range(live.shape[0]):
         for c in range(live.shape[1]):
             at = (pl.ds(o * tile, tile), pl.ds(c * tile, tile))
@@ -204,29 +197,24 @@
     anywhere = pl.BlockSpec(memory_space=pl.ANY)
     in_hbm = pl.BlockSpec(memory_space=pltpu.HBM)
 
+    def after(values, others):
+        return lax.optimization_barrier((values, others))[0]
+
     def params(*buffers):
         size = sum(math.prod(shape) * jnp.dtype(kind).itemsize for shape, kind in buffers)
         return pltpu.CompilerParams(vmem_limit_bytes=size + SPARE_VMEM)
 
     parcel = (1, height, tile)
-    parcels = pl.pallas_call(
+    *parcels, masked = pl.pallas_call(
         functools.partial(pack_kernel, n_v, cap),
-        out_shape=[jax.ShapeDtypeStruct(parcel, dtype)] * n_v,
-        in_specs=[in_smem, in_hbm],
-        out_specs=[in_vmem] * n_v,
-        scratch_shapes=[pltpu.SMEM((n_v * cap,), jnp.int32)] * 2
-        + [pltpu.VMEM(integrals.shape, dtype), pltpu.SemaphoreType.DMA],
+        out_shape=[jax.ShapeDtypeStruct(parcel, dtype)] * n_v
+        + [jax.ShapeDtypeStruct(amplitudes.shape, amplitudes.dtype)],
+        in_specs=[in_smem, in_smem, in_vmem, in_vmem],
+        out_specs=[in_vmem] * (n_v + 1),
+        scratch_shapes=[pltpu.SMEM((n_v * cap,), jnp.int32)] * 2,
         compiler_params=pltpu.CompilerParams(vmem_limit_bytes=ALL_VMEM),
         name="pack",
-    )(integral_columns.T, integrals)
-    masked = pl.pallas_call(
-        mask_kernel,
-        out_shape=jax.ShapeDtypeStruct(amplitudes.shape, amplitudes.dtype),
-        in_specs=[in_smem, in_vmem],
-        out_specs=in_vmem,
-        compiler_params=params(((4, n_rows, width), dtype)),
-        name="mask",
-    )(tile_live, amplitudes)
+    )(integral_columns.T, tile_live, integrals, amplitudes)
 
     def across_v(value, j):
         name = "amplitudes" if value.ndim == 2 else "parcels"
@@ -249,29 +237,30 @@
     def join(values):
         return jnp.concatenate(values) if len(values) > 1 else values[0]
 
-    def after(values, others):
-        return lax.optimization_barrier((values, others))[0]
-
     others = list(range(1, n_v))
     groups = {"near": [0], "early": others[: n_v // 2 - 1], "late": others[n_v // 2 - 1 :]}
     arrived = {0: parcels[0]} | {j: across_v(parcels[j], j) for j in others}
     hops = {name: [join([arrived[j] for j in groups[name]])] for name in groups}
+    for name in ("near", "early"):
+        hops[name].append(next_on_ring(hops[name][0], f"{name}_hop_1"))
+    hops["late"][0] = after(hops["late"][0], (hops["near"][1], hops["early"][0]))
     groups["first"] = groups["near"] + groups["early"]
-    for name in ("near", "early", "late"):
-        hops[name].append(next_on_ring(hops[name][0], f"{name}_hop_1"))
+    hops["late"].append(next_on_ring(hops["late"][0], "late_hop_1"))
     hops["first"] = [None, join([hops["near"][1], hops["early"][1]])]
     for hop in range(2, n_z):
         for name in ("first", "late"):
             hops[name].append(next_on_ring(hops[name][-1], f"{name}_hop_{hop}"))
 
     a_parts = {0: masked}
-    ready = after(masked, hops["late"][0])
+    with jax.named_scope("twin_amplitudes_0"):
+        a_twins = {0: across_core(masked)}
+    ready = after(masked, a_twins[0])
     for j in others:
         a_parts[j] = across_v(ready, j)
-    a_parts = after(a_parts, (hops["first"][2], hops["late"][2]))
-    own_a = jnp.stack([a_parts[j] for j in range(n_v)])
-    with jax.named_scope("twin_amplitudes"):
-        amps = jnp.concatenate([own_a, across_core(own_a)], axis=1)
+    for j in others:
+        with jax.named_scope(f"twin_amplitudes_{j}"):
+            a_twins[j] = across_core(after(a_parts[j], hops["first"][2]))
+    amps = jnp.stack([jnp.concatenate([a_parts[j], a_twins[j]]) for j in range(n_v)])
 
     sums = (rows + 1, CORES * n_rows, tile)
     pairs = (max(cap // 2, 1), 2 * tile, 2 * tile)

time: 76.9 us -> 75.8 us (0.986)
  starting transfers between devices: 22.6 us -> 27.3 us
  waiting for transfers between devices: 33.7 us -> 29.6 us
  local copies, waits for them, and re-layouts: 1.84 us -> 0.39 us
  other arithmetic: 0.83 us -> 1.93 us
  Pallas kernels: 16.4 us -> 15.6 us
    ppermute x7, starting transfers between devices: 13.9 us -> 16.5 us  [next_on_ring(): return lax.ppermute(value, 'opair', pairs)]
    ppermute x6, waiting for transfers between devices: 17.8 us -> 15.7 us  [across_v(): return lax.ppermute(value, 'vpair', [(i, i ^ j) for i in range(n_v)])]
    another operation x1 -> x5, other arithmetic: 0.26 us -> 1.89 us  [on_device(): jnp.stack([jnp.concatenate([a_parts[j], a_twins[j]]) for j in range(n_v)])]
    unnamed x18 -> x13, local copies, waits for them, and re-layouts: 1.79 us -> 0.36 us
    ppermute x6, starting transfers between devices: 8.55 us -> 9.76 us  [across_v(): return lax.ppermute(value, 'vpair', [(i, i ^ j) for i in range(n_v)])]
    ppermute x7, waiting for transfers between devices: 13.2 us -> 12.1 us  [next_on_ring(): return lax.ppermute(value, 'opair', pairs)]
    ppermute x3 -> x6, waiting for transfers between devices: 2.69 us -> 1.74 us  [across_core(): return lax.ppermute(value, 'opair', [(i, i ^ 1) for i in range(n_o)])]
    ppermute x3 -> x6, starting transfers between devices: 0.14 us -> 1.04 us  [across_core(): return lax.ppermute(value, 'opair', [(i, i ^ 1) for i in range(n_o)])]
  transfers between devices with their start and end apart: 16 -> 19, of which waited for: 10 -> 10; matrix products, arithmetic and copies ran while one was open for 1% -> 3% of each run, Pallas kernels for 13% -> 12%
where the time goes in v5:
time: 75.8 us; the launch traced here: 75.6 us
  waiting for transfers between devices  29.6 us (39%)
  starting transfers between devices  27.3 us (36%)
  Pallas kernels  15.6 us (21%)
  other arithmetic  1.93 us (3%)
  between operations  0.77 us (1%)
    ppermute x7, starting transfers between devices, next_on_ring(): return lax.ppermute(value, 'opair', pairs)  16.5 us
    ppermute x6, waiting for transfers between devices, across_v(): return lax.ppermute(value, 'vpair', [(i, i ^ j) for i in range(n_v)])  15.7 us
    ppermute x7, waiting for transfers between devices, next_on_ring(): return lax.ppermute(value, 'opair', pairs)  12.1 us
    ppermute x6, starting transfers between devices, across_v(): return lax.ppermute(value, 'vpair', [(i, i ^ j) for i in range(n_v)])  9.76 us
    pallas_call x2, Pallas kernels, ladder_call(): pl.pallas_call(functools.partial(kernel, cap, layout), out_shape=out_shap...  8.87 us
    pallas_call x1, Pallas kernels, on_device(): pl.pallas_call(functools.partial(update_kernel, cap, behind), out_shape=[...  3.98 us
    pallas_call x1, Pallas kernels, on_device(): pl.pallas_call(functools.partial(pack_kernel, n_v, cap), out_shape=[jax.S...  2.78 us
    another operation x5, other arithmetic, on_device(): jnp.stack([jnp.concatenate([a_parts[j], a_twins[j]]) for j in range(n_v)])  1.89 us
  transfers between devices with their start and end apart: 19, of which 10 were waited for; matrix products, arithmetic and copies ran while one was open for 3% of the time, Pallas kernels for 12%

profile of v5, /device:TPU:0, one launch (start us, length us, event | category | flops | bytes accessed | tf_op | source)
XLA Modules:
  0.0 75.6 jit_solution(317054398422982286)
XLA Ops:
  0.6 2.8 %pack.1 = (bf16[1,784,128]{2,1,0:T(8,128)(2,1)}, bf16[1,784,128]{2,1,0:T(8,128)(2,1)}, bf16[1,784,128]{2,1,0:T(8,128)(2,1)}, bf16[1,784,128]{2,1,0:T(8,128)(2,1)}, bf16[256,1024]{1,0:T(8,128)(2,1)}) custom-call(s32[3,8]{1,0:T(4,128)} %bitcast.13, s32[2,8]{1,0:T(2,128)} %live.3, bf16[8,3,128,128]{3,2,1,0:T(8,128)(2,1)} %integrals.1, bf16[256,1024]{1,0:T(8,128)(2,1)} %amplitudes.3), custom_call_target="tpu_custom_call" | custom-call | tf_op jit(solution)/shard_map/pack/pallas_call | solution.py:208
  3.9 2.5 %collective-permute-start.3 = (bf16[1,784,128]{2,1,0:T(8,128)(2,1)}, bf16[1,784,128]{2,1,0:T(8,128)(2,1)S(1)}, u32[]{:S(2)}, u32[]{:S(2)}) collective-permute-start(bf16[1,784,128]{2,1,0:T(8,128)(2,1)} %get-tuple-element.20), channel_id=1, source_target_pairs={{0,1},{1,0},{2,3},{3,2},{4,5},{5,4},{6,7},{7,6},{8,9},{9,8},{10,11... | collective-permute-start | bytes 602120 | tf_op jit(solution)/shard_map/parcels_from_partner_1/ppermute | solution.py:222
  6.3 2.6 %collective-permute-start.2 = (bf16[1,784,128]{2,1,0:T(8,128)(2,1)}, bf16[1,784,128]{2,1,0:T(8,128)(2,1)S(1)}, u32[]{:S(2)}, u32[]{:S(2)}) collective-permute-start(bf16[1,784,128]{2,1,0:T(8,128)(2,1)} %get-tuple-element.19.refs_0_), channel_id=1, source_target_pairs={{0,16},{4,20},{16,24},{20,28},{24,8},{28,12},{8,0},{12,4},{1,17},{... | collective-permute-start | bytes 602120 | tf_op jit(solution)/shard_map/near_hop_1/ppermute | solution.py:235
  8.9 3.3 %collective-permute-done.3.refs_1_ = bf16[1,784,128]{2,1,0:T(8,128)(2,1)S(1)} collective-permute-done((bf16[1,784,128]{2,1,0:T(8,128)(2,1)}, bf16[1,784,128]{2,1,0:T(8,128)(2,1)S(1)}, u32[]{:S(2)}, u32[]{:S(2)}) %collective-permute-start.3) | collective-permute-done | bytes 200736 | tf_op jit(solution)/shard_map/parcels_from_partner_1/ppermute | solution.py:222
  12.2 2.8 %collective-permute-start.4 = (bf16[1,784,128]{2,1,0:T(8,128)(2,1)S(1)}, bf16[1,784,128]{2,1,0:T(8,128)(2,1)S(1)}, u32[]{:S(2)}, u32[]{:S(2)}) collective-permute-start(bf16[1,784,128]{2,1,0:T(8,128)(2,1)S(1)} %collective-permute-done.3.refs_1_), channel_id=1, source_target_pairs={{0,16},{4,20},{16,24},{20,28},{24,8},{28,12},{8,0},{12,4},{1,17},{... | collective-permute-start | bytes 602120 | tf_op jit(solution)/shard_map/early_hop_1/ppermute | solution.py:235
  15.1 1.5 %collective-permute-start.11 = (bf16[1,784,128]{2,1,0:T(8,128)(2,1)}, bf16[1,784,128]{2,1,0:T(8,128)(2,1)S(1)}, u32[]{:S(2)}, u32[]{:S(2)}) collective-permute-start(bf16[1,784,128]{2,1,0:T(8,128)(2,1)} %get-tuple-element.24), channel_id=1, source_target_pairs={{0,2},{1,3},{2,0},{3,1},{4,6},{5,7},{6,4},{7,5},{8,10},{9,11},{10,... | collective-permute-start | bytes 602120 | tf_op jit(solution)/shard_map/parcels_from_partner_2/ppermute | solution.py:222
  16.6 1.4 %collective-permute-start.12 = (bf16[1,784,128]{2,1,0:T(8,128)(2,1)}, bf16[1,784,128]{2,1,0:T(8,128)(2,1)S(1)}, u32[]{:S(2)}, u32[]{:S(2)}) collective-permute-start(bf16[1,784,128]{2,1,0:T(8,128)(2,1)} %get-tuple-element.25), channel_id=1, source_target_pairs={{0,3},{1,2},{2,1},{3,0},{4,7},{5,6},{6,5},{7,4},{8,11},{9,10},{10,... | collective-permute-start | bytes 602120 | tf_op jit(solution)/shard_map/parcels_from_partner_3/ppermute | solution.py:222
  19.2 3.4 %collective-permute-start.5 = (bf16[2,784,128]{2,1,0:T(8,128)(2,1)S(1)}, bf16[2,784,128]{2,1,0:T(8,128)(2,1)S(1)}, u32[]{:S(2)}, u32[]{:S(2)}) collective-permute-start(bf16[2,784,128]{2,1,0:T(8,128)(2,1)S(1)} %constant_dynamic-update-slice_fusion.refs_3_), channel_id=1, source_target_pairs={{0,16},{4,20},{16,24},{20,28},{24,8},{28,12},{8,0},{12,4},{1,17},{... | collective-permute-start | bytes 1204232 | tf_op jit(solution)/shard_map/first_hop_2/ppermute | solution.py:235
  22.7 1.5 %collective-permute-start.7 = (bf16[256,1024]{1,0:T(8,128)(2,1)}, bf16[256,1024]{1,0:T(8,128)(2,1)S(1)}, u32[]{:S(2)}, u32[]{:S(2)}) collective-permute-start(bf16[256,1024]{1,0:T(8,128)(2,1)} %get-tuple-element.18), channel_id=1, source_target_pairs={{0,2},{1,3},{2,0},{3,1},{4,6},{5,7},{6,4},{7,5},{8,10},{9,11},{10,... | collective-permute-start | bytes 1572872 | tf_op jit(solution)/shard_map/amplitudes_from_partner_2/ppermute | solution.py:222
  24.2 2.8 %collective-permute-done.11 = bf16[1,784,128]{2,1,0:T(8,128)(2,1)S(1)} collective-permute-done((bf16[1,784,128]{2,1,0:T(8,128)(2,1)}, bf16[1,784,128]{2,1,0:T(8,128)(2,1)S(1)}, u32[]{:S(2)}, u32[]{:S(2)}) %collective-permute-start.11) | collective-permute-done | bytes 200736 | tf_op jit(solution)/shard_map/parcels_from_partner_2/ppermute | solution.py:222
  27.0 2.1 %collective-permute-start.13 = (bf16[2,784,128]{2,1,0:T(8,128)(2,1)S(1)}, bf16[2,784,128]{2,1,0:T(8,128)(2,1)S(1)}, u32[]{:S(2)}, u32[]{:S(2)}) collective-permute-start(bf16[2,784,128]{2,1,0:T(8,128)(2,1)S(1)} %pad_maximum_fusion.1.refs_2_), channel_id=1, source_target_pairs={{0,16},{4,20},{16,24},{20,28},{24,8},{28,12},{8,0},{12,4},{1,17},{... | collective-permute-start | bytes 1204232 | tf_op jit(solution)/shard_map/late_hop_1/ppermute | solution.py:235
  29.1 2.3 %collective-permute-start.9 = (bf16[256,1024]{1,0:T(8,128)(2,1)}, bf16[256,1024]{1,0:T(8,128)(2,1)S(1)}, u32[]{:S(2)}, u32[]{:S(2)}) collective-permute-start(bf16[256,1024]{1,0:T(8,128)(2,1)} %get-tuple-element.18), channel_id=1, source_target_pairs={{0,3},{1,2},{2,1},{3,0},{4,7},{5,6},{6,5},{7,4},{8,11},{9,10},{10,... | collective-permute-start | bytes 1572872 | tf_op jit(solution)/shard_map/amplitudes_from_partner_3/ppermute | solution.py:222
  32.4 3.5 %collective-permute-done.1 = bf16[256,1024]{1,0:T(8,128)(2,1)S(1)} collective-permute-done((bf16[256,1024]{1,0:T(8,128)(2,1)}, bf16[256,1024]{1,0:T(8,128)(2,1)S(1)}, u32[]{:S(2)}, u32[]{:S(2)}) %collective-permute-start.1) | collective-permute-done | bytes 524320 | tf_op jit(solution)/shard_map/amplitudes_from_partner_1/ppermute | solution.py:222
  35.9 2.9 %collective-permute-done.13.refs_5_ = bf16[2,784,128]{2,1,0:T(8,128)(2,1)S(1)} collective-permute-done((bf16[2,784,128]{2,1,0:T(8,128)(2,1)S(1)}, bf16[2,784,128]{2,1,0:T(8,128)(2,1)S(1)}, u32[]{:S(2)}, u32[]{:S(2)}) %collective-permute-start.13) | collective-permute-done | bytes 401440 | tf_op jit(solution)/shard_map/late_hop_1/ppermute | solution.py:235
  38.8 3.4 %collective-permute-start.14 = (bf16[2,784,128]{2,1,0:T(8,128)(2,1)S(1)}, bf16[2,784,128]{2,1,0:T(8,128)(2,1)S(1)}, u32[]{:S(2)}, u32[]{:S(2)}) collective-permute-start(bf16[2,784,128]{2,1,0:T(8,128)(2,1)S(1)} %collective-permute-done.13.refs_5_), channel_id=1, source_target_pairs={{0,16},{4,20},{16,24},{20,28},{24,8},{28,12},{8,0},{12,4},{1,17},{... | collective-permute-start | bytes 1204232 | tf_op jit(solution)/shard_map/late_hop_2/ppermute | solution.py:235
  42.2 6.2 %collective-permute-done.7 = bf16[256,1024]{1,0:T(8,128)(2,1)S(1)} collective-permute-done((bf16[256,1024]{1,0:T(8,128)(2,1)}, bf16[256,1024]{1,0:T(8,128)(2,1)S(1)}, u32[]{:S(2)}, u32[]{:S(2)}) %collective-permute-start.7) | collective-permute-done | bytes 524320 | tf_op jit(solution)/shard_map/amplitudes_from_partner_2/ppermute | solution.py:222
  48.9 1.1 %maximum_bitcast_fusion = bf16[1,512,1024]{2,1,0:T(8,128)(2,1)S(1)} fusion(bf16[256,1024]{1,0:T(8,128)(2,1)S(1)} %collective-permute-done, bf16[256,1024]{1,0:T(8,128)(2,1)} %get-tuple-element.18), kind=kLoop, calls=%fused_computation.1 | loop fusion | flops 2097152 | bytes 2097152 | tf_op jit(solution)/shard_map/stack | solution.py:263
  50.0 1.6 %collective-permute-start.15 = (bf16[2,784,128]{2,1,0:T(8,128)(2,1)S(1)}, bf16[2,784,128]{2,1,0:T(8,128)(2,1)S(1)}, u32[]{:S(2)}, u32[]{:S(2)}) collective-permute-start(bf16[2,784,128]{2,1,0:T(8,128)(2,1)S(1)} %collective-permute-done.5.refs_4_), channel_id=1, source_target_pairs={{0,16},{4,20},{16,24},{20,28},{24,8},{28,12},{8,0},{12,4},{1,17},{... | collective-permute-start | bytes 1204232 | tf_op jit(solution)/shard_map/first_hop_3/ppermute | solution.py:235
  53.4 5.9 %ladder_first.1 = (f32[9,512,128]{2,1,0:T(8,128)S(1)}, f32[256,128]{1,0:T(8,128)S(1)}) custom-call(f32[2,128]{1,0:T(2,128)S(1)} %bitcast.12, bf16[4,512,1024]{2,1,0:T(8,128)(2,1)S(1)} %pad_maximum_fusion.amps.refs_0_, bf16[1,784,128]{2,1,0:T(8,128)(2,1)S(1)} %copy-done.2, bf16[1,784,128]{2,1,0:T(8,128)(2,1)S(1)} %collective-permute-done.3.refs_1_, ...), custom_call_target="tpu_custom_call" | custom-call | flops 100000000 | bytes 1048576 | tf_op jit(solution)/shard_map/ladder_first/pallas_call | solution.py:271
  59.3 3.0 %collective-permute-done.15.refs_1_ = bf16[2,784,128]{2,1,0:T(8,128)(2,1)S(1)} collective-permute-done((bf16[2,784,128]{2,1,0:T(8,128)(2,1)S(1)}, bf16[2,784,128]{2,1,0:T(8,128)(2,1)S(1)}, u32[]{:S(2)}, u32[]{:S(2)}) %collective-permute-start.15) | collective-permute-done | bytes 401440 | tf_op jit(solution)/shard_map/first_hop_3/ppermute | solution.py:235
  62.2 3.0 %ladder_second.1 = (f32[8,256,128]{2,1,0:T(8,128)S(1)}, bf16[8,256,128]{2,1,0:T(8,128)(2,1)S(1)}) custom-call(f32[9,512,128]{2,1,0:T(8,128)S(1)} %get-tuple-element.27.before, bf16[4,512,1024]{2,1,0:T(8,128)(2,1)S(1)} %pad_maximum_fusion.amps.refs_0_, bf16[2,784,128]{2,1,0:T(8,128)(2,1)S(1)} %collective-permute-done.14.refs_0_, ...), custom_call_target="tpu_custom_call" | custom-call | flops 1000000000 | bytes 1048576 | tf_op jit(solution)/shard_map/ladder_second/pallas_call | solution.py:271
  65.3 4.5 %collective-permute-done.17.refs_1_ = bf16[2,784,128]{2,1,0:T(8,128)(2,1)S(1)} collective-permute-done((bf16[2,784,128]{2,1,0:T(8,128)(2,1)S(1)}, bf16[2,784,128]{2,1,0:T(8,128)(2,1)S(1)}, u32[]{:S(2)}, u32[]{:S(2)}) %collective-permute-start.17) | collective-permute-done | bytes 401440 | tf_op jit(solution)/shard_map/late_hop_3/ppermute | solution.py:235
  69.9 1.7 %collective-permute-done.18.refs_2_ = bf16[2,784,128]{2,1,0:T(8,128)(2,1)S(1)} collective-permute-done((bf16[2,784,128]{2,1,0:T(8,128)(2,1)S(1)}, bf16[2,784,128]{2,1,0:T(8,128)(2,1)S(1)}, u32[]{:S(2)}, u32[]{:S(2)}) %collective-permute-start.18) | collective-permute-done | bytes 401440 | tf_op jit(solution)/shard_map/ppermute | solution.py:225
  71.6 4.0 %update.1 = (bf16[256,1024]{1,0:T(8,128)(2,1)}, f32[256,1024]{1,0:T(8,128)}) custom-call(s32[2,8]{1,0:T(2,128)S(1)} %copy-done.4, bf16[256,1024]{1,0:T(8,128)(2,1)S(1)} %copy-done, bf16[256,1024]{1,0:T(8,128)(2,1)S(1)} %copy-done.1, f32[8,256,128]{2,1,0:T(8,128)S(1)} %get-tuple-element.28.own, bf16[8,256,128]{2,1,0:T(8,128)(2,1)S(1)} %collective-permute-done.16.twin, ...), custom_call_target="tpu_custom_call" | custom-call | tf_op jit(solution)/shard_map/update/pallas_call | solution.py:331
  (38 shorter events, 5.1 us)
Async XLA Ops:
  3.4 14.6 %collective-permute-start = (bf16[256,1024]{1,0:T(8,128)(2,1)}, bf16[256,1024]{1,0:T(8,128)(2,1)S(1)}, u32[]{:S(2)}, u32[]{:S(2)}) collective-permute-start(bf16[256,1024]{1,0:T(8,128)(2,1)} %get-tuple-element.18), channel_id=1, source_target_pairs={{0,4},{4,0},{8,12},{12,8},{16,20},{20,16},{24,28},{28,24},{1,5},{5... | collective-permute-start | bytes 1572872 | tf_op jit(solution)/shard_map/twin_amplitudes_0/ppermute | solution.py:225
  3.9 8.4 %collective-permute-start.3 = (bf16[1,784,128]{2,1,0:T(8,128)(2,1)}, bf16[1,784,128]{2,1,0:T(8,128)(2,1)S(1)}, u32[]{:S(2)}, u32[]{:S(2)}) collective-permute-start(bf16[1,784,128]{2,1,0:T(8,128)(2,1)} %get-tuple-element.20), channel_id=1, source_target_pairs={{0,1},{1,0},{2,3},{3,2},{4,5},{5,4},{6,7},{7,6},{8,9},{9,8},{10,11... | collective-permute-start | bytes 602120 | tf_op jit(solution)/shard_map/parcels_from_partner_1/ppermute | solution.py:222
  6.3 12.2 %collective-permute-start.2 = (bf16[1,784,128]{2,1,0:T(8,128)(2,1)}, bf16[1,784,128]{2,1,0:T(8,128)(2,1)S(1)}, u32[]{:S(2)}, u32[]{:S(2)}) collective-permute-start(bf16[1,784,128]{2,1,0:T(8,128)(2,1)} %get-tuple-element.19.refs_0_), channel_id=1, source_target_pairs={{0,16},{4,20},{16,24},{20,28},{24,8},{28,12},{8,0},{12,4},{1,17},{... | collective-permute-start | bytes 602120 | tf_op jit(solution)/shard_map/near_hop_1/ppermute | solution.py:235
  12.2 7.0 %collective-permute-start.4 = (bf16[1,784,128]{2,1,0:T(8,128)(2,1)S(1)}, bf16[1,784,128]{2,1,0:T(8,128)(2,1)S(1)}, u32[]{:S(2)}, u32[]{:S(2)}) collective-permute-start(bf16[1,784,128]{2,1,0:T(8,128)(2,1)S(1)} %collective-permute-done.3.refs_1_), channel_id=1, source_target_pairs={{0,16},{4,20},{16,24},{20,28},{24,8},{28,12},{8,0},{12,4},{1,17},{... | collective-permute-start | bytes 602120 | tf_op jit(solution)/shard_map/early_hop_1/ppermute | solution.py:235
  15.1 11.9 %collective-permute-start.11 = (bf16[1,784,128]{2,1,0:T(8,128)(2,1)}, bf16[1,784,128]{2,1,0:T(8,128)(2,1)S(1)}, u32[]{:S(2)}, u32[]{:S(2)}) collective-permute-start(bf16[1,784,128]{2,1,0:T(8,128)(2,1)} %get-tuple-element.24), channel_id=1, source_target_pairs={{0,2},{1,3},{2,0},{3,1},{4,6},{5,7},{6,4},{7,5},{8,10},{9,11},{10,... | collective-permute-start | bytes 602120 | tf_op jit(solution)/shard_map/parcels_from_partner_2/ppermute | solution.py:222
  16.6 10.4 %collective-permute-start.12 = (bf16[1,784,128]{2,1,0:T(8,128)(2,1)}, bf16[1,784,128]{2,1,0:T(8,128)(2,1)S(1)}, u32[]{:S(2)}, u32[]{:S(2)}) collective-permute-start(bf16[1,784,128]{2,1,0:T(8,128)(2,1)} %get-tuple-element.25), channel_id=1, source_target_pairs={{0,3},{1,2},{2,1},{3,0},{4,7},{5,6},{6,5},{7,4},{8,11},{9,10},{10,... | collective-permute-start | bytes 602120 | tf_op jit(solution)/shard_map/parcels_from_partner_3/ppermute | solution.py:222
  18.0 17.9 %collective-permute-start.1 = (bf16[256,1024]{1,0:T(8,128)(2,1)}, bf16[256,1024]{1,0:T(8,128)(2,1)S(1)}, u32[]{:S(2)}, u32[]{:S(2)}) collective-permute-start(bf16[256,1024]{1,0:T(8,128)(2,1)} %get-tuple-element.18), channel_id=1, source_target_pairs={{0,1},{1,0},{2,3},{3,2},{4,5},{5,4},{6,7},{7,6},{8,9},{9,8},{10,11... | collective-permute-start | bytes 1572872 | tf_op jit(solution)/shard_map/amplitudes_from_partner_1/ppermute | solution.py:222
  19.2 13.2 %collective-permute-start.5 = (bf16[2,784,128]{2,1,0:T(8,128)(2,1)S(1)}, bf16[2,784,128]{2,1,0:T(8,128)(2,1)S(1)}, u32[]{:S(2)}, u32[]{:S(2)}) collective-permute-start(bf16[2,784,128]{2,1,0:T(8,128)(2,1)S(1)} %constant_dynamic-update-slice_fusion.refs_3_), channel_id=1, source_target_pairs={{0,16},{4,20},{16,24},{20,28},{24,8},{28,12},{8,0},{12,4},{1,17},{... | collective-permute-start | bytes 1204232 | tf_op jit(solution)/shard_map/first_hop_2/ppermute | solution.py:235
  22.7 25.7 %collective-permute-start.7 = (bf16[256,1024]{1,0:T(8,128)(2,1)}, bf16[256,1024]{1,0:T(8,128)(2,1)S(1)}, u32[]{:S(2)}, u32[]{:S(2)}) collective-permute-start(bf16[256,1024]{1,0:T(8,128)(2,1)} %get-tuple-element.18), channel_id=1, source_target_pairs={{0,2},{1,3},{2,0},{3,1},{4,6},{5,7},{6,4},{7,5},{8,10},{9,11},{10,... | collective-permute-start | bytes 1572872 | tf_op jit(solution)/shard_map/amplitudes_from_partner_2/ppermute | solution.py:222
  27.0 11.8 %collective-permute-start.13 = (bf16[2,784,128]{2,1,0:T(8,128)(2,1)S(1)}, bf16[2,784,128]{2,1,0:T(8,128)(2,1)S(1)}, u32[]{:S(2)}, u32[]{:S(2)}) collective-permute-start(bf16[2,784,128]{2,1,0:T(8,128)(2,1)S(1)} %pad_maximum_fusion.1.refs_2_), channel_id=1, source_target_pairs={{0,16},{4,20},{16,24},{20,28},{24,8},{28,12},{8,0},{12,4},{1,17},{... | collective-permute-start | bytes 1204232 | tf_op jit(solution)/shard_map/late_hop_1/ppermute | solution.py:235
  29.1 19.3 %collective-permute-start.9 = (bf16[256,1024]{1,0:T(8,128)(2,1)}, bf16[256,1024]{1,0:T(8,128)(2,1)S(1)}, u32[]{:S(2)}, u32[]{:S(2)}) collective-permute-start(bf16[256,1024]{1,0:T(8,128)(2,1)} %get-tuple-element.18), channel_id=1, source_target_pairs={{0,3},{1,2},{2,1},{3,0},{4,7},{5,6},{6,5},{7,4},{8,11},{9,10},{10,... | collective-permute-start | bytes 1572872 | tf_op jit(solution)/shard_map/amplitudes_from_partner_3/ppermute | solution.py:222
  35.9 16.3 %collective-permute-start.6 = (bf16[256,1024]{1,0:T(8,128)(2,1)S(1)}, bf16[256,1024]{1,0:T(8,128)(2,1)S(1)}, u32[]{:S(2)}, u32[]{:S(2)}) collective-permute-start(bf16[256,1024]{1,0:T(8,128)(2,1)S(1)} %collective-permute-done.1), channel_id=1, source_target_pairs={{0,4},{4,0},{8,12},{12,8},{16,20},{20,16},{24,28},{28,24},{1,5},{5... | collective-permute-start | bytes 1572872 | tf_op jit(solution)/shard_map/twin_amplitudes_1/ppermute | solution.py:225
  38.8 12.8 %collective-permute-start.14 = (bf16[2,784,128]{2,1,0:T(8,128)(2,1)S(1)}, bf16[2,784,128]{2,1,0:T(8,128)(2,1)S(1)}, u32[]{:S(2)}, u32[]{:S(2)}) collective-permute-start(bf16[2,784,128]{2,1,0:T(8,128)(2,1)S(1)} %collective-permute-done.13.refs_5_), channel_id=1, source_target_pairs={{0,16},{4,20},{16,24},{20,28},{24,8},{28,12},{8,0},{12,4},{1,17},{... | collective-permute-start | bytes 1204232 | tf_op jit(solution)/shard_map/late_hop_2/ppermute | solution.py:235
  48.4 3.9 %collective-permute-start.8 = (bf16[256,1024]{1,0:T(8,128)(2,1)S(1)}, bf16[256,1024]{1,0:T(8,128)(2,1)S(1)}, u32[]{:S(2)}, u32[]{:S(2)}) collective-permute-start(bf16[256,1024]{1,0:T(8,128)(2,1)S(1)} %collective-permute-done.7), channel_id=1, source_target_pairs={{0,4},{4,0},{8,12},{12,8},{16,20},{20,16},{24,28},{28,24},{1,5},{5... | collective-permute-start | bytes 1572872 | tf_op jit(solution)/shard_map/twin_amplitudes_2/ppermute | solution.py:225
  48.4 4.0 %collective-permute-start.10 = (bf16[256,1024]{1,0:T(8,128)(2,1)S(1)}, bf16[256,1024]{1,0:T(8,128)(2,1)S(1)}, u32[]{:S(2)}, u32[]{:S(2)}) collective-permute-start(bf16[256,1024]{1,0:T(8,128)(2,1)S(1)} %collective-permute-done.9), channel_id=1, source_target_pairs={{0,4},{4,0},{8,12},{12,8},{16,20},{20,16},{24,28},{28,24},{1,5},{5... | collective-permute-start | bytes 1572872 | tf_op jit(solution)/shard_map/twin_amplitudes_3/ppermute | solution.py:225
  50.0 12.2 %collective-permute-start.15 = (bf16[2,784,128]{2,1,0:T(8,128)(2,1)S(1)}, bf16[2,784,128]{2,1,0:T(8,128)(2,1)S(1)}, u32[]{:S(2)}, u32[]{:S(2)}) collective-permute-start(bf16[2,784,128]{2,1,0:T(8,128)(2,1)S(1)} %collective-permute-done.5.refs_4_), channel_id=1, source_target_pairs={{0,16},{4,20},{16,24},{20,28},{24,8},{28,12},{8,0},{12,4},{1,17},{... | collective-permute-start | bytes 1204232 | tf_op jit(solution)/shard_map/first_hop_3/ppermute | solution.py:235
  51.6 18.2 %collective-permute-start.17 = (bf16[2,784,128]{2,1,0:T(8,128)(2,1)S(1)}, bf16[2,784,128]{2,1,0:T(8,128)(2,1)S(1)}, u32[]{:S(2)}, u32[]{:S(2)}) collective-permute-start(bf16[2,784,128]{2,1,0:T(8,128)(2,1)S(1)} %collective-permute-done.14.refs_0_), channel_id=1, source_target_pairs={{0,16},{4,20},{16,24},{20,28},{24,8},{28,12},{8,0},{12,4},{1,17},{... | collective-permute-start | bytes 1204232 | tf_op jit(solution)/shard_map/late_hop_3/ppermute | solution.py:235
  52.5 0.9 %copy-start.2 = (bf16[1,784,128]{2,1,0:T(8,128)(2,1)S(1)}, bf16[1,784,128]{2,1,0:T(8,128)(2,1)}, u32[]{:S(2)}) copy-start(bf16[1,784,128]{2,1,0:T(8,128)(2,1)} %get-tuple-element.19.refs_0_) | copy-start | bytes 602116
  62.2 9.4 %copy-start = (bf16[256,1024]{1,0:T(8,128)(2,1)S(1)}, bf16[256,1024]{1,0:T(8,128)(2,1)}, u32[]{:S(2)}) copy-start(bf16[256,1024]{1,0:T(8,128)(2,1)} %amplitudes.3) | copy-start | bytes 1572868
  62.2 9.4 %copy-start.1 = (bf16[256,1024]{1,0:T(8,128)(2,1)S(1)}, bf16[256,1024]{1,0:T(8,128)(2,1)}, u32[]{:S(2)}) copy-start(bf16[256,1024]{1,0:T(8,128)(2,1)} %driver.1) | copy-start | bytes 1572868
  62.2 9.4 %copy-start.3 = (f32[1024]{0:T(1024)S(1)}, f32[1024]{0:T(1024)}, u32[]{:S(2)}) copy-start(f32[1024]{0:T(1024)} %param.13) | copy-start | bytes 12292
  62.2 9.4 %copy-start.4 = (s32[2,8]{1,0:T(2,128)S(1)}, s32[2,8]{1,0:T(2,128)}, u32[]{:S(2)}) copy-start(s32[2,8]{1,0:T(2,128)} %live.3) | copy-start | bytes 196
  65.3 6.3 %collective-permute-start.16 = (bf16[8,256,128]{2,1,0:T(8,128)(2,1)S(1)}, bf16[8,256,128]{2,1,0:T(8,128)(2,1)S(1)}, u32[]{:S(2)}, u32[]{:S(2)}) collective-permute-start(bf16[8,256,128]{2,1,0:T(8,128)(2,1)S(1)} %get-tuple-element.29), channel_id=1, source_target_pairs={{0,4},{4,0},{8,12},{12,8},{16,20},{20,16},{24,28},{28,24},{1,5},{5... | collective-permute-start | bytes 1572872 | tf_op jit(solution)/shard_map/ppermute | solution.py:225
  69.9 1.7 %collective-permute-start.18 = (bf16[2,784,128]{2,1,0:T(8,128)(2,1)S(1)}, bf16[2,784,128]{2,1,0:T(8,128)(2,1)S(1)}, u32[]{:S(2)}, u32[]{:S(2)}) collective-permute-start(bf16[2,784,128]{2,1,0:T(8,128)(2,1)S(1)} %collective-permute-done.17.refs_1_), channel_id=1, source_target_pairs={{0,4},{4,0},{8,12},{12,8},{16,20},{20,16},{24,28},{28,24},{1,5},{5... | collective-permute-start | bytes 1204232 | tf_op jit(solution)/shard_map/ppermute | solution.py:225
  (1 other events, 0.9 us)

commit v6 on v5

--- a/solution.py
+++ b/solution.py
@@ -251,16 +251,29 @@
         for name in ("first", "late"):
             hops[name].append(next_on_ring(hops[name][-1], f"{name}_hop_{hop}"))
 
-    a_parts = {0: masked}
-    with jax.named_scope("twin_amplitudes_0"):
-        a_twins = {0: across_core(masked)}
-    ready = after(masked, a_twins[0])
-    for j in others:
-        a_parts[j] = across_v(ready, j)
-    for j in others:
-        with jax.named_scope(f"twin_amplitudes_{j}"):
-            a_twins[j] = across_core(after(a_parts[j], hops["first"][2]))
-    amps = jnp.stack([jnp.concatenate([a_parts[j], a_twins[j]]) for j in range(n_v)])
+    def gather_amplitudes(value, bits):
+        held, ids = value[None], [0]
+        twin_held = None
+        for bit in bits:
+            with jax.named_scope(f"amplitudes_bit_{bit}"):
+                arrived_now = lax.ppermute(held, "vpair", [(i, i ^ bit) for i in range(n_v)])
+            with jax.named_scope(f"twin_of_bit_{bit}"):
+                part = arrived_now if twin_held is not None else jnp.concatenate([held, arrived_now])
+                twin_now = across_core(after(part, hops["late"][1]))
+            twin_held = twin_now if twin_held is None else jnp.concatenate([twin_held, twin_now])
+            held, ids = jnp.concatenate([held, arrived_now]), ids + [i ^ bit for i in ids]
+        return {j: (held[i], twin_held[i]) for i, j in enumerate(ids)}
+
+    bits = [1 << i for i in range((n_v - 1).bit_length())]
+    ready = after(masked, (hops["late"][0], hops["early"][1]))
+    upper = gather_amplitudes(ready[: n_rows // 2], bits)
+    lower = gather_amplitudes(ready[n_rows // 2 :], bits[::-1])
+    amps = jnp.stack(
+        [
+            jnp.concatenate([upper[j][0], lower[j][0], upper[j][1], lower[j][1]])
+            for j in range(n_v)
+        ]
+    )
 
     sums = (rows + 1, CORES * n_rows, tile)
     pairs = (max(cap // 2, 1), 2 * tile, 2 * tile)

time: 75.8 us -> 72.1 us (0.951)
  waiting for transfers between devices: 29.6 us -> 22.8 us
  starting transfers between devices: 27.3 us -> 29.9 us
  local copies, waits for them, and re-layouts: 0.39 us -> 1.68 us
  other arithmetic: 1.93 us -> 1.03 us
    ppermute x6 -> x3, waiting for transfers between devices: 15.7 us -> 3.22 us  [across_v(): return lax.ppermute(value, 'vpair', [(i, i ^ j) for i in range(n_v)])]
    ppermute x6 -> x3, starting transfers between devices: 9.76 us -> 4.46 us  [across_v(): return lax.ppermute(value, 'vpair', [(i, i ^ j) for i in range(n_v)])]
    ppermute x0 -> x4, starting transfers between devices: none -> 4.68 us  [gather_amplitudes(): lax.ppermute(held, 'vpair', [(i, i ^ bit) for i in range(n_v)])]
    ppermute x7, waiting for transfers between devices: 12.1 us -> 16 us  [next_on_ring(): return lax.ppermute(value, 'opair', pairs)]
    ppermute x7, starting transfers between devices: 16.5 us -> 19.8 us  [next_on_ring(): return lax.ppermute(value, 'opair', pairs)]
    ppermute x6, waiting for transfers between devices: 1.74 us -> 3.55 us  [across_core(): return lax.ppermute(value, 'opair', [(i, i ^ 1) for i in range(n_o)])]
    broadcast_in_dim x0 -> x1, local copies, waits for them, and re-layouts: none -> 1.06 us  [gather_amplitudes(): held, ids = (value[None], [0])]
    another operation x5 -> x4, other arithmetic: 1.89 us -> 0.89 us  [on_device(): jnp.stack([jnp.concatenate([upper[j][0], lower[j][0], upper[j][1], lower[...]
  transfers between devices with their start and end apart: 19 -> 20, of which waited for: 10 -> 10; matrix products, arithmetic and copies ran while one was open for 3% -> 2% of each run, Pallas kernels for 12% -> 12%
where the time goes in v6:
time: 72.1 us; the launch traced here: 71.9 us
  starting transfers between devices  29.9 us (41%)
  waiting for transfers between devices  22.8 us (32%)
  Pallas kernels  15.6 us (22%)
  local copies, waits for them, and re-layouts  1.68 us (2%)
  other arithmetic  1.03 us (1%)
  between operations  0.9 us (1%)
    ppermute x7, starting transfers between devices, next_on_ring(): return lax.ppermute(value, 'opair', pairs)  19.8 us
    ppermute x7, waiting for transfers between devices, next_on_ring(): return lax.ppermute(value, 'opair', pairs)  16 us
    pallas_call x2, Pallas kernels, ladder_call(): pl.pallas_call(functools.partial(kernel, cap, layout), out_shape=out_shap...  8.88 us
    ppermute x4, starting transfers between devices, gather_amplitudes(): lax.ppermute(held, 'vpair', [(i, i ^ bit) for i in range(n_v)])  4.68 us
    ppermute x3, starting transfers between devices, across_v(): return lax.ppermute(value, 'vpair', [(i, i ^ j) for i in range(n_v)])  4.46 us
    pallas_call x1, Pallas kernels, on_device(): pl.pallas_call(functools.partial(update_kernel, cap, behind), out_shape=[...  3.98 us
    ppermute x6, waiting for transfers between devices, across_core(): return lax.ppermute(value, 'opair', [(i, i ^ 1) for i in range(n_o)])  3.55 us
    ppermute x3, waiting for transfers between devices, across_v(): return lax.ppermute(value, 'vpair', [(i, i ^ j) for i in range(n_v)])  3.22 us
  transfers between devices with their start and end apart: 20, of which 10 were waited for; matrix products, arithmetic and copies ran while one was open for 2% of the time, Pallas kernels for 12%

profile of v6, /device:TPU:0, one launch (start us, length us, event | category | flops | bytes accessed | tf_op | source)
XLA Modules:
  0.0 71.9 jit_solution(14684391793631710752)
XLA Ops:
  0.6 2.8 %pack.1 = (bf16[1,784,128]{2,1,0:T(8,128)(2,1)}, bf16[1,784,128]{2,1,0:T(8,128)(2,1)}, bf16[1,784,128]{2,1,0:T(8,128)(2,1)}, bf16[1,784,128]{2,1,0:T(8,128)(2,1)}, bf16[256,1024]{1,0:T(8,128)(2,1)}) custom-call(s32[3,8]{1,0:T(4,128)} %bitcast.45, s32[2,8]{1,0:T(2,128)} %live.3, bf16[8,3,128,128]{3,2,1,0:T(8,128)(2,1)} %integrals.1, bf16[256,1024]{1,0:T(8,128)(2,1)} %amplitudes.3), custom_call_target="tpu_custom_call" | custom-call | tf_op jit(solution)/shard_map/pack/pallas_call | solution.py:208
  3.4 2.9 %collective-permute-start.3 = (bf16[1,784,128]{2,1,0:T(8,128)(2,1)}, bf16[1,784,128]{2,1,0:T(8,128)(2,1)S(1)}, u32[]{:S(2)}, u32[]{:S(2)}) collective-permute-start(bf16[1,784,128]{2,1,0:T(8,128)(2,1)} %get-tuple-element.22), channel_id=1, source_target_pairs={{0,1},{1,0},{2,3},{3,2},{4,5},{5,4},{6,7},{7,6},{8,9},{9,8},{10,11... | collective-permute-start | bytes 602120 | tf_op jit(solution)/shard_map/parcels_from_partner_1/ppermute | solution.py:222
  6.3 1.5 %collective-permute-start = (bf16[1,784,128]{2,1,0:T(8,128)(2,1)}, bf16[1,784,128]{2,1,0:T(8,128)(2,1)S(1)}, u32[]{:S(2)}, u32[]{:S(2)}) collective-permute-start(bf16[1,784,128]{2,1,0:T(8,128)(2,1)} %get-tuple-element.19), channel_id=1, source_target_pairs={{0,2},{1,3},{2,0},{3,1},{4,6},{5,7},{6,4},{7,5},{8,10},{9,11},{10,... | collective-permute-start | bytes 602120 | tf_op jit(solution)/shard_map/parcels_from_partner_2/ppermute | solution.py:222
  7.9 3.1 %collective-permute-start.2 = (bf16[1,784,128]{2,1,0:T(8,128)(2,1)}, bf16[1,784,128]{2,1,0:T(8,128)(2,1)S(1)}, u32[]{:S(2)}, u32[]{:S(2)}) collective-permute-start(bf16[1,784,128]{2,1,0:T(8,128)(2,1)} %get-tuple-element.21.refs_0_), channel_id=1, source_target_pairs={{0,16},{4,20},{16,24},{20,28},{24,8},{28,12},{8,0},{12,4},{1,17},{... | collective-permute-start | bytes 602120 | tf_op jit(solution)/shard_map/near_hop_1/ppermute | solution.py:235
  10.9 1.4 %collective-permute-done.3.refs_1_ = bf16[1,784,128]{2,1,0:T(8,128)(2,1)S(1)} collective-permute-done((bf16[1,784,128]{2,1,0:T(8,128)(2,1)}, bf16[1,784,128]{2,1,0:T(8,128)(2,1)S(1)}, u32[]{:S(2)}, u32[]{:S(2)}) %collective-permute-start.3) | collective-permute-done | bytes 200736 | tf_op jit(solution)/shard_map/parcels_from_partner_1/ppermute | solution.py:222
  12.4 3.2 %collective-permute-start.4 = (bf16[1,784,128]{2,1,0:T(8,128)(2,1)S(1)}, bf16[1,784,128]{2,1,0:T(8,128)(2,1)S(1)}, u32[]{:S(2)}, u32[]{:S(2)}) collective-permute-start(bf16[1,784,128]{2,1,0:T(8,128)(2,1)S(1)} %collective-permute-done.3.refs_1_), channel_id=1, source_target_pairs={{0,16},{4,20},{16,24},{20,28},{24,8},{28,12},{8,0},{12,4},{1,17},{... | collective-permute-start | bytes 602120 | tf_op jit(solution)/shard_map/early_hop_1/ppermute | solution.py:235
  15.5 1.8 %collective-permute-done = bf16[1,784,128]{2,1,0:T(8,128)(2,1)S(1)} collective-permute-done((bf16[1,784,128]{2,1,0:T(8,128)(2,1)}, bf16[1,784,128]{2,1,0:T(8,128)(2,1)S(1)}, u32[]{:S(2)}, u32[]{:S(2)}) %collective-permute-start) | collective-permute-done | bytes 200736 | tf_op jit(solution)/shard_map/parcels_from_partner_2/ppermute | solution.py:222
  17.4 1.5 %collective-permute-done.4 = bf16[1,784,128]{2,1,0:T(8,128)(2,1)S(1)} collective-permute-done((bf16[1,784,128]{2,1,0:T(8,128)(2,1)S(1)}, bf16[1,784,128]{2,1,0:T(8,128)(2,1)S(1)}, u32[]{:S(2)}, u32[]{:S(2)}) %collective-permute-start.4) | collective-permute-done | bytes 200736 | tf_op jit(solution)/shard_map/early_hop_1/ppermute | solution.py:235
  19.9 1.6 %collective-permute-start.8 = (bf16[1,128,1024]{2,1,0:T(8,128)(2,1)S(1)}, bf16[1,128,1024]{2,1,0:T(8,128)(2,1)S(1)}, u32[]{:S(2)}, u32[]{:S(2)}) collective-permute-start(bf16[1,128,1024]{2,1,0:T(8,128)(2,1)S(1)} %get-tuple-element.47), channel_id=1, source_target_pairs={{0,2},{1,3},{2,0},{3,1},{4,6},{5,7},{6,4},{7,5},{8,10},{9,11},{10,... | collective-permute-start | bytes 786440 | tf_op jit(solution)/shard_map/amplitudes_bit_2/ppermute | solution.py:259
  21.5 3.4 %collective-permute-start.6 = (bf16[2,784,128]{2,1,0:T(8,128)(2,1)S(1)}, bf16[2,784,128]{2,1,0:T(8,128)(2,1)S(1)}, u32[]{:S(2)}, u32[]{:S(2)}) collective-permute-start(bf16[2,784,128]{2,1,0:T(8,128)(2,1)S(1)} %pad_maximum_fusion.3.refs_2_), channel_id=1, source_target_pairs={{0,16},{4,20},{16,24},{20,28},{24,8},{28,12},{8,0},{12,4},{1,17},{... | collective-permute-start | bytes 1204232 | tf_op jit(solution)/shard_map/late_hop_1/ppermute | solution.py:235
  24.9 1.5 %collective-permute-start.5 = (bf16[1,128,1024]{2,1,0:T(8,128)(2,1)S(1)}, bf16[1,128,1024]{2,1,0:T(8,128)(2,1)S(1)}, u32[]{:S(2)}, u32[]{:S(2)}) collective-permute-start(bf16[1,128,1024]{2,1,0:T(8,128)(2,1)S(1)} %get-tuple-element.46), channel_id=1, source_target_pairs={{0,1},{1,0},{2,3},{3,2},{4,5},{5,4},{6,7},{7,6},{8,9},{9,8},{10,11... | collective-permute-start | bytes 786440 | tf_op jit(solution)/shard_map/amplitudes_bit_1/ppermute | solution.py:259
  26.4 1.5 %collective-permute-start.10 = (bf16[2,128,1024]{2,1,0:T(8,128)(2,1)S(1)}, bf16[2,128,1024]{2,1,0:T(8,128)(2,1)S(1)}, u32[]{:S(2)}, u32[]{:S(2)}) collective-permute-start(bf16[2,128,1024]{2,1,0:T(8,128)(2,1)S(1)} %pad_maximum_fusion.2), channel_id=1, source_target_pairs={{0,1},{1,0},{2,3},{3,2},{4,5},{5,4},{6,7},{7,6},{8,9},{9,8},{10,11... | collective-permute-start | bytes 1572872 | tf_op jit(solution)/shard_map/amplitudes_bit_1/ppermute | solution.py:259
  28.0 3.4 %collective-permute-start.14 = (bf16[2,784,128]{2,1,0:T(8,128)(2,1)S(1)}, bf16[2,784,128]{2,1,0:T(8,128)(2,1)S(1)}, u32[]{:S(2)}, u32[]{:S(2)}) collective-permute-start(bf16[2,784,128]{2,1,0:T(8,128)(2,1)S(1)} %constant_dynamic-update-slice_fusion.refs_3_), channel_id=1, source_target_pairs={{0,16},{4,20},{16,24},{20,28},{24,8},{28,12},{8,0},{12,4},{1,17},{... | collective-permute-start | bytes 1204232 | tf_op jit(solution)/shard_map/first_hop_2/ppermute | solution.py:235
  31.5 3.0 %collective-permute-done.6.refs_5_ = bf16[2,784,128]{2,1,0:T(8,128)(2,1)S(1)} collective-permute-done((bf16[2,784,128]{2,1,0:T(8,128)(2,1)S(1)}, bf16[2,784,128]{2,1,0:T(8,128)(2,1)S(1)}, u32[]{:S(2)}, u32[]{:S(2)}) %collective-permute-start.6) | collective-permute-done | bytes 401440 | tf_op jit(solution)/shard_map/late_hop_1/ppermute | solution.py:235
  34.4 3.4 %collective-permute-start.15 = (bf16[2,784,128]{2,1,0:T(8,128)(2,1)S(1)}, bf16[2,784,128]{2,1,0:T(8,128)(2,1)S(1)}, u32[]{:S(2)}, u32[]{:S(2)}) collective-permute-start(bf16[2,784,128]{2,1,0:T(8,128)(2,1)S(1)} %collective-permute-done.6.refs_5_), channel_id=1, source_target_pairs={{0,16},{4,20},{16,24},{20,28},{24,8},{28,12},{8,0},{12,4},{1,17},{... | collective-permute-start | bytes 1204232 | tf_op jit(solution)/shard_map/late_hop_2/ppermute | solution.py:235
  38.0 5.0 %collective-permute-done.14.refs_4_ = bf16[2,784,128]{2,1,0:T(8,128)(2,1)S(1)} collective-permute-done((bf16[2,784,128]{2,1,0:T(8,128)(2,1)S(1)}, bf16[2,784,128]{2,1,0:T(8,128)(2,1)S(1)}, u32[]{:S(2)}, u32[]{:S(2)}) %collective-permute-start.14) | collective-permute-done | bytes 401440 | tf_op jit(solution)/shard_map/first_hop_2/ppermute | solution.py:235
  43.0 5.5 %collective-permute-done.15.refs_0_ = bf16[2,784,128]{2,1,0:T(8,128)(2,1)S(1)} collective-permute-done((bf16[2,784,128]{2,1,0:T(8,128)(2,1)S(1)}, bf16[2,784,128]{2,1,0:T(8,128)(2,1)S(1)}, u32[]{:S(2)}, u32[]{:S(2)}) %collective-permute-start.15) | collective-permute-done | bytes 401440 | tf_op jit(solution)/shard_map/late_hop_2/ppermute | solution.py:235
  48.5 3.4 %collective-permute-start.16 = (bf16[2,784,128]{2,1,0:T(8,128)(2,1)S(1)}, bf16[2,784,128]{2,1,0:T(8,128)(2,1)S(1)}, u32[]{:S(2)}, u32[]{:S(2)}) collective-permute-start(bf16[2,784,128]{2,1,0:T(8,128)(2,1)S(1)} %collective-permute-done.14.refs_4_), channel_id=1, source_target_pairs={{0,16},{4,20},{16,24},{20,28},{24,8},{28,12},{8,0},{12,4},{1,17},{... | collective-permute-start | bytes 1204232 | tf_op jit(solution)/shard_map/first_hop_3/ppermute | solution.py:235
  52.8 1.2 %collective-permute-done.11 = bf16[2,128,1024]{2,1,0:T(8,128)(2,1)S(1)} collective-permute-done((bf16[2,128,1024]{2,1,0:T(8,128)(2,1)S(1)}, bf16[2,128,1024]{2,1,0:T(8,128)(2,1)S(1)}, u32[]{:S(2)}, u32[]{:S(2)}) %collective-permute-start.11) | collective-permute-done | bytes 524320 | tf_op jit(solution)/shard_map/twin_of_bit_1/ppermute | solution.py:225
  55.9 5.9 %ladder_first.1 = (f32[9,512,128]{2,1,0:T(8,128)S(1)}, f32[256,128]{1,0:T(8,128)S(1)}) custom-call(f32[2,128]{1,0:T(2,128)S(1)} %bitcast.42, bf16[4,512,1024]{2,1,0:T(8,128)(2,1)S(1)} %pad_maximum_fusion.amps.refs_0_, bf16[1,784,128]{2,1,0:T(8,128)(2,1)S(1)} %copy-done.2, bf16[1,784,128]{2,1,0:T(8,128)(2,1)S(1)} %collective-permute-done.3.refs_1_, ...), custom_call_target="tpu_custom_call" | custom-call | flops 100000000 | bytes 1048576 | tf_op jit(solution)/shard_map/ladder_first/pallas_call | solution.py:284
  61.9 3.0 %ladder_second.1 = (f32[8,256,128]{2,1,0:T(8,128)S(1)}, bf16[8,256,128]{2,1,0:T(8,128)(2,1)S(1)}) custom-call(f32[9,512,128]{2,1,0:T(8,128)S(1)} %get-tuple-element.29.before, bf16[4,512,1024]{2,1,0:T(8,128)(2,1)S(1)} %pad_maximum_fusion.amps.refs_0_, bf16[2,784,128]{2,1,0:T(8,128)(2,1)S(1)} %collective-permute-done.15.refs_0_, ...), custom_call_target="tpu_custom_call" | custom-call | flops 1000000000 | bytes 1048576 | tf_op jit(solution)/shard_map/ladder_second/pallas_call | solution.py:284
  65.1 1.1 %collective-permute-done.18.refs_1_ = bf16[2,784,128]{2,1,0:T(8,128)(2,1)S(1)} collective-permute-done((bf16[2,784,128]{2,1,0:T(8,128)(2,1)S(1)}, bf16[2,784,128]{2,1,0:T(8,128)(2,1)S(1)}, u32[]{:S(2)}, u32[]{:S(2)}) %collective-permute-start.18) | collective-permute-done | bytes 401440 | tf_op jit(solution)/shard_map/late_hop_3/ppermute | solution.py:235
  66.2 1.7 %collective-permute-done.19.refs_2_ = bf16[2,784,128]{2,1,0:T(8,128)(2,1)S(1)} collective-permute-done((bf16[2,784,128]{2,1,0:T(8,128)(2,1)S(1)}, bf16[2,784,128]{2,1,0:T(8,128)(2,1)S(1)}, u32[]{:S(2)}, u32[]{:S(2)}) %collective-permute-start.19) | collective-permute-done | bytes 401440 | tf_op jit(solution)/shard_map/ppermute | solution.py:225
  68.0 4.0 %update.1 = (bf16[256,1024]{1,0:T(8,128)(2,1)}, f32[256,1024]{1,0:T(8,128)}) custom-call(s32[2,8]{1,0:T(2,128)S(1)} %copy-done.4, bf16[256,1024]{1,0:T(8,128)(2,1)S(1)} %copy-done, bf16[256,1024]{1,0:T(8,128)(2,1)S(1)} %copy-done.1, f32[8,256,128]{2,1,0:T(8,128)S(1)} %get-tuple-element.30.own, bf16[8,256,128]{2,1,0:T(8,128)(2,1)S(1)} %collective-permute-done.17.twin, ...), custom_call_target="tpu_custom_call" | custom-call | tf_op jit(solution)/shard_map/update/pallas_call | solution.py:344
  (50 shorter events, 4.4 us)
Async XLA Ops:
  3.4 9.0 %collective-permute-start.3 = (bf16[1,784,128]{2,1,0:T(8,128)(2,1)}, bf16[1,784,128]{2,1,0:T(8,128)(2,1)S(1)}, u32[]{:S(2)}, u32[]{:S(2)}) collective-permute-start(bf16[1,784,128]{2,1,0:T(8,128)(2,1)} %get-tuple-element.22), channel_id=1, source_target_pairs={{0,1},{1,0},{2,3},{3,2},{4,5},{5,4},{6,7},{7,6},{8,9},{9,8},{10,11... | collective-permute-start | bytes 602120 | tf_op jit(solution)/shard_map/parcels_from_partner_1/ppermute | solution.py:222
  6.3 11.0 %collective-permute-start = (bf16[1,784,128]{2,1,0:T(8,128)(2,1)}, bf16[1,784,128]{2,1,0:T(8,128)(2,1)S(1)}, u32[]{:S(2)}, u32[]{:S(2)}) collective-permute-start(bf16[1,784,128]{2,1,0:T(8,128)(2,1)} %get-tuple-element.19), channel_id=1, source_target_pairs={{0,2},{1,3},{2,0},{3,1},{4,6},{5,7},{6,4},{7,5},{8,10},{9,11},{10,... | collective-permute-start | bytes 602120 | tf_op jit(solution)/shard_map/parcels_from_partner_2/ppermute | solution.py:222
  7.9 9.4 %collective-permute-start.1 = (bf16[1,784,128]{2,1,0:T(8,128)(2,1)}, bf16[1,784,128]{2,1,0:T(8,128)(2,1)S(1)}, u32[]{:S(2)}, u32[]{:S(2)}) collective-permute-start(bf16[1,784,128]{2,1,0:T(8,128)(2,1)} %get-tuple-element.20), channel_id=1, source_target_pairs={{0,3},{1,2},{2,1},{3,0},{4,7},{5,6},{6,5},{7,4},{8,11},{9,10},{10,... | collective-permute-start | bytes 602120 | tf_op jit(solution)/shard_map/parcels_from_partner_3/ppermute | solution.py:222
  7.9 9.5 %collective-permute-start.2 = (bf16[1,784,128]{2,1,0:T(8,128)(2,1)}, bf16[1,784,128]{2,1,0:T(8,128)(2,1)S(1)}, u32[]{:S(2)}, u32[]{:S(2)}) collective-permute-start(bf16[1,784,128]{2,1,0:T(8,128)(2,1)} %get-tuple-element.21.refs_0_), channel_id=1, source_target_pairs={{0,16},{4,20},{16,24},{20,28},{24,8},{28,12},{8,0},{12,4},{1,17},{... | collective-permute-start | bytes 602120 | tf_op jit(solution)/shard_map/near_hop_1/ppermute | solution.py:235
  12.4 6.5 %collective-permute-start.4 = (bf16[1,784,128]{2,1,0:T(8,128)(2,1)S(1)}, bf16[1,784,128]{2,1,0:T(8,128)(2,1)S(1)}, u32[]{:S(2)}, u32[]{:S(2)}) collective-permute-start(bf16[1,784,128]{2,1,0:T(8,128)(2,1)S(1)} %collective-permute-done.3.refs_1_), channel_id=1, source_target_pairs={{0,16},{4,20},{16,24},{20,28},{24,8},{28,12},{8,0},{12,4},{1,17},{... | collective-permute-start | bytes 602120 | tf_op jit(solution)/shard_map/early_hop_1/ppermute | solution.py:235
  19.9 6.5 %collective-permute-start.8 = (bf16[1,128,1024]{2,1,0:T(8,128)(2,1)S(1)}, bf16[1,128,1024]{2,1,0:T(8,128)(2,1)S(1)}, u32[]{:S(2)}, u32[]{:S(2)}) collective-permute-start(bf16[1,128,1024]{2,1,0:T(8,128)(2,1)S(1)} %get-tuple-element.47), channel_id=1, source_target_pairs={{0,2},{1,3},{2,0},{3,1},{4,6},{5,7},{6,4},{7,5},{8,10},{9,11},{10,... | collective-permute-start | bytes 786440 | tf_op jit(solution)/shard_map/amplitudes_bit_2/ppermute | solution.py:259
  21.5 12.9 %collective-permute-start.6 = (bf16[2,784,128]{2,1,0:T(8,128)(2,1)S(1)}, bf16[2,784,128]{2,1,0:T(8,128)(2,1)S(1)}, u32[]{:S(2)}, u32[]{:S(2)}) collective-permute-start(bf16[2,784,128]{2,1,0:T(8,128)(2,1)S(1)} %pad_maximum_fusion.3.refs_2_), channel_id=1, source_target_pairs={{0,16},{4,20},{16,24},{20,28},{24,8},{28,12},{8,0},{12,4},{1,17},{... | collective-permute-start | bytes 1204232 | tf_op jit(solution)/shard_map/late_hop_1/ppermute | solution.py:235
  24.9 12.9 %collective-permute-start.5 = (bf16[1,128,1024]{2,1,0:T(8,128)(2,1)S(1)}, bf16[1,128,1024]{2,1,0:T(8,128)(2,1)S(1)}, u32[]{:S(2)}, u32[]{:S(2)}) collective-permute-start(bf16[1,128,1024]{2,1,0:T(8,128)(2,1)S(1)} %get-tuple-element.46), channel_id=1, source_target_pairs={{0,1},{1,0},{2,3},{3,2},{4,5},{5,4},{6,7},{7,6},{8,9},{9,8},{10,11... | collective-permute-start | bytes 786440 | tf_op jit(solution)/shard_map/amplitudes_bit_1/ppermute | solution.py:259
  26.4 25.5 %collective-permute-start.10 = (bf16[2,128,1024]{2,1,0:T(8,128)(2,1)S(1)}, bf16[2,128,1024]{2,1,0:T(8,128)(2,1)S(1)}, u32[]{:S(2)}, u32[]{:S(2)}) collective-permute-start(bf16[2,128,1024]{2,1,0:T(8,128)(2,1)S(1)} %pad_maximum_fusion.2), channel_id=1, source_target_pairs={{0,1},{1,0},{2,3},{3,2},{4,5},{5,4},{6,7},{7,6},{8,9},{9,8},{10,11... | collective-permute-start | bytes 1572872 | tf_op jit(solution)/shard_map/amplitudes_bit_1/ppermute | solution.py:259
  28.0 15.0 %collective-permute-start.14 = (bf16[2,784,128]{2,1,0:T(8,128)(2,1)S(1)}, bf16[2,784,128]{2,1,0:T(8,128)(2,1)S(1)}, u32[]{:S(2)}, u32[]{:S(2)}) collective-permute-start(bf16[2,784,128]{2,1,0:T(8,128)(2,1)S(1)} %constant_dynamic-update-slice_fusion.refs_3_), channel_id=1, source_target_pairs={{0,16},{4,20},{16,24},{20,28},{24,8},{28,12},{8,0},{12,4},{1,17},{... | collective-permute-start | bytes 1204232 | tf_op jit(solution)/shard_map/first_hop_2/ppermute | solution.py:235
  34.4 14.1 %collective-permute-start.15 = (bf16[2,784,128]{2,1,0:T(8,128)(2,1)S(1)}, bf16[2,784,128]{2,1,0:T(8,128)(2,1)S(1)}, u32[]{:S(2)}, u32[]{:S(2)}) collective-permute-start(bf16[2,784,128]{2,1,0:T(8,128)(2,1)S(1)} %collective-permute-done.6.refs_5_), channel_id=1, source_target_pairs={{0,16},{4,20},{16,24},{20,28},{24,8},{28,12},{8,0},{12,4},{1,17},{... | collective-permute-start | bytes 1204232 | tf_op jit(solution)/shard_map/late_hop_2/ppermute | solution.py:235
  37.9 14.1 %collective-permute-start.12 = (bf16[2,128,1024]{2,1,0:T(8,128)(2,1)S(1)}, bf16[2,128,1024]{2,1,0:T(8,128)(2,1)S(1)}, u32[]{:S(2)}, u32[]{:S(2)}) collective-permute-start(bf16[2,128,1024]{2,1,0:T(8,128)(2,1)S(1)} %pad_maximum_fusion.1), channel_id=1, source_target_pairs={{0,2},{1,3},{2,0},{3,1},{4,6},{5,7},{6,4},{7,5},{8,10},{9,11},{10,... | collective-permute-start | bytes 1572872 | tf_op jit(solution)/shard_map/amplitudes_bit_2/ppermute | solution.py:259
  37.9 14.2 %collective-permute-start.7 = (bf16[2,128,1024]{2,1,0:T(8,128)(2,1)S(1)}, bf16[2,128,1024]{2,1,0:T(8,128)(2,1)S(1)}, u32[]{:S(2)}, u32[]{:S(2)}) collective-permute-start(bf16[2,128,1024]{2,1,0:T(8,128)(2,1)S(1)} %pad_maximum_fusion.1), channel_id=1, source_target_pairs={{0,4},{4,0},{8,12},{12,8},{16,20},{20,16},{24,28},{28,24},{1,5},{5... | collective-permute-start | bytes 1572872 | tf_op jit(solution)/shard_map/twin_of_bit_1/ppermute | solution.py:225
  43.0 9.7 %collective-permute-start.9 = (bf16[2,128,1024]{2,1,0:T(8,128)(2,1)S(1)}, bf16[2,128,1024]{2,1,0:T(8,128)(2,1)S(1)}, u32[]{:S(2)}, u32[]{:S(2)}) collective-permute-start(bf16[2,128,1024]{2,1,0:T(8,128)(2,1)S(1)} %pad_maximum_fusion.2), channel_id=1, source_target_pairs={{0,4},{4,0},{8,12},{12,8},{16,20},{20,16},{24,28},{28,24},{1,5},{5... | collective-permute-start | bytes 1572872 | tf_op jit(solution)/shard_map/twin_of_bit_2/ppermute | solution.py:225
  48.5 13.3 %collective-permute-start.16 = (bf16[2,784,128]{2,1,0:T(8,128)(2,1)S(1)}, bf16[2,784,128]{2,1,0:T(8,128)(2,1)S(1)}, u32[]{:S(2)}, u32[]{:S(2)}) collective-permute-start(bf16[2,784,128]{2,1,0:T(8,128)(2,1)S(1)} %collective-permute-done.14.refs_4_), channel_id=1, source_target_pairs={{0,16},{4,20},{16,24},{20,28},{24,8},{28,12},{8,0},{12,4},{1,17},{... | collective-permute-start | bytes 1204232 | tf_op jit(solution)/shard_map/first_hop_3/ppermute | solution.py:235
  51.9 14.3 %collective-permute-start.18 = (bf16[2,784,128]{2,1,0:T(8,128)(2,1)S(1)}, bf16[2,784,128]{2,1,0:T(8,128)(2,1)S(1)}, u32[]{:S(2)}, u32[]{:S(2)}) collective-permute-start(bf16[2,784,128]{2,1,0:T(8,128)(2,1)S(1)} %collective-permute-done.15.refs_0_), channel_id=1, source_target_pairs={{0,16},{4,20},{16,24},{20,28},{24,8},{28,12},{8,0},{12,4},{1,17},{... | collective-permute-start | bytes 1204232 | tf_op jit(solution)/shard_map/late_hop_3/ppermute | solution.py:235
  52.0 2.0 %collective-permute-start.11 = (bf16[2,128,1024]{2,1,0:T(8,128)(2,1)S(1)}, bf16[2,128,1024]{2,1,0:T(8,128)(2,1)S(1)}, u32[]{:S(2)}, u32[]{:S(2)}) collective-permute-start(bf16[2,128,1024]{2,1,0:T(8,128)(2,1)S(1)} %collective-permute-done.10), channel_id=1, source_target_pairs={{0,4},{4,0},{8,12},{12,8},{16,20},{20,16},{24,28},{28,24},{1,5},{5... | collective-permute-start | bytes 1572872 | tf_op jit(solution)/shard_map/twin_of_bit_1/ppermute | solution.py:225
  52.1 2.6 %collective-permute-start.13 = (bf16[2,128,1024]{2,1,0:T(8,128)(2,1)S(1)}, bf16[2,128,1024]{2,1,0:T(8,128)(2,1)S(1)}, u32[]{:S(2)}, u32[]{:S(2)}) collective-permute-start(bf16[2,128,1024]{2,1,0:T(8,128)(2,1)S(1)} %collective-permute-done.12), channel_id=1, source_target_pairs={{0,4},{4,0},{8,12},{12,8},{16,20},{20,16},{24,28},{28,24},{1,5},{5... | collective-permute-start | bytes 1572872 | tf_op jit(solution)/shard_map/twin_of_bit_2/ppermute | solution.py:225
  61.8 6.1 %copy-start = (bf16[256,1024]{1,0:T(8,128)(2,1)S(1)}, bf16[256,1024]{1,0:T(8,128)(2,1)}, u32[]{:S(2)}) copy-start(bf16[256,1024]{1,0:T(8,128)(2,1)} %amplitudes.3) | copy-start | bytes 1572868
  61.8 6.1 %copy-start.1 = (bf16[256,1024]{1,0:T(8,128)(2,1)S(1)}, bf16[256,1024]{1,0:T(8,128)(2,1)}, u32[]{:S(2)}) copy-start(bf16[256,1024]{1,0:T(8,128)(2,1)} %driver.1) | copy-start | bytes 1572868
  61.8 6.1 %copy-start.3 = (f32[1024]{0:T(1024)S(1)}, f32[1024]{0:T(1024)}, u32[]{:S(2)}) copy-start(f32[1024]{0:T(1024)} %param.13) | copy-start | bytes 12292
  61.9 6.1 %copy-start.4 = (s32[2,8]{1,0:T(2,128)S(1)}, s32[2,8]{1,0:T(2,128)}, u32[]{:S(2)}) copy-start(s32[2,8]{1,0:T(2,128)} %live.3) | copy-start | bytes 196
  64.9 3.0 %collective-permute-start.17 = (bf16[8,256,128]{2,1,0:T(8,128)(2,1)S(1)}, bf16[8,256,128]{2,1,0:T(8,128)(2,1)S(1)}, u32[]{:S(2)}, u32[]{:S(2)}) collective-permute-start(bf16[8,256,128]{2,1,0:T(8,128)(2,1)S(1)} %get-tuple-element.31), channel_id=1, source_target_pairs={{0,4},{4,0},{8,12},{12,8},{16,20},{20,16},{24,28},{28,24},{1,5},{5... | collective-permute-start | bytes 1572872 | tf_op jit(solution)/shard_map/ppermute | solution.py:225
  66.2 1.7 %collective-permute-start.19 = (bf16[2,784,128]{2,1,0:T(8,128)(2,1)S(1)}, bf16[2,784,128]{2,1,0:T(8,128)(2,1)S(1)}, u32[]{:S(2)}, u32[]{:S(2)}) collective-permute-start(bf16[2,784,128]{2,1,0:T(8,128)(2,1)S(1)} %collective-permute-done.18.refs_1_), channel_id=1, source_target_pairs={{0,4},{4,0},{8,12},{12,8},{16,20},{20,16},{24,28},{28,24},{1,5},{5... | collective-permute-start | bytes 1204232 | tf_op jit(solution)/shard_map/ppermute | solution.py:225
  (3 other events, 3.8 us)

commit v7 on v6

--- a/solution.py
+++ b/solution.py
@@ -17,9 +17,20 @@
 
 
 def pack_kernel(n_v, cap, columns, live, integrals, amplitudes, *refs):
-    parcels, (masked, origin, codes) = refs[:n_v], refs[n_v:]
+    parcels, halves, refs = refs[:n_v], refs[n_v : n_v + 2], refs[n_v + 2 :]
+    origin, codes, tiles, plain, boxes, masked, in_sems, out_sems = refs
     rows, slots, tile, _ = integrals.shape
     me = lax.axis_index("vpair")
+    copies_in = [
+        pltpu.make_async_copy(integrals, tiles, in_sems.at[0]),
+        pltpu.make_async_copy(amplitudes, plain, in_sems.at[1]),
+    ]
+    copies_out = [pltpu.make_async_copy(boxes.at[j], parcels[j], out_sems.at[j]) for j in range(n_v)]
+    copies_out += [
+        pltpu.make_async_copy(masked.at[i], halves[i], out_sems.at[n_v + i]) for i in range(2)
+    ]
+    for copy in copies_in:
+        copy.start()
     counts = [jnp.int32(0)] * n_v
     for i in range(n_v * cap):
         origin[i] = 0
@@ -35,23 +46,36 @@
             at = partner * cap + place
             origin[at] = row * slots + slot
             codes[at] = row * rows + lax.rem(column, rows)
+    copies_in[0].wait()
     lane = lax.broadcasted_iota(jnp.int32, (NOTE_ROWS, tile), 1)
     for j in range(n_v):
         note = jnp.full((NOTE_ROWS, tile), -1, jnp.int32)
         for k in range(cap):
             entry = origin[j * cap + k]
-            parcels[j][0, pl.ds(k * tile, tile)] = integrals[
+            boxes[j, 0, pl.ds(k * tile, tile)] = tiles[
                 lax.div(entry, slots), lax.rem(entry, slots)
             ]
             note = jnp.where(lane == k, codes[j * cap + k], note)
-        parcels[j][0, pl.ds(cap * tile, NOTE_ROWS)] = note.astype(jnp.float32).astype(
-            integrals.dtype
-        )
+        boxes[j, 0, pl.ds(cap * tile, NOTE_ROWS)] = note.astype(jnp.float32).astype(boxes.dtype)
+        copies_out[j].start()
+    copies_in[1].wait()
+    half_rows = masked.shape[1]
     for o in range(live.shape[0]):
         for c in range(live.shape[1]):
-            at = (pl.ds(o * tile, tile), pl.ds(c * tile, tile))
+            lanes = pl.ds(c * tile, tile)
             kept = live[o, c].astype(jnp.float32)
-            masked[at] = (amplitudes[at].astype(jnp.float32) * kept).astype(masked.dtype)
+            value = (plain[pl.ds(o * tile, tile), lanes].astype(jnp.float32) * kept).astype(
+                masked.dtype
+            )
+            for first in range(o * tile, (o + 1) * tile, half_rows):
+                rows_here = min(half_rows, tile)
+                masked[first // half_rows, pl.ds(first % half_rows, rows_here), lanes] = value[
+                    first - o * tile : first - o * tile + rows_here
+                ]
+    for copy in copies_out[n_v:]:
+        copy.start()
+    for copy in copies_out:
+        copy.wait()
 
 
 def read_notes(arrays, notes_wide, notes, sem):
@@ -121,8 +145,8 @@
         unit += len(partners)
 
 
-def first_ladder_kernel(cap, layout, occupied, amps, *refs):
-    arrays, (total, occupied_out, notes_wide, notes, pairs, sem) = (
+def first_ladder_kernel(cap, layout, occupied, virtual, amps, *refs):
+    arrays, (total, occupied_out, inverse, notes_wide, notes, pairs, sem) = (
         refs[: len(layout)],
         refs[len(layout) :],
     )
@@ -130,27 +154,38 @@
     add_arrays(arrays, layout, cap, rows, amps, notes_wide, notes, pairs, total, sem)
     tile = occupied_out.shape[-1]
     for o in range(occupied.shape[0]):
-        wide = jnp.broadcast_to(occupied[pl.ds(o, 1)], (tile, tile))
-        occupied_out[pl.ds(o * tile, tile)] = wide.T
-
-
-def second_ladder_kernel(cap, layout, before, amps, *refs):
-    arrays, (own, twin, total, notes_wide, notes, pairs, sem) = (
+        here = pl.ds(o * tile, tile)
+        column = jnp.broadcast_to(occupied[pl.ds(o, 1)], (tile, tile)).T
+        occupied_out[here] = column
+        for c in range(rows):
+            lanes = pl.ds(c * tile, tile)
+            inverse[here, lanes] = 1.0 / (column - virtual[:, lanes])
+
+
+def second_ladder_kernel(
+    cap, layout, before, driver, amplitudes, occupied, virtual, amps, *refs
+):
+    arrays, (base, twin, total, notes_wide, notes, pairs, sem) = (
         refs[: len(layout)],
         refs[len(layout) :],
     )
-    rows, n_rows, _ = own.shape
+    rows, n_rows, tile = twin.shape
     add_arrays(arrays, layout, cap, rows, amps, notes_wide, notes, pairs, total, sem)
-    own[...] = before[:rows, :n_rows] + total[:rows, :n_rows]
     twin[...] = (before[:rows, n_rows:] + total[:rows, n_rows:]).astype(twin.dtype)
-
-
-def update_kernel(cap, partners, live, amplitudes, driver, own, twin, occupied, virtual, *refs):
+    for c in range(rows):
+        lanes = pl.ds(c * tile, tile)
+        own = before[c, :n_rows] + total[c, :n_rows]
+        denominator = occupied[...] - virtual[:, lanes]
+        plain = amplitudes[:, lanes].astype(jnp.float32)
+        base[:, lanes] = driver[:, lanes].astype(jnp.float32) + own + denominator * plain
+
+
+def update_kernel(cap, partners, live, amplitudes, base, inverse, twin, *refs):
     amps, *arrays = refs[: 1 + CORES]
     new, residual, new_buf, residual_buf, notes_wide, notes, pairs, total, sem, sems = refs[
         1 + CORES :
     ]
-    rows, _, tile = own.shape
+    rows, _, tile = twin.shape
     layout = [partners] * CORES
     add_arrays(arrays, layout, cap, rows, amps, notes_wide, notes, pairs, total, sem)
     copies = []
@@ -160,13 +195,10 @@
             here = pl.ds(o * tile, tile)
             at = (here, lanes)
             kept = live[o, c].astype(jnp.float32)
-            plain = amplitudes[at].astype(jnp.float32)
-            masked = (plain * kept).astype(jnp.bfloat16).astype(jnp.float32)
-            denominator = occupied[here, :] - virtual[:, lanes]
-            ladder = own[c, here] + twin[c, here].astype(jnp.float32) + total[c, here]
-            rest = (driver[at].astype(jnp.float32) + ladder + denominator * plain) * kept
+            masked = (amplitudes[at].astype(jnp.float32) * kept).astype(jnp.bfloat16)
+            rest = (base[at] + (twin[c, here].astype(jnp.float32) + total[c, here])) * kept
             residual_buf[at] = rest
-            new_buf[at] = (masked - rest / denominator).astype(new.dtype)
+            new_buf[at] = (masked.astype(jnp.float32) - rest * inverse[at]).astype(new.dtype)
         for i, (source, target) in enumerate(((new_buf, new), (residual_buf, residual))):
             copies.append(
                 pltpu.make_async_copy(source.at[:, lanes], target.at[:, lanes], sems.at[i, c])
@@ -205,13 +237,22 @@
         return pltpu.CompilerParams(vmem_limit_bytes=size + SPARE_VMEM)
 
     parcel = (1, height, tile)
-    *parcels, masked = pl.pallas_call(
+    half = (n_rows // 2, width)
+    *parcels, upper, lower = pl.pallas_call(
         functools.partial(pack_kernel, n_v, cap),
         out_shape=[jax.ShapeDtypeStruct(parcel, dtype)] * n_v
-        + [jax.ShapeDtypeStruct(amplitudes.shape, amplitudes.dtype)],
-        in_specs=[in_smem, in_smem, in_vmem, in_vmem],
-        out_specs=[in_vmem] * (n_v + 1),
-        scratch_shapes=[pltpu.SMEM((n_v * cap,), jnp.int32)] * 2,
+        + [jax.ShapeDtypeStruct(half, amplitudes.dtype)] * 2,
+        in_specs=[in_smem, in_smem, in_hbm, in_hbm],
+        out_specs=[in_hbm] * (n_v + 2),
+        scratch_shapes=[pltpu.SMEM((n_v * cap,), jnp.int32)] * 2
+        + [
+            pltpu.VMEM(integrals.shape, dtype),
+            pltpu.VMEM(amplitudes.shape, amplitudes.dtype),
+            pltpu.VMEM((n_v, *parcel), dtype),
+            pltpu.VMEM((2, *half), amplitudes.dtype),
+            pltpu.SemaphoreType.DMA((2,)),
+            pltpu.SemaphoreType.DMA((n_v + 2,)),
+        ],
         compiler_params=pltpu.CompilerParams(vmem_limit_bytes=ALL_VMEM),
         name="pack",
     )(integral_columns.T, tile_live, integrals, amplitudes)
@@ -241,8 +282,9 @@
     groups = {"near": [0], "early": others[: n_v // 2 - 1], "late": others[n_v // 2 - 1 :]}
     arrived = {0: parcels[0]} | {j: across_v(parcels[j], j) for j in others}
     hops = {name: [join([arrived[j] for j in groups[name]])] for name in groups}
-    for name in ("near", "early"):
-        hops[name].append(next_on_ring(hops[name][0], f"{name}_hop_1"))
+    hops["near"].append(next_on_ring(hops["near"][0], "near_hop_1"))
+    hops["early"][0] = after(hops["early"][0], hops["near"][1])
+    hops["early"].append(next_on_ring(hops["early"][0], "early_hop_1"))
     hops["late"][0] = after(hops["late"][0], (hops["near"][1], hops["early"][0]))
     groups["first"] = groups["near"] + groups["early"]
     hops["late"].append(next_on_ring(hops["late"][0], "late_hop_1"))
@@ -265,9 +307,8 @@
         return {j: (held[i], twin_held[i]) for i, j in enumerate(ids)}
 
     bits = [1 << i for i in range((n_v - 1).bit_length())]
-    ready = after(masked, (hops["late"][0], hops["early"][1]))
-    upper = gather_amplitudes(ready[: n_rows // 2], bits)
-    lower = gather_amplitudes(ready[n_rows // 2 :], bits[::-1])
+    upper, lower = after((upper, lower), (hops["late"][0], hops["early"][1]))
+    upper, lower = gather_amplitudes(upper, bits), gather_amplitudes(lower, bits[::-1])
     amps = jnp.stack(
         [
             jnp.concatenate([upper[j][0], lower[j][0], upper[j][1], lower[j][1]])
@@ -284,7 +325,7 @@
         return pl.pallas_call(
             functools.partial(kernel, cap, layout),
             out_shape=out_shape,
-            in_specs=[in_vmem] * (2 + len(arrays)),
+            in_specs=[in_vmem] * (len(before) + 1 + len(arrays)),
             out_specs=[in_vmem] * len(out_shape),
             scratch_shapes=extra_scratch
             + [
@@ -295,9 +336,7 @@
             ],
             compiler_params=params(
                 ((n_units, height, tile), dtype),
-                (sums, jnp.float32),
-                (sums, jnp.float32),
-                (sums, jnp.float32),
+                *[(sums, jnp.float32)] * 4,
                 (amps.shape, dtype),
             ),
             cost_estimate=pl.CostEstimate(
@@ -306,30 +345,32 @@
                 transcendentals=0,
             ),
             name=name,
-        )(before, amps, *arrays)
+        )(*before, amps, *arrays)
 
     tail = [("late", n_z - 2), ("first", n_z - 1)]
     head = [("near", 0), ("early", 0), ("late", 0)]
     head += [("first", hop) for hop in range(1, n_z - 1)]
     head += [("late", hop) for hop in range(1, n_z - 2)]
-    total, occupied = ladder_call(
+    virtual = virtual_energy.reshape(1, width)
+    total, occupied, inverse = ladder_call(
         first_ladder_kernel,
         head,
-        occupied_energy.reshape(-1, tile),
+        [occupied_energy.reshape(-1, tile), virtual],
         [
             jax.ShapeDtypeStruct(sums, jnp.float32),
             jax.ShapeDtypeStruct((n_rows, tile), jnp.float32),
+            jax.ShapeDtypeStruct((n_rows, width), jnp.float32),
         ],
         [],
         FIRST_FLOPS,
         "ladder_first",
     )
-    own, twin = ladder_call(
+    base, twin = ladder_call(
         second_ladder_kernel,
         tail,
-        total,
+        [total, driver_terms, amplitudes, occupied, virtual],
         [
-            jax.ShapeDtypeStruct((rows, n_rows, tile), jnp.float32),
+            jax.ShapeDtypeStruct((n_rows, width), jnp.float32),
             jax.ShapeDtypeStruct((rows, n_rows, tile), jnp.bfloat16),
         ],
         [pltpu.VMEM(sums, jnp.float32)],
@@ -347,7 +388,7 @@
             jax.ShapeDtypeStruct((n_rows, width), jnp.bfloat16),
             jax.ShapeDtypeStruct((n_rows, width), jnp.float32),
         ],
-        in_specs=[in_smem] + [in_vmem] * (7 + CORES),
+        in_specs=[in_smem] + [in_vmem] * (5 + CORES),
         out_specs=[in_hbm] * 2,
         scratch_shapes=[
             pltpu.VMEM((n_rows, width), jnp.bfloat16),
@@ -366,11 +407,9 @@
     )(
         tile_live,
         amplitudes,
-        driver_terms,
-        own,
+        base,
+        inverse,
         twin,
-        occupied,
-        virtual_energy.reshape(1, width),
         amps,
         last,
         across_core(last),

time: 72.1 us -> 71.6 us (level)
  starting transfers between devices: 29.9 us -> 25.8 us
  waiting for transfers between devices: 22.8 us -> 25.8 us
  local copies, waits for them, and re-layouts: 1.68 us -> 0.61 us
  other arithmetic: 1.03 us -> 1.95 us
    ppermute x7, starting transfers between devices: 19.8 us -> 16.5 us  [next_on_ring(): return lax.ppermute(value, 'opair', pairs)]
    ppermute x3, waiting for transfers between devices: 3.22 us -> 6.03 us  [across_v(): return lax.ppermute(value, 'vpair', [(i, i ^ j) for i in range(n_v)])]
    ppermute x4, waiting for transfers between devices: 0.01 us -> 1.1 us  [gather_amplitudes(): lax.ppermute(held, 'vpair', [(i, i ^ bit) for i in range(n_v)])]
    broadcast_in_dim x1 -> x0, local copies, waits for them, and re-layouts: 1.06 us -> none  [gather_amplitudes(): held, ids = (value[None], [0])]
    ppermute x7, waiting for transfers between devices: 16 us -> 15.1 us  [next_on_ring(): return lax.ppermute(value, 'opair', pairs)]
    ppermute x3, starting transfers between devices: 4.46 us -> 3.49 us  [across_v(): return lax.ppermute(value, 'vpair', [(i, i ^ j) for i in range(n_v)])]
    concatenate x2, other arithmetic: 0.1 us -> 1.05 us  [gather_amplitudes(): jnp.concatenate([held, arrived_now])]
  transfers between devices with their start and end apart: 20 -> 20, of which waited for: 10 -> 12; matrix products, arithmetic and copies ran while one was open for 2% -> 3% of each run, Pallas kernels for 12% -> 13%
where the time goes in v7:
time: 71.6 us; the launch traced here: 71.4 us
  starting transfers between devices  25.8 us (36%)
  waiting for transfers between devices  25.8 us (36%)
  Pallas kernels  16.3 us (23%)
  other arithmetic  1.95 us (3%)
  between operations  0.9 us (1%)
    ppermute x7, starting transfers between devices, next_on_ring(): return lax.ppermute(value, 'opair', pairs)  16.5 us
    ppermute x7, waiting for transfers between devices, next_on_ring(): return lax.ppermute(value, 'opair', pairs)  15.1 us
    pallas_call x2, Pallas kernels, ladder_call(): pl.pallas_call(functools.partial(kernel, cap, layout), out_shape=out_shap...  9.37 us
    ppermute x3, waiting for transfers between devices, across_v(): return lax.ppermute(value, 'vpair', [(i, i ^ j) for i in range(n_v)])  6.03 us
    ppermute x4, starting transfers between devices, gather_amplitudes(): lax.ppermute(held, 'vpair', [(i, i ^ bit) for i in range(n_v)])  4.86 us
    pallas_call x1, Pallas kernels, on_device(): pl.pallas_call(functools.partial(update_kernel, cap, behind), out_shape=[...  3.9 us
    ppermute x6, waiting for transfers between devices, across_core(): return lax.ppermute(value, 'opair', [(i, i ^ 1) for i in range(n_o)])  3.62 us
    ppermute x3, starting transfers between devices, across_v(): return lax.ppermute(value, 'vpair', [(i, i ^ j) for i in range(n_v)])  3.49 us
  transfers between devices with their start and end apart: 20, of which 12 were waited for; matrix products, arithmetic and copies ran while one was open for 3% of the time, Pallas kernels for 13%

profile of v7, /device:TPU:0, one launch (start us, length us, event | category | flops | bytes accessed | tf_op | source)
XLA Modules:
  0.0 71.4 jit_solution(4386492885149676317)
XLA Ops:
  0.6 3.0 %pack.1 = (bf16[1,784,128]{2,1,0:T(8,128)(2,1)}, bf16[1,784,128]{2,1,0:T(8,128)(2,1)}, bf16[1,784,128]{2,1,0:T(8,128)(2,1)}, bf16[1,784,128]{2,1,0:T(8,128)(2,1)...) custom-call(s32[3,8]{1,0:T(4,128)} %bitcast.48, s32[2,8]{1,0:T(2,128)} %live.3, ...), custom_call_target="tpu_custom_call" | custom-call | tf_op jit(solution)/shard_map/pack/pallas_call | solution.py:241
  3.7 4.1 %collective-permute-start.2 = (bf16[1,784,128]{2,1,0:T(8,128)(2,1)}, bf16[1,784,128]{2,1,0:T(8,128)(2,1)S(1)}, u32[]{:S(2)}, u32[]{:S(2)}) collective-permute-start(bf16[1,784,128]{2,1,0:T(8,128)(2,1)} %get-tuple-element.26.refs_0_), channel_id=1, source_target_pairs={{0,16},{4,20},{16,24},{20,28},{24,8},{28,12},{8,0},{12,4},{1,17},{... | collective-permute-start | bytes 602120 | tf_op jit(solution)/shard_map/near_hop_1/ppermute | solution.py:276
  7.7 1.5 %collective-permute-start.3 = (bf16[1,784,128]{2,1,0:T(8,128)(2,1)}, bf16[1,784,128]{2,1,0:T(8,128)(2,1)S(1)}, u32[]{:S(2)}, u32[]{:S(2)}) collective-permute-start(bf16[1,784,128]{2,1,0:T(8,128)(2,1)} %get-tuple-element.27), channel_id=1, source_target_pairs={{0,1},{1,0},{2,3},{3,2},{4,5},{5,4},{6,7},{7,6},{8,9},{9,8},{10,11... | collective-permute-start | bytes 602120 | tf_op jit(solution)/shard_map/parcels_from_partner_1/ppermute | solution.py:263
  9.2 1.5 %collective-permute-start = (bf16[1,784,128]{2,1,0:T(8,128)(2,1)}, bf16[1,784,128]{2,1,0:T(8,128)(2,1)S(1)}, u32[]{:S(2)}, u32[]{:S(2)}) collective-permute-start(bf16[1,784,128]{2,1,0:T(8,128)(2,1)} %get-tuple-element.24), channel_id=1, source_target_pairs={{0,2},{1,3},{2,0},{3,1},{4,6},{5,7},{6,4},{7,5},{8,10},{9,11},{10,... | collective-permute-start | bytes 602120 | tf_op jit(solution)/shard_map/parcels_from_partner_2/ppermute | solution.py:263
  11.2 1.1 %collective-permute-done.2 = bf16[1,784,128]{2,1,0:T(8,128)(2,1)S(1)} collective-permute-done((bf16[1,784,128]{2,1,0:T(8,128)(2,1)}, bf16[1,784,128]{2,1,0:T(8,128)(2,1)S(1)}, u32[]{:S(2)}, u32[]{:S(2)}) %collective-permute-start.2) | collective-permute-done | bytes 200736 | tf_op jit(solution)/shard_map/near_hop_1/ppermute | solution.py:276
  12.3 3.6 %collective-permute-done.3.refs_1_ = bf16[1,784,128]{2,1,0:T(8,128)(2,1)S(1)} collective-permute-done((bf16[1,784,128]{2,1,0:T(8,128)(2,1)}, bf16[1,784,128]{2,1,0:T(8,128)(2,1)S(1)}, u32[]{:S(2)}, u32[]{:S(2)}) %collective-permute-start.3) | collective-permute-done | bytes 200736 | tf_op jit(solution)/shard_map/parcels_from_partner_1/ppermute | solution.py:263
  15.9 1.6 %collective-permute-start.4 = (bf16[1,784,128]{2,1,0:T(8,128)(2,1)S(1)}, bf16[1,784,128]{2,1,0:T(8,128)(2,1)S(1)}, u32[]{:S(2)}, u32[]{:S(2)}) collective-permute-start(bf16[1,784,128]{2,1,0:T(8,128)(2,1)S(1)} %collective-permute-done.3.refs_1_), channel_id=1, source_target_pairs={{0,16},{4,20},{16,24},{20,28},{24,8},{28,12},{8,0},{12,4},{1,17},{... | collective-permute-start | bytes 602120 | tf_op jit(solution)/shard_map/early_hop_1/ppermute | solution.py:276
  17.4 2.5 %collective-permute-done = bf16[1,784,128]{2,1,0:T(8,128)(2,1)S(1)} collective-permute-done((bf16[1,784,128]{2,1,0:T(8,128)(2,1)}, bf16[1,784,128]{2,1,0:T(8,128)(2,1)S(1)}, u32[]{:S(2)}, u32[]{:S(2)}) %collective-permute-start) | collective-permute-done | bytes 200736 | tf_op jit(solution)/shard_map/parcels_from_partner_2/ppermute | solution.py:263
  20.0 1.6 %collective-permute-done.4 = bf16[1,784,128]{2,1,0:T(8,128)(2,1)S(1)} collective-permute-done((bf16[1,784,128]{2,1,0:T(8,128)(2,1)S(1)}, bf16[1,784,128]{2,1,0:T(8,128)(2,1)S(1)}, u32[]{:S(2)}, u32[]{:S(2)}) %collective-permute-start.4) | collective-permute-done | bytes 200736 | tf_op jit(solution)/shard_map/early_hop_1/ppermute | solution.py:276
  21.6 1.7 %collective-permute-start.8 = (bf16[1,128,1024]{2,1,0:T(8,128)(2,1)}, bf16[1,128,1024]{2,1,0:T(8,128)(2,1)S(1)}, u32[]{:S(2)}, u32[]{:S(2)}) collective-permute-start(bf16[1,128,1024]{2,1,0:T(8,128)(2,1)} %bitcast.44), channel_id=1, source_target_pairs={{0,2},{1,3},{2,0},{3,1},{4,6},{5,7},{6,4},{7,5},{8,10},{9,11},{10,... | collective-permute-start | bytes 786440 | tf_op jit(solution)/shard_map/amplitudes_bit_2/ppermute | solution.py:301
  23.3 2.2 %collective-permute-start.6 = (bf16[2,784,128]{2,1,0:T(8,128)(2,1)S(1)}, bf16[2,784,128]{2,1,0:T(8,128)(2,1)S(1)}, u32[]{:S(2)}, u32[]{:S(2)}) collective-permute-start(bf16[2,784,128]{2,1,0:T(8,128)(2,1)S(1)} %pad_maximum_fusion.3.refs_2_), channel_id=1, source_target_pairs={{0,16},{4,20},{16,24},{20,28},{24,8},{28,12},{8,0},{12,4},{1,17},{... | collective-permute-start | bytes 1204232 | tf_op jit(solution)/shard_map/late_hop_1/ppermute | solution.py:276
  25.6 1.5 %collective-permute-start.5 = (bf16[1,128,1024]{2,1,0:T(8,128)(2,1)}, bf16[1,128,1024]{2,1,0:T(8,128)(2,1)S(1)}, u32[]{:S(2)}, u32[]{:S(2)}) collective-permute-start(bf16[1,128,1024]{2,1,0:T(8,128)(2,1)} %bitcast.42), channel_id=1, source_target_pairs={{0,1},{1,0},{2,3},{3,2},{4,5},{5,4},{6,7},{7,6},{8,9},{9,8},{10,11... | collective-permute-start | bytes 786440 | tf_op jit(solution)/shard_map/amplitudes_bit_1/ppermute | solution.py:301
  27.1 1.1 %collective-permute-done.8 = bf16[1,128,1024]{2,1,0:T(8,128)(2,1)S(1)} collective-permute-done((bf16[1,128,1024]{2,1,0:T(8,128)(2,1)}, bf16[1,128,1024]{2,1,0:T(8,128)(2,1)S(1)}, u32[]{:S(2)}, u32[]{:S(2)}) %collective-permute-start.8) | collective-permute-done | bytes 262176 | tf_op jit(solution)/shard_map/amplitudes_bit_2/ppermute | solution.py:301
  29.2 1.6 %collective-permute-start.10 = (bf16[2,128,1024]{2,1,0:T(8,128)(2,1)S(1)}, bf16[2,128,1024]{2,1,0:T(8,128)(2,1)S(1)}, u32[]{:S(2)}, u32[]{:S(2)}) collective-permute-start(bf16[2,128,1024]{2,1,0:T(8,128)(2,1)S(1)} %pad_maximum_fusion.2), channel_id=1, source_target_pairs={{0,1},{1,0},{2,3},{3,2},{4,5},{5,4},{6,7},{7,6},{8,9},{9,8},{10,11... | collective-permute-start | bytes 1572872 | tf_op jit(solution)/shard_map/amplitudes_bit_1/ppermute | solution.py:301
  30.8 2.5 %collective-permute-start.14 = (bf16[2,784,128]{2,1,0:T(8,128)(2,1)S(1)}, bf16[2,784,128]{2,1,0:T(8,128)(2,1)S(1)}, u32[]{:S(2)}, u32[]{:S(2)}) collective-permute-start(bf16[2,784,128]{2,1,0:T(8,128)(2,1)S(1)} %constant_dynamic-update-slice_fusion.refs_3_), channel_id=1, source_target_pairs={{0,16},{4,20},{16,24},{20,28},{24,8},{28,12},{8,0},{12,4},{1,17},{... | collective-permute-start | bytes 1204232 | tf_op jit(solution)/shard_map/first_hop_2/ppermute | solution.py:276
  33.5 3.4 %collective-permute-start.15 = (bf16[2,784,128]{2,1,0:T(8,128)(2,1)S(1)}, bf16[2,784,128]{2,1,0:T(8,128)(2,1)S(1)}, u32[]{:S(2)}, u32[]{:S(2)}) collective-permute-start(bf16[2,784,128]{2,1,0:T(8,128)(2,1)S(1)} %collective-permute-done.6.refs_5_), channel_id=1, source_target_pairs={{0,16},{4,20},{16,24},{20,28},{24,8},{28,12},{8,0},{12,4},{1,17},{... | collective-permute-start | bytes 1204232 | tf_op jit(solution)/shard_map/late_hop_2/ppermute | solution.py:276
  37.2 5.9 %collective-permute-done.14.refs_4_ = bf16[2,784,128]{2,1,0:T(8,128)(2,1)S(1)} collective-permute-done((bf16[2,784,128]{2,1,0:T(8,128)(2,1)S(1)}, bf16[2,784,128]{2,1,0:T(8,128)(2,1)S(1)}, u32[]{:S(2)}, u32[]{:S(2)}) %collective-permute-start.14) | collective-permute-done | bytes 401440 | tf_op jit(solution)/shard_map/first_hop_2/ppermute | solution.py:276
  43.1 5.8 %collective-permute-done.15.refs_0_ = bf16[2,784,128]{2,1,0:T(8,128)(2,1)S(1)} collective-permute-done((bf16[2,784,128]{2,1,0:T(8,128)(2,1)S(1)}, bf16[2,784,128]{2,1,0:T(8,128)(2,1)S(1)}, u32[]{:S(2)}, u32[]{:S(2)}) %collective-permute-start.15) | collective-permute-done | bytes 401440 | tf_op jit(solution)/shard_map/late_hop_2/ppermute | solution.py:276
  48.9 2.7 %collective-permute-start.16 = (bf16[2,784,128]{2,1,0:T(8,128)(2,1)S(1)}, bf16[2,784,128]{2,1,0:T(8,128)(2,1)S(1)}, u32[]{:S(2)}, u32[]{:S(2)}) collective-permute-start(bf16[2,784,128]{2,1,0:T(8,128)(2,1)S(1)} %collective-permute-done.14.refs_4_), channel_id=1, source_target_pairs={{0,16},{4,20},{16,24},{20,28},{24,8},{28,12},{8,0},{12,4},{1,17},{... | collective-permute-start | bytes 1204232 | tf_op jit(solution)/shard_map/first_hop_3/ppermute | solution.py:276
  52.5 1.1 %collective-permute-done.11 = bf16[2,128,1024]{2,1,0:T(8,128)(2,1)S(1)} collective-permute-done((bf16[2,128,1024]{2,1,0:T(8,128)(2,1)S(1)}, bf16[2,128,1024]{2,1,0:T(8,128)(2,1)S(1)}, u32[]{:S(2)}, u32[]{:S(2)}) %collective-permute-start.11) | collective-permute-done | bytes 524320 | tf_op jit(solution)/shard_map/twin_of_bit_1/ppermute | solution.py:266
  55.5 6.1 %ladder_first.1 = (f32[9,512,128]{2,1,0:T(8,128)S(1)}, f32[256,128]{1,0:T(8,128)S(1)}, f32[256,1024]{1,0:T(8,128)S(1)}) custom-call(f32[2,128]{1,0:T(2,128)S(1)} %bitcast.41, f32[1,1024]{1,0:T(1,128)S(1)} %bitcast.39, bf16[4,512,1024]{2,1,0:T(8,128)(2,1)S(1)} %pad_maximum_fusion.amps.refs_0_, bf16[1,784,128]{2,1,0:T(8,128)(2,1)S(1)} %copy-done.2, ...), custom_call_target="tpu_custom_call" | custom-call | flops 100000000 | bytes 1048576 | tf_op jit(solution)/shard_map/ladder_first/pallas_call | solution.py:325
  61.7 3.3 %ladder_second.1 = (f32[256,1024]{1,0:T(8,128)S(1)}, bf16[8,256,128]{2,1,0:T(8,128)(2,1)S(1)}) custom-call(f32[9,512,128]{2,1,0:T(8,128)S(1)} %get-tuple-element.36.before, bf16[256,1024]{1,0:T(8,128)(2,1)S(1)} %copy-done.1, bf16[256,1024]{1,0:T(8,128)(2,1)S(1)} %copy-done, f32[256,128]{1,0:T(8,128)S(1)} %get-tuple-element.37.occupied, ...), custom_call_target="tpu_custom_call" | custom-call | flops 1000000000 | bytes 1048576 | tf_op jit(solution)/shard_map/ladder_second/pallas_call | solution.py:325
  65.6 1.9 %collective-permute-done.19.refs_2_ = bf16[2,784,128]{2,1,0:T(8,128)(2,1)S(1)} collective-permute-done((bf16[2,784,128]{2,1,0:T(8,128)(2,1)S(1)}, bf16[2,784,128]{2,1,0:T(8,128)(2,1)S(1)}, u32[]{:S(2)}, u32[]{:S(2)}) %collective-permute-start.19) | collective-permute-done | bytes 401440 | tf_op jit(solution)/shard_map/ppermute | solution.py:266
  67.5 3.9 %update.1 = (bf16[256,1024]{1,0:T(8,128)(2,1)}, f32[256,1024]{1,0:T(8,128)}) custom-call(s32[2,8]{1,0:T(2,128)S(1)} %copy-done.4, bf16[256,1024]{1,0:T(8,128)(2,1)S(1)} %copy-done, f32[256,1024]{1,0:T(8,128)S(1)} %get-tuple-element.38.base, f32[256,1024]{1,0:T(8,128)S(1)} %get-tuple-element.39.inverse, ...), custom_call_target="tpu_custom_call" | custom-call | tf_op jit(solution)/shard_map/update/pallas_call | solution.py:385
  (52 shorter events, 5.4 us)
Async XLA Ops:
  3.6 33.3 %copy-start.6 = (bf16[128,1024]{1,0:T(8,128)(2,1)S(1)}, bf16[128,1024]{1,0:T(8,128)(2,1)}, u32[]{:S(2)}) copy-start(bf16[128,1024]{1,0:T(8,128)(2,1)} %get-tuple-element.30) | copy-start | bytes 786436
  3.7 8.7 %collective-permute-start.2 = (bf16[1,784,128]{2,1,0:T(8,128)(2,1)}, bf16[1,784,128]{2,1,0:T(8,128)(2,1)S(1)}, u32[]{:S(2)}, u32[]{:S(2)}) collective-permute-start(bf16[1,784,128]{2,1,0:T(8,128)(2,1)} %get-tuple-element.26.refs_0_), channel_id=1, source_target_pairs={{0,16},{4,20},{16,24},{20,28},{24,8},{28,12},{8,0},{12,4},{1,17},{... | collective-permute-start | bytes 602120 | tf_op jit(solution)/shard_map/near_hop_1/ppermute | solution.py:276
  7.7 8.1 %collective-permute-start.3 = (bf16[1,784,128]{2,1,0:T(8,128)(2,1)}, bf16[1,784,128]{2,1,0:T(8,128)(2,1)S(1)}, u32[]{:S(2)}, u32[]{:S(2)}) collective-permute-start(bf16[1,784,128]{2,1,0:T(8,128)(2,1)} %get-tuple-element.27), channel_id=1, source_target_pairs={{0,1},{1,0},{2,3},{3,2},{4,5},{5,4},{6,7},{7,6},{8,9},{9,8},{10,11... | collective-permute-start | bytes 602120 | tf_op jit(solution)/shard_map/parcels_from_partner_1/ppermute | solution.py:263
  9.2 10.7 %collective-permute-start = (bf16[1,784,128]{2,1,0:T(8,128)(2,1)}, bf16[1,784,128]{2,1,0:T(8,128)(2,1)S(1)}, u32[]{:S(2)}, u32[]{:S(2)}) collective-permute-start(bf16[1,784,128]{2,1,0:T(8,128)(2,1)} %get-tuple-element.24), channel_id=1, source_target_pairs={{0,2},{1,3},{2,0},{3,1},{4,6},{5,7},{6,4},{7,5},{8,10},{9,11},{10,... | collective-permute-start | bytes 602120 | tf_op jit(solution)/shard_map/parcels_from_partner_2/ppermute | solution.py:263
  10.8 9.2 %collective-permute-start.1 = (bf16[1,784,128]{2,1,0:T(8,128)(2,1)}, bf16[1,784,128]{2,1,0:T(8,128)(2,1)S(1)}, u32[]{:S(2)}, u32[]{:S(2)}) collective-permute-start(bf16[1,784,128]{2,1,0:T(8,128)(2,1)} %get-tuple-element.25), channel_id=1, source_target_pairs={{0,3},{1,2},{2,1},{3,0},{4,7},{5,6},{6,5},{7,4},{8,11},{9,10},{10,... | collective-permute-start | bytes 602120 | tf_op jit(solution)/shard_map/parcels_from_partner_3/ppermute | solution.py:263
  15.9 5.7 %collective-permute-start.4 = (bf16[1,784,128]{2,1,0:T(8,128)(2,1)S(1)}, bf16[1,784,128]{2,1,0:T(8,128)(2,1)S(1)}, u32[]{:S(2)}, u32[]{:S(2)}) collective-permute-start(bf16[1,784,128]{2,1,0:T(8,128)(2,1)S(1)} %collective-permute-done.3.refs_1_), channel_id=1, source_target_pairs={{0,16},{4,20},{16,24},{20,28},{24,8},{28,12},{8,0},{12,4},{1,17},{... | collective-permute-start | bytes 602120 | tf_op jit(solution)/shard_map/early_hop_1/ppermute | solution.py:276
  21.6 6.6 %collective-permute-start.8 = (bf16[1,128,1024]{2,1,0:T(8,128)(2,1)}, bf16[1,128,1024]{2,1,0:T(8,128)(2,1)S(1)}, u32[]{:S(2)}, u32[]{:S(2)}) collective-permute-start(bf16[1,128,1024]{2,1,0:T(8,128)(2,1)} %bitcast.44), channel_id=1, source_target_pairs={{0,2},{1,3},{2,0},{3,1},{4,6},{5,7},{6,4},{7,5},{8,10},{9,11},{10,... | collective-permute-start | bytes 786440 | tf_op jit(solution)/shard_map/amplitudes_bit_2/ppermute | solution.py:301
  23.3 10.2 %collective-permute-start.6 = (bf16[2,784,128]{2,1,0:T(8,128)(2,1)S(1)}, bf16[2,784,128]{2,1,0:T(8,128)(2,1)S(1)}, u32[]{:S(2)}, u32[]{:S(2)}) collective-permute-start(bf16[2,784,128]{2,1,0:T(8,128)(2,1)S(1)} %pad_maximum_fusion.3.refs_2_), channel_id=1, source_target_pairs={{0,16},{4,20},{16,24},{20,28},{24,8},{28,12},{8,0},{12,4},{1,17},{... | collective-permute-start | bytes 1204232 | tf_op jit(solution)/shard_map/late_hop_1/ppermute | solution.py:276
  25.6 11.3 %collective-permute-start.5 = (bf16[1,128,1024]{2,1,0:T(8,128)(2,1)}, bf16[1,128,1024]{2,1,0:T(8,128)(2,1)S(1)}, u32[]{:S(2)}, u32[]{:S(2)}) collective-permute-start(bf16[1,128,1024]{2,1,0:T(8,128)(2,1)} %bitcast.42), channel_id=1, source_target_pairs={{0,1},{1,0},{2,3},{3,2},{4,5},{5,4},{6,7},{7,6},{8,9},{9,8},{10,11... | collective-permute-start | bytes 786440 | tf_op jit(solution)/shard_map/amplitudes_bit_1/ppermute | solution.py:301
  29.2 22.4 %collective-permute-start.10 = (bf16[2,128,1024]{2,1,0:T(8,128)(2,1)S(1)}, bf16[2,128,1024]{2,1,0:T(8,128)(2,1)S(1)}, u32[]{:S(2)}, u32[]{:S(2)}) collective-permute-start(bf16[2,128,1024]{2,1,0:T(8,128)(2,1)S(1)} %pad_maximum_fusion.2), channel_id=1, source_target_pairs={{0,1},{1,0},{2,3},{3,2},{4,5},{5,4},{6,7},{7,6},{8,9},{9,8},{10,11... | collective-permute-start | bytes 1572872 | tf_op jit(solution)/shard_map/amplitudes_bit_1/ppermute | solution.py:301
  30.8 12.3 %collective-permute-start.14 = (bf16[2,784,128]{2,1,0:T(8,128)(2,1)S(1)}, bf16[2,784,128]{2,1,0:T(8,128)(2,1)S(1)}, u32[]{:S(2)}, u32[]{:S(2)}) collective-permute-start(bf16[2,784,128]{2,1,0:T(8,128)(2,1)S(1)} %constant_dynamic-update-slice_fusion.refs_3_), channel_id=1, source_target_pairs={{0,16},{4,20},{16,24},{20,28},{24,8},{28,12},{8,0},{12,4},{1,17},{... | collective-permute-start | bytes 1204232 | tf_op jit(solution)/shard_map/first_hop_2/ppermute | solution.py:276
  33.5 15.3 %collective-permute-start.15 = (bf16[2,784,128]{2,1,0:T(8,128)(2,1)S(1)}, bf16[2,784,128]{2,1,0:T(8,128)(2,1)S(1)}, u32[]{:S(2)}, u32[]{:S(2)}) collective-permute-start(bf16[2,784,128]{2,1,0:T(8,128)(2,1)S(1)} %collective-permute-done.6.refs_5_), channel_id=1, source_target_pairs={{0,16},{4,20},{16,24},{20,28},{24,8},{28,12},{8,0},{12,4},{1,17},{... | collective-permute-start | bytes 1204232 | tf_op jit(solution)/shard_map/late_hop_2/ppermute | solution.py:276
  37.0 15.4 %copy-start.7 = (bf16[128,1024]{1,0:T(8,128)(2,1)S(1)}, bf16[128,1024]{1,0:T(8,128)(2,1)}, u32[]{:S(2)}) copy-start(bf16[128,1024]{1,0:T(8,128)(2,1)} %get-tuple-element.31) | copy-start | bytes 786436
  37.0 14.6 %collective-permute-start.12 = (bf16[2,128,1024]{2,1,0:T(8,128)(2,1)S(1)}, bf16[2,128,1024]{2,1,0:T(8,128)(2,1)S(1)}, u32[]{:S(2)}, u32[]{:S(2)}) collective-permute-start(bf16[2,128,1024]{2,1,0:T(8,128)(2,1)S(1)} %pad_maximum_fusion.1), channel_id=1, source_target_pairs={{0,2},{1,3},{2,0},{3,1},{4,6},{5,7},{6,4},{7,5},{8,10},{9,11},{10,... | collective-permute-start | bytes 1572872 | tf_op jit(solution)/shard_map/amplitudes_bit_2/ppermute | solution.py:301
  37.1 14.7 %collective-permute-start.7 = (bf16[2,128,1024]{2,1,0:T(8,128)(2,1)S(1)}, bf16[2,128,1024]{2,1,0:T(8,128)(2,1)S(1)}, u32[]{:S(2)}, u32[]{:S(2)}) collective-permute-start(bf16[2,128,1024]{2,1,0:T(8,128)(2,1)S(1)} %pad_maximum_fusion.1), channel_id=1, source_target_pairs={{0,4},{4,0},{8,12},{12,8},{16,20},{20,16},{24,28},{28,24},{1,5},{5... | collective-permute-start | bytes 1572872 | tf_op jit(solution)/shard_map/twin_of_bit_1/ppermute | solution.py:266
  43.1 9.3 %collective-permute-start.9 = (bf16[2,128,1024]{2,1,0:T(8,128)(2,1)S(1)}, bf16[2,128,1024]{2,1,0:T(8,128)(2,1)S(1)}, u32[]{:S(2)}, u32[]{:S(2)}) collective-permute-start(bf16[2,128,1024]{2,1,0:T(8,128)(2,1)S(1)} %pad_maximum_fusion.2), channel_id=1, source_target_pairs={{0,4},{4,0},{8,12},{12,8},{16,20},{20,16},{24,28},{28,24},{1,5},{5... | collective-permute-start | bytes 1572872 | tf_op jit(solution)/shard_map/twin_of_bit_2/ppermute | solution.py:266
  48.9 12.7 %collective-permute-start.16 = (bf16[2,784,128]{2,1,0:T(8,128)(2,1)S(1)}, bf16[2,784,128]{2,1,0:T(8,128)(2,1)S(1)}, u32[]{:S(2)}, u32[]{:S(2)}) collective-permute-start(bf16[2,784,128]{2,1,0:T(8,128)(2,1)S(1)} %collective-permute-done.14.refs_4_), channel_id=1, source_target_pairs={{0,16},{4,20},{16,24},{20,28},{24,8},{28,12},{8,0},{12,4},{1,17},{... | collective-permute-start | bytes 1204232 | tf_op jit(solution)/shard_map/first_hop_3/ppermute | solution.py:276
  51.6 14.1 %collective-permute-start.18 = (bf16[2,784,128]{2,1,0:T(8,128)(2,1)S(1)}, bf16[2,784,128]{2,1,0:T(8,128)(2,1)S(1)}, u32[]{:S(2)}, u32[]{:S(2)}) collective-permute-start(bf16[2,784,128]{2,1,0:T(8,128)(2,1)S(1)} %collective-permute-done.15.refs_0_), channel_id=1, source_target_pairs={{0,16},{4,20},{16,24},{20,28},{24,8},{28,12},{8,0},{12,4},{1,17},{... | collective-permute-start | bytes 1204232 | tf_op jit(solution)/shard_map/late_hop_3/ppermute | solution.py:276
  51.6 2.0 %collective-permute-start.11 = (bf16[2,128,1024]{2,1,0:T(8,128)(2,1)S(1)}, bf16[2,128,1024]{2,1,0:T(8,128)(2,1)S(1)}, u32[]{:S(2)}, u32[]{:S(2)}) collective-permute-start(bf16[2,128,1024]{2,1,0:T(8,128)(2,1)S(1)} %collective-permute-done.10), channel_id=1, source_target_pairs={{0,4},{4,0},{8,12},{12,8},{16,20},{20,16},{24,28},{28,24},{1,5},{5... | collective-permute-start | bytes 1572872 | tf_op jit(solution)/shard_map/twin_of_bit_1/ppermute | solution.py:266
  51.8 2.6 %collective-permute-start.13 = (bf16[2,128,1024]{2,1,0:T(8,128)(2,1)S(1)}, bf16[2,128,1024]{2,1,0:T(8,128)(2,1)S(1)}, u32[]{:S(2)}, u32[]{:S(2)}) collective-permute-start(bf16[2,128,1024]{2,1,0:T(8,128)(2,1)S(1)} %collective-permute-done.12), channel_id=1, source_target_pairs={{0,4},{4,0},{8,12},{12,8},{16,20},{20,16},{24,28},{28,24},{1,5},{5... | collective-permute-start | bytes 1572872 | tf_op jit(solution)/shard_map/twin_of_bit_2/ppermute | solution.py:266
  55.5 6.1 %copy-start = (bf16[256,1024]{1,0:T(8,128)(2,1)S(1)}, bf16[256,1024]{1,0:T(8,128)(2,1)}, u32[]{:S(2)}) copy-start(bf16[256,1024]{1,0:T(8,128)(2,1)} %amplitudes.5) | copy-start | bytes 1572868
  55.5 6.1 %copy-start.1 = (bf16[256,1024]{1,0:T(8,128)(2,1)S(1)}, bf16[256,1024]{1,0:T(8,128)(2,1)}, u32[]{:S(2)}) copy-start(bf16[256,1024]{1,0:T(8,128)(2,1)} %driver.1) | copy-start | bytes 1572868
  64.9 2.6 %collective-permute-start.17 = (bf16[8,256,128]{2,1,0:T(8,128)(2,1)S(1)}, bf16[8,256,128]{2,1,0:T(8,128)(2,1)S(1)}, u32[]{:S(2)}, u32[]{:S(2)}) collective-permute-start(bf16[8,256,128]{2,1,0:T(8,128)(2,1)S(1)} %get-tuple-element.40), channel_id=1, source_target_pairs={{0,4},{4,0},{8,12},{12,8},{16,20},{20,16},{24,28},{28,24},{1,5},{5... | collective-permute-start | bytes 1572872 | tf_op jit(solution)/shard_map/ppermute | solution.py:266
  65.6 1.9 %collective-permute-start.19 = (bf16[2,784,128]{2,1,0:T(8,128)(2,1)S(1)}, bf16[2,784,128]{2,1,0:T(8,128)(2,1)S(1)}, u32[]{:S(2)}, u32[]{:S(2)}) collective-permute-start(bf16[2,784,128]{2,1,0:T(8,128)(2,1)S(1)} %collective-permute-done.18.refs_1_), channel_id=1, source_target_pairs={{0,4},{4,0},{8,12},{12,8},{16,20},{20,16},{24,28},{28,24},{1,5},{5... | collective-permute-start | bytes 1204232 | tf_op jit(solution)/shard_map/ppermute | solution.py:266
  (4 other events, 8.6 us)

commit v8 on v7

--- a/solution.py
+++ b/solution.py
@@ -12,8 +12,9 @@
 ALL_VMEM = 60 * 1024 * 1024
 CORES = 2
 NOTE_ROWS = 16
-FIRST_FLOPS = 10**8
-SECOND_FLOPS = 10**9
+FIRST_FLOPS = 10**9
+MIDDLE_FLOPS = 10**8
+LAST_FLOPS = 10**9
 
 
 def pack_kernel(n_v, cap, columns, live, integrals, amplitudes, *refs):
@@ -95,7 +96,7 @@
     pairs[...] = jnp.zeros_like(pairs)
 
 
-def add_unit(array, member, unit, j, n_rows, cap, rows, amps, notes, pairs, total):
+def add_unit(array, member, unit, blocks, cap, rows, notes, pairs, total):
     tile = array.shape[-1]
 
     def place(k):
@@ -104,7 +105,7 @@
         row = jnp.where(used, lax.div(code, rows), 0)
         column = jnp.where(used, lax.rem(code, rows), rows)
         lanes = pl.ds(pl.multiple_of(row * tile, tile), tile)
-        return amps[j, pl.ds(0, n_rows), lanes], column
+        return jnp.concatenate([ref[index, :, lanes] for ref, index in blocks]), column
 
     for k in range(0, cap - 1, 2):
         pair = pairs.at[k // 2]
@@ -127,31 +128,33 @@
         )
 
 
-def add_arrays(arrays, layout, cap, rows, amps, notes_wide, notes, pairs, total, sem):
+def add_arrays(arrays, layout, amps, where, cap, rows, notes_wide, notes, pairs, total, sem):
     copy = read_notes(arrays, notes_wide, notes, sem)
     pairs[...] = jnp.zeros_like(pairs)
     total[...] = jnp.zeros_like(total)
     copy.wait()
     unit = 0
     for array, partners in zip(arrays, layout):
-
-        def one(i, carry, unit=unit, array=array, partners=partners):
-            add_unit(
-                array, i, unit + i, partners[0] + i, total.shape[1], cap, rows, amps, notes, pairs, total
-            )
-            return carry
-
-        lax.fori_loop(0, len(partners), one, 0)
-        unit += len(partners)
-
-
-def first_ladder_kernel(cap, layout, occupied, virtual, amps, *refs):
-    arrays, (total, occupied_out, inverse, notes_wide, notes, pairs, sem) = (
-        refs[: len(layout)],
-        refs[len(layout) :],
-    )
+        for member, partner in enumerate(partners):
+            blocks = [(amps[number], index) for number, index in where[partner]]
+            add_unit(array, member, unit, blocks, cap, rows, notes, pairs, total)
+            unit += 1
+
+
+def split_refs(refs, *counts):
+    parts = []
+    for count in counts:
+        parts.append(refs[:count])
+        refs = refs[count:]
+    return *parts, refs
+
+
+def first_ladder_kernel(cap, layout, where, occupied, virtual, *refs):
+    n_amps = 1 + max(number for blocks in where.values() for number, _ in blocks)
+    amps, arrays, refs = split_refs(refs, n_amps, len(layout))
+    total, occupied_out, inverse, *scratch = refs
     rows = total.shape[0] - 1
-    add_arrays(arrays, layout, cap, rows, amps, notes_wide, notes, pairs, total, sem)
+    add_arrays(arrays, layout, amps, where, cap, rows, *scratch[:3], total, scratch[3])
     tile = occupied_out.shape[-1]
     for o in range(occupied.shape[0]):
         here = pl.ds(o * tile, tile)
@@ -162,32 +165,39 @@
             inverse[here, lanes] = 1.0 / (column - virtual[:, lanes])
 
 
-def second_ladder_kernel(
-    cap, layout, before, driver, amplitudes, occupied, virtual, amps, *refs
-):
-    arrays, (base, twin, total, notes_wide, notes, pairs, sem) = (
-        refs[: len(layout)],
-        refs[len(layout) :],
-    )
+def middle_ladder_kernel(cap, layout, where, before, driver, amplitudes, occupied, virtual, *refs):
+    n_amps = 1 + max(number for blocks in where.values() for number, _ in blocks)
+    amps, arrays, refs = split_refs(refs, n_amps, len(layout))
+    total, base, *scratch = refs
+    rows = total.shape[0] - 1
+    tile = occupied.shape[-1]
+    add_arrays(arrays, layout, amps, where, cap, rows, *scratch[:3], total, scratch[3])
+    total[...] += before[...]
+    for c in range(rows):
+        lanes = pl.ds(c * tile, tile)
+        denominator = occupied[...] - virtual[:, lanes]
+        plain = amplitudes[:, lanes].astype(jnp.float32)
+        base[:, lanes] = driver[:, lanes].astype(jnp.float32) + denominator * plain
+
+
+def last_ladder_kernel(cap, layout, where, before, base, *refs):
+    n_amps = 1 + max(number for blocks in where.values() for number, _ in blocks)
+    amps, arrays, refs = split_refs(refs, n_amps, len(layout))
+    whole, twin, total, *scratch = refs
     rows, n_rows, tile = twin.shape
-    add_arrays(arrays, layout, cap, rows, amps, notes_wide, notes, pairs, total, sem)
+    add_arrays(arrays, layout, amps, where, cap, rows, *scratch[:3], total, scratch[3])
     twin[...] = (before[:rows, n_rows:] + total[:rows, n_rows:]).astype(twin.dtype)
     for c in range(rows):
         lanes = pl.ds(c * tile, tile)
-        own = before[c, :n_rows] + total[c, :n_rows]
-        denominator = occupied[...] - virtual[:, lanes]
-        plain = amplitudes[:, lanes].astype(jnp.float32)
-        base[:, lanes] = driver[:, lanes].astype(jnp.float32) + own + denominator * plain
-
-
-def update_kernel(cap, partners, live, amplitudes, base, inverse, twin, *refs):
-    amps, *arrays = refs[: 1 + CORES]
-    new, residual, new_buf, residual_buf, notes_wide, notes, pairs, total, sem, sems = refs[
-        1 + CORES :
-    ]
+        whole[:, lanes] = base[:, lanes] + before[c, :n_rows] + total[c, :n_rows]
+
+
+def update_kernel(cap, partners, where, live, amplitudes, base, inverse, twin, *refs):
+    n_amps = 1 + max(number for blocks in where.values() for number, _ in blocks)
+    amps, arrays, outs, refs = split_refs(refs, n_amps, CORES, 2)
+    new_buf, residual_buf, *scratch, total, sem, sems = refs
     rows, _, tile = twin.shape
-    layout = [partners] * CORES
-    add_arrays(arrays, layout, cap, rows, amps, notes_wide, notes, pairs, total, sem)
+    add_arrays(arrays, [partners] * CORES, amps, where, cap, rows, *scratch, total, sem)
     copies = []
     for c in range(rows):
         lanes = pl.ds(c * tile, tile)
@@ -198,10 +208,10 @@
             masked = (amplitudes[at].astype(jnp.float32) * kept).astype(jnp.bfloat16)
             rest = (base[at] + (twin[c, here].astype(jnp.float32) + total[c, here])) * kept
             residual_buf[at] = rest
-            new_buf[at] = (masked.astype(jnp.float32) - rest * inverse[at]).astype(new.dtype)
-        for i, (source, target) in enumerate(((new_buf, new), (residual_buf, residual))):
+            new_buf[at] = (masked.astype(jnp.float32) - rest * inverse[at]).astype(new_buf.dtype)
+        for i, source in enumerate((new_buf, residual_buf)):
             copies.append(
-                pltpu.make_async_copy(source.at[:, lanes], target.at[:, lanes], sems.at[i, c])
+                pltpu.make_async_copy(source.at[:, lanes], outs[i].at[:, lanes], sems.at[i, c])
             )
             copies[-1].start()
     for copy in copies:
@@ -289,43 +299,52 @@
     groups["first"] = groups["near"] + groups["early"]
     hops["late"].append(next_on_ring(hops["late"][0], "late_hop_1"))
     hops["first"] = [None, join([hops["near"][1], hops["early"][1]])]
-    for hop in range(2, n_z):
-        for name in ("first", "late"):
-            hops[name].append(next_on_ring(hops[name][-1], f"{name}_hop_{hop}"))
-
     def gather_amplitudes(value, bits):
-        held, ids = value[None], [0]
-        twin_held = None
+        pieces, own, twin = [value[None]], {0: (value[None], 0)}, {}
+        ids = [0]
         for bit in bits:
+            held = join(pieces)
             with jax.named_scope(f"amplitudes_bit_{bit}"):
-                arrived_now = lax.ppermute(held, "vpair", [(i, i ^ bit) for i in range(n_v)])
+                now = lax.ppermute(held, "vpair", [(i, i ^ bit) for i in range(n_v)])
+            new_ids = [i ^ bit for i in ids]
+            own |= {j: (now, i) for i, j in enumerate(new_ids)}
             with jax.named_scope(f"twin_of_bit_{bit}"):
-                part = arrived_now if twin_held is not None else jnp.concatenate([held, arrived_now])
-                twin_now = across_core(after(part, hops["late"][1]))
-            twin_held = twin_now if twin_held is None else jnp.concatenate([twin_held, twin_now])
-            held, ids = jnp.concatenate([held, arrived_now]), ids + [i ^ bit for i in ids]
-        return {j: (held[i], twin_held[i]) for i, j in enumerate(ids)}
+                part, part_ids = (now, new_ids) if twin else (join([held, now]), ids + new_ids)
+                swapped = across_core(after(part, hops["late"][1]))
+            twin |= {j: (swapped, i) for i, j in enumerate(part_ids)}
+            pieces.append(now)
+            ids = ids + new_ids
+        return own, twin
 
     bits = [1 << i for i in range((n_v - 1).bit_length())]
     upper, lower = after((upper, lower), (hops["late"][0], hops["early"][1]))
-    upper, lower = gather_amplitudes(upper, bits), gather_amplitudes(lower, bits[::-1])
-    amps = jnp.stack(
-        [
-            jnp.concatenate([upper[j][0], lower[j][0], upper[j][1], lower[j][1]])
-            for j in range(n_v)
-        ]
-    )
+    upper_own, upper_twin = gather_amplitudes(upper, bits)
+    lower_own, lower_twin = gather_amplitudes(lower, bits[::-1])
+
+    def blocks_of(partners, *sources):
+        amps, where = [], {}
+        for j in partners:
+            where[j] = []
+            for source in sources:
+                array, index = source[j]
+                if not any(array is other for other in amps):
+                    amps.append(array)
+                number = [array is other for other in amps].index(True)
+                where[j].append((number, index))
+        return amps, where
 
     sums = (rows + 1, CORES * n_rows, tile)
     pairs = (max(cap // 2, 1), 2 * tile, 2 * tile)
 
     def ladder_call(kernel, found, before, out_shape, extra_scratch, flops, name):
         arrays, layout = [hops[name][hop] for name, hop in found], [groups[name] for name, _ in found]
-        n_units = sum(len(partners) for partners in layout)
+        partners = sorted({j for part in layout for j in part})
+        amps, where = blocks_of(partners, upper_own, lower_own, upper_twin, lower_twin)
+        n_units = sum(len(part) for part in layout)
         return pl.pallas_call(
-            functools.partial(kernel, cap, layout),
+            functools.partial(kernel, cap, layout, where),
             out_shape=out_shape,
-            in_specs=[in_vmem] * (len(before) + 1 + len(arrays)),
+            in_specs=[in_vmem] * (len(before) + len(amps) + len(arrays)),
             out_specs=[in_vmem] * len(out_shape),
             scratch_shapes=extra_scratch
             + [
@@ -337,7 +356,7 @@
             compiler_params=params(
                 ((n_units, height, tile), dtype),
                 *[(sums, jnp.float32)] * 4,
-                (amps.shape, dtype),
+                ((n_v, CORES * n_rows, width), dtype),
             ),
             cost_estimate=pl.CostEstimate(
                 flops=flops,
@@ -345,50 +364,54 @@
                 transcendentals=0,
             ),
             name=name,
-        )(*before, amps, *arrays)
-
-    tail = [("late", n_z - 2), ("first", n_z - 1)]
-    head = [("near", 0), ("early", 0), ("late", 0)]
-    head += [("first", hop) for hop in range(1, n_z - 1)]
-    head += [("late", hop) for hop in range(1, n_z - 2)]
+        )(*before, *amps, *arrays)
+
     virtual = virtual_energy.reshape(1, width)
+    whole = jax.ShapeDtypeStruct((n_rows, width), jnp.float32)
+    all_sums = jax.ShapeDtypeStruct(sums, jnp.float32)
     total, occupied, inverse = ladder_call(
         first_ladder_kernel,
-        head,
+        [("near", 0), ("early", 0), ("late", 0), ("first", 1), ("late", 1)],
         [occupied_energy.reshape(-1, tile), virtual],
-        [
-            jax.ShapeDtypeStruct(sums, jnp.float32),
-            jax.ShapeDtypeStruct((n_rows, tile), jnp.float32),
-            jax.ShapeDtypeStruct((n_rows, width), jnp.float32),
-        ],
+        [all_sums, jax.ShapeDtypeStruct((n_rows, tile), jnp.float32), whole],
         [],
         FIRST_FLOPS,
         "ladder_first",
     )
+    for hop in range(2, n_z):
+        for name in ("first", "late"):
+            hops[name].append(next_on_ring(hops[name][-1], f"{name}_hop_{hop}"))
+    total, base = ladder_call(
+        middle_ladder_kernel,
+        [(name, hop) for hop in range(2, n_z - 1) for name in ("first", "late")],
+        [total, driver_terms, amplitudes, occupied, virtual],
+        [all_sums, whole],
+        [],
+        MIDDLE_FLOPS,
+        "ladder_middle",
+    )
     base, twin = ladder_call(
-        second_ladder_kernel,
-        tail,
-        [total, driver_terms, amplitudes, occupied, virtual],
-        [
-            jax.ShapeDtypeStruct((n_rows, width), jnp.float32),
-            jax.ShapeDtypeStruct((rows, n_rows, tile), jnp.bfloat16),
-        ],
+        last_ladder_kernel,
+        [("first", n_z - 1)],
+        [total, base],
+        [whole, jax.ShapeDtypeStruct((rows, n_rows, tile), jnp.bfloat16)],
         [pltpu.VMEM(sums, jnp.float32)],
-        SECOND_FLOPS,
-        "ladder_second",
+        LAST_FLOPS,
+        "ladder_last",
     )
     last, behind = after(hops["late"][-1], twin), groups["late"]
     twin = across_core(twin)
 
     n_last = CORES * len(behind)
+    amps, where = blocks_of(behind, upper_own, lower_own)
     sums = (rows + 1, n_rows, tile)
     return pl.pallas_call(
-        functools.partial(update_kernel, cap, behind),
+        functools.partial(update_kernel, cap, behind, where),
         out_shape=[
             jax.ShapeDtypeStruct((n_rows, width), jnp.bfloat16),
             jax.ShapeDtypeStruct((n_rows, width), jnp.float32),
         ],
-        in_specs=[in_smem] + [in_vmem] * (5 + CORES),
+        in_specs=[in_smem] + [in_vmem] * (4 + len(amps) + CORES),
         out_specs=[in_hbm] * 2,
         scratch_shapes=[
             pltpu.VMEM((n_rows, width), jnp.bfloat16),
@@ -401,7 +424,7 @@
             pltpu.SemaphoreType.DMA((2, rows)),
         ],
         compiler_params=params(
-            (amps.shape, dtype), ((n_last, height, tile), dtype), *[(sums, jnp.float32)] * 5
+            ((n_v, n_rows, width), dtype), ((n_last, height, tile), dtype), *[(sums, jnp.float32)] * 5
         ),
         name="update",
     )(
@@ -410,7 +433,7 @@
         base,
         inverse,
         twin,
-        amps,
+        *amps,
         last,
         across_core(last),
     )

time: 71.6 us -> 72.5 us (1.013)
  waiting for transfers between devices: 25.8 us -> 30 us
  starting transfers between devices: 25.8 us -> 23.6 us
    ppermute x4, waiting for transfers between devices: 1.1 us -> 6.57 us  [gather_amplitudes(): now = lax.ppermute(held, 'vpair', [(i, i ^ bit) for i in range(n_v)])]
    concatenate x1 -> x3, other arithmetic: 0.04 us -> 2.04 us  [join(): return jnp.concatenate(values) if len(values) > 1 else values[0]]
    ppermute x6, waiting for transfers between devices: 3.62 us -> 1.74 us  [across_core(): return lax.ppermute(value, 'opair', [(i, i ^ 1) for i in range(n_o)])]
    ppermute x7, starting transfers between devices: 16.5 us -> 14.9 us  [next_on_ring(): return lax.ppermute(value, 'opair', pairs)]
    concatenate x2 -> x0, other arithmetic: 1.05 us -> none  [gather_amplitudes(): jnp.concatenate([held, arrived_now])]
    ppermute x6, starting transfers between devices: 0.99 us -> 0.08 us  [across_core(): return lax.ppermute(value, 'opair', [(i, i ^ 1) for i in range(n_o)])]
    another operation x5 -> x0, other arithmetic: 0.86 us -> none  [on_device(): jnp.stack([jnp.concatenate([upper[j][0], lower[j][0], upper[j][1], lower[...]
    pallas_call x3 -> x4, Pallas kernels: 13.3 us -> 12.6 us  [the longest x3 9.14 us: ladder_call(): pl.pallas_call(functools.partial(kernel, cap, layout, where), out_shape=o...]
  transfers between devices with their start and end apart: 20 -> 20, of which waited for: 12 -> 13; matrix products, arithmetic and copies ran while one was open for 3% -> 3% of each run, Pallas kernels for 13% -> 13%
where the time goes in v8:
time: 72.5 us; the launch traced here: 72.3 us
  waiting for transfers between devices  30 us (41%)
  starting transfers between devices  23.6 us (33%)
  Pallas kernels  15.8 us (22%)
  other arithmetic  2.04 us (3%)
  between operations  0.83 us (1%)
    ppermute x7, waiting for transfers between devices, next_on_ring(): return lax.ppermute(value, 'opair', pairs)  15.7 us
    ppermute x7, starting transfers between devices, next_on_ring(): return lax.ppermute(value, 'opair', pairs)  14.9 us
    pallas_call x3, Pallas kernels, ladder_call(): pl.pallas_call(functools.partial(kernel, cap, layout, where), out_shape=o...  9.14 us
    ppermute x4, waiting for transfers between devices, gather_amplitudes(): now = lax.ppermute(held, 'vpair', [(i, i ^ bit) for i in range(n_v)])  6.57 us
    ppermute x3, waiting for transfers between devices, across_v(): return lax.ppermute(value, 'vpair', [(i, i ^ j) for i in range(n_v)])  6.03 us
    ppermute x4, starting transfers between devices, gather_amplitudes(): now = lax.ppermute(held, 'vpair', [(i, i ^ bit) for i in range(n_v)])  5.12 us
    ppermute x3, starting transfers between devices, across_v(): return lax.ppermute(value, 'vpair', [(i, i ^ j) for i in range(n_v)])  3.49 us
    pallas_call x1, Pallas kernels, on_device(): pl.pallas_call(functools.partial(update_kernel, cap, behind, where), out_...  3.49 us
  transfers between devices with their start and end apart: 20, of which 13 were waited for; matrix products, arithmetic and copies ran while one was open for 3% of the time, Pallas kernels for 13%

profile of v8, /device:TPU:0, one launch (start us, length us, event | category | flops | bytes accessed | tf_op | source)
XLA Modules:
  0.0 72.3 jit_solution(5051424401360066478)
XLA Ops:
  0.7 3.1 %pack.1 = (bf16[1,784,128]{2,1,0:T(8,128)(2,1)}, bf16[1,784,128]{2,1,0:T(8,128)(2,1)}, bf16[1,784,128]{2,1,0:T(8,128)(2,1)}, bf16[1,784,128]{2,1,0:T(8,128)(2,1)...) custom-call(s32[3,8]{1,0:T(4,128)} %bitcast.18, s32[2,8]{1,0:T(2,128)} %live.3, ...), custom_call_target="tpu_custom_call" | custom-call | tf_op jit(solution)/shard_map/pack/pallas_call | solution.py:251
  3.8 4.1 %collective-permute-start.2 = (bf16[1,784,128]{2,1,0:T(8,128)(2,1)}, bf16[1,784,128]{2,1,0:T(8,128)(2,1)S(1)}, u32[]{:S(2)}, u32[]{:S(2)}) collective-permute-start(bf16[1,784,128]{2,1,0:T(8,128)(2,1)} %get-tuple-element.28.refs_10_), channel_id=1, source_target_pairs={{0,16},{4,20},{16,24},{20,28},{24,8},{28,12},{8,0},{12,4},{1,17},{... | collective-permute-start | bytes 602120 | tf_op jit(solution)/shard_map/near_hop_1/ppermute | solution.py:286
  7.9 1.5 %collective-permute-start.3 = (bf16[1,784,128]{2,1,0:T(8,128)(2,1)}, bf16[1,784,128]{2,1,0:T(8,128)(2,1)S(1)}, u32[]{:S(2)}, u32[]{:S(2)}) collective-permute-start(bf16[1,784,128]{2,1,0:T(8,128)(2,1)} %get-tuple-element.29), channel_id=1, source_target_pairs={{0,1},{1,0},{2,3},{3,2},{4,5},{5,4},{6,7},{7,6},{8,9},{9,8},{10,11... | collective-permute-start | bytes 602120 | tf_op jit(solution)/shard_map/parcels_from_partner_1/ppermute | solution.py:273
  9.4 1.5 %collective-permute-start = (bf16[1,784,128]{2,1,0:T(8,128)(2,1)}, bf16[1,784,128]{2,1,0:T(8,128)(2,1)S(1)}, u32[]{:S(2)}, u32[]{:S(2)}) collective-permute-start(bf16[1,784,128]{2,1,0:T(8,128)(2,1)} %get-tuple-element.26), channel_id=1, source_target_pairs={{0,2},{1,3},{2,0},{3,1},{4,6},{5,7},{6,4},{7,5},{8,10},{9,11},{10,... | collective-permute-start | bytes 602120 | tf_op jit(solution)/shard_map/parcels_from_partner_2/ppermute | solution.py:273
  12.5 3.6 %collective-permute-done.3.refs_11_ = bf16[1,784,128]{2,1,0:T(8,128)(2,1)S(1)} collective-permute-done((bf16[1,784,128]{2,1,0:T(8,128)(2,1)}, bf16[1,784,128]{2,1,0:T(8,128)(2,1)S(1)}, u32[]{:S(2)}, u32[]{:S(2)}) %collective-permute-start.3) | collective-permute-done | bytes 200736 | tf_op jit(solution)/shard_map/parcels_from_partner_1/ppermute | solution.py:273
  16.0 1.6 %collective-permute-start.4 = (bf16[1,784,128]{2,1,0:T(8,128)(2,1)S(1)}, bf16[1,784,128]{2,1,0:T(8,128)(2,1)S(1)}, u32[]{:S(2)}, u32[]{:S(2)}) collective-permute-start(bf16[1,784,128]{2,1,0:T(8,128)(2,1)S(1)} %collective-permute-done.3.refs_11_), channel_id=1, source_target_pairs={{0,16},{4,20},{16,24},{20,28},{24,8},{28,12},{8,0},{12,4},{1,17},{... | collective-permute-start | bytes 602120 | tf_op jit(solution)/shard_map/early_hop_1/ppermute | solution.py:286
  17.6 2.5 %collective-permute-done = bf16[1,784,128]{2,1,0:T(8,128)(2,1)S(1)} collective-permute-done((bf16[1,784,128]{2,1,0:T(8,128)(2,1)}, bf16[1,784,128]{2,1,0:T(8,128)(2,1)S(1)}, u32[]{:S(2)}, u32[]{:S(2)}) %collective-permute-start) | collective-permute-done | bytes 200736 | tf_op jit(solution)/shard_map/parcels_from_partner_2/ppermute | solution.py:273
  20.1 1.6 %collective-permute-done.4 = bf16[1,784,128]{2,1,0:T(8,128)(2,1)S(1)} collective-permute-done((bf16[1,784,128]{2,1,0:T(8,128)(2,1)S(1)}, bf16[1,784,128]{2,1,0:T(8,128)(2,1)S(1)}, u32[]{:S(2)}, u32[]{:S(2)}) %collective-permute-start.4) | collective-permute-done | bytes 200736 | tf_op jit(solution)/shard_map/early_hop_1/ppermute | solution.py:286
  23.3 1.5 %collective-permute-start.8 = (bf16[1,128,1024]{2,1,0:T(8,128)(2,1)}, bf16[1,128,1024]{2,1,0:T(8,128)(2,1)S(1)}, u32[]{:S(2)}, u32[]{:S(2)}) collective-permute-start(bf16[1,128,1024]{2,1,0:T(8,128)(2,1)} %bitcast.10), channel_id=1, source_target_pairs={{0,2},{1,3},{2,0},{3,1},{4,6},{5,7},{6,4},{7,5},{8,10},{9,11},{10,... | collective-permute-start | bytes 786440 | tf_op jit(solution)/shard_map/amplitudes_bit_2/ppermute | solution.py:308
  24.8 2.5 %collective-permute-start.6 = (bf16[2,784,128]{2,1,0:T(8,128)(2,1)S(1)}, bf16[2,784,128]{2,1,0:T(8,128)(2,1)S(1)}, u32[]{:S(2)}, u32[]{:S(2)}) collective-permute-start(bf16[2,784,128]{2,1,0:T(8,128)(2,1)S(1)} %pad_maximum_fusion.2.refs_12_), channel_id=1, source_target_pairs={{0,16},{4,20},{16,24},{20,28},{24,8},{28,12},{8,0},{12,4},{1,17},{... | collective-permute-start | bytes 1204232 | tf_op jit(solution)/shard_map/late_hop_1/ppermute | solution.py:286
  29.3 1.6 %collective-permute-start.12 = (bf16[2,128,1024]{2,1,0:T(8,128)(2,1)S(1)}, bf16[2,128,1024]{2,1,0:T(8,128)(2,1)S(1)}, u32[]{:S(2)}, u32[]{:S(2)}) collective-permute-start(bf16[2,128,1024]{2,1,0:T(8,128)(2,1)S(1)} %pad_maximum_fusion), channel_id=1, source_target_pairs={{0,2},{1,3},{2,0},{3,1},{4,6},{5,7},{6,4},{7,5},{8,10},{9,11},{10,... | collective-permute-start | bytes 1572872 | tf_op jit(solution)/shard_map/amplitudes_bit_2/ppermute | solution.py:308
  33.5 2.6 %collective-permute-start.14 = (bf16[2,784,128]{2,1,0:T(8,128)(2,1)S(1)}, bf16[2,784,128]{2,1,0:T(8,128)(2,1)S(1)}, u32[]{:S(2)}, u32[]{:S(2)}) collective-permute-start(bf16[2,784,128]{2,1,0:T(8,128)(2,1)S(1)} %constant_dynamic-update-slice_fusion.refs_13_), channel_id=1, source_target_pairs={{0,16},{4,20},{16,24},{20,28},{24,8},{28,12},{8,0},{12,4},{1,17},{... | collective-permute-start | bytes 1204232 | tf_op jit(solution)/shard_map/first_hop_2/ppermute | solution.py:286
  36.2 1.6 %collective-permute-start.15 = (bf16[2,784,128]{2,1,0:T(8,128)(2,1)S(1)}, bf16[2,784,128]{2,1,0:T(8,128)(2,1)S(1)}, u32[]{:S(2)}, u32[]{:S(2)}) collective-permute-start(bf16[2,784,128]{2,1,0:T(8,128)(2,1)S(1)} %collective-permute-done.6.refs_14_), channel_id=1, source_target_pairs={{0,16},{4,20},{16,24},{20,28},{24,8},{28,12},{8,0},{12,4},{1,17},{... | collective-permute-start | bytes 1204232 | tf_op jit(solution)/shard_map/late_hop_2/ppermute | solution.py:286
  37.8 3.3 %collective-permute-done.12.refs_7_.refs_0_ = bf16[2,128,1024]{2,1,0:T(8,128)(2,1)S(1)} collective-permute-done((bf16[2,128,1024]{2,1,0:T(8,128)(2,1)S(1)}, bf16[2,128,1024]{2,1,0:T(8,128)(2,1)S(1)}, u32[]{:S(2)}, u32[]{:S(2)}) %collective-permute-start.12) | collective-permute-done | bytes 524320 | tf_op jit(solution)/shard_map/amplitudes_bit_2/ppermute | solution.py:308
  42.2 3.3 %collective-permute-done.14.refs_10_ = bf16[2,784,128]{2,1,0:T(8,128)(2,1)S(1)} collective-permute-done((bf16[2,784,128]{2,1,0:T(8,128)(2,1)S(1)}, bf16[2,784,128]{2,1,0:T(8,128)(2,1)S(1)}, u32[]{:S(2)}, u32[]{:S(2)}) %collective-permute-start.14) | collective-permute-done | bytes 401440 | tf_op jit(solution)/shard_map/first_hop_2/ppermute | solution.py:286
  45.5 5.4 %collective-permute-done.15.refs_11_ = bf16[2,784,128]{2,1,0:T(8,128)(2,1)S(1)} collective-permute-done((bf16[2,784,128]{2,1,0:T(8,128)(2,1)S(1)}, bf16[2,784,128]{2,1,0:T(8,128)(2,1)S(1)}, u32[]{:S(2)}, u32[]{:S(2)}) %collective-permute-start.15) | collective-permute-done | bytes 401440 | tf_op jit(solution)/shard_map/late_hop_2/ppermute | solution.py:286
  51.0 2.5 %collective-permute-start.16 = (bf16[2,784,128]{2,1,0:T(8,128)(2,1)S(1)}, bf16[2,784,128]{2,1,0:T(8,128)(2,1)S(1)}, u32[]{:S(2)}, u32[]{:S(2)}) collective-permute-start(bf16[2,784,128]{2,1,0:T(8,128)(2,1)S(1)} %collective-permute-done.14.refs_10_), channel_id=1, source_target_pairs={{0,16},{4,20},{16,24},{20,28},{24,8},{28,12},{8,0},{12,4},{1,17},{... | collective-permute-start | bytes 1204232 | tf_op jit(solution)/shard_map/first_hop_3/ppermute | solution.py:286
  53.6 4.1 %ladder_first.1 = (f32[9,512,128]{2,1,0:T(8,128)S(1)}, f32[256,128]{1,0:T(8,128)S(1)}, f32[256,1024]{1,0:T(8,128)S(1)}) custom-call(f32[2,128]{1,0:T(2,128)S(1)} %bitcast.17, f32[1,1024]{1,0:T(1,128)S(1)} %bitcast.15, bf16[1,128,1024]{2,1,0:T(8,128)(2,1)S(1)} %bitcast.7, bf16[1,128,1024]{2,1,0:T(8,128)(2,1)S(1)} %bitcast.12, ...), custom_call_target="tpu_custom_call" | custom-call | flops 1000000000 | bytes 1048576 | tf_op jit(solution)/shard_map/ladder_first/pallas_call | solution.py:344
  57.7 3.0 %ladder_middle.1 = (f32[9,512,128]{2,1,0:T(8,128)S(1)}, f32[256,1024]{1,0:T(8,128)S(1)}) custom-call(f32[9,512,128]{2,1,0:T(8,128)S(1)} %get-tuple-element.38.before, bf16[256,1024]{1,0:T(8,128)(2,1)S(1)} %copy-done.3, bf16[256,1024]{1,0:T(8,128)(2,1)S(1)} %copy-done, f32[256,128]{1,0:T(8,128)S(1)} %get-tuple-element.39.occupied, f32[1,1024]{1,0:T(1,128)S(1)} %bitcast.16, ...), custom_call_target="tpu_custom_call" | custom-call | flops 100000000 | bytes 1048576 | tf_op jit(solution)/shard_map/ladder_middle/pallas_call | solution.py:344
  60.8 2.0 %collective-permute-done.16.refs_7_ = bf16[2,784,128]{2,1,0:T(8,128)(2,1)S(1)} collective-permute-done((bf16[2,784,128]{2,1,0:T(8,128)(2,1)S(1)}, bf16[2,784,128]{2,1,0:T(8,128)(2,1)S(1)}, u32[]{:S(2)}, u32[]{:S(2)}) %collective-permute-start.16) | collective-permute-done | bytes 401440 | tf_op jit(solution)/shard_map/first_hop_3/ppermute | solution.py:286
  62.7 2.0 %ladder_last.1 = (f32[256,1024]{1,0:T(8,128)S(1)}, bf16[8,256,128]{2,1,0:T(8,128)(2,1)S(1)}) custom-call(f32[9,512,128]{2,1,0:T(8,128)S(1)} %get-tuple-element.40.before, f32[256,1024]{1,0:T(8,128)S(1)} %get-tuple-element.41.base, bf16[1,128,1024]{2,1,0:T(8,128)(2,1)S(1)} %bitcast.9, bf16[1,128,1024]{2,1,0:T(8,128)(2,1)S(1)} %bitcast.14, ...), custom_call_target="tpu_custom_call" | custom-call | flops 1000000000 | bytes 1048576 | tf_op jit(solution)/shard_map/ladder_last/pallas_call | solution.py:344
  64.8 2.3 %collective-permute-done.18.refs_3_ = bf16[2,784,128]{2,1,0:T(8,128)(2,1)S(1)} collective-permute-done((bf16[2,784,128]{2,1,0:T(8,128)(2,1)S(1)}, bf16[2,784,128]{2,1,0:T(8,128)(2,1)S(1)}, u32[]{:S(2)}, u32[]{:S(2)}) %collective-permute-start.18) | collective-permute-done | bytes 401440 | tf_op jit(solution)/shard_map/late_hop_3/ppermute | solution.py:286
  67.1 1.7 %collective-permute-done.19.refs_4_ = bf16[2,784,128]{2,1,0:T(8,128)(2,1)S(1)} collective-permute-done((bf16[2,784,128]{2,1,0:T(8,128)(2,1)S(1)}, bf16[2,784,128]{2,1,0:T(8,128)(2,1)S(1)}, u32[]{:S(2)}, u32[]{:S(2)}) %collective-permute-start.19) | collective-permute-done | bytes 401440 | tf_op jit(solution)/shard_map/ppermute | solution.py:276
  68.8 3.5 %update.1 = (bf16[256,1024]{1,0:T(8,128)(2,1)}, f32[256,1024]{1,0:T(8,128)}) custom-call(s32[2,8]{1,0:T(2,128)S(1)} %copy-done.6, bf16[256,1024]{1,0:T(8,128)(2,1)S(1)} %copy-done, f32[256,1024]{1,0:T(8,128)S(1)} %get-tuple-element.42.base, f32[256,1024]{1,0:T(8,128)S(1)} %get-tuple-element.43.inverse, ...), custom_call_target="tpu_custom_call" | custom-call | tf_op jit(solution)/shard_map/update/pallas_call | solution.py:408
  (42 shorter events, 9.1 us)
Async XLA Ops:
  0.6 52.9 %copy-start.5 = (f32[1024]{0:T(1024)S(1)}, f32[1024]{0:T(1024)}, u32[]{:S(2)}) copy-start(f32[1024]{0:T(1024)} %param.13) | copy-start | bytes 12292
  0.6 52.9 %copy-start.7 = (f32[256]{0:T(256)S(1)}, f32[256]{0:T(256)}, u32[]{:S(2)}) copy-start(f32[256]{0:T(256)} %param.12) | copy-start | bytes 3076
  3.8 49.7 %copy-start.1 = (bf16[128,1024]{1,0:T(8,128)(2,1)S(1)}, bf16[128,1024]{1,0:T(8,128)(2,1)}, u32[]{:S(2)}) copy-start(bf16[128,1024]{1,0:T(8,128)(2,1)} %get-tuple-element.32) | copy-start | bytes 786436
  3.8 49.7 %copy-start.2 = (bf16[128,1024]{1,0:T(8,128)(2,1)S(1)}, bf16[128,1024]{1,0:T(8,128)(2,1)}, u32[]{:S(2)}) copy-start(bf16[128,1024]{1,0:T(8,128)(2,1)} %get-tuple-element.33) | copy-start | bytes 786436
  3.8 8.7 %collective-permute-start.2 = (bf16[1,784,128]{2,1,0:T(8,128)(2,1)}, bf16[1,784,128]{2,1,0:T(8,128)(2,1)S(1)}, u32[]{:S(2)}, u32[]{:S(2)}) collective-permute-start(bf16[1,784,128]{2,1,0:T(8,128)(2,1)} %get-tuple-element.28.refs_10_), channel_id=1, source_target_pairs={{0,16},{4,20},{16,24},{20,28},{24,8},{28,12},{8,0},{12,4},{1,17},{... | collective-permute-start | bytes 602120 | tf_op jit(solution)/shard_map/near_hop_1/ppermute | solution.py:286
  7.9 8.1 %collective-permute-start.3 = (bf16[1,784,128]{2,1,0:T(8,128)(2,1)}, bf16[1,784,128]{2,1,0:T(8,128)(2,1)S(1)}, u32[]{:S(2)}, u32[]{:S(2)}) collective-permute-start(bf16[1,784,128]{2,1,0:T(8,128)(2,1)} %get-tuple-element.29), channel_id=1, source_target_pairs={{0,1},{1,0},{2,3},{3,2},{4,5},{5,4},{6,7},{7,6},{8,9},{9,8},{10,11... | collective-permute-start | bytes 602120 | tf_op jit(solution)/shard_map/parcels_from_partner_1/ppermute | solution.py:273
  9.4 10.7 %collective-permute-start = (bf16[1,784,128]{2,1,0:T(8,128)(2,1)}, bf16[1,784,128]{2,1,0:T(8,128)(2,1)S(1)}, u32[]{:S(2)}, u32[]{:S(2)}) collective-permute-start(bf16[1,784,128]{2,1,0:T(8,128)(2,1)} %get-tuple-element.26), channel_id=1, source_target_pairs={{0,2},{1,3},{2,0},{3,1},{4,6},{5,7},{6,4},{7,5},{8,10},{9,11},{10,... | collective-permute-start | bytes 602120 | tf_op jit(solution)/shard_map/parcels_from_partner_2/ppermute | solution.py:273
  10.9 9.2 %collective-permute-start.1 = (bf16[1,784,128]{2,1,0:T(8,128)(2,1)}, bf16[1,784,128]{2,1,0:T(8,128)(2,1)S(1)}, u32[]{:S(2)}, u32[]{:S(2)}) collective-permute-start(bf16[1,784,128]{2,1,0:T(8,128)(2,1)} %get-tuple-element.27), channel_id=1, source_target_pairs={{0,3},{1,2},{2,1},{3,0},{4,7},{5,6},{6,5},{7,4},{8,11},{9,10},{10,... | collective-permute-start | bytes 602120 | tf_op jit(solution)/shard_map/parcels_from_partner_3/ppermute | solution.py:273
  16.0 5.7 %collective-permute-start.4 = (bf16[1,784,128]{2,1,0:T(8,128)(2,1)S(1)}, bf16[1,784,128]{2,1,0:T(8,128)(2,1)S(1)}, u32[]{:S(2)}, u32[]{:S(2)}) collective-permute-start(bf16[1,784,128]{2,1,0:T(8,128)(2,1)S(1)} %collective-permute-done.3.refs_11_), channel_id=1, source_target_pairs={{0,16},{4,20},{16,24},{20,28},{24,8},{28,12},{8,0},{12,4},{1,17},{... | collective-permute-start | bytes 602120 | tf_op jit(solution)/shard_map/early_hop_1/ppermute | solution.py:286
  21.8 6.6 %collective-permute-start.5 = (bf16[1,128,1024]{2,1,0:T(8,128)(2,1)}, bf16[1,128,1024]{2,1,0:T(8,128)(2,1)S(1)}, u32[]{:S(2)}, u32[]{:S(2)}) collective-permute-start(bf16[1,128,1024]{2,1,0:T(8,128)(2,1)} %bitcast.5), channel_id=1, source_target_pairs={{0,1},{1,0},{2,3},{3,2},{4,5},{5,4},{6,7},{7,6},{8,9},{9,8},{10,11... | collective-permute-start | bytes 786440 | tf_op jit(solution)/shard_map/amplitudes_bit_1/ppermute | solution.py:308
  23.3 8.7 %collective-permute-start.8 = (bf16[1,128,1024]{2,1,0:T(8,128)(2,1)}, bf16[1,128,1024]{2,1,0:T(8,128)(2,1)S(1)}, u32[]{:S(2)}, u32[]{:S(2)}) collective-permute-start(bf16[1,128,1024]{2,1,0:T(8,128)(2,1)} %bitcast.10), channel_id=1, source_target_pairs={{0,2},{1,3},{2,0},{3,1},{4,6},{5,7},{6,4},{7,5},{8,10},{9,11},{10,... | collective-permute-start | bytes 786440 | tf_op jit(solution)/shard_map/amplitudes_bit_2/ppermute | solution.py:308
  24.8 11.4 %collective-permute-start.6 = (bf16[2,784,128]{2,1,0:T(8,128)(2,1)S(1)}, bf16[2,784,128]{2,1,0:T(8,128)(2,1)S(1)}, u32[]{:S(2)}, u32[]{:S(2)}) collective-permute-start(bf16[2,784,128]{2,1,0:T(8,128)(2,1)S(1)} %pad_maximum_fusion.2.refs_12_), channel_id=1, source_target_pairs={{0,16},{4,20},{16,24},{20,28},{24,8},{28,12},{8,0},{12,4},{1,17},{... | collective-permute-start | bytes 1204232 | tf_op jit(solution)/shard_map/late_hop_1/ppermute | solution.py:286
  29.3 11.7 %collective-permute-start.12 = (bf16[2,128,1024]{2,1,0:T(8,128)(2,1)S(1)}, bf16[2,128,1024]{2,1,0:T(8,128)(2,1)S(1)}, u32[]{:S(2)}, u32[]{:S(2)}) collective-permute-start(bf16[2,128,1024]{2,1,0:T(8,128)(2,1)S(1)} %pad_maximum_fusion), channel_id=1, source_target_pairs={{0,2},{1,3},{2,0},{3,1},{4,6},{5,7},{6,4},{7,5},{8,10},{9,11},{10,... | collective-permute-start | bytes 1572872 | tf_op jit(solution)/shard_map/amplitudes_bit_2/ppermute | solution.py:308
  33.0 9.2 %collective-permute-start.10 = (bf16[2,128,1024]{2,1,0:T(8,128)(2,1)S(1)}, bf16[2,128,1024]{2,1,0:T(8,128)(2,1)S(1)}, u32[]{:S(2)}, u32[]{:S(2)}) collective-permute-start(bf16[2,128,1024]{2,1,0:T(8,128)(2,1)S(1)} %pad_maximum_fusion.1), channel_id=1, source_target_pairs={{0,1},{1,0},{2,3},{3,2},{4,5},{5,4},{6,7},{7,6},{8,9},{9,8},{10,11... | collective-permute-start | bytes 1572872 | tf_op jit(solution)/shard_map/amplitudes_bit_1/ppermute | solution.py:308
  33.5 12.0 %collective-permute-start.14 = (bf16[2,784,128]{2,1,0:T(8,128)(2,1)S(1)}, bf16[2,784,128]{2,1,0:T(8,128)(2,1)S(1)}, u32[]{:S(2)}, u32[]{:S(2)}) collective-permute-start(bf16[2,784,128]{2,1,0:T(8,128)(2,1)S(1)} %constant_dynamic-update-slice_fusion.refs_13_), channel_id=1, source_target_pairs={{0,16},{4,20},{16,24},{20,28},{24,8},{28,12},{8,0},{12,4},{1,17},{... | collective-permute-start | bytes 1204232 | tf_op jit(solution)/shard_map/first_hop_2/ppermute | solution.py:286
  36.2 14.8 %collective-permute-start.15 = (bf16[2,784,128]{2,1,0:T(8,128)(2,1)S(1)}, bf16[2,784,128]{2,1,0:T(8,128)(2,1)S(1)}, u32[]{:S(2)}, u32[]{:S(2)}) collective-permute-start(bf16[2,784,128]{2,1,0:T(8,128)(2,1)S(1)} %collective-permute-done.6.refs_14_), channel_id=1, source_target_pairs={{0,16},{4,20},{16,24},{20,28},{24,8},{28,12},{8,0},{12,4},{1,17},{... | collective-permute-start | bytes 1204232 | tf_op jit(solution)/shard_map/late_hop_2/ppermute | solution.py:286
  37.8 15.7 %collective-permute-start.9 = (bf16[2,128,1024]{2,1,0:T(8,128)(2,1)S(1)}, bf16[2,128,1024]{2,1,0:T(8,128)(2,1)S(1)}, u32[]{:S(2)}, u32[]{:S(2)}) collective-permute-start(bf16[2,128,1024]{2,1,0:T(8,128)(2,1)S(1)} %pad_maximum_fusion.1), channel_id=1, source_target_pairs={{0,4},{4,0},{8,12},{12,8},{16,20},{20,16},{24,28},{28,24},{1,5},{5... | collective-permute-start | bytes 1572872 | tf_op jit(solution)/shard_map/twin_of_bit_2/ppermute | solution.py:276
  41.1 12.4 %collective-permute-start.7 = (bf16[2,128,1024]{2,1,0:T(8,128)(2,1)S(1)}, bf16[2,128,1024]{2,1,0:T(8,128)(2,1)S(1)}, u32[]{:S(2)}, u32[]{:S(2)}) collective-permute-start(bf16[2,128,1024]{2,1,0:T(8,128)(2,1)S(1)} %pad_maximum_fusion), channel_id=1, source_target_pairs={{0,4},{4,0},{8,12},{12,8},{16,20},{20,16},{24,28},{28,24},{1,5},{5... | collective-permute-start | bytes 1572872 | tf_op jit(solution)/shard_map/twin_of_bit_1/ppermute | solution.py:276
  42.2 11.3 %collective-permute-start.13 = (bf16[2,128,1024]{2,1,0:T(8,128)(2,1)S(1)}, bf16[2,128,1024]{2,1,0:T(8,128)(2,1)S(1)}, u32[]{:S(2)}, u32[]{:S(2)}) collective-permute-start(bf16[2,128,1024]{2,1,0:T(8,128)(2,1)S(1)} %collective-permute-done.12.refs_7_.refs_0_), channel_id=1, source_target_pairs={{0,4},{4,0},{8,12},{12,8},{16,20},{20,16},{24,28},{28,24},{1,5},{5... | collective-permute-start | bytes 1572872 | tf_op jit(solution)/shard_map/twin_of_bit_2/ppermute | solution.py:276
  45.5 7.9 %collective-permute-start.11 = (bf16[2,128,1024]{2,1,0:T(8,128)(2,1)S(1)}, bf16[2,128,1024]{2,1,0:T(8,128)(2,1)S(1)}, u32[]{:S(2)}, u32[]{:S(2)}) collective-permute-start(bf16[2,128,1024]{2,1,0:T(8,128)(2,1)S(1)} %collective-permute-done.10.refs_5_.refs_2_), channel_id=1, source_target_pairs={{0,4},{4,0},{8,12},{12,8},{16,20},{20,16},{24,28},{28,24},{1,5},{5... | collective-permute-start | bytes 1572872 | tf_op jit(solution)/shard_map/twin_of_bit_1/ppermute | solution.py:276
  51.0 11.8 %collective-permute-start.16 = (bf16[2,784,128]{2,1,0:T(8,128)(2,1)S(1)}, bf16[2,784,128]{2,1,0:T(8,128)(2,1)S(1)}, u32[]{:S(2)}, u32[]{:S(2)}) collective-permute-start(bf16[2,784,128]{2,1,0:T(8,128)(2,1)S(1)} %collective-permute-done.14.refs_10_), channel_id=1, source_target_pairs={{0,16},{4,20},{16,24},{20,28},{24,8},{28,12},{8,0},{12,4},{1,17},{... | collective-permute-start | bytes 1204232 | tf_op jit(solution)/shard_map/first_hop_3/ppermute | solution.py:286
  53.4 13.6 %collective-permute-start.18 = (bf16[2,784,128]{2,1,0:T(8,128)(2,1)S(1)}, bf16[2,784,128]{2,1,0:T(8,128)(2,1)S(1)}, u32[]{:S(2)}, u32[]{:S(2)}) collective-permute-start(bf16[2,784,128]{2,1,0:T(8,128)(2,1)S(1)} %collective-permute-done.15.refs_11_), channel_id=1, source_target_pairs={{0,16},{4,20},{16,24},{20,28},{24,8},{28,12},{8,0},{12,4},{1,17},{... | collective-permute-start | bytes 1204232 | tf_op jit(solution)/shard_map/late_hop_3/ppermute | solution.py:286
  64.7 4.1 %collective-permute-start.17 = (bf16[8,256,128]{2,1,0:T(8,128)(2,1)S(1)}, bf16[8,256,128]{2,1,0:T(8,128)(2,1)S(1)}, u32[]{:S(2)}, u32[]{:S(2)}) collective-permute-start(bf16[8,256,128]{2,1,0:T(8,128)(2,1)S(1)} %get-tuple-element.44), channel_id=1, source_target_pairs={{0,4},{4,0},{8,12},{12,8},{16,20},{20,16},{24,28},{28,24},{1,5},{5... | collective-permute-start | bytes 1572872 | tf_op jit(solution)/shard_map/ppermute | solution.py:276
  67.0 1.7 %collective-permute-start.19 = (bf16[2,784,128]{2,1,0:T(8,128)(2,1)S(1)}, bf16[2,784,128]{2,1,0:T(8,128)(2,1)S(1)}, u32[]{:S(2)}, u32[]{:S(2)}) collective-permute-start(bf16[2,784,128]{2,1,0:T(8,128)(2,1)S(1)} %collective-permute-done.18.refs_3_), channel_id=1, source_target_pairs={{0,4},{4,0},{8,12},{12,8},{16,20},{20,16},{24,28},{28,24},{1,5},{5... | collective-permute-start | bytes 1204232 | tf_op jit(solution)/shard_map/ppermute | solution.py:276
  (4 other events, 64.1 us)

commit v9 on v8

--- a/solution.py
+++ b/solution.py
@@ -317,7 +317,7 @@
         return own, twin
 
     bits = [1 << i for i in range((n_v - 1).bit_length())]
-    upper, lower = after((upper, lower), (hops["late"][0], hops["early"][1]))
+    upper, lower = after((upper, lower), hops["near"][1])
     upper_own, upper_twin = gather_amplitudes(upper, bits)
     lower_own, lower_twin = gather_amplitudes(lower, bits[::-1])
 

time: 72.5 us -> 72.7 us (level)
    ppermute x4, waiting for transfers between devices: 6.57 us -> 10.1 us  [gather_amplitudes(): now = lax.ppermute(held, 'vpair', [(i, i ^ bit) for i in range(n_v)])]
    ppermute x3, waiting for transfers between devices: 6.03 us -> 3.49 us  [across_v(): return lax.ppermute(value, 'vpair', [(i, i ^ j) for i in range(n_v)])]
    ppermute x7, waiting for transfers between devices: 15.7 us -> 14.2 us  [next_on_ring(): return lax.ppermute(value, 'opair', pairs)]
  transfers between devices with their start and end apart: 20 -> 20, of which waited for: 13 -> 11; matrix products, arithmetic and copies ran while one was open for 3% -> 3% of each run, Pallas kernels for 13% -> 13%
where the time goes in v9:
time: 72.7 us; the launch traced here: 72.5 us
  waiting for transfers between devices  29.5 us (41%)
  starting transfers between devices  24.2 us (33%)
  Pallas kernels  15.8 us (22%)
  other arithmetic  2.04 us (3%)
  between operations  0.83 us (1%)
    ppermute x7, starting transfers between devices, next_on_ring(): return lax.ppermute(value, 'opair', pairs)  15.4 us
    ppermute x7, waiting for transfers between devices, next_on_ring(): return lax.ppermute(value, 'opair', pairs)  14.2 us
    ppermute x4, waiting for transfers between devices, gather_amplitudes(): now = lax.ppermute(held, 'vpair', [(i, i ^ bit) for i in range(n_v)])  10.1 us
    pallas_call x3, Pallas kernels, ladder_call(): pl.pallas_call(functools.partial(kernel, cap, layout, where), out_shape=o...  9.16 us
    ppermute x4, starting transfers between devices, gather_amplitudes(): now = lax.ppermute(held, 'vpair', [(i, i ^ bit) for i in range(n_v)])  5.2 us
    pallas_call x1, Pallas kernels, on_device(): pl.pallas_call(functools.partial(update_kernel, cap, behind, where), out_...  3.5 us
    ppermute x3, waiting for transfers between devices, across_v(): return lax.ppermute(value, 'vpair', [(i, i ^ j) for i in range(n_v)])  3.49 us
    ppermute x3, starting transfers between devices, across_v(): return lax.ppermute(value, 'vpair', [(i, i ^ j) for i in range(n_v)])  3.49 us
  transfers between devices with their start and end apart: 20, of which 11 were waited for; matrix products, arithmetic and copies ran while one was open for 3% of the time, Pallas kernels for 13%

profile of v9, /device:TPU:0, one launch (start us, length us, event | category | flops | bytes accessed | tf_op | source)
XLA Modules:
  0.0 72.5 jit_solution(7620534637209651636)
XLA Ops:
  0.7 3.1 %pack.1 = (bf16[1,784,128]{2,1,0:T(8,128)(2,1)}, bf16[1,784,128]{2,1,0:T(8,128)(2,1)}, bf16[1,784,128]{2,1,0:T(8,128)(2,1)}, bf16[1,784,128]{2,1,0:T(8,128)(2,1)...) custom-call(s32[3,8]{1,0:T(4,128)} %bitcast.18, s32[2,8]{1,0:T(2,128)} %live.3, ...), custom_call_target="tpu_custom_call" | custom-call | tf_op jit(solution)/shard_map/pack/pallas_call | solution.py:251
  3.8 4.1 %collective-permute-start = (bf16[1,784,128]{2,1,0:T(8,128)(2,1)}, bf16[1,784,128]{2,1,0:T(8,128)(2,1)S(1)}, u32[]{:S(2)}, u32[]{:S(2)}) collective-permute-start(bf16[1,784,128]{2,1,0:T(8,128)(2,1)} %get-tuple-element.26.refs_10_), channel_id=1, source_target_pairs={{0,16},{4,20},{16,24},{20,28},{24,8},{28,12},{8,0},{12,4},{1,17},{... | collective-permute-start | bytes 602120 | tf_op jit(solution)/shard_map/near_hop_1/ppermute | solution.py:286
  7.9 1.5 %collective-permute-start.4 = (bf16[1,784,128]{2,1,0:T(8,128)(2,1)}, bf16[1,784,128]{2,1,0:T(8,128)(2,1)S(1)}, u32[]{:S(2)}, u32[]{:S(2)}) collective-permute-start(bf16[1,784,128]{2,1,0:T(8,128)(2,1)} %get-tuple-element.31), channel_id=1, source_target_pairs={{0,1},{1,0},{2,3},{3,2},{4,5},{5,4},{6,7},{7,6},{8,9},{9,8},{10,11... | collective-permute-start | bytes 602120 | tf_op jit(solution)/shard_map/parcels_from_partner_1/ppermute | solution.py:273
  9.4 1.5 %collective-permute-start.2 = (bf16[1,784,128]{2,1,0:T(8,128)(2,1)}, bf16[1,784,128]{2,1,0:T(8,128)(2,1)S(1)}, u32[]{:S(2)}, u32[]{:S(2)}) collective-permute-start(bf16[1,784,128]{2,1,0:T(8,128)(2,1)} %get-tuple-element.29), channel_id=1, source_target_pairs={{0,2},{1,3},{2,0},{3,1},{4,6},{5,7},{6,4},{7,5},{8,10},{9,11},{10,... | collective-permute-start | bytes 602120 | tf_op jit(solution)/shard_map/parcels_from_partner_2/ppermute | solution.py:273
  12.5 1.5 %collective-permute-start.7 = (bf16[1,128,1024]{2,1,0:T(8,128)(2,1)}, bf16[1,128,1024]{2,1,0:T(8,128)(2,1)S(1)}, u32[]{:S(2)}, u32[]{:S(2)}) collective-permute-start(bf16[1,128,1024]{2,1,0:T(8,128)(2,1)} %bitcast.10), channel_id=1, source_target_pairs={{0,2},{1,3},{2,0},{3,1},{4,6},{5,7},{6,4},{7,5},{8,10},{9,11},{10,... | collective-permute-start | bytes 786440 | tf_op jit(solution)/shard_map/amplitudes_bit_2/ppermute | solution.py:308
  14.0 1.5 %collective-permute-start.1 = (bf16[1,128,1024]{2,1,0:T(8,128)(2,1)}, bf16[1,128,1024]{2,1,0:T(8,128)(2,1)S(1)}, u32[]{:S(2)}, u32[]{:S(2)}) collective-permute-start(bf16[1,128,1024]{2,1,0:T(8,128)(2,1)} %bitcast.5), channel_id=1, source_target_pairs={{0,1},{1,0},{2,3},{3,2},{4,5},{5,4},{6,7},{7,6},{8,9},{9,8},{10,11... | collective-permute-start | bytes 786440 | tf_op jit(solution)/shard_map/amplitudes_bit_1/ppermute | solution.py:308
  16.0 2.7 %collective-permute-start.13 = (bf16[1,784,128]{2,1,0:T(8,128)(2,1)S(1)}, bf16[1,784,128]{2,1,0:T(8,128)(2,1)S(1)}, u32[]{:S(2)}, u32[]{:S(2)}) collective-permute-start(bf16[1,784,128]{2,1,0:T(8,128)(2,1)S(1)} %collective-permute-done.4.refs_11_), channel_id=1, source_target_pairs={{0,16},{4,20},{16,24},{20,28},{24,8},{28,12},{8,0},{12,4},{1,17},{... | collective-permute-start | bytes 602120 | tf_op jit(solution)/shard_map/early_hop_1/ppermute | solution.py:286
  18.8 2.9 %collective-permute-done.2 = bf16[1,784,128]{2,1,0:T(8,128)(2,1)S(1)} collective-permute-done((bf16[1,784,128]{2,1,0:T(8,128)(2,1)}, bf16[1,784,128]{2,1,0:T(8,128)(2,1)S(1)}, u32[]{:S(2)}, u32[]{:S(2)}) %collective-permute-start.2) | collective-permute-done | bytes 200736 | tf_op jit(solution)/shard_map/parcels_from_partner_2/ppermute | solution.py:273
  21.8 1.3 %collective-permute-start.5 = (bf16[2,784,128]{2,1,0:T(8,128)(2,1)S(1)}, bf16[2,784,128]{2,1,0:T(8,128)(2,1)S(1)}, u32[]{:S(2)}, u32[]{:S(2)}) collective-permute-start(bf16[2,784,128]{2,1,0:T(8,128)(2,1)S(1)} %pad_maximum_fusion.2.refs_12_), channel_id=1, source_target_pairs={{0,16},{4,20},{16,24},{20,28},{24,8},{28,12},{8,0},{12,4},{1,17},{... | collective-permute-start | bytes 1204232 | tf_op jit(solution)/shard_map/late_hop_1/ppermute | solution.py:286
  23.0 2.7 %collective-permute-done.7.refs_8_.refs_1_ = bf16[1,128,1024]{2,1,0:T(8,128)(2,1)S(1)} collective-permute-done((bf16[1,128,1024]{2,1,0:T(8,128)(2,1)}, bf16[1,128,1024]{2,1,0:T(8,128)(2,1)S(1)}, u32[]{:S(2)}, u32[]{:S(2)}) %collective-permute-start.7) | collective-permute-done | bytes 262176 | tf_op jit(solution)/shard_map/amplitudes_bit_2/ppermute | solution.py:308
  28.3 1.6 %collective-permute-start.11 = (bf16[2,128,1024]{2,1,0:T(8,128)(2,1)S(1)}, bf16[2,128,1024]{2,1,0:T(8,128)(2,1)S(1)}, u32[]{:S(2)}, u32[]{:S(2)}) collective-permute-start(bf16[2,128,1024]{2,1,0:T(8,128)(2,1)S(1)} %pad_maximum_fusion), channel_id=1, source_target_pairs={{0,2},{1,3},{2,0},{3,1},{4,6},{5,7},{6,4},{7,5},{8,10},{9,11},{10,... | collective-permute-start | bytes 1572872 | tf_op jit(solution)/shard_map/amplitudes_bit_2/ppermute | solution.py:308
  30.0 1.6 %collective-permute-start.14 = (bf16[2,784,128]{2,1,0:T(8,128)(2,1)S(1)}, bf16[2,784,128]{2,1,0:T(8,128)(2,1)S(1)}, u32[]{:S(2)}, u32[]{:S(2)}) collective-permute-start(bf16[2,784,128]{2,1,0:T(8,128)(2,1)S(1)} %constant_dynamic-update-slice_fusion.refs_13_), channel_id=1, source_target_pairs={{0,16},{4,20},{16,24},{20,28},{24,8},{28,12},{8,0},{12,4},{1,17},{... | collective-permute-start | bytes 1204232 | tf_op jit(solution)/shard_map/first_hop_2/ppermute | solution.py:286
  31.6 2.4 %collective-permute-start.15 = (bf16[2,784,128]{2,1,0:T(8,128)(2,1)S(1)}, bf16[2,784,128]{2,1,0:T(8,128)(2,1)S(1)}, u32[]{:S(2)}, u32[]{:S(2)}) collective-permute-start(bf16[2,784,128]{2,1,0:T(8,128)(2,1)S(1)} %collective-permute-done.5.refs_14_), channel_id=1, source_target_pairs={{0,16},{4,20},{16,24},{20,28},{24,8},{28,12},{8,0},{12,4},{1,17},{... | collective-permute-start | bytes 1204232 | tf_op jit(solution)/shard_map/late_hop_2/ppermute | solution.py:286
  34.0 5.1 %collective-permute-done.9.refs_5_.refs_2_ = bf16[2,128,1024]{2,1,0:T(8,128)(2,1)S(1)} collective-permute-done((bf16[2,128,1024]{2,1,0:T(8,128)(2,1)S(1)}, bf16[2,128,1024]{2,1,0:T(8,128)(2,1)S(1)}, u32[]{:S(2)}, u32[]{:S(2)}) %collective-permute-start.9) | collective-permute-done | bytes 524320 | tf_op jit(solution)/shard_map/amplitudes_bit_1/ppermute | solution.py:308
  39.1 2.3 %collective-permute-done.11.refs_7_.refs_0_ = bf16[2,128,1024]{2,1,0:T(8,128)(2,1)S(1)} collective-permute-done((bf16[2,128,1024]{2,1,0:T(8,128)(2,1)S(1)}, bf16[2,128,1024]{2,1,0:T(8,128)(2,1)S(1)}, u32[]{:S(2)}, u32[]{:S(2)}) %collective-permute-start.11) | collective-permute-done | bytes 524320 | tf_op jit(solution)/shard_map/amplitudes_bit_2/ppermute | solution.py:308
  42.3 6.0 %collective-permute-done.15.refs_11_ = bf16[2,784,128]{2,1,0:T(8,128)(2,1)S(1)} collective-permute-done((bf16[2,784,128]{2,1,0:T(8,128)(2,1)S(1)}, bf16[2,784,128]{2,1,0:T(8,128)(2,1)S(1)}, u32[]{:S(2)}, u32[]{:S(2)}) %collective-permute-start.15) | collective-permute-done | bytes 401440 | tf_op jit(solution)/shard_map/late_hop_2/ppermute | solution.py:286
  48.3 3.3 %collective-permute-start.16 = (bf16[2,784,128]{2,1,0:T(8,128)(2,1)S(1)}, bf16[2,784,128]{2,1,0:T(8,128)(2,1)S(1)}, u32[]{:S(2)}, u32[]{:S(2)}) collective-permute-start(bf16[2,784,128]{2,1,0:T(8,128)(2,1)S(1)} %collective-permute-done.14.refs_10_), channel_id=1, source_target_pairs={{0,16},{4,20},{16,24},{20,28},{24,8},{28,12},{8,0},{12,4},{1,17},{... | collective-permute-start | bytes 1204232 | tf_op jit(solution)/shard_map/first_hop_3/ppermute | solution.py:286
  51.7 4.1 %ladder_first.1 = (f32[9,512,128]{2,1,0:T(8,128)S(1)}, f32[256,128]{1,0:T(8,128)S(1)}, f32[256,1024]{1,0:T(8,128)S(1)}) custom-call(f32[2,128]{1,0:T(2,128)S(1)} %bitcast.17, f32[1,1024]{1,0:T(1,128)S(1)} %bitcast.15, bf16[1,128,1024]{2,1,0:T(8,128)(2,1)S(1)} %bitcast.7, bf16[1,128,1024]{2,1,0:T(8,128)(2,1)S(1)} %bitcast.12, ...), custom_call_target="tpu_custom_call" | custom-call | flops 1000000000 | bytes 1048576 | tf_op jit(solution)/shard_map/ladder_first/pallas_call | solution.py:344
  55.9 3.1 %ladder_middle.1 = (f32[9,512,128]{2,1,0:T(8,128)S(1)}, f32[256,1024]{1,0:T(8,128)S(1)}) custom-call(f32[9,512,128]{2,1,0:T(8,128)S(1)} %get-tuple-element.38.before, bf16[256,1024]{1,0:T(8,128)(2,1)S(1)} %copy-done.3, bf16[256,1024]{1,0:T(8,128)(2,1)S(1)} %copy-done, f32[256,128]{1,0:T(8,128)S(1)} %get-tuple-element.39.occupied, f32[1,1024]{1,0:T(1,128)S(1)} %bitcast.16, ...), custom_call_target="tpu_custom_call" | custom-call | flops 100000000 | bytes 1048576 | tf_op jit(solution)/shard_map/ladder_middle/pallas_call | solution.py:344
  58.9 2.4 %collective-permute-done.16.refs_7_ = bf16[2,784,128]{2,1,0:T(8,128)(2,1)S(1)} collective-permute-done((bf16[2,784,128]{2,1,0:T(8,128)(2,1)S(1)}, bf16[2,784,128]{2,1,0:T(8,128)(2,1)S(1)}, u32[]{:S(2)}, u32[]{:S(2)}) %collective-permute-start.16) | collective-permute-done | bytes 401440 | tf_op jit(solution)/shard_map/first_hop_3/ppermute | solution.py:286
  61.3 2.0 %ladder_last.1 = (f32[256,1024]{1,0:T(8,128)S(1)}, bf16[8,256,128]{2,1,0:T(8,128)(2,1)S(1)}) custom-call(f32[9,512,128]{2,1,0:T(8,128)S(1)} %get-tuple-element.40.before, f32[256,1024]{1,0:T(8,128)S(1)} %get-tuple-element.41.base, bf16[1,128,1024]{2,1,0:T(8,128)(2,1)S(1)} %bitcast.9, bf16[1,128,1024]{2,1,0:T(8,128)(2,1)S(1)} %bitcast.14, ...), custom_call_target="tpu_custom_call" | custom-call | flops 1000000000 | bytes 1048576 | tf_op jit(solution)/shard_map/ladder_last/pallas_call | solution.py:344
  63.4 3.9 %collective-permute-done.18.refs_3_ = bf16[2,784,128]{2,1,0:T(8,128)(2,1)S(1)} collective-permute-done((bf16[2,784,128]{2,1,0:T(8,128)(2,1)S(1)}, bf16[2,784,128]{2,1,0:T(8,128)(2,1)S(1)}, u32[]{:S(2)}, u32[]{:S(2)}) %collective-permute-start.18) | collective-permute-done | bytes 401440 | tf_op jit(solution)/shard_map/late_hop_3/ppermute | solution.py:286
  67.3 1.7 %collective-permute-done.19.refs_4_ = bf16[2,784,128]{2,1,0:T(8,128)(2,1)S(1)} collective-permute-done((bf16[2,784,128]{2,1,0:T(8,128)(2,1)S(1)}, bf16[2,784,128]{2,1,0:T(8,128)(2,1)S(1)}, u32[]{:S(2)}, u32[]{:S(2)}) %collective-permute-start.19) | collective-permute-done | bytes 401440 | tf_op jit(solution)/shard_map/ppermute | solution.py:276
  69.0 3.5 %update.1 = (bf16[256,1024]{1,0:T(8,128)(2,1)}, f32[256,1024]{1,0:T(8,128)}) custom-call(s32[2,8]{1,0:T(2,128)S(1)} %copy-done.6, bf16[256,1024]{1,0:T(8,128)(2,1)S(1)} %copy-done, f32[256,1024]{1,0:T(8,128)S(1)} %get-tuple-element.42.base, f32[256,1024]{1,0:T(8,128)S(1)} %get-tuple-element.43.inverse, ...), custom_call_target="tpu_custom_call" | custom-call | tf_op jit(solution)/shard_map/update/pallas_call | solution.py:408
  (42 shorter events, 5.8 us)
Async XLA Ops:
  0.6 51.0 %copy-start.5 = (f32[1024]{0:T(1024)S(1)}, f32[1024]{0:T(1024)}, u32[]{:S(2)}) copy-start(f32[1024]{0:T(1024)} %param.13) | copy-start | bytes 12292
  0.6 51.0 %copy-start.7 = (f32[256]{0:T(256)S(1)}, f32[256]{0:T(256)}, u32[]{:S(2)}) copy-start(f32[256]{0:T(256)} %param.12) | copy-start | bytes 3076
  3.8 47.9 %copy-start.1 = (bf16[128,1024]{1,0:T(8,128)(2,1)S(1)}, bf16[128,1024]{1,0:T(8,128)(2,1)}, u32[]{:S(2)}) copy-start(bf16[128,1024]{1,0:T(8,128)(2,1)} %get-tuple-element.27) | copy-start | bytes 786436
  3.8 47.9 %copy-start.2 = (bf16[128,1024]{1,0:T(8,128)(2,1)S(1)}, bf16[128,1024]{1,0:T(8,128)(2,1)}, u32[]{:S(2)}) copy-start(bf16[128,1024]{1,0:T(8,128)(2,1)} %get-tuple-element.28) | copy-start | bytes 786436
  3.8 8.7 %collective-permute-start = (bf16[1,784,128]{2,1,0:T(8,128)(2,1)}, bf16[1,784,128]{2,1,0:T(8,128)(2,1)S(1)}, u32[]{:S(2)}, u32[]{:S(2)}) collective-permute-start(bf16[1,784,128]{2,1,0:T(8,128)(2,1)} %get-tuple-element.26.refs_10_), channel_id=1, source_target_pairs={{0,16},{4,20},{16,24},{20,28},{24,8},{28,12},{8,0},{12,4},{1,17},{... | collective-permute-start | bytes 602120 | tf_op jit(solution)/shard_map/near_hop_1/ppermute | solution.py:286
  7.9 8.1 %collective-permute-start.4 = (bf16[1,784,128]{2,1,0:T(8,128)(2,1)}, bf16[1,784,128]{2,1,0:T(8,128)(2,1)S(1)}, u32[]{:S(2)}, u32[]{:S(2)}) collective-permute-start(bf16[1,784,128]{2,1,0:T(8,128)(2,1)} %get-tuple-element.31), channel_id=1, source_target_pairs={{0,1},{1,0},{2,3},{3,2},{4,5},{5,4},{6,7},{7,6},{8,9},{9,8},{10,11... | collective-permute-start | bytes 602120 | tf_op jit(solution)/shard_map/parcels_from_partner_1/ppermute | solution.py:273
  9.4 12.3 %collective-permute-start.2 = (bf16[1,784,128]{2,1,0:T(8,128)(2,1)}, bf16[1,784,128]{2,1,0:T(8,128)(2,1)S(1)}, u32[]{:S(2)}, u32[]{:S(2)}) collective-permute-start(bf16[1,784,128]{2,1,0:T(8,128)(2,1)} %get-tuple-element.29), channel_id=1, source_target_pairs={{0,2},{1,3},{2,0},{3,1},{4,6},{5,7},{6,4},{7,5},{8,10},{9,11},{10,... | collective-permute-start | bytes 602120 | tf_op jit(solution)/shard_map/parcels_from_partner_2/ppermute | solution.py:273
  10.9 10.8 %collective-permute-start.3 = (bf16[1,784,128]{2,1,0:T(8,128)(2,1)}, bf16[1,784,128]{2,1,0:T(8,128)(2,1)S(1)}, u32[]{:S(2)}, u32[]{:S(2)}) collective-permute-start(bf16[1,784,128]{2,1,0:T(8,128)(2,1)} %get-tuple-element.30), channel_id=1, source_target_pairs={{0,3},{1,2},{2,1},{3,0},{4,7},{5,6},{6,5},{7,4},{8,11},{9,10},{10,... | collective-permute-start | bytes 602120 | tf_op jit(solution)/shard_map/parcels_from_partner_3/ppermute | solution.py:273
  12.5 13.2 %collective-permute-start.7 = (bf16[1,128,1024]{2,1,0:T(8,128)(2,1)}, bf16[1,128,1024]{2,1,0:T(8,128)(2,1)S(1)}, u32[]{:S(2)}, u32[]{:S(2)}) collective-permute-start(bf16[1,128,1024]{2,1,0:T(8,128)(2,1)} %bitcast.10), channel_id=1, source_target_pairs={{0,2},{1,3},{2,0},{3,1},{4,6},{5,7},{6,4},{7,5},{8,10},{9,11},{10,... | collective-permute-start | bytes 786440 | tf_op jit(solution)/shard_map/amplitudes_bit_2/ppermute | solution.py:308
  14.0 13.3 %collective-permute-start.1 = (bf16[1,128,1024]{2,1,0:T(8,128)(2,1)}, bf16[1,128,1024]{2,1,0:T(8,128)(2,1)S(1)}, u32[]{:S(2)}, u32[]{:S(2)}) collective-permute-start(bf16[1,128,1024]{2,1,0:T(8,128)(2,1)} %bitcast.5), channel_id=1, source_target_pairs={{0,1},{1,0},{2,3},{3,2},{4,5},{5,4},{6,7},{7,6},{8,9},{9,8},{10,11... | collective-permute-start | bytes 786440 | tf_op jit(solution)/shard_map/amplitudes_bit_1/ppermute | solution.py:308
  16.0 13.9 %collective-permute-start.13 = (bf16[1,784,128]{2,1,0:T(8,128)(2,1)S(1)}, bf16[1,784,128]{2,1,0:T(8,128)(2,1)S(1)}, u32[]{:S(2)}, u32[]{:S(2)}) collective-permute-start(bf16[1,784,128]{2,1,0:T(8,128)(2,1)S(1)} %collective-permute-done.4.refs_11_), channel_id=1, source_target_pairs={{0,16},{4,20},{16,24},{20,28},{24,8},{28,12},{8,0},{12,4},{1,17},{... | collective-permute-start | bytes 602120 | tf_op jit(solution)/shard_map/early_hop_1/ppermute | solution.py:286
  21.8 9.8 %collective-permute-start.5 = (bf16[2,784,128]{2,1,0:T(8,128)(2,1)S(1)}, bf16[2,784,128]{2,1,0:T(8,128)(2,1)S(1)}, u32[]{:S(2)}, u32[]{:S(2)}) collective-permute-start(bf16[2,784,128]{2,1,0:T(8,128)(2,1)S(1)} %pad_maximum_fusion.2.refs_12_), channel_id=1, source_target_pairs={{0,16},{4,20},{16,24},{20,28},{24,8},{28,12},{8,0},{12,4},{1,17},{... | collective-permute-start | bytes 1204232 | tf_op jit(solution)/shard_map/late_hop_1/ppermute | solution.py:286
  26.7 12.4 %collective-permute-start.9 = (bf16[2,128,1024]{2,1,0:T(8,128)(2,1)S(1)}, bf16[2,128,1024]{2,1,0:T(8,128)(2,1)S(1)}, u32[]{:S(2)}, u32[]{:S(2)}) collective-permute-start(bf16[2,128,1024]{2,1,0:T(8,128)(2,1)S(1)} %pad_maximum_fusion.1), channel_id=1, source_target_pairs={{0,1},{1,0},{2,3},{3,2},{4,5},{5,4},{6,7},{7,6},{8,9},{9,8},{10,11... | collective-permute-start | bytes 1572872 | tf_op jit(solution)/shard_map/amplitudes_bit_1/ppermute | solution.py:308
  28.3 13.1 %collective-permute-start.11 = (bf16[2,128,1024]{2,1,0:T(8,128)(2,1)S(1)}, bf16[2,128,1024]{2,1,0:T(8,128)(2,1)S(1)}, u32[]{:S(2)}, u32[]{:S(2)}) collective-permute-start(bf16[2,128,1024]{2,1,0:T(8,128)(2,1)S(1)} %pad_maximum_fusion), channel_id=1, source_target_pairs={{0,2},{1,3},{2,0},{3,1},{4,6},{5,7},{6,4},{7,5},{8,10},{9,11},{10,... | collective-permute-start | bytes 1572872 | tf_op jit(solution)/shard_map/amplitudes_bit_2/ppermute | solution.py:308
  30.0 12.3 %collective-permute-start.14 = (bf16[2,784,128]{2,1,0:T(8,128)(2,1)S(1)}, bf16[2,784,128]{2,1,0:T(8,128)(2,1)S(1)}, u32[]{:S(2)}, u32[]{:S(2)}) collective-permute-start(bf16[2,784,128]{2,1,0:T(8,128)(2,1)S(1)} %constant_dynamic-update-slice_fusion.refs_13_), channel_id=1, source_target_pairs={{0,16},{4,20},{16,24},{20,28},{24,8},{28,12},{8,0},{12,4},{1,17},{... | collective-permute-start | bytes 1204232 | tf_op jit(solution)/shard_map/first_hop_2/ppermute | solution.py:286
  31.6 16.7 %collective-permute-start.15 = (bf16[2,784,128]{2,1,0:T(8,128)(2,1)S(1)}, bf16[2,784,128]{2,1,0:T(8,128)(2,1)S(1)}, u32[]{:S(2)}, u32[]{:S(2)}) collective-permute-start(bf16[2,784,128]{2,1,0:T(8,128)(2,1)S(1)} %collective-permute-done.5.refs_14_), channel_id=1, source_target_pairs={{0,16},{4,20},{16,24},{20,28},{24,8},{28,12},{8,0},{12,4},{1,17},{... | collective-permute-start | bytes 1204232 | tf_op jit(solution)/shard_map/late_hop_2/ppermute | solution.py:286
  34.0 17.6 %collective-permute-start.8 = (bf16[2,128,1024]{2,1,0:T(8,128)(2,1)S(1)}, bf16[2,128,1024]{2,1,0:T(8,128)(2,1)S(1)}, u32[]{:S(2)}, u32[]{:S(2)}) collective-permute-start(bf16[2,128,1024]{2,1,0:T(8,128)(2,1)S(1)} %pad_maximum_fusion.1), channel_id=1, source_target_pairs={{0,4},{4,0},{8,12},{12,8},{16,20},{20,16},{24,28},{28,24},{1,5},{5... | collective-permute-start | bytes 1572872 | tf_op jit(solution)/shard_map/twin_of_bit_2/ppermute | solution.py:276
  39.1 12.5 %collective-permute-start.6 = (bf16[2,128,1024]{2,1,0:T(8,128)(2,1)S(1)}, bf16[2,128,1024]{2,1,0:T(8,128)(2,1)S(1)}, u32[]{:S(2)}, u32[]{:S(2)}) collective-permute-start(bf16[2,128,1024]{2,1,0:T(8,128)(2,1)S(1)} %pad_maximum_fusion), channel_id=1, source_target_pairs={{0,4},{4,0},{8,12},{12,8},{16,20},{20,16},{24,28},{28,24},{1,5},{5... | collective-permute-start | bytes 1572872 | tf_op jit(solution)/shard_map/twin_of_bit_1/ppermute | solution.py:276
  41.4 10.2 %collective-permute-start.10 = (bf16[2,128,1024]{2,1,0:T(8,128)(2,1)S(1)}, bf16[2,128,1024]{2,1,0:T(8,128)(2,1)S(1)}, u32[]{:S(2)}, u32[]{:S(2)}) collective-permute-start(bf16[2,128,1024]{2,1,0:T(8,128)(2,1)S(1)} %collective-permute-done.9.refs_5_.refs_2_), channel_id=1, source_target_pairs={{0,4},{4,0},{8,12},{12,8},{16,20},{20,16},{24,28},{28,24},{1,5},{5... | collective-permute-start | bytes 1572872 | tf_op jit(solution)/shard_map/twin_of_bit_1/ppermute | solution.py:276
  42.3 9.4 %collective-permute-start.12 = (bf16[2,128,1024]{2,1,0:T(8,128)(2,1)S(1)}, bf16[2,128,1024]{2,1,0:T(8,128)(2,1)S(1)}, u32[]{:S(2)}, u32[]{:S(2)}) collective-permute-start(bf16[2,128,1024]{2,1,0:T(8,128)(2,1)S(1)} %collective-permute-done.11.refs_7_.refs_0_), channel_id=1, source_target_pairs={{0,4},{4,0},{8,12},{12,8},{16,20},{20,16},{24,28},{28,24},{1,5},{5... | collective-permute-start | bytes 1572872 | tf_op jit(solution)/shard_map/twin_of_bit_2/ppermute | solution.py:276
  48.3 13.1 %collective-permute-start.16 = (bf16[2,784,128]{2,1,0:T(8,128)(2,1)S(1)}, bf16[2,784,128]{2,1,0:T(8,128)(2,1)S(1)}, u32[]{:S(2)}, u32[]{:S(2)}) collective-permute-start(bf16[2,784,128]{2,1,0:T(8,128)(2,1)S(1)} %collective-permute-done.14.refs_10_), channel_id=1, source_target_pairs={{0,16},{4,20},{16,24},{20,28},{24,8},{28,12},{8,0},{12,4},{1,17},{... | collective-permute-start | bytes 1204232 | tf_op jit(solution)/shard_map/first_hop_3/ppermute | solution.py:286
  51.6 15.7 %collective-permute-start.18 = (bf16[2,784,128]{2,1,0:T(8,128)(2,1)S(1)}, bf16[2,784,128]{2,1,0:T(8,128)(2,1)S(1)}, u32[]{:S(2)}, u32[]{:S(2)}) collective-permute-start(bf16[2,784,128]{2,1,0:T(8,128)(2,1)S(1)} %collective-permute-done.15.refs_11_), channel_id=1, source_target_pairs={{0,16},{4,20},{16,24},{20,28},{24,8},{28,12},{8,0},{12,4},{1,17},{... | collective-permute-start | bytes 1204232 | tf_op jit(solution)/shard_map/late_hop_3/ppermute | solution.py:286
  63.3 5.7 %collective-permute-start.17 = (bf16[8,256,128]{2,1,0:T(8,128)(2,1)S(1)}, bf16[8,256,128]{2,1,0:T(8,128)(2,1)S(1)}, u32[]{:S(2)}, u32[]{:S(2)}) collective-permute-start(bf16[8,256,128]{2,1,0:T(8,128)(2,1)S(1)} %get-tuple-element.44), channel_id=1, source_target_pairs={{0,4},{4,0},{8,12},{12,8},{16,20},{20,16},{24,28},{28,24},{1,5},{5... | collective-permute-start | bytes 1572872 | tf_op jit(solution)/shard_map/ppermute | solution.py:276
  67.3 1.7 %collective-permute-start.19 = (bf16[2,784,128]{2,1,0:T(8,128)(2,1)S(1)}, bf16[2,784,128]{2,1,0:T(8,128)(2,1)S(1)}, u32[]{:S(2)}, u32[]{:S(2)}) collective-permute-start(bf16[2,784,128]{2,1,0:T(8,128)(2,1)S(1)} %collective-permute-done.18.refs_3_), channel_id=1, source_target_pairs={{0,4},{4,0},{8,12},{12,8},{16,20},{20,16},{24,28},{28,24},{1,5},{5... | collective-permute-start | bytes 1204232 | tf_op jit(solution)/shard_map/ppermute | solution.py:276
  (4 other events, 63.9 us)

commit v10 on v9

--- a/solution.py
+++ b/solution.py
@@ -12,7 +12,7 @@
 ALL_VMEM = 60 * 1024 * 1024
 CORES = 2
 NOTE_ROWS = 16
-FIRST_FLOPS = 10**9
+FIRST_FLOPS = 10**6
 MIDDLE_FLOPS = 10**8
 LAST_FLOPS = 10**9
 
@@ -303,14 +303,14 @@
         pieces, own, twin = [value[None]], {0: (value[None], 0)}, {}
         ids = [0]
         for bit in bits:
-            held = join(pieces)
+            held = after(join(pieces), hops["early"][1]) if twin else join(pieces)
             with jax.named_scope(f"amplitudes_bit_{bit}"):
                 now = lax.ppermute(held, "vpair", [(i, i ^ bit) for i in range(n_v)])
             new_ids = [i ^ bit for i in ids]
             own |= {j: (now, i) for i, j in enumerate(new_ids)}
             with jax.named_scope(f"twin_of_bit_{bit}"):
                 part, part_ids = (now, new_ids) if twin else (join([held, now]), ids + new_ids)
-                swapped = across_core(after(part, hops["late"][1]))
+                swapped = across_core(part)
             twin |= {j: (swapped, i) for i, j in enumerate(part_ids)}
             pieces.append(now)
             ids = ids + new_ids

time: 72.7 us -> 70.9 us (0.975)
  waiting for transfers between devices: 29.5 us -> 25.3 us
  starting transfers between devices: 24.2 us -> 26.7 us
    ppermute x4, waiting for transfers between devices: 10.1 us -> 2.7 us  [gather_amplitudes(): now = lax.ppermute(held, 'vpair', [(i, i ^ bit) for i in range(n_v)])]
    ppermute x7, waiting for transfers between devices: 14.2 us -> 17.3 us  [next_on_ring(): return lax.ppermute(value, 'opair', pairs)]
    ppermute x7, starting transfers between devices: 15.4 us -> 17.3 us  [next_on_ring(): return lax.ppermute(value, 'opair', pairs)]
  transfers between devices with their start and end apart: 20 -> 20, of which waited for: 11 -> 8; matrix products, arithmetic and copies ran while one was open for 3% -> 3% of each run, Pallas kernels for 13% -> 13%
where the time goes in v10:
time: 70.9 us; the launch traced here: 70.7 us
  starting transfers between devices  26.7 us (38%)
  waiting for transfers between devices  25.3 us (36%)
  Pallas kernels  15.8 us (22%)
  other arithmetic  2.04 us (3%)
  between operations  0.85 us (1%)
    ppermute x7, waiting for transfers between devices, next_on_ring(): return lax.ppermute(value, 'opair', pairs)  17.3 us
    ppermute x7, starting transfers between devices, next_on_ring(): return lax.ppermute(value, 'opair', pairs)  17.3 us
    pallas_call x3, Pallas kernels, ladder_call(): pl.pallas_call(functools.partial(kernel, cap, layout, where), out_shape=o...  9.16 us
    ppermute x4, starting transfers between devices, gather_amplitudes(): now = lax.ppermute(held, 'vpair', [(i, i ^ bit) for i in range(n_v)])  5.2 us
    pallas_call x1, Pallas kernels, on_device(): pl.pallas_call(functools.partial(update_kernel, cap, behind, where), out_...  3.5 us
    ppermute x3, waiting for transfers between devices, across_v(): return lax.ppermute(value, 'vpair', [(i, i ^ j) for i in range(n_v)])  3.49 us
    ppermute x3, starting transfers between devices, across_v(): return lax.ppermute(value, 'vpair', [(i, i ^ j) for i in range(n_v)])  3.49 us
    pallas_call x1, Pallas kernels, on_device(): pl.pallas_call(functools.partial(pack_kernel, n_v, cap), out_shape=[jax.S...  3.14 us
  transfers between devices with their start and end apart: 20, of which 8 were waited for; matrix products, arithmetic and copies ran while one was open for 3% of the time, Pallas kernels for 13%

profile of v10, /device:TPU:0, one launch (start us, length us, event | category | flops | bytes accessed | tf_op | source)
XLA Modules:
  0.0 70.7 jit_solution(1539047737317802659)
XLA Ops:
  0.7 3.1 %pack.1 = (bf16[1,784,128]{2,1,0:T(8,128)(2,1)}, bf16[1,784,128]{2,1,0:T(8,128)(2,1)}, bf16[1,784,128]{2,1,0:T(8,128)(2,1)}, bf16[1,784,128]{2,1,0:T(8,128)(2,1)...) custom-call(s32[3,8]{1,0:T(4,128)} %bitcast.18, s32[2,8]{1,0:T(2,128)} %live.3, ...), custom_call_target="tpu_custom_call" | custom-call | tf_op jit(solution)/shard_map/pack/pallas_call | solution.py:251
  3.8 4.1 %collective-permute-start = (bf16[1,784,128]{2,1,0:T(8,128)(2,1)}, bf16[1,784,128]{2,1,0:T(8,128)(2,1)S(1)}, u32[]{:S(2)}, u32[]{:S(2)}) collective-permute-start(bf16[1,784,128]{2,1,0:T(8,128)(2,1)} %get-tuple-element.24.refs_10_), channel_id=1, source_target_pairs={{0,16},{4,20},{16,24},{20,28},{24,8},{28,12},{8,0},{12,4},{1,17},{... | collective-permute-start | bytes 602120 | tf_op jit(solution)/shard_map/near_hop_1/ppermute | solution.py:286
  7.9 1.5 %collective-permute-start.5 = (bf16[1,784,128]{2,1,0:T(8,128)(2,1)}, bf16[1,784,128]{2,1,0:T(8,128)(2,1)S(1)}, u32[]{:S(2)}, u32[]{:S(2)}) collective-permute-start(bf16[1,784,128]{2,1,0:T(8,128)(2,1)} %get-tuple-element.27), channel_id=1, source_target_pairs={{0,1},{1,0},{2,3},{3,2},{4,5},{5,4},{6,7},{7,6},{8,9},{9,8},{10,11... | collective-permute-start | bytes 602120 | tf_op jit(solution)/shard_map/parcels_from_partner_1/ppermute | solution.py:273
  9.4 1.5 %collective-permute-start.11 = (bf16[1,784,128]{2,1,0:T(8,128)(2,1)}, bf16[1,784,128]{2,1,0:T(8,128)(2,1)S(1)}, u32[]{:S(2)}, u32[]{:S(2)}) collective-permute-start(bf16[1,784,128]{2,1,0:T(8,128)(2,1)} %get-tuple-element.31), channel_id=1, source_target_pairs={{0,2},{1,3},{2,0},{3,1},{4,6},{5,7},{6,4},{7,5},{8,10},{9,11},{10,... | collective-permute-start | bytes 602120 | tf_op jit(solution)/shard_map/parcels_from_partner_2/ppermute | solution.py:273
  11.4 1.1 %collective-permute-done = bf16[1,784,128]{2,1,0:T(8,128)(2,1)S(1)} collective-permute-done((bf16[1,784,128]{2,1,0:T(8,128)(2,1)}, bf16[1,784,128]{2,1,0:T(8,128)(2,1)S(1)}, u32[]{:S(2)}, u32[]{:S(2)}) %collective-permute-start) | collective-permute-done | bytes 200736 | tf_op jit(solution)/shard_map/near_hop_1/ppermute | solution.py:286
  12.5 1.5 %collective-permute-start.3 = (bf16[1,128,1024]{2,1,0:T(8,128)(2,1)}, bf16[1,128,1024]{2,1,0:T(8,128)(2,1)S(1)}, u32[]{:S(2)}, u32[]{:S(2)}) collective-permute-start(bf16[1,128,1024]{2,1,0:T(8,128)(2,1)} %bitcast.10), channel_id=1, source_target_pairs={{0,2},{1,3},{2,0},{3,1},{4,6},{5,7},{6,4},{7,5},{8,10},{9,11},{10,... | collective-permute-start | bytes 786440 | tf_op jit(solution)/shard_map/amplitudes_bit_2/ppermute | solution.py:308
  14.0 1.5 %collective-permute-start.1 = (bf16[1,128,1024]{2,1,0:T(8,128)(2,1)}, bf16[1,128,1024]{2,1,0:T(8,128)(2,1)S(1)}, u32[]{:S(2)}, u32[]{:S(2)}) collective-permute-start(bf16[1,128,1024]{2,1,0:T(8,128)(2,1)} %bitcast.5), channel_id=1, source_target_pairs={{0,1},{1,0},{2,3},{3,2},{4,5},{5,4},{6,7},{7,6},{8,9},{9,8},{10,11... | collective-permute-start | bytes 786440 | tf_op jit(solution)/shard_map/amplitudes_bit_1/ppermute | solution.py:308
  16.0 2.7 %collective-permute-start.6 = (bf16[1,784,128]{2,1,0:T(8,128)(2,1)S(1)}, bf16[1,784,128]{2,1,0:T(8,128)(2,1)S(1)}, u32[]{:S(2)}, u32[]{:S(2)}) collective-permute-start(bf16[1,784,128]{2,1,0:T(8,128)(2,1)S(1)} %collective-permute-done.5.refs_11_), channel_id=1, source_target_pairs={{0,16},{4,20},{16,24},{20,28},{24,8},{28,12},{8,0},{12,4},{1,17},{... | collective-permute-start | bytes 602120 | tf_op jit(solution)/shard_map/early_hop_1/ppermute | solution.py:286
  18.8 2.9 %collective-permute-done.11 = bf16[1,784,128]{2,1,0:T(8,128)(2,1)S(1)} collective-permute-done((bf16[1,784,128]{2,1,0:T(8,128)(2,1)}, bf16[1,784,128]{2,1,0:T(8,128)(2,1)S(1)}, u32[]{:S(2)}, u32[]{:S(2)}) %collective-permute-start.11) | collective-permute-done | bytes 200736 | tf_op jit(solution)/shard_map/parcels_from_partner_2/ppermute | solution.py:273
  21.8 1.3 %collective-permute-start.13 = (bf16[2,784,128]{2,1,0:T(8,128)(2,1)S(1)}, bf16[2,784,128]{2,1,0:T(8,128)(2,1)S(1)}, u32[]{:S(2)}, u32[]{:S(2)}) collective-permute-start(bf16[2,784,128]{2,1,0:T(8,128)(2,1)S(1)} %pad_maximum_fusion.2.refs_12_), channel_id=1, source_target_pairs={{0,16},{4,20},{16,24},{20,28},{24,8},{28,12},{8,0},{12,4},{1,17},{... | collective-permute-start | bytes 1204232 | tf_op jit(solution)/shard_map/late_hop_1/ppermute | solution.py:286
  23.0 2.7 %collective-permute-done.3.refs_8_.refs_1_ = bf16[1,128,1024]{2,1,0:T(8,128)(2,1)S(1)} collective-permute-done((bf16[1,128,1024]{2,1,0:T(8,128)(2,1)}, bf16[1,128,1024]{2,1,0:T(8,128)(2,1)S(1)}, u32[]{:S(2)}, u32[]{:S(2)}) %collective-permute-start.3) | collective-permute-done | bytes 262176 | tf_op jit(solution)/shard_map/amplitudes_bit_2/ppermute | solution.py:308
  28.3 1.6 %collective-permute-start.9 = (bf16[2,128,1024]{2,1,0:T(8,128)(2,1)S(1)}, bf16[2,128,1024]{2,1,0:T(8,128)(2,1)S(1)}, u32[]{:S(2)}, u32[]{:S(2)}) collective-permute-start(bf16[2,128,1024]{2,1,0:T(8,128)(2,1)S(1)} %pad_maximum_fusion), channel_id=1, source_target_pairs={{0,2},{1,3},{2,0},{3,1},{4,6},{5,7},{6,4},{7,5},{8,10},{9,11},{10,... | collective-permute-start | bytes 1572872 | tf_op jit(solution)/shard_map/amplitudes_bit_2/ppermute | solution.py:308
  30.0 1.6 %collective-permute-start.14 = (bf16[2,784,128]{2,1,0:T(8,128)(2,1)S(1)}, bf16[2,784,128]{2,1,0:T(8,128)(2,1)S(1)}, u32[]{:S(2)}, u32[]{:S(2)}) collective-permute-start(bf16[2,784,128]{2,1,0:T(8,128)(2,1)S(1)} %constant_dynamic-update-slice_fusion.refs_13_), channel_id=1, source_target_pairs={{0,16},{4,20},{16,24},{20,28},{24,8},{28,12},{8,0},{12,4},{1,17},{... | collective-permute-start | bytes 1204232 | tf_op jit(solution)/shard_map/first_hop_2/ppermute | solution.py:286
  31.6 2.4 %collective-permute-start.15 = (bf16[2,784,128]{2,1,0:T(8,128)(2,1)S(1)}, bf16[2,784,128]{2,1,0:T(8,128)(2,1)S(1)}, u32[]{:S(2)}, u32[]{:S(2)}) collective-permute-start(bf16[2,784,128]{2,1,0:T(8,128)(2,1)S(1)} %collective-permute-done.13.refs_14_), channel_id=1, source_target_pairs={{0,16},{4,20},{16,24},{20,28},{24,8},{28,12},{8,0},{12,4},{1,17},{... | collective-permute-start | bytes 1204232 | tf_op jit(solution)/shard_map/late_hop_2/ppermute | solution.py:286
  34.0 8.3 %collective-permute-done.14.refs_10_ = bf16[2,784,128]{2,1,0:T(8,128)(2,1)S(1)} collective-permute-done((bf16[2,784,128]{2,1,0:T(8,128)(2,1)S(1)}, bf16[2,784,128]{2,1,0:T(8,128)(2,1)S(1)}, u32[]{:S(2)}, u32[]{:S(2)}) %collective-permute-start.14) | collective-permute-done | bytes 401440 | tf_op jit(solution)/shard_map/first_hop_2/ppermute | solution.py:286
  42.8 2.5 %collective-permute-start.16 = (bf16[2,784,128]{2,1,0:T(8,128)(2,1)S(1)}, bf16[2,784,128]{2,1,0:T(8,128)(2,1)S(1)}, u32[]{:S(2)}, u32[]{:S(2)}) collective-permute-start(bf16[2,784,128]{2,1,0:T(8,128)(2,1)S(1)} %collective-permute-done.14.refs_10_), channel_id=1, source_target_pairs={{0,16},{4,20},{16,24},{20,28},{24,8},{28,12},{8,0},{12,4},{1,17},{... | collective-permute-start | bytes 1204232 | tf_op jit(solution)/shard_map/first_hop_3/ppermute | solution.py:286
  45.3 5.2 %collective-permute-done.15.refs_11_ = bf16[2,784,128]{2,1,0:T(8,128)(2,1)S(1)} collective-permute-done((bf16[2,784,128]{2,1,0:T(8,128)(2,1)S(1)}, bf16[2,784,128]{2,1,0:T(8,128)(2,1)S(1)}, u32[]{:S(2)}, u32[]{:S(2)}) %collective-permute-start.15) | collective-permute-done | bytes 401440 | tf_op jit(solution)/shard_map/late_hop_2/ppermute | solution.py:286
  50.6 2.8 %collective-permute-start.18 = (bf16[2,784,128]{2,1,0:T(8,128)(2,1)S(1)}, bf16[2,784,128]{2,1,0:T(8,128)(2,1)S(1)}, u32[]{:S(2)}, u32[]{:S(2)}) collective-permute-start(bf16[2,784,128]{2,1,0:T(8,128)(2,1)S(1)} %collective-permute-done.15.refs_11_), channel_id=1, source_target_pairs={{0,16},{4,20},{16,24},{20,28},{24,8},{28,12},{8,0},{12,4},{1,17},{... | collective-permute-start | bytes 1204232 | tf_op jit(solution)/shard_map/late_hop_3/ppermute | solution.py:286
  53.4 4.2 %ladder_first.1 = (f32[9,512,128]{2,1,0:T(8,128)S(1)}, f32[256,128]{1,0:T(8,128)S(1)}, f32[256,1024]{1,0:T(8,128)S(1)}) custom-call(f32[2,128]{1,0:T(2,128)S(1)} %bitcast.17, f32[1,1024]{1,0:T(1,128)S(1)} %bitcast.15, bf16[1,128,1024]{2,1,0:T(8,128)(2,1)S(1)} %bitcast.7, bf16[1,128,1024]{2,1,0:T(8,128)(2,1)S(1)} %bitcast.12, ...), custom_call_target="tpu_custom_call" | custom-call | flops 1000000 | bytes 1048576 | tf_op jit(solution)/shard_map/ladder_first/pallas_call | solution.py:344
  57.6 3.1 %ladder_middle.1 = (f32[9,512,128]{2,1,0:T(8,128)S(1)}, f32[256,1024]{1,0:T(8,128)S(1)}) custom-call(f32[9,512,128]{2,1,0:T(8,128)S(1)} %get-tuple-element.34.before, bf16[256,1024]{1,0:T(8,128)(2,1)S(1)} %copy-done.3, bf16[256,1024]{1,0:T(8,128)(2,1)S(1)} %copy-done, f32[256,128]{1,0:T(8,128)S(1)} %get-tuple-element.35.occupied, f32[1,1024]{1,0:T(1,128)S(1)} %bitcast.16, ...), custom_call_target="tpu_custom_call" | custom-call | flops 100000000 | bytes 1048576 | tf_op jit(solution)/shard_map/ladder_middle/pallas_call | solution.py:344
  60.7 2.0 %ladder_last.1 = (f32[256,1024]{1,0:T(8,128)S(1)}, bf16[8,256,128]{2,1,0:T(8,128)(2,1)S(1)}) custom-call(f32[9,512,128]{2,1,0:T(8,128)S(1)} %get-tuple-element.36.before, f32[256,1024]{1,0:T(8,128)S(1)} %get-tuple-element.37.base, bf16[1,128,1024]{2,1,0:T(8,128)(2,1)S(1)} %bitcast.9, bf16[1,128,1024]{2,1,0:T(8,128)(2,1)S(1)} %bitcast.14, ...), custom_call_target="tpu_custom_call" | custom-call | flops 1000000000 | bytes 1048576 | tf_op jit(solution)/shard_map/ladder_last/pallas_call | solution.py:344
  62.7 2.7 %collective-permute-done.18.refs_3_ = bf16[2,784,128]{2,1,0:T(8,128)(2,1)S(1)} collective-permute-done((bf16[2,784,128]{2,1,0:T(8,128)(2,1)S(1)}, bf16[2,784,128]{2,1,0:T(8,128)(2,1)S(1)}, u32[]{:S(2)}, u32[]{:S(2)}) %collective-permute-start.18) | collective-permute-done | bytes 401440 | tf_op jit(solution)/shard_map/late_hop_3/ppermute | solution.py:286
  65.5 1.7 %collective-permute-done.19.refs_4_ = bf16[2,784,128]{2,1,0:T(8,128)(2,1)S(1)} collective-permute-done((bf16[2,784,128]{2,1,0:T(8,128)(2,1)S(1)}, bf16[2,784,128]{2,1,0:T(8,128)(2,1)S(1)}, u32[]{:S(2)}, u32[]{:S(2)}) %collective-permute-start.19) | collective-permute-done | bytes 401440 | tf_op jit(solution)/shard_map/ppermute | solution.py:276
  67.2 3.5 %update.1 = (bf16[256,1024]{1,0:T(8,128)(2,1)}, f32[256,1024]{1,0:T(8,128)}) custom-call(s32[2,8]{1,0:T(2,128)S(1)} %copy-done.6, bf16[256,1024]{1,0:T(8,128)(2,1)S(1)} %copy-done, f32[256,1024]{1,0:T(8,128)S(1)} %get-tuple-element.38.base, f32[256,1024]{1,0:T(8,128)S(1)} %get-tuple-element.39.inverse, ...), custom_call_target="tpu_custom_call" | custom-call | tf_op jit(solution)/shard_map/update/pallas_call | solution.py:408
  (42 shorter events, 4.4 us)
Async XLA Ops:
  0.6 52.7 %copy-start.5 = (f32[1024]{0:T(1024)S(1)}, f32[1024]{0:T(1024)}, u32[]{:S(2)}) copy-start(f32[1024]{0:T(1024)} %param.13) | copy-start | bytes 12292
  0.6 52.7 %copy-start.7 = (f32[256]{0:T(256)S(1)}, f32[256]{0:T(256)}, u32[]{:S(2)}) copy-start(f32[256]{0:T(256)} %param.12) | copy-start | bytes 3076
  3.8 49.6 %copy-start.1 = (bf16[128,1024]{1,0:T(8,128)(2,1)S(1)}, bf16[128,1024]{1,0:T(8,128)(2,1)}, u32[]{:S(2)}) copy-start(bf16[128,1024]{1,0:T(8,128)(2,1)} %get-tuple-element.25) | copy-start | bytes 786436
  3.8 49.6 %copy-start.2 = (bf16[128,1024]{1,0:T(8,128)(2,1)S(1)}, bf16[128,1024]{1,0:T(8,128)(2,1)}, u32[]{:S(2)}) copy-start(bf16[128,1024]{1,0:T(8,128)(2,1)} %get-tuple-element.26) | copy-start | bytes 786436
  3.8 8.7 %collective-permute-start = (bf16[1,784,128]{2,1,0:T(8,128)(2,1)}, bf16[1,784,128]{2,1,0:T(8,128)(2,1)S(1)}, u32[]{:S(2)}, u32[]{:S(2)}) collective-permute-start(bf16[1,784,128]{2,1,0:T(8,128)(2,1)} %get-tuple-element.24.refs_10_), channel_id=1, source_target_pairs={{0,16},{4,20},{16,24},{20,28},{24,8},{28,12},{8,0},{12,4},{1,17},{... | collective-permute-start | bytes 602120 | tf_op jit(solution)/shard_map/near_hop_1/ppermute | solution.py:286
  7.9 8.1 %collective-permute-start.5 = (bf16[1,784,128]{2,1,0:T(8,128)(2,1)}, bf16[1,784,128]{2,1,0:T(8,128)(2,1)S(1)}, u32[]{:S(2)}, u32[]{:S(2)}) collective-permute-start(bf16[1,784,128]{2,1,0:T(8,128)(2,1)} %get-tuple-element.27), channel_id=1, source_target_pairs={{0,1},{1,0},{2,3},{3,2},{4,5},{5,4},{6,7},{7,6},{8,9},{9,8},{10,11... | collective-permute-start | bytes 602120 | tf_op jit(solution)/shard_map/parcels_from_partner_1/ppermute | solution.py:273
  9.4 12.3 %collective-permute-start.11 = (bf16[1,784,128]{2,1,0:T(8,128)(2,1)}, bf16[1,784,128]{2,1,0:T(8,128)(2,1)S(1)}, u32[]{:S(2)}, u32[]{:S(2)}) collective-permute-start(bf16[1,784,128]{2,1,0:T(8,128)(2,1)} %get-tuple-element.31), channel_id=1, source_target_pairs={{0,2},{1,3},{2,0},{3,1},{4,6},{5,7},{6,4},{7,5},{8,10},{9,11},{10,... | collective-permute-start | bytes 602120 | tf_op jit(solution)/shard_map/parcels_from_partner_2/ppermute | solution.py:273
  10.9 10.8 %collective-permute-start.12 = (bf16[1,784,128]{2,1,0:T(8,128)(2,1)}, bf16[1,784,128]{2,1,0:T(8,128)(2,1)S(1)}, u32[]{:S(2)}, u32[]{:S(2)}) collective-permute-start(bf16[1,784,128]{2,1,0:T(8,128)(2,1)} %get-tuple-element.32), channel_id=1, source_target_pairs={{0,3},{1,2},{2,1},{3,0},{4,7},{5,6},{6,5},{7,4},{8,11},{9,10},{10,... | collective-permute-start | bytes 602120 | tf_op jit(solution)/shard_map/parcels_from_partner_3/ppermute | solution.py:273
  12.5 13.2 %collective-permute-start.3 = (bf16[1,128,1024]{2,1,0:T(8,128)(2,1)}, bf16[1,128,1024]{2,1,0:T(8,128)(2,1)S(1)}, u32[]{:S(2)}, u32[]{:S(2)}) collective-permute-start(bf16[1,128,1024]{2,1,0:T(8,128)(2,1)} %bitcast.10), channel_id=1, source_target_pairs={{0,2},{1,3},{2,0},{3,1},{4,6},{5,7},{6,4},{7,5},{8,10},{9,11},{10,... | collective-permute-start | bytes 786440 | tf_op jit(solution)/shard_map/amplitudes_bit_2/ppermute | solution.py:308
  14.0 13.3 %collective-permute-start.1 = (bf16[1,128,1024]{2,1,0:T(8,128)(2,1)}, bf16[1,128,1024]{2,1,0:T(8,128)(2,1)S(1)}, u32[]{:S(2)}, u32[]{:S(2)}) collective-permute-start(bf16[1,128,1024]{2,1,0:T(8,128)(2,1)} %bitcast.5), channel_id=1, source_target_pairs={{0,1},{1,0},{2,3},{3,2},{4,5},{5,4},{6,7},{7,6},{8,9},{9,8},{10,11... | collective-permute-start | bytes 786440 | tf_op jit(solution)/shard_map/amplitudes_bit_1/ppermute | solution.py:308
  16.0 10.7 %collective-permute-start.6 = (bf16[1,784,128]{2,1,0:T(8,128)(2,1)S(1)}, bf16[1,784,128]{2,1,0:T(8,128)(2,1)S(1)}, u32[]{:S(2)}, u32[]{:S(2)}) collective-permute-start(bf16[1,784,128]{2,1,0:T(8,128)(2,1)S(1)} %collective-permute-done.5.refs_11_), channel_id=1, source_target_pairs={{0,16},{4,20},{16,24},{20,28},{24,8},{28,12},{8,0},{12,4},{1,17},{... | collective-permute-start | bytes 602120 | tf_op jit(solution)/shard_map/early_hop_1/ppermute | solution.py:286
  21.8 9.8 %collective-permute-start.13 = (bf16[2,784,128]{2,1,0:T(8,128)(2,1)S(1)}, bf16[2,784,128]{2,1,0:T(8,128)(2,1)S(1)}, u32[]{:S(2)}, u32[]{:S(2)}) collective-permute-start(bf16[2,784,128]{2,1,0:T(8,128)(2,1)S(1)} %pad_maximum_fusion.2.refs_12_), channel_id=1, source_target_pairs={{0,16},{4,20},{16,24},{20,28},{24,8},{28,12},{8,0},{12,4},{1,17},{... | collective-permute-start | bytes 1204232 | tf_op jit(solution)/shard_map/late_hop_1/ppermute | solution.py:286
  26.7 15.5 %collective-permute-start.7 = (bf16[2,128,1024]{2,1,0:T(8,128)(2,1)S(1)}, bf16[2,128,1024]{2,1,0:T(8,128)(2,1)S(1)}, u32[]{:S(2)}, u32[]{:S(2)}) collective-permute-start(bf16[2,128,1024]{2,1,0:T(8,128)(2,1)S(1)} %pad_maximum_fusion.1), channel_id=1, source_target_pairs={{0,1},{1,0},{2,3},{3,2},{4,5},{5,4},{6,7},{7,6},{8,9},{9,8},{10,11... | collective-permute-start | bytes 1572872 | tf_op jit(solution)/shard_map/amplitudes_bit_1/ppermute | solution.py:308
  28.3 14.4 %collective-permute-start.9 = (bf16[2,128,1024]{2,1,0:T(8,128)(2,1)S(1)}, bf16[2,128,1024]{2,1,0:T(8,128)(2,1)S(1)}, u32[]{:S(2)}, u32[]{:S(2)}) collective-permute-start(bf16[2,128,1024]{2,1,0:T(8,128)(2,1)S(1)} %pad_maximum_fusion), channel_id=1, source_target_pairs={{0,2},{1,3},{2,0},{3,1},{4,6},{5,7},{6,4},{7,5},{8,10},{9,11},{10,... | collective-permute-start | bytes 1572872 | tf_op jit(solution)/shard_map/amplitudes_bit_2/ppermute | solution.py:308
  30.0 12.3 %collective-permute-start.14 = (bf16[2,784,128]{2,1,0:T(8,128)(2,1)S(1)}, bf16[2,784,128]{2,1,0:T(8,128)(2,1)S(1)}, u32[]{:S(2)}, u32[]{:S(2)}) collective-permute-start(bf16[2,784,128]{2,1,0:T(8,128)(2,1)S(1)} %constant_dynamic-update-slice_fusion.refs_13_), channel_id=1, source_target_pairs={{0,16},{4,20},{16,24},{20,28},{24,8},{28,12},{8,0},{12,4},{1,17},{... | collective-permute-start | bytes 1204232 | tf_op jit(solution)/shard_map/first_hop_2/ppermute | solution.py:286
  31.6 11.2 %collective-permute-start.4 = (bf16[2,128,1024]{2,1,0:T(8,128)(2,1)S(1)}, bf16[2,128,1024]{2,1,0:T(8,128)(2,1)S(1)}, u32[]{:S(2)}, u32[]{:S(2)}) collective-permute-start(bf16[2,128,1024]{2,1,0:T(8,128)(2,1)S(1)} %pad_maximum_fusion.1), channel_id=1, source_target_pairs={{0,4},{4,0},{8,12},{12,8},{16,20},{20,16},{24,28},{28,24},{1,5},{5... | collective-permute-start | bytes 1572872 | tf_op jit(solution)/shard_map/twin_of_bit_2/ppermute | solution.py:276
  31.6 19.0 %collective-permute-start.15 = (bf16[2,784,128]{2,1,0:T(8,128)(2,1)S(1)}, bf16[2,784,128]{2,1,0:T(8,128)(2,1)S(1)}, u32[]{:S(2)}, u32[]{:S(2)}) collective-permute-start(bf16[2,784,128]{2,1,0:T(8,128)(2,1)S(1)} %collective-permute-done.13.refs_14_), channel_id=1, source_target_pairs={{0,16},{4,20},{16,24},{20,28},{24,8},{28,12},{8,0},{12,4},{1,17},{... | collective-permute-start | bytes 1204232 | tf_op jit(solution)/shard_map/late_hop_2/ppermute | solution.py:286
  42.3 11.1 %collective-permute-start.2 = (bf16[2,128,1024]{2,1,0:T(8,128)(2,1)S(1)}, bf16[2,128,1024]{2,1,0:T(8,128)(2,1)S(1)}, u32[]{:S(2)}, u32[]{:S(2)}) collective-permute-start(bf16[2,128,1024]{2,1,0:T(8,128)(2,1)S(1)} %pad_maximum_fusion), channel_id=1, source_target_pairs={{0,4},{4,0},{8,12},{12,8},{16,20},{20,16},{24,28},{28,24},{1,5},{5... | collective-permute-start | bytes 1572872 | tf_op jit(solution)/shard_map/twin_of_bit_1/ppermute | solution.py:276
  42.3 11.1 %collective-permute-start.8 = (bf16[2,128,1024]{2,1,0:T(8,128)(2,1)S(1)}, bf16[2,128,1024]{2,1,0:T(8,128)(2,1)S(1)}, u32[]{:S(2)}, u32[]{:S(2)}) collective-permute-start(bf16[2,128,1024]{2,1,0:T(8,128)(2,1)S(1)} %collective-permute-done.7.refs_5_.refs_2_), channel_id=1, source_target_pairs={{0,4},{4,0},{8,12},{12,8},{16,20},{20,16},{24,28},{28,24},{1,5},{5... | collective-permute-start | bytes 1572872 | tf_op jit(solution)/shard_map/twin_of_bit_1/ppermute | solution.py:276
  42.8 10.6 %collective-permute-start.10 = (bf16[2,128,1024]{2,1,0:T(8,128)(2,1)S(1)}, bf16[2,128,1024]{2,1,0:T(8,128)(2,1)S(1)}, u32[]{:S(2)}, u32[]{:S(2)}) collective-permute-start(bf16[2,128,1024]{2,1,0:T(8,128)(2,1)S(1)} %collective-permute-done.9.refs_7_.refs_0_), channel_id=1, source_target_pairs={{0,4},{4,0},{8,12},{12,8},{16,20},{20,16},{24,28},{28,24},{1,5},{5... | collective-permute-start | bytes 1572872 | tf_op jit(solution)/shard_map/twin_of_bit_2/ppermute | solution.py:276
  42.8 17.8 %collective-permute-start.16 = (bf16[2,784,128]{2,1,0:T(8,128)(2,1)S(1)}, bf16[2,784,128]{2,1,0:T(8,128)(2,1)S(1)}, u32[]{:S(2)}, u32[]{:S(2)}) collective-permute-start(bf16[2,784,128]{2,1,0:T(8,128)(2,1)S(1)} %collective-permute-done.14.refs_10_), channel_id=1, source_target_pairs={{0,16},{4,20},{16,24},{20,28},{24,8},{28,12},{8,0},{12,4},{1,17},{... | collective-permute-start | bytes 1204232 | tf_op jit(solution)/shard_map/first_hop_3/ppermute | solution.py:286
  50.6 14.9 %collective-permute-start.18 = (bf16[2,784,128]{2,1,0:T(8,128)(2,1)S(1)}, bf16[2,784,128]{2,1,0:T(8,128)(2,1)S(1)}, u32[]{:S(2)}, u32[]{:S(2)}) collective-permute-start(bf16[2,784,128]{2,1,0:T(8,128)(2,1)S(1)} %collective-permute-done.15.refs_11_), channel_id=1, source_target_pairs={{0,16},{4,20},{16,24},{20,28},{24,8},{28,12},{8,0},{12,4},{1,17},{... | collective-permute-start | bytes 1204232 | tf_op jit(solution)/shard_map/late_hop_3/ppermute | solution.py:286
  62.6 4.6 %collective-permute-start.17 = (bf16[8,256,128]{2,1,0:T(8,128)(2,1)S(1)}, bf16[8,256,128]{2,1,0:T(8,128)(2,1)S(1)}, u32[]{:S(2)}, u32[]{:S(2)}) collective-permute-start(bf16[8,256,128]{2,1,0:T(8,128)(2,1)S(1)} %get-tuple-element.40), channel_id=1, source_target_pairs={{0,4},{4,0},{8,12},{12,8},{16,20},{20,16},{24,28},{28,24},{1,5},{5... | collective-permute-start | bytes 1572872 | tf_op jit(solution)/shard_map/ppermute | solution.py:276
  65.5 1.7 %collective-permute-start.19 = (bf16[2,784,128]{2,1,0:T(8,128)(2,1)S(1)}, bf16[2,784,128]{2,1,0:T(8,128)(2,1)S(1)}, u32[]{:S(2)}, u32[]{:S(2)}) collective-permute-start(bf16[2,784,128]{2,1,0:T(8,128)(2,1)S(1)} %collective-permute-done.18.refs_3_), channel_id=1, source_target_pairs={{0,4},{4,0},{8,12},{12,8},{16,20},{20,16},{24,28},{28,24},{1,5},{5... | collective-permute-start | bytes 1204232 | tf_op jit(solution)/shard_map/ppermute | solution.py:276
  (4 other events, 64.5 us)
